TPU v7x, 32 devices: a whole 2x2x4 slice. The times are simulated.
32 devices in a mesh: wide: 8 (over y, x, core), narrow: 4 (over z).
Axes of the slice: x: 2, y: 2, z: 4, core: 2. Of those that a mesh axis runs over, the one named last changes fastest.
Arguments:
- patches: bfloat16 [16384, 192], P(('wide', 'narrow')), may hold values from -6 to 6
- var_ids: int32 [48], replicated, may hold values from 0 to 47, each once
- segment_ids: int32 [32, 512], P(('wide', 'narrow')), may hold values from 0 to 3, never falling along the last dimension, each value on 1 to 256 neighbouring positions
- pad_mask: int32 [32, 512], P(('wide', 'narrow')), may hold values 0 or 1
- embed_weight: bfloat16 [192, 1024], P(None, 'narrow'), may hold values from -3 to 3
- var_embed: bfloat16 [48, 1024], P(None, 'narrow'), may hold values from -3 to 3
- agg_query: bfloat16 [1024], P('narrow'), may hold values from -6 to 6
- key_weight: bfloat16 [1024, 1024], P('narrow'), may hold values from -0.1875 to 0.1875
- value_weight: bfloat16 [1024, 1024], P('narrow'), may hold values from -0.1875 to 0.1875
- agg_out_weight: bfloat16 [1024, 1024], P('narrow'), may hold values from -0.75 to 0.75
- agg_out_bias: bfloat16 [1024], P('narrow'), may hold values from -3 to 3
- norm_one_gain: bfloat16 [1024], P('narrow'), may hold values from 0.5 to 1.5
- norm_one_bias: bfloat16 [1024], P('narrow'), may hold values from -2 to 2
- qkv_weight: bfloat16 [1024, 3072], P('narrow'), may hold values from -0.1875 to 0.1875
- attn_out_weight: bfloat16 [1024, 1024], P('narrow'), may hold values from -1.5 to 1.5
- attn_out_bias: bfloat16 [1024], P('narrow'), may hold values from -2 to 2
- norm_two_gain: bfloat16 [1024], P('narrow'), may hold values from 0.5 to 1.5
- norm_two_bias: bfloat16 [1024], P('narrow'), may hold values from -2 to 2
- mlp_in_weight: bfloat16 [1024, 4096], P('narrow'), may hold values from -0.1875 to 0.1875
- mlp_in_bias: bfloat16 [4096], P('narrow'), may hold values from -3 to 3
- mlp_out_weight: bfloat16 [4096, 1024], P('narrow'), may hold values from -0.125 to 0.125
- mlp_out_bias: bfloat16 [1024], P('narrow'), may hold values from -2 to 2
- cotangent: bfloat16 [16384, 1024], P(('wide', 'narrow')), may hold values from -16 to 16
Outputs:
- block_out: bfloat16 [16384, 1024], P(('wide', 'narrow'))
- patches_grad: float32 [16384, 192], P(('wide', 'narrow'))
- embed_weight_grad: float32 [192, 1024], P(None, 'narrow')
- var_embed_grad: float32 [48, 1024], P(None, 'narrow')
- agg_query_grad: float32 [1024], P('narrow')
- key_weight_grad: float32 [1024, 1024], P('narrow')
- value_weight_grad: float32 [1024, 1024], P('narrow')
- agg_out_weight_grad: float32 [1024, 1024], P('narrow')
- agg_out_bias_grad: float32 [1024], P('narrow')
- norm_one_gain_grad: float32 [1024], P('narrow')
- norm_one_bias_grad: float32 [1024], P('narrow')
- qkv_weight_grad: float32 [1024, 3072], P('narrow')
- attn_out_weight_grad: float32 [1024, 1024], P('narrow')
- attn_out_bias_grad: float32 [1024], P('narrow')
- norm_two_gain_grad: float32 [1024], P('narrow')
- norm_two_bias_grad: float32 [1024], P('narrow')
- mlp_in_weight_grad: float32 [1024, 4096], P('narrow')
- mlp_in_bias_grad: float32 [4096], P('narrow')
- mlp_out_weight_grad: float32 [4096, 1024], P('narrow')
- mlp_out_bias_grad: float32 [1024], P('narrow')
Inputs may be any that keep to these rules, and one draw needn't show every extreme that they name: `var_ids`: each of the 48 variables stands once. `segment_ids`: along each row the segment number never falls; a segment holds at most half of the 512 positions.
All inputs are finite; a program needn't handle non-finite values. No bound on the sum of `pad_mask` on one device may be relied on, other than what follows from the above.
Results may differ from a plain program's by a relative error of at most 0.02.
Values may be sent and summed in bfloat16 or wider, within the bound.
No kernel may reach another device: no remote copies, remote signals or barrier semaphores. Data moves between devices by JAX's collectives and lax.ppermute only.
A program may use at most 256 MiB of HBM per device.

v0:
```python
import jax
import jax.numpy as jnp
from jax import lax
from jax.sharding import PartitionSpec as P

D = 1024
HEADS = 16
HEAD_DIM = 64
VARS = 48
PIX = 4


norm_eps = 1e-06
masked_out = -1e30


def layer_norm(values, gain_row, shift_row):
    average = jnp.mean(values, axis=-1, keepdims=True)
    centered = values - average
    variance = jnp.mean(centered * centered, axis=-1, keepdims=True)
    return centered * lax.rsqrt(variance + norm_eps) * gain_row + shift_row


def exact_gelu(values):
    return jax.nn.gelu(values, approximate=False)


def embed_tokens(pixels, embed_table, offsets):
    embedded = jnp.einsum("tcj,cjd->tcd", pixels, embed_table, preferred_element_type=jnp.float32)
    return (embedded + offsets[None]).astype(jnp.bfloat16)


def attention_mask(segments, padding, start_row, block_rows):
    row_index = start_row + jnp.arange(block_rows, dtype=jnp.int32)
    key_index = jnp.arange(segments.shape[0], dtype=jnp.int32)
    same_doc = segments[:, None] == segments[None, :]
    return same_doc & ((padding[None, :] == 1) | (row_index[:, None] == key_index[None, :]))


def block_scores(query_block, keys_all, allowed):
    raw_scores = jnp.einsum(
        "qhe,khe->hqk", query_block, keys_all, preferred_element_type=jnp.float32
    ) * HEAD_DIM ** (-0.5)
    return jnp.where(allowed[None], raw_scores, masked_out)


def per_device(
    patches,
    var_ids,
    segment_ids,
    pad_mask,
    embed_weight,
    var_embed,
    agg_query,
    key_weight,
    value_weight,
    agg_out_weight,
    agg_out_bias,
    norm_one_gain,
    norm_one_bias,
    qkv_weight,
    attn_out_weight,
    attn_out_bias,
    norm_two_gain,
    norm_two_bias,
    mlp_in_weight,
    mlp_in_bias,
    mlp_out_weight,
    mlp_out_bias,
    cotangent,
):
    gathered = (
        lax.all_gather(embed_weight, "narrow", axis=1, tiled=True),
        lax.all_gather(var_embed, "narrow", axis=1, tiled=True),
        lax.all_gather(agg_query, "narrow", axis=0, tiled=True),
        lax.all_gather(key_weight, "narrow", axis=0, tiled=True),
        lax.all_gather(value_weight, "narrow", axis=0, tiled=True),
        lax.all_gather(agg_out_weight, "narrow", axis=0, tiled=True),
        lax.all_gather(agg_out_bias, "narrow", axis=0, tiled=True),
        lax.all_gather(norm_one_gain, "narrow", axis=0, tiled=True),
        lax.all_gather(norm_one_bias, "narrow", axis=0, tiled=True),
        lax.all_gather(qkv_weight, "narrow", axis=0, tiled=True),
        lax.all_gather(attn_out_weight, "narrow", axis=0, tiled=True),
        lax.all_gather(attn_out_bias, "narrow", axis=0, tiled=True),
        lax.all_gather(norm_two_gain, "narrow", axis=0, tiled=True),
        lax.all_gather(norm_two_bias, "narrow", axis=0, tiled=True),
        lax.all_gather(mlp_in_weight, "narrow", axis=0, tiled=True),
        lax.all_gather(mlp_in_bias, "narrow", axis=0, tiled=True),
        lax.all_gather(mlp_out_weight, "narrow", axis=0, tiled=True),
        lax.all_gather(mlp_out_bias, "narrow", axis=0, tiled=True),
    )
    row_count = patches.shape[0]
    scale_by = HEAD_DIM ** (-0.5)
    agg_rows = min(128, row_count)
    attn_rows = min(512, row_count)
    segments = segment_ids[0]
    padding = pad_mask[0]
    chooser = (var_ids[:, None] == jnp.arange(VARS, dtype=jnp.int32)[None, :]).astype(jnp.bfloat16)
    pixel_blocks = patches.reshape(row_count // agg_rows, agg_rows, VARS, PIX)
    embed_table = jnp.dot(
        chooser, gathered[0].reshape(VARS, PIX * D), preferred_element_type=jnp.float32
    )
    embed_table = embed_table.astype(jnp.bfloat16).reshape(VARS, PIX, D)
    offsets = jnp.dot(chooser, gathered[1], preferred_element_type=jnp.float32)
    key_query = jnp.sum(
        gathered[3].reshape(D, HEADS, HEAD_DIM).astype(jnp.float32)
        * gathered[2].reshape(1, HEADS, HEAD_DIM).astype(jnp.float32),
        axis=-1,
    ).astype(jnp.bfloat16)
    value_heads = gathered[4].reshape(D, HEADS, HEAD_DIM)

    def aggregate(pixels):
        tokens = embed_tokens(pixels, embed_table, offsets)
        var_scores = (
            jnp.einsum("tcd,dh->tch", tokens, key_query, preferred_element_type=jnp.float32)
            * scale_by
        )
        var_probs = jax.nn.softmax(var_scores, axis=1)
        pooled = jnp.einsum(
            "tch,tcd->thd",
            var_probs.astype(jnp.bfloat16),
            tokens,
            preferred_element_type=jnp.float32,
        ).astype(jnp.bfloat16)
        merged = jnp.einsum(
            "thd,dhe->the", pooled, value_heads, preferred_element_type=jnp.float32
        ).astype(jnp.bfloat16)
        return (var_probs, pooled, merged)

    var_probs, pooled, merged = lax.map(aggregate, pixel_blocks)
    pooled = pooled.reshape(row_count, HEADS, D)
    merged = merged.reshape(row_count, D)
    patch_state = jnp.dot(merged, gathered[5], preferred_element_type=jnp.float32) + gathered[
        6
    ].astype(jnp.float32)
    normed = layer_norm(
        patch_state, gathered[7].astype(jnp.float32), gathered[8].astype(jnp.float32)
    ).astype(jnp.bfloat16)
    project = jnp.dot(normed, gathered[9], preferred_element_type=jnp.float32).astype(jnp.bfloat16)
    queries = project[:, :D].reshape(row_count, HEADS, HEAD_DIM)
    keys_all = project[:, D : 2 * D].reshape(row_count, HEADS, HEAD_DIM)
    values_all = project[:, 2 * D :].reshape(row_count, HEADS, HEAD_DIM)
    query_blocks = queries.reshape(row_count // attn_rows, attn_rows, HEADS, HEAD_DIM)
    block_starts = jnp.arange(row_count // attn_rows, dtype=jnp.int32) * attn_rows

    def attend(block_in):
        query_block, start_row = block_in
        allowed = attention_mask(segments, padding, start_row, attn_rows)
        masked = block_scores(query_block, keys_all, allowed)
        biggest = jnp.max(masked, axis=-1, keepdims=True)
        raised = jnp.exp(masked - biggest)
        totals = jnp.sum(raised, axis=-1, keepdims=True)
        weights_block = (raised / totals).astype(jnp.bfloat16)
        output_block = jnp.einsum(
            "hqk,khe->qhe", weights_block, values_all, preferred_element_type=jnp.float32
        ).astype(jnp.bfloat16)
        return (output_block, biggest[..., 0] + jnp.log(totals[..., 0]))

    attended, log_totals = lax.map(attend, (query_blocks, block_starts))
    attended = attended.reshape(row_count, D)
    residual = (
        patch_state
        + jnp.dot(attended, gathered[10], preferred_element_type=jnp.float32)
        + gathered[11].astype(jnp.float32)
    )
    normed_two = layer_norm(
        residual, gathered[12].astype(jnp.float32), gathered[13].astype(jnp.float32)
    ).astype(jnp.bfloat16)
    hidden_pre = jnp.dot(normed_two, gathered[14], preferred_element_type=jnp.float32) + gathered[
        15
    ].astype(jnp.float32)
    hidden = exact_gelu(hidden_pre).astype(jnp.bfloat16)
    result = (
        residual
        + jnp.dot(hidden, gathered[16], preferred_element_type=jnp.float32)
        + gathered[17].astype(jnp.float32)
    ).astype(jnp.bfloat16)
    backward_w = (
        lax.all_gather(embed_weight, "narrow", axis=1, tiled=True),
        lax.all_gather(var_embed, "narrow", axis=1, tiled=True),
        lax.all_gather(agg_query, "narrow", axis=0, tiled=True),
        lax.all_gather(key_weight, "narrow", axis=0, tiled=True),
        lax.all_gather(value_weight, "narrow", axis=0, tiled=True),
        lax.all_gather(agg_out_weight, "narrow", axis=0, tiled=True),
        lax.all_gather(agg_out_bias, "narrow", axis=0, tiled=True),
        lax.all_gather(norm_one_gain, "narrow", axis=0, tiled=True),
        lax.all_gather(norm_one_bias, "narrow", axis=0, tiled=True),
        lax.all_gather(qkv_weight, "narrow", axis=0, tiled=True),
        lax.all_gather(attn_out_weight, "narrow", axis=0, tiled=True),
        lax.all_gather(attn_out_bias, "narrow", axis=0, tiled=True),
        lax.all_gather(norm_two_gain, "narrow", axis=0, tiled=True),
        lax.all_gather(norm_two_bias, "narrow", axis=0, tiled=True),
        lax.all_gather(mlp_in_weight, "narrow", axis=0, tiled=True),
        lax.all_gather(mlp_in_bias, "narrow", axis=0, tiled=True),
        lax.all_gather(mlp_out_weight, "narrow", axis=0, tiled=True),
        lax.all_gather(mlp_out_bias, "narrow", axis=0, tiled=True),
    )
    cot_float = cotangent.astype(jnp.float32)
    grad_mlp_out_w = jnp.einsum("tf,td->fd", hidden, cotangent, preferred_element_type=jnp.float32)
    grad_mlp_out_b = jnp.sum(cot_float, axis=0)
    hidden_grad = jnp.einsum(
        "td,fd->tf", cotangent, backward_w[16], preferred_element_type=jnp.float32
    )
    hidden_pre_grad = jax.vjp(exact_gelu, hidden_pre)[1](hidden_grad)[0].astype(jnp.bfloat16)
    grad_mlp_in_w = jnp.einsum(
        "td,tf->df", normed_two, hidden_pre_grad, preferred_element_type=jnp.float32
    )
    grad_mlp_in_b = jnp.sum(hidden_pre_grad.astype(jnp.float32), axis=0)
    normed_two_grad = jnp.einsum(
        "tf,df->td", hidden_pre_grad, backward_w[14], preferred_element_type=jnp.float32
    )
    pull_two = jax.vjp(
        layer_norm, residual, backward_w[12].astype(jnp.float32), backward_w[13].astype(jnp.float32)
    )[1]
    residual_grad, grad_norm_two_gain, grad_norm_two_bias = pull_two(normed_two_grad)
    residual_grad = residual_grad + cot_float
    branch_grad = residual_grad.astype(jnp.bfloat16)
    grad_attn_out_w = jnp.einsum(
        "td,te->de", attended, branch_grad, preferred_element_type=jnp.float32
    )
    grad_attn_out_b = jnp.sum(branch_grad.astype(jnp.float32), axis=0)
    attended_grad = jnp.einsum(
        "te,de->td", branch_grad, backward_w[10], preferred_element_type=jnp.float32
    )
    attended_grad = attended_grad.astype(jnp.bfloat16).reshape(
        row_count // attn_rows, attn_rows, HEADS, HEAD_DIM
    )

    def attend_back(running, block_in):
        key_grad, value_grad = running
        query_block, out_grad, log_block, start_row = block_in
        allowed = attention_mask(segments, padding, start_row, attn_rows)
        masked = block_scores(query_block, keys_all, allowed)
        prob_block = jnp.exp(masked - log_block[..., None])
        prob_grad = jnp.einsum(
            "qhe,khe->hqk", out_grad, values_all, preferred_element_type=jnp.float32
        )
        centre = jnp.sum(prob_block * prob_grad, axis=-1, keepdims=True)
        score_grad = jnp.where(allowed[None], prob_block * (prob_grad - centre), 0.0).astype(
            jnp.bfloat16
        )
        query_grad = (
            jnp.einsum("hqk,khe->qhe", score_grad, keys_all, preferred_element_type=jnp.float32)
            * scale_by
        )
        key_grad = (
            key_grad
            + jnp.einsum(
                "hqk,qhe->khe", score_grad, query_block, preferred_element_type=jnp.float32
            )
            * scale_by
        )
        value_grad = value_grad + jnp.einsum(
            "hqk,qhe->khe",
            prob_block.astype(jnp.bfloat16),
            out_grad,
            preferred_element_type=jnp.float32,
        )
        return ((key_grad, value_grad), query_grad)

    zero_heads = jnp.zeros((row_count, HEADS, HEAD_DIM), jnp.float32)
    (key_grad, value_grad), query_grad = lax.scan(
        attend_back,
        (zero_heads, zero_heads),
        (query_blocks, attended_grad, log_totals, block_starts),
    )
    project_grad = jnp.concatenate(
        [
            query_grad.reshape(row_count, D),
            key_grad.reshape(row_count, D),
            value_grad.reshape(row_count, D),
        ],
        axis=1,
    ).astype(jnp.bfloat16)
    grad_qkv_w = jnp.einsum("td,te->de", normed, project_grad, preferred_element_type=jnp.float32)
    normed_grad = jnp.einsum(
        "te,de->td", project_grad, backward_w[9], preferred_element_type=jnp.float32
    )
    pull_one = jax.vjp(
        layer_norm,
        patch_state,
        backward_w[7].astype(jnp.float32),
        backward_w[8].astype(jnp.float32),
    )[1]
    state_grad, grad_norm_one_gain, grad_norm_one_bias = pull_one(normed_grad)
    state_grad = (state_grad + residual_grad).astype(jnp.bfloat16)
    grad_agg_out_w = jnp.einsum("td,te->de", merged, state_grad, preferred_element_type=jnp.float32)
    grad_agg_out_b = jnp.sum(state_grad.astype(jnp.float32), axis=0)
    merged_grad = jnp.einsum(
        "te,de->td", state_grad, backward_w[5], preferred_element_type=jnp.float32
    )
    merged_grad = merged_grad.astype(jnp.bfloat16).reshape(row_count, HEADS, HEAD_DIM)
    grad_value_w = jnp.einsum(
        "thd,the->dhe", pooled, merged_grad, preferred_element_type=jnp.float32
    ).reshape(D, D)
    pooled_grad = jnp.einsum(
        "the,dhe->thd",
        merged_grad,
        backward_w[4].reshape(D, HEADS, HEAD_DIM),
        preferred_element_type=jnp.float32,
    ).astype(jnp.bfloat16)

    def aggregate_back(running, block_in):
        key_query_grad, table_grad, offset_grad = running
        pixels, prob_block, pooled_block = block_in
        tokens = embed_tokens(pixels, embed_table, offsets)
        prob_grad = jnp.einsum(
            "thd,tcd->tch", pooled_block, tokens, preferred_element_type=jnp.float32
        )
        centre = jnp.sum(prob_block * prob_grad, axis=1, keepdims=True)
        score_grad = (prob_block * (prob_grad - centre)).astype(jnp.bfloat16)
        token_grad = jnp.einsum(
            "tch,thd->tcd",
            prob_block.astype(jnp.bfloat16),
            pooled_block,
            preferred_element_type=jnp.float32,
        )
        token_grad = (
            token_grad
            + jnp.einsum("tch,dh->tcd", score_grad, key_query, preferred_element_type=jnp.float32)
            * scale_by
        ).astype(jnp.bfloat16)
        key_query_grad = (
            key_query_grad
            + jnp.einsum("tcd,tch->dh", tokens, score_grad, preferred_element_type=jnp.float32)
            * scale_by
        )
        table_grad = table_grad + jnp.einsum(
            "tcj,tcd->cjd", pixels, token_grad, preferred_element_type=jnp.float32
        )
        offset_grad = offset_grad + jnp.sum(token_grad.astype(jnp.float32), axis=0)
        pixel_grad = jnp.einsum(
            "tcd,cjd->tcj", token_grad, embed_table, preferred_element_type=jnp.float32
        )
        return (
            (key_query_grad, table_grad, offset_grad),
            pixel_grad.reshape(pixels.shape[0], VARS * PIX),
        )

    start_sums = (
        jnp.zeros((D, HEADS), jnp.float32),
        jnp.zeros((VARS, PIX, D), jnp.float32),
        jnp.zeros((VARS, D), jnp.float32),
    )
    (key_query_grad, table_grad, offset_grad), pixel_grad = lax.scan(
        aggregate_back,
        start_sums,
        (pixel_blocks, var_probs, pooled_grad.reshape(row_count // agg_rows, agg_rows, HEADS, D)),
    )
    chooser_float = chooser.astype(jnp.float32)
    grad_embed_w = jnp.einsum(
        "cv,cx->vx",
        chooser_float,
        table_grad.reshape(VARS, PIX * D),
        precision=lax.Precision.HIGHEST,
    ).reshape(VARS * PIX, D)
    grad_var_embed = jnp.einsum(
        "cv,cd->vd", chooser_float, offset_grad, precision=lax.Precision.HIGHEST
    )
    grad_agg_query = jnp.sum(
        key_query_grad[:, :, None] * backward_w[3].reshape(D, HEADS, HEAD_DIM).astype(jnp.float32),
        axis=0,
    ).reshape(D)
    shard_sums = (
        lax.psum_scatter(
            grad_embed_w.astype(jnp.bfloat16), "narrow", scatter_dimension=1, tiled=True
        ).astype(jnp.float32),
        lax.psum_scatter(
            grad_var_embed.astype(jnp.bfloat16), "narrow", scatter_dimension=1, tiled=True
        ).astype(jnp.float32),
        lax.psum_scatter(
            grad_agg_query.astype(jnp.bfloat16), "narrow", scatter_dimension=0, tiled=True
        ).astype(jnp.float32),
        lax.psum_scatter(
            key_query_grad.astype(jnp.bfloat16), "narrow", scatter_dimension=0, tiled=True
        ).astype(jnp.float32),
        lax.psum_scatter(
            grad_value_w.astype(jnp.bfloat16), "narrow", scatter_dimension=0, tiled=True
        ).astype(jnp.float32),
        lax.psum_scatter(
            grad_agg_out_w.astype(jnp.bfloat16), "narrow", scatter_dimension=0, tiled=True
        ).astype(jnp.float32),
        lax.psum_scatter(
            grad_agg_out_b.astype(jnp.bfloat16), "narrow", scatter_dimension=0, tiled=True
        ).astype(jnp.float32),
        lax.psum_scatter(
            grad_norm_one_gain.astype(jnp.bfloat16), "narrow", scatter_dimension=0, tiled=True
        ).astype(jnp.float32),
        lax.psum_scatter(
            grad_norm_one_bias.astype(jnp.bfloat16), "narrow", scatter_dimension=0, tiled=True
        ).astype(jnp.float32),
        lax.psum_scatter(
            grad_qkv_w.astype(jnp.bfloat16), "narrow", scatter_dimension=0, tiled=True
        ).astype(jnp.float32),
        lax.psum_scatter(
            grad_attn_out_w.astype(jnp.bfloat16), "narrow", scatter_dimension=0, tiled=True
        ).astype(jnp.float32),
        lax.psum_scatter(
            grad_attn_out_b.astype(jnp.bfloat16), "narrow", scatter_dimension=0, tiled=True
        ).astype(jnp.float32),
        lax.psum_scatter(
            grad_norm_two_gain.astype(jnp.bfloat16), "narrow", scatter_dimension=0, tiled=True
        ).astype(jnp.float32),
        lax.psum_scatter(
            grad_norm_two_bias.astype(jnp.bfloat16), "narrow", scatter_dimension=0, tiled=True
        ).astype(jnp.float32),
        lax.psum_scatter(
            grad_mlp_in_w.astype(jnp.bfloat16), "narrow", scatter_dimension=0, tiled=True
        ).astype(jnp.float32),
        lax.psum_scatter(
            grad_mlp_in_b.astype(jnp.bfloat16), "narrow", scatter_dimension=0, tiled=True
        ).astype(jnp.float32),
        lax.psum_scatter(
            grad_mlp_out_w.astype(jnp.bfloat16), "narrow", scatter_dimension=0, tiled=True
        ).astype(jnp.float32),
        lax.psum_scatter(
            grad_mlp_out_b.astype(jnp.bfloat16), "narrow", scatter_dimension=0, tiled=True
        ).astype(jnp.float32),
    )
    summed = lax.psum(
        (
            shard_sums[0],
            shard_sums[1],
            shard_sums[2],
            shard_sums[3],
            shard_sums[4],
            shard_sums[5],
            shard_sums[6],
            shard_sums[7],
            shard_sums[8],
            shard_sums[9],
            shard_sums[10],
            shard_sums[11],
            shard_sums[12],
            shard_sums[13],
            shard_sums[14],
            shard_sums[15],
            shard_sums[16],
            shard_sums[17],
        ),
        "wide",
    )
    grad_key_w = (
        jnp.repeat(summed[3], HEAD_DIM, axis=1) * backward_w[2].astype(jnp.float32)[None, :]
    )
    return (
        result,
        pixel_grad.reshape(row_count, VARS * PIX),
        summed[0],
        summed[1],
        summed[2],
        grad_key_w,
        summed[4],
        summed[5],
        summed[6],
        summed[7],
        summed[8],
        summed[9],
        summed[10],
        summed[11],
        summed[12],
        summed[13],
        summed[14],
        summed[15],
        summed[16],
        summed[17],
    )


def solution(mesh):
    return jax.shard_map(
        per_device,
        mesh=mesh,
        in_specs=(
            P(("wide", "narrow"), None),
            P(),
            P(("wide", "narrow"), None),
            P(("wide", "narrow"), None),
            P(None, "narrow"),
            P(None, "narrow"),
            P("narrow"),
            P("narrow", None),
            P("narrow", None),
            P("narrow", None),
            P("narrow"),
            P("narrow"),
            P("narrow"),
            P("narrow", None),
            P("narrow", None),
            P("narrow"),
            P("narrow"),
            P("narrow"),
            P("narrow", None),
            P("narrow"),
            P("narrow", None),
            P("narrow"),
            P(("wide", "narrow"), None),
        ),
        out_specs=(
            P(("wide", "narrow"), None),
            P(("wide", "narrow"), None),
            P(None, "narrow"),
            P(None, "narrow"),
            P("narrow"),
            P("narrow", None),
            P("narrow", None),
            P("narrow", None),
            P("narrow"),
            P("narrow"),
            P("narrow"),
            P("narrow", None),
            P("narrow", None),
            P("narrow"),
            P("narrow"),
            P("narrow"),
            P("narrow", None),
            P("narrow"),
            P("narrow", None),
            P("narrow"),
        ),
        check_vma=False,
    )
```

profile of v0, /device:TPU:0, one launch (start us, length us, event | category | flops | bytes accessed | tf_op | source)
XLA Modules:
  0.0 2079.5 jit_solution(6210996134657133553)
XLA Ops:
  13.7 12.6 all-gather
  26.3 7.7 all-gather.6
  34.0 10.1 all-gather.5
  44.2 7.8 all-gather.4
  52.0 9.4 all-gather.3
  61.4 7.7 all-gather.2
  69.1 9.5 all-gather.1
  78.7 14.4 all_gather.79
  93.7 14.1 all_gather.65
  107.9 14.3 all_gather.64
  130.0 134.4 %while.7 = (s32[]{:T(128)}, f32[4,128,48,16]{1,3,2,0:T(8,128)}, bf16[4,128,16,1024]{3,2,1,0:T(8,128)(2,1)}, bf16[4,128,16,64]{1,3,2,0:T(8,128)(2,1)}, bf16[4,128...) while((s32[]{:T(128)}, f32[4,128,48,16]{1,3,2,0:T(8,128)}, ...), condition=%wide.region_4.5_spmd, body=%wide.region_1.4_spmd.sunk | while | flops 737112064 | bytes 114892984 | solution.py:130
  140.0 20.3 bitcast_dynamic-update-slice_fusion.5
  173.5 20.3 bitcast_dynamic-update-slice_fusion.5
  206.9 20.4 bitcast_dynamic-update-slice_fusion.5
  240.4 20.3 bitcast_dynamic-update-slice_fusion.5
  273.4 7.0 convolution_convert_fusion.6
  287.4 7.5 fusion.114
  294.9 8.3 fusion.52
  303.3 8.8 fusion.79
  312.1 6.9 all-gather.24.cloned.1.call-done
  324.0 144.8 %all-gather.26.cloned.1.call-done = bf16[1024,4096]{1,0:T(8,128)(2,1)} async-done(((bf16[256,4096]{1,0:T(8,128)(2,1)}), bf16[1024,4096]{1,0:T(8,128)(2,1)}) %all-gather.26.cloned.1.call-update) | async-done | bytes 8388624 | tf_op jit(solution)/shard_map/all_gather | solution.py:87
  468.8 12.3 fusion.103
  481.1 137.1 %all-gather.28.cloned.1.call-done = bf16[4096,1024]{1,0:T(8,128)(2,1)} async-done(((bf16[1024,1024]{1,0:T(8,128)(2,1)}), bf16[4096,1024]{1,0:T(8,128)(2,1)}) %all-gather.28.cloned.1.call-update) | async-done | bytes 8388624 | tf_op jit(solution)/shard_map/all_gather | solution.py:89
  618.3 28.3 %fusion.105 = (bf16[4096]{0:T(1024)(128)(2,1)}, bf16[512,4096]{1,0:T(8,128)(2,1)S(1)}, f32[512,4096]{1,0:T(8,128)}) fusion(f32[512,4096]{1,0:T(8,128)} %fusion.103, f32[4096]{0:T(1024)S(1)} %copy-done.44, bf16[512,1024]{1,0:T(8,128)(2,1)S(1)} %copy-done.29, bf16[4096,1024]{1,0:T(8,128)(2,1)} %all-gather.28.cloned.1.call-done), kind=kOutput, calls=%fused_computation.169 | convolution fusion | flops 4450152448 | bytes 30433280 | tf_op jit(solution)/shard_map/td,fd->tf/dot_general | solution.py:201
  659.9 9.4 fusion.118
  669.2 9.4 fusion.80
  678.7 24.2 %multiply_convert_fusion.2 = bf16[16,64,512]{2,1,0:T(8,128)(2,1)} fusion(bf16[512,16,64]{0,2,1:T(8,128)(2,1)} %bitcast.243, f32[16,512,512]{1,2,0:T(8,128)} %fusion.118, f32[16,512,512]{1,2,0:T(8,128)} %get-tuple-element.419, f32[16,512]{1,0:T(8,128)S(1)} %log_add_fusion, pred[512,512]{0,1:T(8,128)(4,1)S(1)} %fusion.89), kind=kOutput, calls=%fused_computation.105 | convolution fusion | flops 567288320 | bytes 35946496 | tf_op jit(solution)/shard_map/while/body/eval_jaxpr/hqk,khe->qhe/dot_general | solution.py:243
  702.9 23.6 %multiply_convert_fusion.1 = bf16[16,64,512]{2,1,0:T(8,128)(2,1)} fusion(bf16[512,16,64]{0,2,1:T(8,128)(2,1)S(1)} %bitcast.241, f32[16,512,512]{1,2,0:T(8,128)} %fusion.118, f32[16,512,512]{1,2,0:T(8,128)} %get-tuple-element.419, f32[16,512]{1,0:T(8,128)S(1)} %log_add_fusion, pred[512,512]{0,1:T(8,128)(4,1)S(1)} %fusion.89), kind=kOutput, calls=%fused_computation.104 | convolution fusion | flops 567288320 | bytes 35946496 | tf_op jit(solution)/shard_map/while/body/eval_jaxpr/hqk,qhe->khe/dot_general | solution.py:248
  726.5 8.2 multiply_reduce_fusion.3
  741.5 9.6 convolution_convert_fusion
  751.1 420.5 %while.8 = (s32[]{:T(128)}, f32[1024,16]{0,1:T(8,128)}, f32[48,4,1024]{2,1,0:T(4,128)}, f32[48,1024]{1,0:T(8,128)S(1)}, f32[4,128,192]{1,0,2:T(4,128)}, /*index=...) while((s32[]{:T(128)}, f32[1024,16]{0,1:T(8,128)}, ...), condition=%wide.region_19.20_spmd.clone, body=%wide.region_16.19_spmd.clone.sunk | while | flops 1001322496 | bytes 207667440 | solution.py:345
  761.5 20.3 fusion.219
  789.3 10.1 fusion.222
  799.4 18.1 convert_reduce_fusion.3
  817.6 13.0 fusion.224
  830.6 18.3 fusion.223
  866.0 20.3 fusion.219
  893.6 10.1 fusion.222
  903.7 18.1 convert_reduce_fusion.3
  921.9 13.0 fusion.224
  935.0 18.5 fusion.223
  970.4 20.3 fusion.219
  998.2 10.1 fusion.222
  1008.3 18.1 convert_reduce_fusion.3
  1026.5 13.0 fusion.224
  1039.5 18.3 fusion.223
  1075.0 20.3 fusion.219
  1102.6 10.1 fusion.222
  1112.7 18.1 convert_reduce_fusion.3
  1130.9 13.0 fusion.224
  1143.9 18.5 fusion.223
  1182.2 25.3 %fusion.72 = bf16[16,64,1024]{2,1,0:T(8,128)(2,1)} fusion(bf16[512,16,64]{0,2,1:T(8,128)(2,1)S(1)} %bitcast.239, bf16[512,16,1024]{2,1,0:T(8,128)(2,1)} %bitcast.276), kind=kOutput, calls=%fused_computation.114 | convolution fusion | flops 1074790400 | bytes 19922944 | tf_op jit(solution)/shard_map/thd,the->dhe/dot_general | solution.py:293
  1215.8 8.4 convolution_convert_fusion.3
  1225.8 9.2 convolution_convert_fusion.2
  1235.8 8.3 multiply_convert_fusion
  1255.4 8.1 all-gather.7
  1264.9 18.6 all-reduce.10
  1283.9 11.0 add_convert_fusion.5
  1294.9 28.0 %reduce-scatter.16.cloned.1.call-done = bf16[256,1024]{1,0:T(8,128)(2,1)} async-done(((bf16[1024,1024]{1,0:T(8,128)(2,1)}), bf16[256,1024]{1,0:T(8,128)(2,1)}) %reduce-scatter.16.cloned.1.call-update) | async-done | bytes 524304 | tf_op jit(solution)/shard_map/reduce_scatter | solution.py:377
  1322.9 46.2 %reduce-scatter.18.cloned.1.call-done = bf16[256,1024]{1,0:T(8,128)(2,1)} async-done(((bf16[1024,1024]{1,0:T(8,128)(2,1)}), bf16[256,1024]{1,0:T(8,128)(2,1)}) %reduce-scatter.18.cloned.1.call-update) | async-done | bytes 524304 | tf_op jit(solution)/shard_map/reduce_scatter | solution.py:380
  1369.1 112.3 %reduce-scatter.20.cloned.1.call-done = bf16[256,3072]{1,0:T(8,128)(2,1)} async-done(((bf16[1024,3072]{1,0:T(8,128)(2,1)}), bf16[256,3072]{1,0:T(8,128)(2,1)}) %reduce-scatter.20.cloned.1.call-update) | async-done | bytes 1572880 | tf_op jit(solution)/shard_map/reduce_scatter | solution.py:392
  1481.4 147.2 %reduce-scatter.24.cloned.1.call-done = bf16[256,4096]{1,0:T(8,128)(2,1)} async-done(((bf16[1024,4096]{1,0:T(8,128)(2,1)}), bf16[256,4096]{1,0:T(8,128)(2,1)}) %reduce-scatter.24.cloned.1.call-update) | async-done | bytes 2097168 | tf_op jit(solution)/shard_map/reduce_scatter | solution.py:407
  1628.6 147.4 %reduce-scatter.26.cloned.1.call-done = bf16[1024,1024]{1,0:T(8,128)(2,1)} async-done(((bf16[4096,1024]{1,0:T(8,128)(2,1)}), bf16[1024,1024]{1,0:T(8,128)(2,1)}) %reduce-scatter.26.cloned.1.call-update) | async-done | bytes 2097168 | tf_op jit(solution)/shard_map/reduce_scatter | solution.py:413
  1776.1 295.1 %all-reduce.12 = (f32[192,256]{1,0:T(8,128)}, f32[48,256]{1,0:T(8,128)}, f32[256]{0:T(256)}, f32[256,16]{0,1:T(8,128)S(1)}, f32[256,1024]{1,0:T(8,128)}, /*index...) all-reduce(bf16[192,256]{1,0:T(8,128)(2,1)} %reduce-scatter.10.clon, ...), channel_id=1, replica_groups=mesh['wide'=8,'narrow'=4] {'wide'}, use_global_device_ids=true, to_apply=%region_21.22 | all-reduce | flops 3738624 | bytes 22437888 | tf_op jit(solution)/shard_map/psum | solution.py:420
  (407 shorter events, 228.2 us)
Async XLA Ops:
  7.3 71.5 %copy-start.77 = (bf16[1024]{0:T(1024)(128)(2,1)S(1)}, bf16[1024]{0:T(1024)(128)(2,1)}, u32[]{:S(2)}) copy-start(bf16[1024]{0:T(1024)(128)(2,1)} %param.46) | copy-start | bytes 6148
  7.3 86.4 %copy-start.48 = (bf16[48,256]{1,0:T(8,128)(2,1)S(1)}, bf16[48,256]{1,0:T(8,128)(2,1)}, u32[]{:S(2)}) copy-start(bf16[48,256]{1,0:T(8,128)(2,1)} %param.32) | copy-start | bytes 73732
  7.3 100.5 %copy-start.42 = (bf16[512,192]{0,1:T(8,128)(2,1)S(1)}, bf16[512,192]{0,1:T(8,128)(2,1)}, u32[]{:S(2)}) copy-start(bf16[512,192]{0,1:T(8,128)(2,1)} %param.27) | copy-start | bytes 589828
  7.3 100.6 %copy-start.43 = (bf16[192,256]{1,0:T(8,128)(2,1)S(1)}, bf16[192,256]{1,0:T(8,128)(2,1)}, u32[]{:S(2)}) copy-start(bf16[192,256]{1,0:T(8,128)(2,1)} %param.31) | copy-start | bytes 294916
  7.3 115.1 %copy-start.71 = (s32[48]{0:T(128)S(1)}, s32[48]{0:T(128)}, u32[]{:S(2)}) copy-start(s32[48]{0:T(128)} %param.28) | copy-start | bytes 580
  7.3 116.2 %all-gather.18.cloned.1.call-start = ((), (), s32[]{:S(2)}) async-start(), calls=%async_computation.10 | async-start | bytes 2621440 | tf_op jit(solution)/shard_map/all_gather | solution.py:77
  8.1 115.2 %copy-start.62 = (s32[1,512]{1,0:T(1,128)S(1)}, s32[1,512]{1,0:T(1,128)}, u32[]{:S(2)}) copy-start(s32[1,512]{1,0:T(1,128)} %param.29) | copy-start | bytes 6148
  8.1 119.4 %all-gather.16.cloned.1.call-start = ((), (), s32[]{:S(2)}) async-start(), calls=%async_computation.9 | async-start | bytes 2621440 | tf_op jit(solution)/shard_map/all_gather | solution.py:76
  10.2 256.7 %all-gather.20.cloned.1.call-start = ((), (), s32[]{:S(2)}) async-start(), calls=%async_computation.11 | async-start | bytes 2621440 | tf_op jit(solution)/shard_map/all_gather | solution.py:78
  10.9 262.4 %all-gather.22.cloned.1.call-start = ((), (), s32[]{:S(2)}) async-start(), calls=%async_computation.12 | async-start | bytes 7864320 | tf_op jit(solution)/shard_map/all_gather | solution.py:82
  11.5 307.5 %all-gather.24.cloned.1.call-start = ((), (), s32[]{:S(2)}) async-start(), calls=%async_computation.13 | async-start | bytes 2621440 | tf_op jit(solution)/shard_map/all_gather | solution.py:83
  12.1 456.7 %all-gather.26.cloned.1.call-start = ((), (), s32[]{:S(2)}) async-start(), calls=%async_computation.14 | async-start | bytes 10485760 | tf_op jit(solution)/shard_map/all_gather | solution.py:87
  12.7 605.6 %all-gather.28.cloned.1.call-start = ((), (), s32[]{:S(2)}) async-start(), calls=%async_computation.15 | async-start | bytes 10485760 | tf_op jit(solution)/shard_map/all_gather | solution.py:89
  13.4 1281.5 %reduce-scatter.14.cloned.1.call-start = ((), (), s32[]{:S(2)}) async-start(), calls=%async_computation.18 | async-start | bytes 40960 | tf_op jit(solution)/shard_map/reduce_scatter | solution.py:374
  26.3 103.7 %copy-start.46 = (bf16[4,1,256]{2,1,0:T(2,128)(2,1)}, bf16[4,1,256]{2,1,0:T(2,128)(2,1)S(1)}, u32[]{:S(2)}) copy-start(bf16[4,1,256]{2,1,0:T(2,128)(2,1)S(1)} %all-gather) | copy-start | bytes 6148
  34.0 434.8 %copy-start.73 = (f32[4,1,256]{2,1,0:T(1,128)}, f32[4,1,256]{2,1,0:T(1,128)S(1)}, u32[]{:S(2)}) copy-start(f32[4,1,256]{2,1,0:T(1,128)S(1)} %convert_element_type.341) | copy-start | bytes 12292
  44.2 607.9 %copy-start.59 = (f32[4,1,256]{2,1,0:T(1,128)}, f32[4,1,256]{2,1,0:T(1,128)S(1)}, u32[]{:S(2)}) copy-start(f32[4,1,256]{2,1,0:T(1,128)S(1)} %convert_element_type.340) | copy-start | bytes 12292
  61.4 211.9 %copy-start.75 = (f32[4,1,256]{2,1,0:T(1,128)}, f32[4,1,256]{2,1,0:T(1,128)S(1)}, u32[]{:S(2)}) copy-start(f32[4,1,256]{2,1,0:T(1,128)S(1)} %convert_element_type.338) | copy-start | bytes 12292
  69.1 204.2 %copy-start.56 = (f32[4,1,256]{2,1,0:T(1,128)}, f32[4,1,256]{2,1,0:T(1,128)S(1)}, u32[]{:S(2)}) copy-start(f32[4,1,256]{2,1,0:T(1,128)S(1)} %convert_element_type.337) | copy-start | bytes 12292
  78.6 656.1 %copy-start.40 = (f32[4,1,256]{2,1,0:T(1,128)}, f32[4,1,256]{2,1,0:T(1,128)S(1)}, u32[]{:S(2)}) copy-start(f32[4,1,256]{2,1,0:T(1,128)S(1)} %convert_element_type.336) | copy-start | bytes 12292
  140.0 20.3 copy-start.13
  173.5 20.3 copy-start.13
  206.9 20.4 copy-start.13
  240.4 20.3 copy-start.13
  264.4 15.9 copy-start.2
  264.4 15.9 copy-start.6
  264.4 15.9 copy-start.20
  264.4 15.9 copy-start.33
  266.8 13.5 copy-start.22
  287.4 15.8 copy-start.28
  303.3 15.7 copy-start.9
  322.3 329.8 %copy-start.52 = (f32[512]{0:T(512)}, f32[512]{0:T(512)S(1)}, u32[]{:S(2)}) copy-start(f32[512]{0:T(512)S(1)} %broadcast_multiply_fusion) | copy-start | bytes 6148
  324.0 328.1 %copy-start.68 = (f32[512]{0:T(512)}, f32[512]{0:T(512)S(1)}, u32[]{:S(2)}) copy-start(f32[512]{0:T(512)S(1)} %fusion.98) | copy-start | bytes 6148
  468.8 149.5 %copy-start.29 = (bf16[512,1024]{1,0:T(8,128)(2,1)S(1)}, bf16[512,1024]{1,0:T(8,128)(2,1)}, u32[]{:S(2)}) copy-start(bf16[512,1024]{1,0:T(8,128)(2,1)} %param.49) | copy-start | bytes 3145732
  468.8 149.5 %copy-start.44 = (f32[4096]{0:T(1024)S(1)}, f32[4096]{0:T(1024)}, u32[]{:S(2)}) copy-start(f32[4096]{0:T(1024)} %convert_element_type.283) | copy-start | bytes 49156
  618.2 28.3 %copy-start.17 = (f32[512,1024]{1,0:T(8,128)S(1)}, f32[512,1024]{1,0:T(8,128)}, u32[]{:S(2)}) copy-start(f32[512,1024]{1,0:T(8,128)} %copy-done.16) | copy-start | bytes 6291460
  618.2 28.3 %copy-start.83 = (bf16[1024,4096]{1,0:T(8,128)(2,1)S(1)}, bf16[1024,4096]{1,0:T(8,128)(2,1)}, u32[]{:S(2)}) copy-start(bf16[1024,4096]{1,0:T(8,128)(2,1)} %all-gather.26.cloned.1.call-done) | copy-start | bytes 25165828
  678.7 24.2 %copy-start.26 = (bf16[512,1024]{0,1:T(8,128)(2,1)S(1)}, bf16[512,1024]{0,1:T(8,128)(2,1)}, u32[]{:S(2)}) copy-start(bf16[512,1024]{0,1:T(8,128)(2,1)} %copy-done.25) | copy-start | bytes 3145732
  702.9 23.6 %copy-start.50 = (f32[512]{0:T(512)S(1)}, f32[512]{0:T(512)}, u32[]{:S(2)}) copy-start(f32[512]{0:T(512)} %copy-done.49) | copy-start | bytes 6148
  702.9 23.6 %copy-start.57 = (f32[4,1,256]{2,1,0:T(1,128)S(1)}, f32[4,1,256]{2,1,0:T(1,128)}, u32[]{:S(2)}) copy-start(f32[4,1,256]{2,1,0:T(1,128)} %copy-done.56) | copy-start | bytes 12292
  702.9 23.6 %copy-start.66 = (f32[512]{0:T(512)S(1)}, f32[512]{0:T(512)}, u32[]{:S(2)}) copy-start(f32[512]{0:T(512)} %copy-done.65) | copy-start | bytes 6148
  751.1 422.1 %copy-start.72 = (s32[48]{0:T(128)S(1)}, s32[48]{0:T(128)}, u32[]{:S(2)}) copy-start(s32[48]{0:T(128)} %param.28) | copy-start | bytes 580
  761.5 20.3 copy-start.1
  817.6 13.0 copy-start.4
  866.0 20.3 copy-start.1
  921.9 13.0 copy-start.4
  970.4 20.3 copy-start.1
  1026.5 13.0 copy-start.4
  1075.0 20.3 copy-start.1
  1130.9 13.0 copy-start.4
  1173.2 121.7 %reduce-scatter.12.cloned.1.call-start = ((), (), s32[]{:S(2)}) async-start(), calls=%async_computation.17 | async-start | bytes 122880 | tf_op jit(solution)/shard_map/reduce_scatter | solution.py:368
  1175.8 119.1 %reduce-scatter.10.cloned.1.call-start = ((), (), s32[]{:S(2)}) async-start(), calls=%async_computation.16 | async-start | bytes 491520 | tf_op jit(solution)/shard_map/reduce_scatter | solution.py:365
  1177.5 117.4 %reduce-scatter.22.cloned.1.call-start = ((), (), s32[]{:S(2)}) async-start(), calls=%async_computation.22 | async-start | bytes 2621440 | tf_op jit(solution)/shard_map/reduce_scatter | solution.py:395
  1181.8 141.2 %reduce-scatter.16.cloned.1.call-start = ((), (), s32[]{:S(2)}) async-start(), calls=%async_computation.19 | async-start | bytes 2621440 | tf_op jit(solution)/shard_map/reduce_scatter | solution.py:377
  1211.7 157.5 %reduce-scatter.18.cloned.1.call-start = ((), (), s32[]{:S(2)}) async-start(), calls=%async_computation.20 | async-start | bytes 2621440 | tf_op jit(solution)/shard_map/reduce_scatter | solution.py:380
  1215.7 265.7 %reduce-scatter.20.cloned.1.call-start = ((), (), s32[]{:S(2)}) async-start(), calls=%async_computation.21 | async-start | bytes 7864320 | tf_op jit(solution)/shard_map/reduce_scatter | solution.py:392
  1224.2 404.4 %reduce-scatter.24.cloned.1.call-start = ((), (), s32[]{:S(2)}) async-start(), calls=%async_computation.23 | async-start | bytes 10485760 | tf_op jit(solution)/shard_map/reduce_scatter | solution.py:407
  1235.1 541.0 %reduce-scatter.26.cloned.1.call-start = ((), (), s32[]{:S(2)}) async-start(), calls=%async_computation.24 | async-start | bytes 10485760 | tf_op jit(solution)/shard_map/reduce_scatter | solution.py:413
  1252.9 12.0 copy-start.61
  1252.9 12.0 copy-start.63
  1252.9 12.0 copy-start.64
  1252.9 12.0 copy-start.70
  1252.9 12.0 copy-start.78
  1252.9 12.0 copy-start.79
  (62 other events, 333.3 us)
Sparse Core Ops, SparseCore 0:
  9.7 48.8 all-gather.17
  60.8 49.8 all-gather.15
  112.2 44.4 all-gather.19
  158.1 115.1 all-gather.21
  274.8 44.1 all-gather.23
  320.4 148.3 all-gather.25
  470.3 147.8 all-gather.27
  1173.3 17.1 reduce-scatter.13
  1193.4 17.2 reduce-scatter.11
  1212.8 18.7 reduce-scatter.9
  1234.0 42.6 reduce-scatter.21
  1279.4 43.4 reduce-scatter.15
  1325.9 43.1 reduce-scatter.17
  1371.3 110.0 reduce-scatter.19
  1483.6 144.9 reduce-scatter.23
  1630.8 145.1 reduce-scatter.25
where the time goes:
time: 2080 us
  waiting for transfers between devices  775 us (37%)
  matrix products  718 us (35%)
  blocking collectives  429 us (21%)
  local copies, waits for them, and re-layouts  90.5 us (4%)
  other arithmetic  32.7 us (2%)
    psum x1, blocking collectives, per_device(): lax.psum((shard_sums[0], shard_sums[1], shard_sums[2], shard_sums[3], sha...  295 us
    reduce_scatter x1, waiting for transfers between devices, per_device(): lax.psum_scatter(grad_mlp_out_w.astype(jnp.bfloat16), 'narrow', scatter_d...  147 us
    reduce_scatter x1, waiting for transfers between devices, per_device(): lax.psum_scatter(grad_mlp_in_w.astype(jnp.bfloat16), 'narrow', scatter_di...  147 us
    all_gather x1, waiting for transfers between devices, per_device(): lax.all_gather(mlp_in_weight, 'narrow', axis=0, tiled=True)  145 us
    all_gather x1, waiting for transfers between devices, per_device(): lax.all_gather(mlp_out_weight, 'narrow', axis=0, tiled=True)  137 us
    reduce_scatter x1, waiting for transfers between devices, per_device(): lax.psum_scatter(grad_qkv_w.astype(jnp.bfloat16), 'narrow', scatter_dimen...  112 us
    dot_general x4, matrix products, aggregate(): jnp.einsum('tch,tcd->thd', var_probs.astype(jnp.bfloat16), tokens, prefer...  81.2 us
    dot_general x4, matrix products, aggregate_back(): jnp.einsum('thd,tcd->tch', pooled_block, tokens, preferred_element_type=j...  81.2 us
  transfers between devices with their start and end apart: 16, of which 9 were waited for; matrix products, arithmetic and copies ran while one was open for 14% of the time, Pallas kernels for 0%

commit v1 on v0

v1 whole, which is shorter than its diff:
```python
import functools

import jax
import jax.numpy as jnp
import numpy as np
from jax import lax
from jax.experimental import pallas as pl
from jax.experimental.pallas import tpu as pltpu
from jax.sharding import PartitionSpec as P

D = 1024
HEADS = 16
HEAD_DIM = 64
VARS = 48
PIX = 4
PATCH_COLS = VARS * PIX
COLS = 256
PAIRS = HEADS // 2
SUB = 8

norm_eps = 1e-06
masked_out = -1e30
scale_by = HEAD_DIM ** (-0.5)
f32 = jnp.float32
bf16 = jnp.bfloat16
MB = 1 << 20


def dot(a, b):
    return jnp.dot(a, b, preferred_element_type=f32)


def dot_nt(a, b):
    return lax.dot_general(a, b, (((1,), (1,)), ((), ())), preferred_element_type=f32)


def dot_tn(a, b):
    return lax.dot_general(a, b, (((0,), (0,)), ((), ())), preferred_element_type=f32)


def split_two(a):
    high = a.astype(bf16)
    return high, (a - high.astype(f32)).astype(bf16)


def swap_wide(a, bits):
    size = lax.axis_size("wide")
    return lax.ppermute(a, "wide", [(i, i ^ bits) for i in range(size)])


def turn_narrow(a, by):
    size = lax.axis_size("narrow")
    return lax.ppermute(a, "narrow", [(i, (i + by) % size) for i in range(size)])


def take(a, at, axis):
    return lax.dynamic_index_in_dim(a, at, axis, keepdims=False)


def spread_plane(piece):
    half = piece.shape[-2] // 2
    from_x = swap_wide(piece, 2)
    from_y = swap_wide(piece, 4)
    low = swap_wide(from_x[..., :half, :], 4)
    high = swap_wide(from_y[..., half:, :], 2)
    here = [(0, 0, piece), (2, 0, from_x), (4, 0, from_y), (6, 0, low), (6, half, high)]
    there = [(bits | 1, start, swap_wide(part, 1)) for bits, start, part in here]
    return here + there


def assemble_kernel(layout, n_shards, n_parts, spot, *refs):
    shards = refs[:n_shards]
    parts = refs[n_shards : n_shards + n_parts]
    fulls = refs[n_shards + n_parts : 2 * n_shards + n_parts]
    sems = refs[-1]
    z, p = spot[0], spot[1]
    copies = []

    def start(src, dst):
        copy = pltpu.make_async_copy(src, dst, sems.at[len(copies)])
        copy.start()
        copies.append(copy)

    for shard, full in zip(shards, fulls):
        rows = shard.shape[0]
        start(shard, full.at[pl.ds(pl.multiple_of(z * rows, rows), rows), :])
    for (bits, first), part in zip(layout, parts):
        count = part.shape[1]
        for turn in range(1, 4):
            origin = lax.rem(z - turn + 4, 4)
            left = 0
            for full in fulls:
                rows, width = full.shape[0] // 4, full.shape[1]
                at = origin * rows + (p ^ bits) * (rows // SUB) + first
                start(
                    part.at[turn - 1, :, left : left + width],
                    full.at[pl.ds(pl.multiple_of(at, 16), count), :],
                )
                left += width
    for copy in copies:
        copy.wait()


def assemble(shards, parts, spot):
    layout = tuple((bits, first) for bits, first, _ in parts)
    arrays = [part for _, _, part in parts]
    n_copies = len(shards) * (1 + 3 * len(parts))
    return pl.pallas_call(
        functools.partial(assemble_kernel, layout, len(shards), len(parts)),
        out_shape=[jax.ShapeDtypeStruct((4 * s.shape[0], s.shape[1]), s.dtype) for s in shards],
        in_specs=[pl.BlockSpec(memory_space=pltpu.SMEM)]
        + [pl.BlockSpec(memory_space=pl.ANY)] * (len(shards) + len(arrays)),
        out_specs=[pl.BlockSpec(memory_space=pltpu.VMEM)] * len(shards),
        scratch_shapes=[pltpu.SemaphoreType.DMA((n_copies,))],
        compiler_params=pltpu.CompilerParams(vmem_limit_bytes=40 * MB),
        cost_estimate=pl.CostEstimate(
            flops=0, transcendentals=0, bytes_accessed=sum(16 * s.size for s in shards)
        ),
        name="assemble",
    )(spot, *shards, *arrays)


def pieces_of(shards, p):
    return jnp.concatenate(
        [
            lax.dynamic_slice_in_dim(s, p * (s.shape[0] // SUB), s.shape[0] // SUB, 0)
            for s in shards
        ],
        axis=1,
    )


def gather(shards, p, spot):
    piece = pieces_of(shards, p)
    bundle = jnp.stack([turn_narrow(piece, turn) for turn in (1, 2, 3)])
    return assemble(shards, spread_plane(bundle), spot)


def add_two(a, b):
    return (a.astype(f32) + b.astype(f32)).astype(bf16)


def reduce_plane(grad, x, y, z):
    sent_x = take(grad[:, :, :, 0], 1 - x, 2)
    sent_y = take(grad[:, :, :, 1], 1 - y, 1)
    got_x = swap_wide(sent_x, 2)
    got_y = swap_wide(sent_y, 4)
    first = add_two(take(grad[:, :, :, 0], x, 2), got_x)
    second = add_two(take(grad[:, :, :, 1], y, 1), got_y)
    got_first = swap_wide(take(first, 1 - y, 1), 4)
    got_second = swap_wide(take(second, 1 - x, 1), 2)
    both = jnp.stack(
        [add_two(take(first, y, 1), got_first), add_two(take(second, x, 1), got_second)], axis=1
    )
    total = take(both, z, 0).astype(f32)
    for turn in (1, 2, 3):
        total = total + turn_narrow(take(both, (z + turn) % 4, 0), turn).astype(f32)
    return across_groups(total.astype(bf16))


def across_groups(a):
    groups = lax.axis_size("wide") // SUB
    if groups == 1:
        return a
    members = [[g * SUB + i for g in range(groups)] for i in range(SUB)]
    return lax.psum(a.astype(f32), "wide", axis_index_groups=members).astype(bf16)


def place_kernel(layout, spans, row_split, n_parts, spot, *refs):
    parts, outs = refs[:n_parts], refs[n_parts:]
    p = spot[1]
    for (bits, first), part in zip(layout, parts):
        at = p ^ bits
        core, quarter = at & 1, at >> 1
        count = part.shape[0]
        left = 0
        for out, span in zip(outs, spans):
            rows = out.shape[0] // (SUB if row_split else 4)
            row = quarter * rows + first
            column = 0
            if row_split:
                row = row + core * (out.shape[0] // 2)
            else:
                column = pl.multiple_of(core * span, 128)
            out[pl.ds(pl.multiple_of(row, 16), count), pl.ds(column, span)] = part[
                :, left : left + span
            ].astype(f32)
            left += span


def place(parts, shapes, row_split, spot):
    layout = tuple((bits, first) for bits, first, _ in parts)
    arrays = [part for _, _, part in parts]
    spans = tuple(s[1] if row_split else s[1] // 2 for s in shapes)
    return pl.pallas_call(
        functools.partial(place_kernel, layout, spans, row_split, len(arrays)),
        out_shape=[jax.ShapeDtypeStruct(s, f32) for s in shapes],
        grid_spec=pltpu.PrefetchScalarGridSpec(
            num_scalar_prefetch=1,
            grid=(1,),
            in_specs=[pl.BlockSpec(a.shape, lambda i, s: (0, 0)) for a in arrays],
            out_specs=[pl.BlockSpec(s, lambda i, s: (0, 0)) for s in shapes],
        ),
        compiler_params=pltpu.CompilerParams(vmem_limit_bytes=40 * MB),
        cost_estimate=pl.CostEstimate(
            flops=0, transcendentals=0, bytes_accessed=sum(6 * s[0] * s[1] for s in shapes)
        ),
        name="place",
    )(spot, *arrays)


def reduce_grad(half, shapes, row_split, x, y, z, spot):
    rows, width = half.shape
    view = half.reshape(4, 2, 2, 2, rows // 32, width)
    piece = reduce_plane(view, x, y, z).reshape(rows // 16, width)
    return place(spread_plane(piece), shapes, row_split, spot)


def sum_all(a, p, z):
    rows = a.shape[0] // SUB
    view = a.reshape(SUB, rows, a.shape[1])
    total = take(view, p, 0).astype(f32)
    for bits in range(1, SUB):
        total = total + swap_wide(take(view, p ^ bits, 0), bits).astype(f32)
    mine = total.astype(bf16)
    total = mine.astype(f32)
    for turn in (1, 2, 3):
        total = total + turn_narrow(mine, turn).astype(f32)
    return share_plane(across_groups(total.astype(bf16)), p)


def share_plane(piece, p):
    found = jnp.stack([piece] + [swap_wide(piece, bits) for bits in range(1, SUB)])
    return jnp.take(found, jnp.arange(SUB) ^ p, axis=0)


def pair_probs(pixels, same, keys_row):
    high, low = split_two(same * keys_row)
    scores = dot(high, pixels) + dot(low, pixels)
    biggest = jnp.max(scores[PATCH_COLS : PATCH_COLS + VARS], axis=0, keepdims=True)
    raised = jnp.exp(scores - biggest)
    total = jnp.sum(raised[PATCH_COLS : PATCH_COLS + VARS], axis=0, keepdims=True)
    return raised * (1.0 / total)


def variable_kernel(pixels_ref, same_ref, keys_ref, table_ref, merged_ref):
    pixels = pixels_ref[...]
    pixels_wide = pixels.astype(f32)
    same = same_ref[...]
    parts = []
    for i in range(2):
        probs = pair_probs(pixels, same, keys_ref[0, i : i + 1, :])
        weighted = (probs * pixels_wide).astype(bf16)
        parts.append(dot(table_ref[i * HEAD_DIM : (i + 1) * HEAD_DIM, :], weighted))
    merged_ref[...] = jnp.concatenate(parts, axis=0).T.astype(bf16)


def variable_forward(pixels, same, keys_rows, table_t):
    rows = pixels.shape[1]
    return pl.pallas_call(
        variable_kernel,
        out_shape=jax.ShapeDtypeStruct((rows, D), bf16),
        grid=(PAIRS,),
        in_specs=[
            pl.BlockSpec((COLS, rows), lambda h: (0, 0)),
            pl.BlockSpec((COLS, COLS), lambda h: (0, 0)),
            pl.BlockSpec((1, 2, COLS), lambda h: (h, 0, 0)),
            pl.BlockSpec((128, COLS), lambda h: (h, 0)),
        ],
        out_specs=pl.BlockSpec((rows, 128), lambda h: (0, h)),
        compiler_params=pltpu.CompilerParams(vmem_limit_bytes=40 * MB),
        cost_estimate=pl.CostEstimate(
            flops=6 * HEADS * rows * COLS * COLS,
            transcendentals=HEADS * rows * COLS,
            bytes_accessed=4 * rows * D,
        ),
        name="variable_forward",
    )(pixels, same, keys_rows, table_t)


def variable_back_kernel(
    pixels_ref, same_ref, keys_ref, keys_col_ref, table_ref, grad_ref, x_ref, zed_ref, pixel_ref
):
    step = pl.program_id(0)
    pixels = pixels_ref[...]
    pixels_wide = pixels.astype(f32)
    same = same_ref[...]
    same_low = same.astype(bf16)
    grad_t = grad_ref[...].astype(f32).T.astype(bf16)
    sums = []
    pixel_grad = None
    for i in range(2):
        probs = pair_probs(pixels, same, keys_ref[0, i : i + 1, :])
        weighted = (probs * pixels_wide).astype(bf16)
        grad_i = grad_t[i * HEAD_DIM : (i + 1) * HEAD_DIM, :]
        spread = dot(table_ref[:, i * HEAD_DIM : (i + 1) * HEAD_DIM], grad_i)
        high, low = split_two(spread * pixels_wide)
        prob_grad = dot(same_low, high) + dot(same_low, low)
        lifted = probs * prob_grad
        centre = jnp.sum(lifted[PATCH_COLS : PATCH_COLS + VARS], axis=0, keepdims=True)
        score_grad = lifted - probs * centre
        x_ref[i * HEAD_DIM : (i + 1) * HEAD_DIM, :] = dot_nt(grad_i, weighted).astype(bf16)
        sums.append(jnp.sum(score_grad * pixels_wide, axis=1, keepdims=True))
        term = probs * spread + score_grad * keys_col_ref[0, :, i : i + 1]
        pixel_grad = term if pixel_grad is None else pixel_grad + term
    zed_ref[0] = jnp.concatenate(sums, axis=1)

    @pl.when(step == 0)
    def _():
        pixel_ref[...] = pixel_grad

    @pl.when(step > 0)
    def _():
        pixel_ref[...] += pixel_grad


def variable_back(pixels, same, keys_rows, keys_cols, table, grad):
    rows = pixels.shape[1]
    return pl.pallas_call(
        variable_back_kernel,
        out_shape=[
            jax.ShapeDtypeStruct((D, COLS), bf16),
            jax.ShapeDtypeStruct((PAIRS, COLS, 2), f32),
            jax.ShapeDtypeStruct((COLS, rows), f32),
        ],
        grid=(PAIRS,),
        in_specs=[
            pl.BlockSpec((COLS, rows), lambda h: (0, 0)),
            pl.BlockSpec((COLS, COLS), lambda h: (0, 0)),
            pl.BlockSpec((1, 2, COLS), lambda h: (h, 0, 0)),
            pl.BlockSpec((1, COLS, 2), lambda h: (h, 0, 0)),
            pl.BlockSpec((COLS, 128), lambda h: (0, h)),
            pl.BlockSpec((rows, 128), lambda h: (0, h)),
        ],
        out_specs=[
            pl.BlockSpec((128, COLS), lambda h: (h, 0)),
            pl.BlockSpec((1, COLS, 2), lambda h: (h, 0, 0)),
            pl.BlockSpec((COLS, rows), lambda h: (0, 0)),
        ],
        compiler_params=pltpu.CompilerParams(vmem_limit_bytes=40 * MB),
        cost_estimate=pl.CostEstimate(
            flops=10 * HEADS * rows * COLS * COLS,
            transcendentals=HEADS * rows * COLS,
            bytes_accessed=4 * rows * D,
        ),
        name="variable_back",
    )(pixels, same, keys_rows, keys_cols, table, grad)


def mask_rows(segment_col, segment_row, padding_col, rows):
    key_at = lax.broadcasted_iota(jnp.int32, (rows, rows), 0)
    query_at = lax.broadcasted_iota(jnp.int32, (rows, rows), 1)
    allowed = (segment_col == segment_row) & ((padding_col == 1) | (key_at == query_at))
    return jnp.where(allowed, 0.0, masked_out).astype(f32)


def attention_kernel(q_ref, k_ref, v_ref, seg_row, seg_col, pad_col, out_ref, log_ref, mask_ref):
    rows = q_ref.shape[0]

    @pl.when(pl.program_id(0) == 0)
    def _():
        mask_ref[...] = mask_rows(seg_col[...], seg_row[...], pad_col[...], rows)

    q_t = (q_ref[...].astype(f32) * scale_by).T.astype(bf16)
    v_t = v_ref[...].astype(f32).T.astype(bf16)
    outs, logs = [], []
    for i in range(2):
        span = slice(i * HEAD_DIM, (i + 1) * HEAD_DIM)
        scores = dot(k_ref[:, span], q_t[span, :]) + mask_ref[...]
        biggest = jnp.max(scores, axis=0, keepdims=True)
        raised = jnp.exp(scores - biggest)
        total = jnp.sum(raised, axis=0, keepdims=True)
        outs.append(dot(v_t[span, :], raised.astype(bf16)) * (1.0 / total))
        logs.append(biggest + jnp.log(total))
    out_ref[...] = jnp.concatenate(outs, axis=0).T.astype(bf16)
    log_ref[0] = jnp.concatenate(logs, axis=0)


def attention(project, seg_row, seg_col, pad_col):
    rows = project.shape[0]
    column = lambda first: pl.BlockSpec((rows, 128), lambda h: (0, first * PAIRS + h))
    return pl.pallas_call(
        attention_kernel,
        out_shape=[
            jax.ShapeDtypeStruct((rows, D), bf16),
            jax.ShapeDtypeStruct((PAIRS, 2, rows), f32),
        ],
        grid=(PAIRS,),
        in_specs=[
            column(0),
            column(1),
            column(2),
            pl.BlockSpec((1, rows), lambda h: (0, 0)),
            pl.BlockSpec((rows, 1), lambda h: (0, 0)),
            pl.BlockSpec((rows, 1), lambda h: (0, 0)),
        ],
        out_specs=[column(0), pl.BlockSpec((1, 2, rows), lambda h: (h, 0, 0))],
        scratch_shapes=[pltpu.VMEM((rows, rows), f32)],
        compiler_params=pltpu.CompilerParams(vmem_limit_bytes=40 * MB),
        cost_estimate=pl.CostEstimate(
            flops=8 * rows * rows * D, transcendentals=HEADS * rows * rows, bytes_accessed=8 * rows * D
        ),
        name="attention",
    )(project, project, project, seg_row, seg_col, pad_col)


def attention_back_kernel(
    q_ref, k_ref, v_ref, grad_ref, log_ref, seg_row, seg_col, pad_col, out_ref, mask_ref
):
    rows = q_ref.shape[0]
    step = pl.program_id(0)

    @pl.when(step == 0)
    def _():
        mask_ref[...] = mask_rows(seg_col[...], seg_row[...], pad_col[...], rows)

    q_scaled = q_ref[...].astype(f32) * scale_by
    q_low = q_scaled.astype(bf16)
    q_t = q_scaled.T.astype(bf16)
    k_t = (k_ref[...].astype(f32) * scale_by).T.astype(bf16)
    grad_t = grad_ref[...].astype(f32).T.astype(bf16)
    q_grads, k_grads, v_grads = [], [], []
    for i in range(2):
        span = slice(i * HEAD_DIM, (i + 1) * HEAD_DIM)
        scores = dot(k_ref[:, span], q_t[span, :]) + mask_ref[...]
        probs = jnp.exp(scores - log_ref[0, i : i + 1, :])
        prob_grad = dot(v_ref[:, span], grad_t[span, :])
        lifted = probs * prob_grad
        centre = jnp.sum(lifted, axis=0, keepdims=True)
        score_grad = (lifted - probs * centre).astype(bf16)
        v_grads.append(dot(probs.astype(bf16), grad_ref[:, span]))
        k_grads.append(dot(score_grad, q_low[:, span]))
        q_grads.append(dot(k_t[span, :], score_grad))
    at = lambda first: pl.ds(pl.multiple_of(first * D + step * 128, 128), 128)
    out_ref[:, at(0)] = jnp.concatenate(q_grads, axis=0).T.astype(bf16)
    out_ref[:, at(1)] = jnp.concatenate(k_grads, axis=1).astype(bf16)
    out_ref[:, at(2)] = jnp.concatenate(v_grads, axis=1).astype(bf16)


def attention_back(project, grad, logs, seg_row, seg_col, pad_col):
    rows = project.shape[0]
    column = lambda first: pl.BlockSpec((rows, 128), lambda h: (0, first * PAIRS + h))
    return pl.pallas_call(
        attention_back_kernel,
        out_shape=jax.ShapeDtypeStruct((rows, 3 * D), bf16),
        grid=(PAIRS,),
        in_specs=[
            column(0),
            column(1),
            column(2),
            column(0),
            pl.BlockSpec((1, 2, rows), lambda h: (h, 0, 0)),
            pl.BlockSpec((1, rows), lambda h: (0, 0)),
            pl.BlockSpec((rows, 1), lambda h: (0, 0)),
            pl.BlockSpec((rows, 1), lambda h: (0, 0)),
        ],
        out_specs=pl.BlockSpec((rows, 3 * D), lambda h: (0, 0)),
        scratch_shapes=[pltpu.VMEM((rows, rows), f32)],
        compiler_params=pltpu.CompilerParams(vmem_limit_bytes=40 * MB),
        cost_estimate=pl.CostEstimate(
            flops=20 * rows * rows * D,
            transcendentals=HEADS * rows * rows,
            bytes_accessed=16 * rows * D,
        ),
        name="attention_back",
    )(project, project, project, grad, logs, seg_row, seg_col, pad_col)


def normalise(values):
    average = jnp.mean(values, axis=-1, keepdims=True)
    centered = values - average
    variance = jnp.mean(centered * centered, axis=-1, keepdims=True)
    inverse = lax.rsqrt(variance + norm_eps)
    return centered * inverse, inverse


def normalise_back(grad, gain, unit, inverse):
    scaled = grad * gain
    first = jnp.mean(scaled, axis=-1, keepdims=True)
    second = jnp.mean(scaled * unit, axis=-1, keepdims=True)
    return inverse * (scaled - first - unit * second)


def gelu_pair(values):
    below = 0.5 * (1.0 + lax.erf(values * (0.5**0.5)))
    density = jnp.exp(-0.5 * values * values) * ((0.5 / np.pi) ** 0.5)
    return values * below, below + values * density


def columns_half(a, core):
    span = a.shape[1] // 2
    return lax.dynamic_slice_in_dim(a, core * span, span, 1)


def per_device(
    patches,
    var_ids,
    segment_ids,
    pad_mask,
    embed_weight,
    var_embed,
    agg_query,
    key_weight,
    value_weight,
    agg_out_weight,
    agg_out_bias,
    norm_one_gain,
    norm_one_bias,
    qkv_weight,
    attn_out_weight,
    attn_out_bias,
    norm_two_gain,
    norm_two_bias,
    mlp_in_weight,
    mlp_in_bias,
    mlp_out_weight,
    mlp_out_bias,
    cotangent,
):
    rows = patches.shape[0]
    wide, z = lax.axis_index("wide"), lax.axis_index("narrow")
    p = wide % SUB
    core, x, y = p & 1, (p >> 1) & 1, p >> 2
    spot = jnp.stack([z, p]).astype(jnp.int32)
    shard = D // 4

    vectors = jnp.concatenate(
        [
            agg_query,
            agg_out_bias,
            norm_one_gain,
            norm_one_bias,
            attn_out_bias,
            norm_two_gain,
            norm_two_bias,
            mlp_out_bias,
            mlp_in_bias,
        ]
    ).reshape(-1, 128)
    around = jnp.stack([vectors] + [turn_narrow(vectors, turn) for turn in (1, 2, 3)])
    around = jnp.take(around, (z - jnp.arange(4)) % 4, axis=0).reshape(4, -1)
    whole = [around[:, i * shard : (i + 1) * shard].reshape(D) for i in range(8)]
    query_full = whole[0]
    agg_out_b, gain_one, bias_one, attn_out_b, gain_two, bias_two, mlp_out_b = [
        v.astype(f32) for v in whole[1:]
    ]
    mlp_in_b = around[:, 8 * shard :].reshape(4 * D).astype(f32)
    cot_there = swap_wide(cotangent, 1)

    line = jnp.arange(COLS, dtype=jnp.int32)
    variable = jnp.where(line < PATCH_COLS, line // PIX, (line - PATCH_COLS) % VARS)
    same = (variable[:, None] == variable[None, :]) & (line[None, :] < PATCH_COLS + VARS)
    same = same.astype(f32)
    chosen = jnp.take(var_ids, variable)
    source = jnp.where(line < PATCH_COLS, chosen * PIX + line % PIX, chosen + PATCH_COLS)
    source = jnp.where(line < PATCH_COLS + VARS, source, -1)
    chooser = (source[:, None] == line[None, :]).astype(bf16)
    embed_rows = jnp.concatenate(
        [embed_weight, var_embed, jnp.zeros((COLS - PATCH_COLS - VARS, shard), bf16)]
    )
    embed_rows = dot(chooser, embed_rows).astype(bf16)
    key_query = jnp.sum(
        key_weight.reshape(shard, HEADS, HEAD_DIM).astype(f32)
        * query_full.reshape(1, HEADS, HEAD_DIM).astype(f32),
        axis=-1,
    ).astype(bf16)
    keys_part = dot_nt(key_query.T, embed_rows) * scale_by
    value_part = lax.dynamic_slice_in_dim(value_weight, p * 128, 128, 1)
    table_part = dot(embed_rows, value_part).astype(bf16)
    keys_t = keys_part
    table_own = table_part.astype(f32)
    for turn in (1, 2, 3):
        keys_t = keys_t + turn_narrow(keys_part, turn)
        table_own = table_own + turn_narrow(table_part, turn).astype(f32)
    table_all = share_plane(table_own.astype(bf16), p)
    table = table_all.transpose(1, 0, 2).reshape(COLS, D)
    table_t = table_all.transpose(0, 2, 1).reshape(D, COLS)
    keys_rows = keys_t.reshape(PAIRS, 2, COLS)
    keys_cols = keys_rows.transpose(0, 2, 1)

    (agg_out_w,) = gather([agg_out_weight], p, spot)
    qkv_w, attn_out_w = gather([qkv_weight, attn_out_weight], p, spot)
    (mlp_in_w,) = gather([mlp_in_weight], p, spot)
    (mlp_out_w,) = gather([mlp_out_weight], p, spot)

    pixels = jnp.concatenate(
        [
            patches.T,
            jnp.ones((VARS, rows), bf16),
            jnp.zeros((COLS - PATCH_COLS - VARS, rows), bf16),
        ]
    )
    merged = variable_forward(pixels, same, keys_rows, table_t)
    merged_there = swap_wide(merged, 1)
    patch_state = dot(merged, agg_out_w) + agg_out_b
    unit_one, inverse_one = normalise(patch_state)
    normed = (unit_one * gain_one + bias_one).astype(bf16)
    normed_there = swap_wide(normed, 1)
    project = dot(normed, qkv_w).astype(bf16)
    seg_row, seg_col, pad_col = segment_ids, segment_ids.T, pad_mask.T
    attended, logs = attention(project, seg_row, seg_col, pad_col)
    attended_there = swap_wide(attended, 1)
    residual = patch_state + dot(attended, attn_out_w) + attn_out_b
    unit_two, inverse_two = normalise(residual)
    normed_two = (unit_two * gain_two + bias_two).astype(bf16)
    normed_two_there = swap_wide(normed_two, 1)
    hidden_pre = dot(normed_two, mlp_in_w) + mlp_in_b
    hidden, slope = gelu_pair(hidden_pre)
    hidden, slope = hidden.astype(bf16), slope.astype(bf16)
    result = (residual + dot(hidden, mlp_out_w) + mlp_out_b).astype(bf16)

    cot_float = cotangent.astype(f32)
    cot_both = jnp.concatenate([cotangent, cot_there])
    hidden_view = hidden.reshape(rows, 4, 2, D // 2)
    hidden_got = swap_wide(take(hidden_view, 1 - core, 2), 1)
    hidden_both = jnp.concatenate([take(hidden_view, core, 2), hidden_got]).reshape(2 * rows, -1)
    grad_mlp_out = dot_tn(hidden_both, cot_both).astype(bf16)
    (grad_mlp_out_w,) = reduce_grad(grad_mlp_out, [(D, D)], True, x, y, z, spot)

    hidden_pre_grad = (dot_nt(cotangent, mlp_out_w) * slope.astype(f32)).astype(bf16)
    pre_got = swap_wide(columns_half(hidden_pre_grad, 1 - core), 1)
    pre_both = jnp.concatenate([columns_half(hidden_pre_grad, core), pre_got])
    normed_two_both = jnp.concatenate([normed_two, normed_two_there])
    grad_mlp_in = dot_tn(normed_two_both, pre_both).astype(bf16)
    (grad_mlp_in_w,) = reduce_grad(grad_mlp_in, [(shard, 4 * D)], False, x, y, z, spot)

    normed_two_grad = dot_nt(hidden_pre_grad, mlp_in_w)
    residual_grad = cot_float + normalise_back(normed_two_grad, gain_two, unit_two, inverse_two)
    branch_grad = residual_grad.astype(bf16)
    branch_got = swap_wide(columns_half(branch_grad, 1 - core), 1)
    branch_both = jnp.concatenate([columns_half(branch_grad, core), branch_got])
    attended_both = jnp.concatenate([attended, attended_there])
    grad_attn_out = dot_tn(attended_both, branch_both).astype(bf16)
    attended_grad = dot_nt(branch_grad, attn_out_w).astype(bf16)
    project_grad = attention_back(project, attended_grad, logs, seg_row, seg_col, pad_col)
    project_got = swap_wide(columns_half(project_grad, 1 - core), 1)
    project_both = jnp.concatenate([columns_half(project_grad, core), project_got])
    normed_both = jnp.concatenate([normed, normed_there])
    grad_qkv = dot_tn(normed_both, project_both).astype(bf16)
    grad_qkv_w, grad_attn_out_w = reduce_grad(
        jnp.concatenate([grad_qkv, grad_attn_out], axis=1),
        [(shard, 3 * D), (shard, D)],
        False,
        x,
        y,
        z,
        spot,
    )

    normed_grad = dot_nt(project_grad, qkv_w)
    state_grad = residual_grad + normalise_back(normed_grad, gain_one, unit_one, inverse_one)
    state_grad = state_grad.astype(bf16)
    state_got = swap_wide(columns_half(state_grad, 1 - core), 1)
    state_both = jnp.concatenate([columns_half(state_grad, core), state_got])
    merged_both = jnp.concatenate([merged, merged_there])
    grad_agg_out = dot_tn(merged_both, state_both).astype(bf16)
    (grad_agg_out_w,) = reduce_grad(grad_agg_out, [(shard, D)], False, x, y, z, spot)
    merged_grad = dot_nt(state_grad, agg_out_w).astype(bf16)

    cross, zed, pixel_grad = variable_back(pixels, same, keys_rows, keys_cols, table, merged_grad)
    patches_grad = pixel_grad[:PATCH_COLS].T
    zed_high, zed_low = split_two(zed.transpose(0, 2, 1).reshape(HEADS, COLS))
    column_sums = [
        jnp.sum(state_grad.astype(f32), axis=0),
        jnp.sum(normed_grad * unit_one, axis=0),
        jnp.sum(normed_grad, axis=0),
        jnp.sum(branch_grad.astype(f32), axis=0),
        jnp.sum(normed_two_grad * unit_two, axis=0),
        jnp.sum(normed_two_grad, axis=0),
        jnp.sum(cot_float, axis=0),
        jnp.sum(hidden_pre_grad.astype(f32), axis=0),
    ]
    small = jnp.concatenate(column_sums).astype(bf16).reshape(-1, COLS)
    used = D + 2 * HEADS + small.shape[0]
    padded = -(-used // 128) * 128
    small = jnp.concatenate(
        [cross, zed_high, zed_low, small, jnp.zeros((padded - used, COLS), bf16)]
    )
    small = sum_all(small, p, z).reshape(padded, COLS)
    cross = small[:D]
    zed = small[D : D + HEADS].astype(f32) + small[D + HEADS : D + 2 * HEADS].astype(f32)
    sums = small[D + 2 * HEADS : used].astype(f32)
    own = lambda i: take(sums[4 * i : 4 * i + 4], z, 0)
    grad_mlp_in_b = lax.dynamic_slice_in_dim(sums[28:44], 4 * z, 4, 0).reshape(D)

    zed_both = split_two(zed)
    grad_embed = dot(value_weight, cross).T + sum(
        dot_nt(part.T, key_query) for part in zed_both
    ) * scale_by
    grad_embed = lax.dot_general(
        chooser.astype(f32),
        grad_embed,
        (((0,), (0,)), ((), ())),
        precision=lax.Precision.HIGHEST,
        preferred_element_type=f32,
    )
    grad_value_w = dot_nt(embed_rows.T, cross)
    query_grad = sum(dot_nt(embed_rows.T, part) for part in zed_both) * scale_by
    grad_key_w = jnp.repeat(query_grad, HEAD_DIM, axis=1) * query_full.astype(f32)[None, :]
    grad_query = jnp.sum(
        jnp.repeat(query_grad, HEAD_DIM, axis=1) * key_weight.astype(f32), axis=0
    )
    grad_query = grad_query.astype(bf16).reshape(4, shard)
    grad_agg_query = take(grad_query, z, 0).astype(f32)
    for turn in (1, 2, 3):
        grad_agg_query = grad_agg_query + turn_narrow(
            take(grad_query, (z + turn) % 4, 0), turn
        ).astype(f32)

    return (
        result,
        patches_grad,
        grad_embed[:PATCH_COLS],
        grad_embed[PATCH_COLS : PATCH_COLS + VARS],
        grad_agg_query,
        grad_key_w,
        grad_value_w,
        grad_agg_out_w,
        own(0),
        own(1),
        own(2),
        grad_qkv_w,
        grad_attn_out_w,
        own(3),
        own(4),
        own(5),
        grad_mlp_in_w,
        grad_mlp_in_b,
        grad_mlp_out_w,
        own(6),
    )


def solution(mesh):
    rows, shard = P(("wide", "narrow"), None), P("narrow", None)
    wide_shard, vector = P(None, "narrow"), P("narrow")
    return jax.shard_map(
        per_device,
        mesh=mesh,
        in_specs=(
            rows,
            P(),
            rows,
            rows,
            wide_shard,
            wide_shard,
            vector,
            shard,
            shard,
            shard,
            vector,
            vector,
            vector,
            shard,
            shard,
            vector,
            vector,
            vector,
            shard,
            vector,
            shard,
            vector,
            rows,
        ),
        out_specs=(
            rows,
            rows,
            wide_shard,
            wide_shard,
            vector,
            shard,
            shard,
            shard,
            vector,
            vector,
            vector,
            shard,
            shard,
            vector,
            vector,
            vector,
            shard,
            vector,
            shard,
            vector,
        ),
        check_vma=False,
    )
```

time: 2080 us -> 775 us (0.37)
  matrix products: 718 us -> 78.5 us
  waiting for transfers between devices: 775 us -> 248 us
  blocking collectives: 429 us -> 0 us
  starting transfers between devices: 1.26 us -> 147 us
  Pallas kernels: 0 us -> 87.9 us
  local copies, waits for them, and re-layouts: 90.5 us -> 143 us
  other arithmetic: 32.7 us -> 56.7 us
    dot_general x71 -> x25, matrix products: 718 us -> 78.5 us  [the longest x8 31.1 us: dot(): return jnp.dot(a, b, preferred_element_type=f32)]
    reduce_scatter x9 -> x0, waiting for transfers between devices: 481 us -> none  [the longest x1 147 us: per_device(): lax.psum_scatter(grad_mlp_out_w.astype(jnp.bfloat16), 'narrow', scatter_d...]
    psum x1 -> x0, blocking collectives: 295 us -> none  [per_device(): lax.psum((shard_sums[0], shard_sums[1], shard_sums[2], shard_sums[3], sha...]
    all_gather x7 -> x0, waiting for transfers between devices: 290 us -> none  [the longest x1 145 us: per_device(): lax.all_gather(mlp_in_weight, 'narrow', axis=0, tiled=True)]
    ppermute x0 -> x158, waiting for transfers between devices: none -> 248 us  [the longest x119 168 us: swap_wide(): return lax.ppermute(a, 'wide', [(i, i ^ bits) for i in range(size)])]
    ppermute x0 -> x158, starting transfers between devices: none -> 147 us  [the longest x119 79.9 us: swap_wide(): return lax.ppermute(a, 'wide', [(i, i ^ bits) for i in range(size)])]
    all_gather x11 -> x0, blocking collectives: 116 us -> none  [the longest x1 14.4 us: per_device(): lax.all_gather(mlp_in_bias, 'narrow', axis=0, tiled=True)]
    pallas_call x0 -> x12, Pallas kernels: none -> 87.9 us  [the longest x4 23.2 us: assemble(): pl.pallas_call(functools.partial(assemble_kernel, layout, len(shards), le...]
  transfers between devices with their start and end apart: 16 -> 158, of which waited for: 9 -> 43; matrix products, arithmetic and copies ran while one was open for 14% -> 27% of each run, Pallas kernels for 0% -> 6%
where the time goes in v1:
time: 775 us; the launch traced here: 765 us
  waiting for transfers between devices  248 us (32%)
  starting transfers between devices  147 us (19%)
  local copies, waits for them, and re-layouts  143 us (18%)
  Pallas kernels  87.9 us (11%)
  matrix products  78.5 us (10%)
  other arithmetic  56.7 us (7%)
    ppermute x119, waiting for transfers between devices, swap_wide(): return lax.ppermute(a, 'wide', [(i, i ^ bits) for i in range(size)])  168 us
    ppermute x39, waiting for transfers between devices, turn_narrow(): lax.ppermute(a, 'narrow', [(i, (i + by) % size) for i in range(size)])  80.3 us
    ppermute x119, starting transfers between devices, swap_wide(): return lax.ppermute(a, 'wide', [(i, i ^ bits) for i in range(size)])  79.9 us
    ppermute x39, starting transfers between devices, turn_narrow(): lax.ppermute(a, 'narrow', [(i, (i + by) % size) for i in range(size)])  67.1 us
    unnamed x320, local copies, waits for them, and re-layouts  59.4 us
    dot_general x8, matrix products, dot(): return jnp.dot(a, b, preferred_element_type=f32)  31.1 us
    select_n x1, other arithmetic, per_device(): source = jnp.where(line < PATCH_COLS + VARS, source, -1)  25.7 us
    dot_general x11, matrix products, dot_nt(): lax.dot_general(a, b, (((1,), (1,)), ((), ())), preferred_element_type=f32)  23.7 us
  transfers between devices with their start and end apart: 158, of which 43 were waited for; matrix products, arithmetic and copies ran while one was open for 27% of the time, Pallas kernels for 6%

profile of v1, /device:TPU:0, one launch (start us, length us, event | category | flops | bytes accessed | tf_op | source)
XLA Modules:
  0.0 765.0 jit_solution(12365436068262518008)
XLA Ops:
  8.1 5.0 collective-permute-start.2
  20.8 4.5 compare_select_fusion.1
  25.4 25.7 %fusion.160 = s32[256]{0:T(256)S(1)} fusion(pred[256]{0:T(512)(128)(4,1)S(1)} %get-tuple-element.233, pred[256]{0:T(512)(128)(4,1)S(1)} %get-tuple-element.234, pred[256]{0:T(512)(128)(4,1)S(1)} %get-tuple-element.235, pred[256]{0:T(512)(128)(4,1)S(1)} %get-tuple-element.236, pred[256]{0:T(512)(128)(4,1)S(1)} %get-tuple-element.237, ...), kind=kLoop, calls=%fused_computation.461 | loop fusion | flops 19200 | bytes 12708 | tf_op jit(solution)/shard_map/jit(_where)/select_n | solution.py:556
  75.1 3.2 collective-permute-start.18
  80.3 3.2 collective-permute-start.30
  88.2 2.9 collective-permute-start.14
  92.6 5.0 collective-permute-start.29
  97.6 3.8 collective-permute-start.42
  103.1 4.7 collective-permute-done.20.refs_3_
  110.0 2.9 collective-permute-start.41
  112.9 3.7 collective-permute-done.29
  116.7 10.0 %collective-permute-start.53 = (bf16[128,1024]{1,0:T(8,128)(2,1)}, bf16[128,1024]{1,0:T(8,128)(2,1)S(1)}, u32[]{:S(2)}, u32[]{:S(2)}) collective-permute-start(bf16[128,1024]{1,0:T(8,128)(2,1)} %constant_dynamic-slice_fusion.38), channel_id=1, source_target_pairs={{0,2},{1,3},{2,0},{3,1},{4,6},{5,7},{6,4},{7,5},{8,10},{9,11},{10,... | collective-permute-start | bytes 786440 | tf_op jit(solution)/shard_map/ppermute | solution.py:53
  126.8 7.2 collective-permute-start.52
  134.0 15.2 %collective-permute-done.41 = bf16[32,4096]{1,0:T(8,128)(2,1)S(1)} collective-permute-done((bf16[32,4096]{1,0:T(8,128)(2,1)}, bf16[32,4096]{1,0:T(8,128)(2,1)S(1)}, u32[]{:S(2)}, u32[]{:S(2)}) %collective-permute-start.41) | collective-permute-done | bytes 262176 | tf_op jit(solution)/shard_map/ppermute | solution.py:53
  162.1 8.9 %collective-permute-done.22.refs_5_ = bf16[3,16,1024]{2,1,0:T(8,128)(2,1)S(1)} collective-permute-done((bf16[3,16,1024]{2,1,0:T(8,128)(2,1)S(1)}, bf16[3,16,1024]{2,1,0:T(8,128)(2,1)S(1)}, u32[]{:S(2)}, u32[]{:S(2)}) %collective-permute-start.22) | collective-permute-done | bytes 98336 | tf_op jit(solution)/shard_map/ppermute | solution.py:48
  189.3 9.4 %variable_forward.1 = bf16[512,1024]{1,0:T(8,128)(2,1)S(1)} custom-call(bf16[256,512]{1,0:T(8,128)(2,1)S(1)} %copy-done.28, f32[256,256]{1,0:T(8,128)S(1)} %copy-done.30, f32[8,2,256]{2,1,0:T(2,128)S(1)} %reshape.518.keys_ref, bf16[1024,256]{1,0:T(8,128)(2,1)S(1)} %bitcast.418), custom_call_target="tpu_custom_call" | custom-call | flops 3221225472 | bytes 2097152 | tf_op jit(solution)/shard_map/variable_forward/pallas_call | solution.py:260
  205.4 5.1 collective-permute-done.44.refs_3_
  212.4 14.9 %collective-permute-done.56.refs_3_ = bf16[3,128,1024]{2,1,0:T(8,128)(2,1)} collective-permute-done((bf16[3,128,1024]{2,1,0:T(8,128)(2,1)S(1)}, bf16[3,128,1024]{2,1,0:T(8,128)(2,1)}, u32[]{:S(2)}, u32[]{:S(2)}) %collective-permute-start.56) | collective-permute-done | bytes 786464 | tf_op jit(solution)/shard_map/ppermute | solution.py:48
  227.8 7.7 %collective-permute-done.33.refs_5_ = bf16[3,16,4096]{2,1,0:T(8,128)(2,1)S(1)} collective-permute-done((bf16[3,16,4096]{2,1,0:T(8,128)(2,1)S(1)}, bf16[3,16,4096]{2,1,0:T(8,128)(2,1)S(1)}, u32[]{:S(2)}, u32[]{:S(2)}) %collective-permute-start.33) | collective-permute-done | bytes 393248 | tf_op jit(solution)/shard_map/ppermute | solution.py:48
  244.6 6.4 assemble.5
  251.0 7.2 convolution_convert_fusion.q_ref.k_ref.v_ref
  258.2 12.0 %attention.1 = (bf16[512,1024]{1,0:T(8,128)(2,1)S(1)}, f32[8,2,512]{2,1,0:T(2,128)S(1)}) custom-call(bf16[512,3072]{1,0:T(8,128)(2,1)S(1)} %convolution_convert_fusion.q_ref.k_ref.v_ref, bf16[512,3072]{1,0:T(8,128)(2,1)S(1)} %convolution_convert_fusion.q_ref.k_ref.v_ref, bf16[512,3072]{1,0:T(8,128)(2,1)S(1)} %convolution_convert_fusion.q_ref.k_ref.v_ref, ...), custom_call_target="tpu_custom_call" | custom-call | flops 2147483648 | bytes 4194304 | tf_op jit(solution)/shard_map/attention/pallas_call | solution.py:382
  274.3 9.5 %collective-permute-done.58.refs_5_ = bf16[3,64,1024]{2,1,0:T(8,128)(2,1)} collective-permute-done((bf16[3,64,1024]{2,1,0:T(8,128)(2,1)S(1)}, bf16[3,64,1024]{2,1,0:T(8,128)(2,1)}, u32[]{:S(2)}, u32[]{:S(2)}) %collective-permute-start.58) | collective-permute-done | bytes 393248 | tf_op jit(solution)/shard_map/ppermute | solution.py:48
  285.0 6.9 assemble.6
  291.9 10.5 %multiply_convert_fusion = (bf16[512,4096]{1,0:T(8,128)(2,1)}, f32[512,4096]{1,0:T(8,128)}) fusion(f32[4096]{0:T(1024)S(1)} %bitcast.467, bf16[512,1024]{1,0:T(8,128)(2,1)S(1)} %add_convert_fusion.2, bf16[1024,4096]{1,0:T(8,128)(2,1)} %assemble.6), kind=kOutput, calls=%fused_computation.11 | convolution fusion | flops 4307550208 | bytes 22036480 | tf_op jit(solution)/shard_map/dot_general | solution.py:30
  302.4 7.9 %reshape.531 = bf16[512,4,2,512]{3,2,1,0:T(2,128)(2,1)} reshape(bf16[512,4096]{1,0:T(8,128)(2,1)} %get-tuple-element.227) | data formatting | bytes 8388608 | tf_op jit(solution)/shard_map/reshape | solution.py:614
  310.4 7.3 assemble.7
  317.7 9.0 %add_convert_fusion.1 = bf16[512,1024]{1,0:T(8,128)(2,1)} fusion(f32[512,1024]{1,0:T(8,128)S(1)} %copy-done.79, bf16[512,4096]{1,0:T(8,128)(2,1)S(1)} %copy-done.89, bf16[4096,1024]{1,0:T(8,128)(2,1)} %assemble.7, f32[1024]{0:T(1024)S(1)} %bitcast.477), kind=kOutput, calls=%fused_computation.65 | convolution fusion | flops 4296540160 | bytes 15732736 | tf_op jit(solution)/shard_map/dot_general | solution.py:30
  326.7 9.9 %fusion.187 = (bf16[4096]{0:T(1024)(128)(2,1)S(1)}, bf16[512,4096]{1,0:T(8,128)(2,1)S(1)}) fusion(f32[512,4096]{1,0:T(8,128)} %get-tuple-element.228, f32[4096]{0:T(1024)S(1)} %bitcast.468, bf16[4096,1024]{1,0:T(8,128)(2,1)S(1)} %copy-done.80, bf16[512,1024]{1,0:T(8,128)(2,1)} %param.45), kind=kOutput, calls=%fused_computation.490 | convolution fusion | flops 4324323328 | bytes 22044672 | tf_op jit(solution)/shard_map/dot_general | solution.py:34
  336.7 5.0 multiply_reduce_fusion
  346.8 16.7 %attention_back.1 = bf16[512,3072]{1,0:T(8,128)(2,1)S(1)} custom-call(bf16[512,3072]{1,0:T(8,128)(2,1)S(1)} %copy-done.2, bf16[512,3072]{1,0:T(8,128)(2,1)S(1)} %copy-done.2, bf16[512,3072]{1,0:T(8,128)(2,1)S(1)} %copy-done.2, bf16[512,1024]{1,0:T(8,128)(2,1)S(1)} %convolution_convert_fusion.3.grad_ref, f32[8,2,512]{2,1,0:T(2,128)S(1)} %get-tuple-element.32.log_ref, ...), custom_call_target="tpu_custom_call" | custom-call | flops 5368709120 | bytes 8388608 | tf_op jit(solution)/shard_map/attention_back/pallas_call | solution.py:443
  363.6 4.0 multiply_reduce_fusion.1
  370.7 14.2 %variable_back.1 = (bf16[1024,256]{1,0:T(8,128)(2,1)S(1)}, f32[8,256,2]{2,1,0:T(8,128)S(1)}, f32[256,512]{1,0:T(8,128)S(1)}) custom-call(bf16[256,512]{1,0:T(8,128)(2,1)S(1)} %copy-done.29, f32[256,256]{1,0:T(8,128)S(1)} %copy-done.31, f32[8,2,256]{2,1,0:T(2,128)S(1)} %reshape.518.keys_ref, f32[8,256,2]{2,1,0:T(8,128)S(1)} %bitcast.415, ...), custom_call_target="tpu_custom_call" | custom-call | flops 5368709120 | bytes 2097152 | tf_op jit(solution)/shard_map/variable_back/pallas_call | solution.py:319
  391.6 4.0 constant_dynamic-slice_fusion.24
  395.6 9.6 %constant_dynamic-slice_fusion.6 = (bf16[512,4,1,512]{3,2,1,0:T(2,128)(2,1)}, bf16[512,4,1,512]{3,2,1,0:T(2,128)(2,1)S(1)}) fusion(bf16[512,4,2,512]{3,2,1,0:T(2,128)(2,1)S(1)} %copy-done.75, s32[]{:T(128)S(6)} %select_n.460, s32[]{:T(128)S(6)} %select_n.461), kind=kLoop, calls=%fused_computation.297 | loop fusion | bytes 8388616 | tf_op jit(solution)/shard_map/jit(dynamic_index_in_dim)/dynamic_slice | solution.py:57
  412.5 10.6 %copy.120 = bf16[512,4,1,512]{0,3,1,2:T(8,128)(2,1)} copy(bf16[512,4,1,512]{3,2,1,0:T(2,128)(2,1)} %get-tuple-element.102) | data formatting | bytes 4194304
  430.7 3.0 collective-permute-done.72
  436.5 3.7 collective-permute-done.75
  440.1 3.8 collective-permute-done.76
  448.3 4.2 collective-permute-done.78
  454.4 3.3 collective-permute-done.79
  457.8 5.0 collective-permute-done.80
  474.0 6.8 collective-permute-done.86
  482.0 6.2 collective-permute-done.88
  489.3 3.8 collective-permute-done.87
  494.3 3.8 collective-permute-done.89
  499.4 3.7 collective-permute-done.92
  509.9 5.5 collective-permute-done.90
  517.8 2.9 fusion.46
  522.7 5.2 convolution_convert_fusion.1
  535.3 5.0 fusion.17
  547.6 4.1 copy.97
  552.7 6.7 fusion.14
  566.9 26.6 %collective-permute-done.107 = bf16[4,32,2048]{2,1,0:T(8,128)(2,1)S(1)} collective-permute-done((bf16[4,32,2048]{2,1,0:T(8,128)(2,1)S(1)}, bf16[4,32,2048]{2,1,0:T(8,128)(2,1)S(1)}, u32[]{:S(2)}, u32[]{:S(2)}) %collective-permute-start.107) | collective-permute-done | bytes 524320 | tf_op jit(solution)/shard_map/ppermute | solution.py:48
  597.8 20.0 %collective-permute-done.142 = bf16[4,2,64,1024]{3,2,0,1:T(8,128)(2,1)S(1)} collective-permute-done((bf16[4,2,64,1024]{3,2,0,1:T(8,128)(2,1)S(1)}, bf16[4,2,64,1024]{3,2,0,1:T(8,128)(2,1)S(1)}, u32[]{:S(2)}, u32[]{:S(2)}) %collective-permute-start.142) | collective-permute-done | bytes 1048608 | tf_op jit(solution)/shard_map/ppermute | solution.py:48
  622.0 3.0 collective-permute-start.82
  625.0 11.6 %collective-permute-done.111 = bf16[2,32,2048]{2,1,0:T(8,128)(2,1)S(1)} collective-permute-done((bf16[2,32,2048]{2,1,0:T(8,128)(2,1)S(1)}, bf16[2,32,2048]{2,1,0:T(8,128)(2,1)S(1)}, u32[]{:S(2)}, u32[]{:S(2)}) %collective-permute-start.111) | collective-permute-done | bytes 262176 | tf_op jit(solution)/shard_map/ppermute | solution.py:53
  639.2 10.6 %collective-permute-done.127 = bf16[4,32,2048]{2,1,0:T(8,128)(2,1)S(1)} collective-permute-done((bf16[4,32,2048]{2,1,0:T(8,128)(2,1)S(1)}, bf16[4,32,2048]{2,1,0:T(8,128)(2,1)S(1)}, u32[]{:S(2)}, u32[]{:S(2)}) %collective-permute-start.127) | collective-permute-done | bytes 524320 | tf_op jit(solution)/shard_map/ppermute | solution.py:48
  656.1 9.3 %collective-permute-done.96.refs_4_ = bf16[32,512]{1,0:T(8,128)(2,1)S(1)} collective-permute-done((bf16[32,512]{1,0:T(8,128)(2,1)S(1)}, bf16[32,512]{1,0:T(8,128)(2,1)S(1)}, u32[]{:S(2)}, u32[]{:S(2)}) %collective-permute-start.96) | collective-permute-done | bytes 32800 | tf_op jit(solution)/shard_map/ppermute | solution.py:48
  666.5 3.6 collective-permute-start.130
  680.0 19.0 %collective-permute-done.129 = bf16[2,32,2048]{2,1,0:T(8,128)(2,1)S(1)} collective-permute-done((bf16[2,32,2048]{2,1,0:T(8,128)(2,1)S(1)}, bf16[2,32,2048]{2,1,0:T(8,128)(2,1)S(1)}, u32[]{:S(2)}, u32[]{:S(2)}) %collective-permute-start.129) | collective-permute-done | bytes 262176 | tf_op jit(solution)/shard_map/ppermute | solution.py:53
  701.1 8.5 %collective-permute-done.147 = bf16[2,64,1024]{2,1,0:T(8,128)(2,1)S(1)} collective-permute-done((bf16[2,64,1024]{2,1,0:T(8,128)(2,1)S(1)}, bf16[2,64,1024]{2,1,0:T(8,128)(2,1)S(1)}, u32[]{:S(2)}, u32[]{:S(2)}) %collective-permute-start.147) | collective-permute-done | bytes 262176 | tf_op jit(solution)/shard_map/ppermute | solution.py:53
  756.6 3.9 place.6
  760.5 4.1 place.7
  (797 shorter events, 270.5 us)
Async XLA Ops:
  8.1 58.3 %collective-permute-start.2 = (bf16[24,128]{1,0:T(8,128)(2,1)S(1)}, bf16[24,128]{1,0:T(8,128)(2,1)S(1)}, u32[]{:S(2)}, u32[]{:S(2)}) collective-permute-start(bf16[24,128]{1,0:T(8,128)(2,1)S(1)} %bitcast.472), channel_id=1, source_target_pairs={{0,3},{1,0},{2,1},{3,2},{4,7},{5,4},{6,5},{7,6},{8,11},{9,8},{10,9... | collective-permute-start | bytes 18440 | tf_op jit(solution)/shard_map/ppermute | solution.py:53
  13.2 53.3 %collective-permute-start.1 = (bf16[24,128]{1,0:T(8,128)(2,1)S(1)}, bf16[24,128]{1,0:T(8,128)(2,1)S(1)}, u32[]{:S(2)}, u32[]{:S(2)}) collective-permute-start(bf16[24,128]{1,0:T(8,128)(2,1)S(1)} %bitcast.473), channel_id=1, source_target_pairs={{0,2},{1,3},{2,0},{3,1},{4,6},{5,7},{6,4},{7,5},{8,10},{9,11},{10,... | collective-permute-start | bytes 18440 | tf_op jit(solution)/shard_map/ppermute | solution.py:53
  13.2 53.3 %collective-permute-start = (bf16[24,128]{1,0:T(8,128)(2,1)S(1)}, bf16[24,128]{1,0:T(8,128)(2,1)S(1)}, u32[]{:S(2)}, u32[]{:S(2)}) collective-permute-start(bf16[24,128]{1,0:T(8,128)(2,1)S(1)} %bitcast.474), channel_id=1, source_target_pairs={{0,1},{1,2},{2,3},{3,0},{4,5},{5,6},{6,7},{7,4},{8,9},{9,10},{10,1... | collective-permute-start | bytes 18440 | tf_op jit(solution)/shard_map/ppermute | solution.py:53
  52.5 27.2 %collective-permute-start.8 = (bf16[256,128]{1,0:T(8,128)(2,1)S(1)}, bf16[256,128]{1,0:T(8,128)(2,1)S(1)}, u32[]{:S(2)}, u32[]{:S(2)}) collective-permute-start(bf16[256,128]{1,0:T(8,128)(2,1)S(1)} %convolution_convert_fusion.5), channel_id=1, source_target_pairs={{0,3},{1,0},{2,1},{3,2},{4,7},{5,4},{6,5},{7,6},{8,11},{9,8},{10,9... | collective-permute-start | bytes 196616 | tf_op jit(solution)/shard_map/ppermute | solution.py:53
  55.4 25.0 %collective-permute-start.7 = (bf16[256,128]{1,0:T(8,128)(2,1)S(1)}, bf16[256,128]{1,0:T(8,128)(2,1)S(1)}, u32[]{:S(2)}, u32[]{:S(2)}) collective-permute-start(bf16[256,128]{1,0:T(8,128)(2,1)S(1)} %convolution_convert_fusion.5), channel_id=1, source_target_pairs={{0,2},{1,3},{2,0},{3,1},{4,6},{5,7},{6,4},{7,5},{8,10},{9,11},{10,... | collective-permute-start | bytes 196616 | tf_op jit(solution)/shard_map/ppermute | solution.py:53
  80.3 32.6 %collective-permute-start.30 = (bf16[32,4096]{1,0:T(8,128)(2,1)S(1)}, bf16[32,4096]{1,0:T(8,128)(2,1)S(1)}, u32[]{:S(2)}, u32[]{:S(2)}) collective-permute-start(bf16[32,4096]{1,0:T(8,128)(2,1)S(1)} %pad_maximum_fusion.4), channel_id=1, source_target_pairs={{0,3},{1,0},{2,1},{3,2},{4,7},{5,4},{6,5},{7,6},{8,11},{9,8},{10,9... | collective-permute-start | bytes 786440 | tf_op jit(solution)/shard_map/ppermute | solution.py:53
  92.6 24.0 %collective-permute-start.29 = (bf16[32,4096]{1,0:T(8,128)(2,1)S(1)}, bf16[32,4096]{1,0:T(8,128)(2,1)S(1)}, u32[]{:S(2)}, u32[]{:S(2)}) collective-permute-start(bf16[32,4096]{1,0:T(8,128)(2,1)S(1)} %pad_maximum_fusion.4), channel_id=1, source_target_pairs={{0,2},{1,3},{2,0},{3,1},{4,6},{5,7},{6,4},{7,5},{8,10},{9,11},{10,... | collective-permute-start | bytes 786440 | tf_op jit(solution)/shard_map/ppermute | solution.py:53
  97.6 29.2 %collective-permute-start.42 = (bf16[32,4096]{1,0:T(8,128)(2,1)}, bf16[32,4096]{1,0:T(8,128)(2,1)S(1)}, u32[]{:S(2)}, u32[]{:S(2)}) collective-permute-start(bf16[32,4096]{1,0:T(8,128)(2,1)} %constant_dynamic-slice_fusion.39), channel_id=1, source_target_pairs={{0,3},{1,0},{2,1},{3,2},{4,7},{5,4},{6,5},{7,6},{8,11},{9,8},{10,9... | collective-permute-start | bytes 786440 | tf_op jit(solution)/shard_map/ppermute | solution.py:53
  110.0 39.3 %collective-permute-start.41 = (bf16[32,4096]{1,0:T(8,128)(2,1)}, bf16[32,4096]{1,0:T(8,128)(2,1)S(1)}, u32[]{:S(2)}, u32[]{:S(2)}) collective-permute-start(bf16[32,4096]{1,0:T(8,128)(2,1)} %constant_dynamic-slice_fusion.39), channel_id=1, source_target_pairs={{0,2},{1,3},{2,0},{3,1},{4,6},{5,7},{6,4},{7,5},{8,10},{9,11},{10,... | collective-permute-start | bytes 786440 | tf_op jit(solution)/shard_map/ppermute | solution.py:53
  112.9 41.1 %collective-permute-start.40 = (bf16[32,4096]{1,0:T(8,128)(2,1)}, bf16[32,4096]{1,0:T(8,128)(2,1)}, u32[]{:S(2)}, u32[]{:S(2)}) collective-permute-start(bf16[32,4096]{1,0:T(8,128)(2,1)} %constant_dynamic-slice_fusion.39), channel_id=1, source_target_pairs={{0,1},{1,2},{2,3},{3,0},{4,5},{5,6},{6,7},{7,4},{8,9},{9,10},{10,1... | collective-permute-start | bytes 786440 | tf_op jit(solution)/shard_map/ppermute | solution.py:53
  116.6 39.0 %collective-permute-start.54 = (bf16[128,1024]{1,0:T(8,128)(2,1)}, bf16[128,1024]{1,0:T(8,128)(2,1)S(1)}, u32[]{:S(2)}, u32[]{:S(2)}) collective-permute-start(bf16[128,1024]{1,0:T(8,128)(2,1)} %constant_dynamic-slice_fusion.38), channel_id=1, source_target_pairs={{0,3},{1,0},{2,1},{3,2},{4,7},{5,4},{6,5},{7,6},{8,11},{9,8},{10,9... | collective-permute-start | bytes 786440 | tf_op jit(solution)/shard_map/ppermute | solution.py:53
  116.7 43.5 %collective-permute-start.53 = (bf16[128,1024]{1,0:T(8,128)(2,1)}, bf16[128,1024]{1,0:T(8,128)(2,1)S(1)}, u32[]{:S(2)}, u32[]{:S(2)}) collective-permute-start(bf16[128,1024]{1,0:T(8,128)(2,1)} %constant_dynamic-slice_fusion.38), channel_id=1, source_target_pairs={{0,2},{1,3},{2,0},{3,1},{4,6},{5,7},{6,4},{7,5},{8,10},{9,11},{10,... | collective-permute-start | bytes 786440 | tf_op jit(solution)/shard_map/ppermute | solution.py:53
  126.8 33.4 %collective-permute-start.52 = (bf16[128,1024]{1,0:T(8,128)(2,1)}, bf16[128,1024]{1,0:T(8,128)(2,1)}, u32[]{:S(2)}, u32[]{:S(2)}) collective-permute-start(bf16[128,1024]{1,0:T(8,128)(2,1)} %constant_dynamic-slice_fusion.38), channel_id=1, source_target_pairs={{0,1},{1,2},{2,3},{3,0},{4,5},{5,6},{6,7},{7,4},{8,9},{9,10},{10,1... | collective-permute-start | bytes 786440 | tf_op jit(solution)/shard_map/ppermute | solution.py:53
  150.0 29.2 %collective-permute-start.31 = (bf16[3,32,4096]{2,1,0:T(8,128)(2,1)S(1)}, bf16[3,32,4096]{2,1,0:T(8,128)(2,1)}, u32[]{:S(2)}, u32[]{:S(2)}) collective-permute-start(bf16[3,32,4096]{2,1,0:T(8,128)(2,1)S(1)} %pad_maximum_fusion.1.refs_2_), channel_id=1, source_target_pairs={{0,8},{4,12},{8,0},{12,4},{16,24},{20,28},{24,16},{28,20},{1,9},{5... | collective-permute-start | bytes 2359304 | tf_op jit(solution)/shard_map/ppermute | solution.py:48
  173.0 31.2 %collective-permute-start.32 = (bf16[3,32,4096]{2,1,0:T(8,128)(2,1)S(1)}, bf16[3,32,4096]{2,1,0:T(8,128)(2,1)}, u32[]{:S(2)}, u32[]{:S(2)}) collective-permute-start(bf16[3,32,4096]{2,1,0:T(8,128)(2,1)S(1)} %pad_maximum_fusion.1.refs_2_), channel_id=1, source_target_pairs={{0,16},{4,20},{8,24},{12,28},{16,0},{20,4},{24,8},{28,12},{1,17},{... | collective-permute-start | bytes 2359304 | tf_op jit(solution)/shard_map/ppermute | solution.py:48
  175.8 29.5 %collective-permute-start.43 = (bf16[3,32,4096]{2,1,0:T(8,128)(2,1)S(1)}, bf16[3,32,4096]{2,1,0:T(8,128)(2,1)}, u32[]{:S(2)}, u32[]{:S(2)}) collective-permute-start(bf16[3,32,4096]{2,1,0:T(8,128)(2,1)S(1)} %pad_maximum_fusion.2.refs_1_), channel_id=1, source_target_pairs={{0,8},{4,12},{8,0},{12,4},{16,24},{20,28},{24,16},{28,20},{1,9},{5... | collective-permute-start | bytes 2359304 | tf_op jit(solution)/shard_map/ppermute | solution.py:48
  178.0 32.5 %collective-permute-start.44 = (bf16[3,32,4096]{2,1,0:T(8,128)(2,1)S(1)}, bf16[3,32,4096]{2,1,0:T(8,128)(2,1)}, u32[]{:S(2)}, u32[]{:S(2)}) collective-permute-start(bf16[3,32,4096]{2,1,0:T(8,128)(2,1)S(1)} %pad_maximum_fusion.2.refs_1_), channel_id=1, source_target_pairs={{0,16},{4,20},{8,24},{12,28},{16,0},{20,4},{24,8},{28,12},{1,17},{... | collective-permute-start | bytes 2359304 | tf_op jit(solution)/shard_map/ppermute | solution.py:48
  178.6 33.8 %collective-permute-start.55 = (bf16[3,128,1024]{2,1,0:T(8,128)(2,1)S(1)}, bf16[3,128,1024]{2,1,0:T(8,128)(2,1)}, u32[]{:S(2)}, u32[]{:S(2)}) collective-permute-start(bf16[3,128,1024]{2,1,0:T(8,128)(2,1)S(1)} %pad_maximum_fusion.3.refs_1_), channel_id=1, source_target_pairs={{0,8},{4,12},{8,0},{12,4},{16,24},{20,28},{24,16},{28,20},{1,9},{5... | collective-permute-start | bytes 2359304 | tf_op jit(solution)/shard_map/ppermute | solution.py:48
  179.2 48.2 %collective-permute-start.56 = (bf16[3,128,1024]{2,1,0:T(8,128)(2,1)S(1)}, bf16[3,128,1024]{2,1,0:T(8,128)(2,1)}, u32[]{:S(2)}, u32[]{:S(2)}) collective-permute-start(bf16[3,128,1024]{2,1,0:T(8,128)(2,1)S(1)} %pad_maximum_fusion.3.refs_1_), channel_id=1, source_target_pairs={{0,16},{4,20},{8,24},{12,28},{16,0},{20,4},{24,8},{28,12},{1,17},{... | collective-permute-start | bytes 2359304 | tf_op jit(solution)/shard_map/ppermute | solution.py:48
  204.2 36.8 %collective-permute-start.35 = (bf16[3,32,4096]{2,1,0:T(8,128)(2,1)S(1)}, bf16[3,32,4096]{2,1,0:T(8,128)(2,1)S(1)}, u32[]{:S(2)}, u32[]{:S(2)}) collective-permute-start(bf16[3,32,4096]{2,1,0:T(8,128)(2,1)S(1)} %pad_maximum_fusion.1.refs_2_), channel_id=1, source_target_pairs={{0,4},{4,0},{8,12},{12,8},{16,20},{20,16},{24,28},{28,24},{1,5},{5... | collective-permute-start | bytes 2359304 | tf_op jit(solution)/shard_map/ppermute | solution.py:48
  205.3 30.1 %collective-permute-start.33 = (bf16[3,16,4096]{2,1,0:T(8,128)(2,1)S(1)}, bf16[3,16,4096]{2,1,0:T(8,128)(2,1)S(1)}, u32[]{:S(2)}, u32[]{:S(2)}) collective-permute-start(bf16[3,16,4096]{2,1,0:T(8,128)(2,1)S(1)} %slice.261), channel_id=1, source_target_pairs={{0,16},{4,20},{8,24},{12,28},{16,0},{20,4},{24,8},{28,12},{1,17},{... | collective-permute-start | bytes 1179656 | tf_op jit(solution)/shard_map/ppermute | solution.py:48
  210.5 25.0 %collective-permute-start.34 = (bf16[3,16,4096]{2,1,0:T(8,128)(2,1)S(1)}, bf16[3,16,4096]{2,1,0:T(8,128)(2,1)S(1)}, u32[]{:S(2)}, u32[]{:S(2)}) collective-permute-start(bf16[3,16,4096]{2,1,0:T(8,128)(2,1)S(1)} %slice.262), channel_id=1, source_target_pairs={{0,8},{4,12},{8,0},{12,4},{16,24},{20,28},{24,16},{28,20},{1,9},{5... | collective-permute-start | bytes 1179656 | tf_op jit(solution)/shard_map/ppermute | solution.py:48
  212.4 28.7 %collective-permute-start.36 = (bf16[3,32,4096]{2,1,0:T(8,128)(2,1)}, bf16[3,32,4096]{2,1,0:T(8,128)(2,1)S(1)}, u32[]{:S(2)}, u32[]{:S(2)}) collective-permute-start(bf16[3,32,4096]{2,1,0:T(8,128)(2,1)} %collective-permute-done.31.refs_3_), channel_id=1, source_target_pairs={{0,4},{4,0},{8,12},{12,8},{16,20},{20,16},{24,28},{28,24},{1,5},{5... | collective-permute-start | bytes 2359304 | tf_op jit(solution)/shard_map/ppermute | solution.py:48
  241.0 30.7 %collective-permute-start.47 = (bf16[3,32,4096]{2,1,0:T(8,128)(2,1)S(1)}, bf16[3,32,4096]{2,1,0:T(8,128)(2,1)S(1)}, u32[]{:S(2)}, u32[]{:S(2)}) collective-permute-start(bf16[3,32,4096]{2,1,0:T(8,128)(2,1)S(1)} %pad_maximum_fusion.2.refs_1_), channel_id=1, source_target_pairs={{0,4},{4,0},{8,12},{12,8},{16,20},{20,16},{24,28},{28,24},{1,5},{5... | collective-permute-start | bytes 2359304 | tf_op jit(solution)/shard_map/ppermute | solution.py:48
  241.1 31.6 %collective-permute-start.45 = (bf16[3,16,4096]{2,1,0:T(8,128)(2,1)S(1)}, bf16[3,16,4096]{2,1,0:T(8,128)(2,1)S(1)}, u32[]{:S(2)}, u32[]{:S(2)}) collective-permute-start(bf16[3,16,4096]{2,1,0:T(8,128)(2,1)S(1)} %slice.266), channel_id=1, source_target_pairs={{0,16},{4,20},{8,24},{12,28},{16,0},{20,4},{24,8},{28,12},{1,17},{... | collective-permute-start | bytes 1179656 | tf_op jit(solution)/shard_map/ppermute | solution.py:48
  242.9 30.5 %collective-permute-start.46 = (bf16[3,16,4096]{2,1,0:T(8,128)(2,1)S(1)}, bf16[3,16,4096]{2,1,0:T(8,128)(2,1)S(1)}, u32[]{:S(2)}, u32[]{:S(2)}) collective-permute-start(bf16[3,16,4096]{2,1,0:T(8,128)(2,1)S(1)} %slice.267), channel_id=1, source_target_pairs={{0,8},{4,12},{8,0},{12,4},{16,24},{20,28},{24,16},{28,20},{1,9},{5... | collective-permute-start | bytes 1179656 | tf_op jit(solution)/shard_map/ppermute | solution.py:48
  244.3 29.1 %collective-permute-start.57 = (bf16[3,64,1024]{2,1,0:T(8,128)(2,1)S(1)}, bf16[3,64,1024]{2,1,0:T(8,128)(2,1)}, u32[]{:S(2)}, u32[]{:S(2)}) collective-permute-start(bf16[3,64,1024]{2,1,0:T(8,128)(2,1)S(1)} %slice.269), channel_id=1, source_target_pairs={{0,16},{4,20},{8,24},{12,28},{16,0},{20,4},{24,8},{28,12},{1,17},{... | collective-permute-start | bytes 1179656 | tf_op jit(solution)/shard_map/ppermute | solution.py:48
  244.6 39.3 %collective-permute-start.48 = (bf16[3,32,4096]{2,1,0:T(8,128)(2,1)}, bf16[3,32,4096]{2,1,0:T(8,128)(2,1)S(1)}, u32[]{:S(2)}, u32[]{:S(2)}) collective-permute-start(bf16[3,32,4096]{2,1,0:T(8,128)(2,1)} %collective-permute-done.43.refs_2_), channel_id=1, source_target_pairs={{0,4},{4,0},{8,12},{12,8},{16,20},{20,16},{24,28},{28,24},{1,5},{5... | collective-permute-start | bytes 2359304 | tf_op jit(solution)/shard_map/ppermute | solution.py:48
  283.9 26.4 %collective-permute-start.59 = (bf16[3,128,1024]{2,1,0:T(8,128)(2,1)S(1)}, bf16[3,128,1024]{2,1,0:T(8,128)(2,1)}, u32[]{:S(2)}, u32[]{:S(2)}) collective-permute-start(bf16[3,128,1024]{2,1,0:T(8,128)(2,1)S(1)} %pad_maximum_fusion.3.refs_1_), channel_id=1, source_target_pairs={{0,4},{4,0},{8,12},{12,8},{16,20},{20,16},{24,28},{28,24},{1,5},{5... | collective-permute-start | bytes 2359304 | tf_op jit(solution)/shard_map/ppermute | solution.py:48
  283.9 26.4 %collective-permute-start.60 = (bf16[3,128,1024]{2,1,0:T(8,128)(2,1)}, bf16[3,128,1024]{2,1,0:T(8,128)(2,1)}, u32[]{:S(2)}, u32[]{:S(2)}) collective-permute-start(bf16[3,128,1024]{2,1,0:T(8,128)(2,1)} %collective-permute-done.55.refs_2_), channel_id=1, source_target_pairs={{0,4},{4,0},{8,12},{12,8},{16,20},{20,16},{24,28},{28,24},{1,5},{5... | collective-permute-start | bytes 2359304 | tf_op jit(solution)/shard_map/ppermute | solution.py:48
  284.4 25.9 %collective-permute-start.61 = (bf16[3,128,1024]{2,1,0:T(8,128)(2,1)}, bf16[3,128,1024]{2,1,0:T(8,128)(2,1)}, u32[]{:S(2)}, u32[]{:S(2)}) collective-permute-start(bf16[3,128,1024]{2,1,0:T(8,128)(2,1)} %collective-permute-done.56.refs_3_), channel_id=1, source_target_pairs={{0,4},{4,0},{8,12},{12,8},{16,20},{20,16},{24,28},{28,24},{1,5},{5... | collective-permute-start | bytes 2359304 | tf_op jit(solution)/shard_map/ppermute | solution.py:48
  284.5 25.9 %collective-permute-start.62 = (bf16[3,64,1024]{2,1,0:T(8,128)(2,1)}, bf16[3,64,1024]{2,1,0:T(8,128)(2,1)}, u32[]{:S(2)}, u32[]{:S(2)}) collective-permute-start(bf16[3,64,1024]{2,1,0:T(8,128)(2,1)} %collective-permute-done.57.refs_4_), channel_id=1, source_target_pairs={{0,4},{4,0},{8,12},{12,8},{16,20},{20,16},{24,28},{28,24},{1,5},{5... | collective-permute-start | bytes 1179656 | tf_op jit(solution)/shard_map/ppermute | solution.py:48
  284.9 25.4 %collective-permute-start.63 = (bf16[3,64,1024]{2,1,0:T(8,128)(2,1)}, bf16[3,64,1024]{2,1,0:T(8,128)(2,1)}, u32[]{:S(2)}, u32[]{:S(2)}) collective-permute-start(bf16[3,64,1024]{2,1,0:T(8,128)(2,1)} %collective-permute-done.58.refs_5_), channel_id=1, source_target_pairs={{0,4},{4,0},{8,12},{12,8},{16,20},{20,16},{24,28},{28,24},{1,5},{5... | collective-permute-start | bytes 1179656 | tf_op jit(solution)/shard_map/ppermute | solution.py:48
  386.5 21.3 %collective-permute-start.70 = (bf16[144,256]{1,0:T(8,128)(2,1)S(1)}, bf16[144,256]{1,0:T(8,128)(2,1)S(1)}, u32[]{:S(2)}, u32[]{:S(2)}) collective-permute-start(bf16[144,256]{1,0:T(8,128)(2,1)S(1)} %get-tuple-element.141), channel_id=1, source_target_pairs={{0,28},{4,24},{8,20},{12,16},{16,12},{20,8},{24,4},{28,0},{1,29},{... | collective-permute-start | bytes 221192 | tf_op jit(solution)/shard_map/ppermute | solution.py:48
  389.5 33.6 %collective-permute-start.68 = (bf16[144,256]{1,0:T(8,128)(2,1)}, bf16[144,256]{1,0:T(8,128)(2,1)}, u32[]{:S(2)}, u32[]{:S(2)}) collective-permute-start(bf16[144,256]{1,0:T(8,128)(2,1)} %get-tuple-element.143), channel_id=1, source_target_pairs={{0,20},{4,16},{8,28},{12,24},{16,4},{20,0},{24,12},{28,8},{1,21},{... | collective-permute-start | bytes 221192 | tf_op jit(solution)/shard_map/ppermute | solution.py:48
  390.6 33.0 %collective-permute-start.67 = (bf16[144,256]{1,0:T(8,128)(2,1)}, bf16[144,256]{1,0:T(8,128)(2,1)}, u32[]{:S(2)}, u32[]{:S(2)}) collective-permute-start(bf16[144,256]{1,0:T(8,128)(2,1)} %get-tuple-element.144), channel_id=1, source_target_pairs={{0,16},{4,20},{8,24},{12,28},{16,0},{20,4},{24,8},{28,12},{1,17},{... | collective-permute-start | bytes 221192 | tf_op jit(solution)/shard_map/ppermute | solution.py:48
  391.3 32.4 %collective-permute-start.66 = (bf16[144,256]{1,0:T(8,128)(2,1)S(1)}, bf16[144,256]{1,0:T(8,128)(2,1)}, u32[]{:S(2)}, u32[]{:S(2)}) collective-permute-start(bf16[144,256]{1,0:T(8,128)(2,1)S(1)} %get-tuple-element.145), channel_id=1, source_target_pairs={{0,12},{4,8},{8,4},{12,0},{16,28},{20,24},{24,20},{28,16},{1,13},{... | collective-permute-start | bytes 221192 | tf_op jit(solution)/shard_map/ppermute | solution.py:48
  423.0 46.1 %collective-permute-start.84 = (bf16[512,1024]{1,0:T(8,128)(2,1)S(1)}, bf16[512,1024]{1,0:T(8,128)(2,1)}, u32[]{:S(2)}, u32[]{:S(2)}) collective-permute-start(bf16[512,1024]{1,0:T(8,128)(2,1)S(1)} %copy-done.74), channel_id=1, source_target_pairs={{0,4},{4,0},{8,12},{12,8},{16,20},{20,16},{24,28},{28,24},{1,5},{5... | collective-permute-start | bytes 3145736 | tf_op jit(solution)/shard_map/ppermute | solution.py:48
  423.6 99.0 %collective-permute-start.102 = (bf16[512,1024]{1,0:T(8,128)(2,1)}, bf16[512,1024]{1,0:T(8,128)(2,1)}, u32[]{:S(2)}, u32[]{:S(2)}) collective-permute-start(bf16[512,1024]{1,0:T(8,128)(2,1)} %copy-done.101), channel_id=1, source_target_pairs={{0,4},{4,0},{8,12},{12,8},{16,20},{20,16},{24,28},{28,24},{1,5},{5... | collective-permute-start | bytes 3145736 | tf_op jit(solution)/shard_map/ppermute | solution.py:48
  430.7 86.1 %collective-permute-start.104 = (bf16[512,1024]{1,0:T(8,128)(2,1)S(1)}, bf16[512,1024]{1,0:T(8,128)(2,1)}, u32[]{:S(2)}, u32[]{:S(2)}) collective-permute-start(bf16[512,1024]{1,0:T(8,128)(2,1)S(1)} %copy-done.72), channel_id=1, source_target_pairs={{0,4},{4,0},{8,12},{12,8},{16,20},{20,16},{24,28},{28,24},{1,5},{5... | collective-permute-start | bytes 3145736 | tf_op jit(solution)/shard_map/ppermute | solution.py:48
  433.7 35.9 %collective-permute-start.85 = (bf16[512,512]{1,0:T(8,128)(2,1)}, bf16[512,512]{1,0:T(8,128)(2,1)}, u32[]{:S(2)}, u32[]{:S(2)}) collective-permute-start(bf16[512,512]{1,0:T(8,128)(2,1)} %get-tuple-element.138), channel_id=1, source_target_pairs={{0,4},{4,0},{8,12},{12,8},{16,20},{20,16},{24,28},{28,24},{1,5},{5... | collective-permute-start | bytes 1572872 | tf_op jit(solution)/shard_map/ppermute | solution.py:48
  462.8 52.7 %collective-permute-start.105 = (bf16[512,512]{1,0:T(8,128)(2,1)}, bf16[512,512]{1,0:T(8,128)(2,1)}, u32[]{:S(2)}, u32[]{:S(2)}) collective-permute-start(bf16[512,512]{1,0:T(8,128)(2,1)} %get-tuple-element.134), channel_id=1, source_target_pairs={{0,4},{4,0},{8,12},{12,8},{16,20},{20,16},{24,28},{28,24},{1,5},{5... | collective-permute-start | bytes 1572872 | tf_op jit(solution)/shard_map/ppermute | solution.py:48
  469.2 53.5 %collective-permute-start.103 = (bf16[512,1536]{1,0:T(8,128)(2,1)}, bf16[512,1536]{1,0:T(8,128)(2,1)}, u32[]{:S(2)}, u32[]{:S(2)}) collective-permute-start(bf16[512,1536]{1,0:T(8,128)(2,1)} %get-tuple-element.111), channel_id=1, source_target_pairs={{0,4},{4,0},{8,12},{12,8},{16,20},{20,16},{24,28},{28,24},{1,5},{5... | collective-permute-start | bytes 4718600 | tf_op jit(solution)/shard_map/ppermute | solution.py:48
  520.7 31.0 %collective-permute-start.141 = (bf16[512,1024]{1,0:T(8,128)(2,1)}, bf16[512,1024]{1,0:T(8,128)(2,1)}, u32[]{:S(2)}, u32[]{:S(2)}) collective-permute-start(bf16[512,1024]{1,0:T(8,128)(2,1)} %param.45), channel_id=1, source_target_pairs={{0,4},{4,0},{8,12},{12,8},{16,20},{20,16},{24,28},{28,24},{1,5},{5... | collective-permute-start | bytes 3145736 | tf_op jit(solution)/shard_map/ppermute | solution.py:48
  522.6 22.4 %collective-permute-start.140 = (bf16[512,4,512]{2,0,1:T(8,128)(2,1)S(1)}, bf16[512,4,512]{2,0,1:T(8,128)(2,1)S(1)}, u32[]{:S(2)}, u32[]{:S(2)}) collective-permute-start(bf16[512,4,512]{2,0,1:T(8,128)(2,1)S(1)} %bitcast.432), channel_id=1, source_target_pairs={{0,4},{4,0},{8,12},{12,8},{16,20},{20,16},{24,28},{28,24},{1,5},{5... | collective-permute-start | bytes 6291464 | tf_op jit(solution)/shard_map/ppermute | solution.py:48
  522.6 128.5 %collective-permute-start.83 = (bf16[256]{0:T(256)(128)(2,1)}, bf16[256]{0:T(256)(128)(2,1)S(1)}, u32[]{:S(2)}, u32[]{:S(2)}) collective-permute-start(bf16[256]{0:T(256)(128)(2,1)} %get-tuple-element.87), channel_id=1, source_target_pairs={{0,3},{1,0},{2,1},{3,2},{4,7},{5,4},{6,5},{7,6},{8,11},{9,8},{10,9... | collective-permute-start | bytes 1544 | tf_op jit(solution)/shard_map/ppermute | solution.py:53
  533.4 26.7 %collective-permute-start.106 = (bf16[4,2,32,2048]{3,2,0,1:T(8,128)(2,1)}, bf16[4,2,32,2048]{3,2,0,1:T(8,128)(2,1)}, u32[]{:S(2)}, u32[]{:S(2)}) collective-permute-start(bf16[4,2,32,2048]{3,2,0,1:T(8,128)(2,1)} %bitcast.398), channel_id=1, source_target_pairs={{0,8},{4,12},{8,0},{12,4},{16,24},{20,28},{24,16},{28,20},{1,9},{5... | collective-permute-start | bytes 3145736 | tf_op jit(solution)/shard_map/ppermute | solution.py:48
  534.3 29.7 %collective-permute-start.108 = (bf16[4,2,32,2048]{3,2,0,1:T(8,128)(2,1)}, bf16[4,2,32,2048]{3,2,0,1:T(8,128)(2,1)}, u32[]{:S(2)}, u32[]{:S(2)}) collective-permute-start(bf16[4,2,32,2048]{3,2,0,1:T(8,128)(2,1)} %bitcast.397), channel_id=1, source_target_pairs={{0,16},{4,20},{8,24},{12,28},{16,0},{20,4},{24,8},{28,12},{1,17},{... | collective-permute-start | bytes 3145736 | tf_op jit(solution)/shard_map/ppermute | solution.py:48
  546.4 49.7 %collective-permute-start.124 = (bf16[4,2,32,2048]{3,2,0,1:T(8,128)(2,1)}, bf16[4,2,32,2048]{3,2,0,1:T(8,128)(2,1)}, u32[]{:S(2)}, u32[]{:S(2)}) collective-permute-start(bf16[4,2,32,2048]{3,2,0,1:T(8,128)(2,1)} %bitcast.396), channel_id=1, source_target_pairs={{0,8},{4,12},{8,0},{12,4},{16,24},{20,28},{24,16},{28,20},{1,9},{5... | collective-permute-start | bytes 3145736 | tf_op jit(solution)/shard_map/ppermute | solution.py:48
  551.8 66.5 %collective-permute-start.126 = (bf16[4,2,32,2048]{3,2,0,1:T(8,128)(2,1)}, bf16[4,2,32,2048]{3,2,0,1:T(8,128)(2,1)S(1)}, u32[]{:S(2)}, u32[]{:S(2)}) collective-permute-start(bf16[4,2,32,2048]{3,2,0,1:T(8,128)(2,1)} %bitcast.434), channel_id=1, source_target_pairs={{0,16},{4,20},{8,24},{12,28},{16,0},{20,4},{24,8},{28,12},{1,17},{... | collective-permute-start | bytes 3145736 | tf_op jit(solution)/shard_map/ppermute | solution.py:48
  562.9 30.6 %collective-permute-start.107 = (bf16[4,32,2048]{2,1,0:T(8,128)(2,1)S(1)}, bf16[4,32,2048]{2,1,0:T(8,128)(2,1)S(1)}, u32[]{:S(2)}, u32[]{:S(2)}) collective-permute-start(bf16[4,32,2048]{2,1,0:T(8,128)(2,1)S(1)} %dynamic-slice_bitcast_fusion.5), channel_id=1, source_target_pairs={{0,16},{4,20},{8,24},{12,28},{16,0},{20,4},{24,8},{28,12},{1,17},{... | collective-permute-start | bytes 1572872 | tf_op jit(solution)/shard_map/ppermute | solution.py:48
  565.7 29.0 %collective-permute-start.109 = (bf16[4,32,2048]{2,1,0:T(8,128)(2,1)S(1)}, bf16[4,32,2048]{2,1,0:T(8,128)(2,1)S(1)}, u32[]{:S(2)}, u32[]{:S(2)}) collective-permute-start(bf16[4,32,2048]{2,1,0:T(8,128)(2,1)S(1)} %dynamic-slice_bitcast_fusion.4), channel_id=1, source_target_pairs={{0,8},{4,12},{8,0},{12,4},{16,24},{20,28},{24,16},{28,20},{1,9},{5... | collective-permute-start | bytes 1572872 | tf_op jit(solution)/shard_map/ppermute | solution.py:48
  593.4 24.4 %collective-permute-start.142 = (bf16[4,2,64,1024]{3,2,0,1:T(8,128)(2,1)S(1)}, bf16[4,2,64,1024]{3,2,0,1:T(8,128)(2,1)S(1)}, u32[]{:S(2)}, u32[]{:S(2)}) collective-permute-start(bf16[4,2,64,1024]{3,2,0,1:T(8,128)(2,1)S(1)} %bitcast.436), channel_id=1, source_target_pairs={{0,8},{4,12},{8,0},{12,4},{16,24},{20,28},{24,16},{28,20},{1,9},{5... | collective-permute-start | bytes 3145736 | tf_op jit(solution)/shard_map/ppermute | solution.py:48
  594.7 25.6 %collective-permute-start.144 = (bf16[4,2,64,1024]{3,2,0,1:T(8,128)(2,1)S(1)}, bf16[4,2,64,1024]{3,2,0,1:T(8,128)(2,1)S(1)}, u32[]{:S(2)}, u32[]{:S(2)}) collective-permute-start(bf16[4,2,64,1024]{3,2,0,1:T(8,128)(2,1)S(1)} %bitcast.435), channel_id=1, source_target_pairs={{0,16},{4,20},{8,24},{12,28},{16,0},{20,4},{24,8},{28,12},{1,17},{... | collective-permute-start | bytes 3145736 | tf_op jit(solution)/shard_map/ppermute | solution.py:48
  596.1 25.9 %collective-permute-start.112 = (bf16[2,32,2048]{2,1,0:T(8,128)(2,1)S(1)}, bf16[2,32,2048]{2,1,0:T(8,128)(2,1)S(1)}, u32[]{:S(2)}, u32[]{:S(2)}) collective-permute-start(bf16[2,32,2048]{2,1,0:T(8,128)(2,1)S(1)} %get-tuple-element.132), channel_id=1, source_target_pairs={{0,3},{1,0},{2,1},{3,2},{4,7},{5,4},{6,5},{7,6},{8,11},{9,8},{10,9... | collective-permute-start | bytes 786440 | tf_op jit(solution)/shard_map/ppermute | solution.py:53
  622.0 29.2 %collective-permute-start.82 = (bf16[256]{0:T(256)(128)(2,1)}, bf16[256]{0:T(256)(128)(2,1)S(1)}, u32[]{:S(2)}, u32[]{:S(2)}) collective-permute-start(bf16[256]{0:T(256)(128)(2,1)} %get-tuple-element.88), channel_id=1, source_target_pairs={{0,2},{1,3},{2,0},{3,1},{4,6},{5,7},{6,4},{7,5},{8,10},{9,11},{10,... | collective-permute-start | bytes 1544 | tf_op jit(solution)/shard_map/ppermute | solution.py:53
  670.0 28.9 %collective-permute-start.129 = (bf16[2,32,2048]{2,1,0:T(8,128)(2,1)S(1)}, bf16[2,32,2048]{2,1,0:T(8,128)(2,1)S(1)}, u32[]{:S(2)}, u32[]{:S(2)}) collective-permute-start(bf16[2,32,2048]{2,1,0:T(8,128)(2,1)S(1)} %get-tuple-element.128), channel_id=1, source_target_pairs={{0,2},{1,3},{2,0},{3,1},{4,6},{5,7},{6,4},{7,5},{8,10},{9,11},{10,... | collective-permute-start | bytes 786440 | tf_op jit(solution)/shard_map/ppermute | solution.py:53
  670.1 28.9 %collective-permute-start.128 = (bf16[2,32,2048]{2,1,0:T(8,128)(2,1)S(1)}, bf16[2,32,2048]{2,1,0:T(8,128)(2,1)S(1)}, u32[]{:S(2)}, u32[]{:S(2)}) collective-permute-start(bf16[2,32,2048]{2,1,0:T(8,128)(2,1)S(1)} %get-tuple-element.127), channel_id=1, source_target_pairs={{0,1},{1,2},{2,3},{3,0},{4,5},{5,6},{6,7},{7,4},{8,9},{9,10},{10,1... | collective-permute-start | bytes 786440 | tf_op jit(solution)/shard_map/ppermute | solution.py:53
  672.8 26.4 %collective-permute-start.117 = (bf16[64,2048]{1,0:T(8,128)(2,1)S(1)}, bf16[64,2048]{1,0:T(8,128)(2,1)S(1)}, u32[]{:S(2)}, u32[]{:S(2)}) collective-permute-start(bf16[64,2048]{1,0:T(8,128)(2,1)S(1)} %bitcast.405), channel_id=1, source_target_pairs={{0,4},{4,0},{8,12},{12,8},{16,20},{20,16},{24,28},{28,24},{1,5},{5... | collective-permute-start | bytes 786440 | tf_op jit(solution)/shard_map/ppermute | solution.py:48
  673.7 26.9 %collective-permute-start.115 = (bf16[32,2048]{1,0:T(8,128)(2,1)S(1)}, bf16[32,2048]{1,0:T(8,128)(2,1)S(1)}, u32[]{:S(2)}, u32[]{:S(2)}) collective-permute-start(bf16[32,2048]{1,0:T(8,128)(2,1)S(1)} %slice.287), channel_id=1, source_target_pairs={{0,16},{4,20},{8,24},{12,28},{16,0},{20,4},{24,8},{28,12},{1,17},{... | collective-permute-start | bytes 393224 | tf_op jit(solution)/shard_map/ppermute | solution.py:48
  677.1 23.4 %collective-permute-start.148 = (bf16[2,64,1024]{2,1,0:T(8,128)(2,1)S(1)}, bf16[2,64,1024]{2,1,0:T(8,128)(2,1)S(1)}, u32[]{:S(2)}, u32[]{:S(2)}) collective-permute-start(bf16[2,64,1024]{2,1,0:T(8,128)(2,1)S(1)} %get-tuple-element.126), channel_id=1, source_target_pairs={{0,3},{1,0},{2,1},{3,2},{4,7},{5,4},{6,5},{7,6},{8,11},{9,8},{10,9... | collective-permute-start | bytes 786440 | tf_op jit(solution)/shard_map/ppermute | solution.py:53
  732.4 28.1 %collective-permute-start.153 = (bf16[128,1024]{1,0:T(8,128)(2,1)S(1)}, bf16[128,1024]{1,0:T(8,128)(2,1)}, u32[]{:S(2)}, u32[]{:S(2)}) collective-permute-start(bf16[128,1024]{1,0:T(8,128)(2,1)S(1)} %bitcast.413), channel_id=1, source_target_pairs={{0,4},{4,0},{8,12},{12,8},{16,20},{20,16},{24,28},{28,24},{1,5},{5... | collective-permute-start | bytes 786440 | tf_op jit(solution)/shard_map/ppermute | solution.py:48
  733.1 27.4 %collective-permute-start.154 = (bf16[128,1024]{1,0:T(8,128)(2,1)S(1)}, bf16[128,1024]{1,0:T(8,128)(2,1)}, u32[]{:S(2)}, u32[]{:S(2)}) collective-permute-start(bf16[128,1024]{1,0:T(8,128)(2,1)S(1)} %collective-permute-done.149.refs_1_), channel_id=1, source_target_pairs={{0,4},{4,0},{8,12},{12,8},{16,20},{20,16},{24,28},{28,24},{1,5},{5... | collective-permute-start | bytes 786440 | tf_op jit(solution)/shard_map/ppermute | solution.py:48
  734.3 26.2 %collective-permute-start.155 = (bf16[128,1024]{1,0:T(8,128)(2,1)S(1)}, bf16[128,1024]{1,0:T(8,128)(2,1)}, u32[]{:S(2)}, u32[]{:S(2)}) collective-permute-start(bf16[128,1024]{1,0:T(8,128)(2,1)S(1)} %collective-permute-done.150.refs_2_), channel_id=1, source_target_pairs={{0,4},{4,0},{8,12},{12,8},{16,20},{20,16},{24,28},{28,24},{1,5},{5... | collective-permute-start | bytes 786440 | tf_op jit(solution)/shard_map/ppermute | solution.py:48
  (229 other events, 2785.9 us)

commit v2 on v1

--- a/solution.py
+++ b/solution.py
@@ -43,9 +43,20 @@
     return high, (a - high.astype(f32)).astype(bf16)
 
 
-def swap_wide(a, bits):
-    size = lax.axis_size("wide")
-    return lax.ppermute(a, "wide", [(i, i ^ bits) for i in range(size)])
+def wide_pairs(bits_of):
+    return [(i, i ^ bits_of(i)) for i in range(lax.axis_size("wide"))]
+
+
+def over_core(a):
+    return lax.ppermute(a, "wide", wide_pairs(lambda i: 1))
+
+
+def over_first(a):
+    return lax.ppermute(a, "wide", wide_pairs(lambda i: 4 if i & 1 else 2))
+
+
+def over_second(a):
+    return lax.ppermute(a, "wide", wide_pairs(lambda i: 2 if i & 1 else 4))
 
 
 def turn_narrow(a, by):
@@ -57,22 +68,73 @@
     return lax.dynamic_index_in_dim(a, at, axis, keepdims=False)
 
 
-def spread_plane(piece):
-    half = piece.shape[-2] // 2
-    from_x = swap_wide(piece, 2)
-    from_y = swap_wide(piece, 4)
-    low = swap_wide(from_x[..., :half, :], 4)
-    high = swap_wide(from_y[..., half:, :], 2)
-    here = [(0, 0, piece), (2, 0, from_x), (4, 0, from_y), (6, 0, low), (6, half, high)]
-    there = [(bits | 1, start, swap_wide(part, 1)) for bits, start, part in here]
-    return here + there
-
-
-def assemble_kernel(layout, n_shards, n_parts, spot, *refs):
-    shards = refs[:n_shards]
-    parts = refs[n_shards : n_shards + n_parts]
-    fulls = refs[n_shards + n_parts : 2 * n_shards + n_parts]
-    sems = refs[-1]
+class Order:
+    def __init__(self):
+        self.last = None
+
+    def hold(self, *arrays):
+        if self.last is not None:
+            arrays = lax.optimization_barrier((*arrays, self.last))[:-1]
+        return arrays[0] if len(arrays) == 1 else arrays
+
+    def mark(self, array):
+        self.last = array
+
+
+class Spread:
+    def __init__(self, own, order):
+        self.order = order
+        self.own = own
+        self.other = over_core(own)
+
+    def near_step(self):
+        other = self.order.hold(self.other)
+        self.other = other
+        both = jnp.stack([self.own, other])
+        self.order.mark(both)
+        self.near = over_first(both)
+
+    def corner_step(self):
+        self.near = self.order.hold(self.near)
+        corner = self.near[0]
+        self.order.mark(corner)
+        self.corner = over_second(corner)
+        self.far = over_core(self.near)
+
+    def last_step(self):
+        self.corner = self.order.hold(self.corner)
+        self.order.mark(self.corner)
+        self.corner_other = over_core(self.corner)
+
+    def parts(self):
+        parts = [self.own, self.other, self.near, self.far, self.corner, self.corner_other]
+        return list(self.order.hold(*parts))
+
+
+def origins(p, parts):
+    own, other, near, far, corner, corner_other = parts
+    first = 2 + 2 * (p & 1)
+    second = 6 - first
+    return [
+        (p, own),
+        (p ^ 1, other),
+        (p ^ first, near.at[0]),
+        (p ^ first ^ 1, near.at[1]),
+        (p ^ second ^ 1, far.at[0]),
+        (p ^ second, far.at[1]),
+        (p ^ 6, corner),
+        (p ^ 7, corner_other),
+    ]
+
+
+def core_and_quarter(place):
+    core, x, y = place & 1, (place >> 1) & 1, place >> 2
+    return core, jnp.where(core == 0, 2 * x + y, 2 * y + x)
+
+
+def assemble_kernel(n_shards, spot, *refs):
+    shards, parts = refs[:n_shards], refs[n_shards : n_shards + 6]
+    fulls, sems = refs[n_shards + 6 : -1], refs[-1]
     z, p = spot[0], spot[1]
     copies = []
 
@@ -84,32 +146,27 @@
     for shard, full in zip(shards, fulls):
         rows = shard.shape[0]
         start(shard, full.at[pl.ds(pl.multiple_of(z * rows, rows), rows), :])
-    for (bits, first), part in zip(layout, parts):
-        count = part.shape[1]
+    for place, part in origins(p, parts):
         for turn in range(1, 4):
             origin = lax.rem(z - turn + 4, 4)
             left = 0
             for full in fulls:
                 rows, width = full.shape[0] // 4, full.shape[1]
-                at = origin * rows + (p ^ bits) * (rows // SUB) + first
-                start(
-                    part.at[turn - 1, :, left : left + width],
-                    full.at[pl.ds(pl.multiple_of(at, 16), count), :],
-                )
+                count = rows // SUB
+                at = pl.multiple_of(origin * rows + place * count, count)
+                start(part.at[turn - 1, :, left : left + width], full.at[pl.ds(at, count), :])
                 left += width
     for copy in copies:
         copy.wait()
 
 
 def assemble(shards, parts, spot):
-    layout = tuple((bits, first) for bits, first, _ in parts)
-    arrays = [part for _, _, part in parts]
-    n_copies = len(shards) * (1 + 3 * len(parts))
+    n_copies = len(shards) * 25
     return pl.pallas_call(
-        functools.partial(assemble_kernel, layout, len(shards), len(parts)),
+        functools.partial(assemble_kernel, len(shards)),
         out_shape=[jax.ShapeDtypeStruct((4 * s.shape[0], s.shape[1]), s.dtype) for s in shards],
         in_specs=[pl.BlockSpec(memory_space=pltpu.SMEM)]
-        + [pl.BlockSpec(memory_space=pl.ANY)] * (len(shards) + len(arrays)),
+        + [pl.BlockSpec(memory_space=pl.ANY)] * (len(shards) + 6),
         out_specs=[pl.BlockSpec(memory_space=pltpu.VMEM)] * len(shards),
         scratch_shapes=[pltpu.SemaphoreType.DMA((n_copies,))],
         compiler_params=pltpu.CompilerParams(vmem_limit_bytes=40 * MB),
@@ -117,7 +174,7 @@
             flops=0, transcendentals=0, bytes_accessed=sum(16 * s.size for s in shards)
         ),
         name="assemble",
-    )(spot, *shards, *arrays)
+    )(spot, *shards, *parts)
 
 
 def pieces_of(shards, p):
@@ -130,31 +187,39 @@
     )
 
 
-def gather(shards, p, spot):
-    piece = pieces_of(shards, p)
-    bundle = jnp.stack([turn_narrow(piece, turn) for turn in (1, 2, 3)])
-    return assemble(shards, spread_plane(bundle), spot)
+def around_narrow(piece):
+    return jnp.stack([turn_narrow(piece, turn) for turn in (1, 2, 3)])
 
 
 def add_two(a, b):
     return (a.astype(f32) + b.astype(f32)).astype(bf16)
 
 
-def reduce_plane(grad, x, y, z):
-    sent_x = take(grad[:, :, :, 0], 1 - x, 2)
-    sent_y = take(grad[:, :, :, 1], 1 - y, 1)
-    got_x = swap_wide(sent_x, 2)
-    got_y = swap_wide(sent_y, 4)
-    first = add_two(take(grad[:, :, :, 0], x, 2), got_x)
-    second = add_two(take(grad[:, :, :, 1], y, 1), got_y)
-    got_first = swap_wide(take(first, 1 - y, 1), 4)
-    got_second = swap_wide(take(second, 1 - x, 1), 2)
-    both = jnp.stack(
-        [add_two(take(first, y, 1), got_first), add_two(take(second, x, 1), got_second)], axis=1
-    )
-    total = take(both, z, 0).astype(f32)
-    for turn in (1, 2, 3):
-        total = total + turn_narrow(take(both, (z + turn) % 4, 0), turn).astype(f32)
+def first_and_second(p):
+    core, x, y = p & 1, (p >> 1) & 1, p >> 2
+    return jnp.where(core == 0, x, y), jnp.where(core == 0, y, x)
+
+
+def reduce_first(grad, p):
+    first, _ = first_and_second(p)
+    axis = grad.ndim - 4
+    return take(grad, first, axis), over_first(take(grad, 1 - first, axis))
+
+
+def reduce_second(grad, p):
+    _, second = first_and_second(p)
+    axis = grad.ndim - 3
+    return take(grad, second, axis), over_second(take(grad, 1 - second, axis))
+
+
+def send_narrow(pick, z):
+    return [pick(z)] + [turn_narrow(pick((z + turn) % 4), turn) for turn in (1, 2, 3)]
+
+
+def add_four(parts):
+    total = parts[0].astype(f32)
+    for part in parts[1:]:
+        total = total + part.astype(f32)
     return across_groups(total.astype(bf16))
 
 
@@ -166,72 +231,85 @@
     return lax.psum(a.astype(f32), "wide", axis_index_groups=members).astype(bf16)
 
 
-def place_kernel(layout, spans, row_split, n_parts, spot, *refs):
-    parts, outs = refs[:n_parts], refs[n_parts:]
-    p = spot[1]
-    for (bits, first), part in zip(layout, parts):
-        at = p ^ bits
-        core, quarter = at & 1, at >> 1
-        count = part.shape[0]
+def place_kernel(spans, shared, spot, *refs):
+    parts, outs = refs[:6], refs[6:]
+    for place, part in origins(spot[1], parts):
+        core, quarter = core_and_quarter(place)
         left = 0
         for out, span in zip(outs, spans):
-            rows = out.shape[0] // (SUB if row_split else 4)
-            row = quarter * rows + first
-            column = 0
-            if row_split:
-                row = row + core * (out.shape[0] // 2)
-            else:
-                column = pl.multiple_of(core * span, 128)
-            out[pl.ds(pl.multiple_of(row, 16), count), pl.ds(column, span)] = part[
-                :, left : left + span
+            count = out.shape[0] // 4
+            row = pl.multiple_of(quarter * count, 16)
+            column = pl.multiple_of(core * span, 128)
+            out[pl.ds(row, count), pl.ds(column, span)] = part[
+                :count, left : left + span
             ].astype(f32)
             left += span
-
-
-def place(parts, shapes, row_split, spot):
-    layout = tuple((bits, first) for bits, first, _ in parts)
-    arrays = [part for _, _, part in parts]
-    spans = tuple(s[1] if row_split else s[1] // 2 for s in shapes)
+        if shared:
+            pair = core * 4 + quarter
+            cross, rest = outs[-2:]
+            row = pl.multiple_of(pair * 128, 128)
+            cross[pl.ds(row, HEAD_DIM), :] = part[64:128, :COLS]
+            cross[pl.ds(row + HEAD_DIM, HEAD_DIM), :] = part[64:128, COLS:]
+            rest[pair] = part[128:, :].astype(f32)
+
+
+def place(parts, shapes, spot, shared=False):
+    spans = tuple(s[1] // 2 for s in shapes)
+    out_shape = [jax.ShapeDtypeStruct(s, f32) for s in shapes]
+    if shared:
+        out_shape.append(jax.ShapeDtypeStruct((D, COLS), bf16))
+        out_shape.append(jax.ShapeDtypeStruct((SUB, 16, 2 * COLS), f32))
     return pl.pallas_call(
-        functools.partial(place_kernel, layout, spans, row_split, len(arrays)),
-        out_shape=[jax.ShapeDtypeStruct(s, f32) for s in shapes],
-        grid_spec=pltpu.PrefetchScalarGridSpec(
-            num_scalar_prefetch=1,
-            grid=(1,),
-            in_specs=[pl.BlockSpec(a.shape, lambda i, s: (0, 0)) for a in arrays],
-            out_specs=[pl.BlockSpec(s, lambda i, s: (0, 0)) for s in shapes],
-        ),
+        functools.partial(place_kernel, spans, shared),
+        out_shape=out_shape,
+        in_specs=[pl.BlockSpec(memory_space=pltpu.SMEM)]
+        + [pl.BlockSpec(memory_space=pltpu.VMEM)] * 6,
+        out_specs=[pl.BlockSpec(memory_space=pltpu.VMEM)] * len(out_shape),
         compiler_params=pltpu.CompilerParams(vmem_limit_bytes=40 * MB),
         cost_estimate=pl.CostEstimate(
             flops=0, transcendentals=0, bytes_accessed=sum(6 * s[0] * s[1] for s in shapes)
         ),
         name="place",
-    )(spot, *arrays)
-
-
-def reduce_grad(half, shapes, row_split, x, y, z, spot):
-    rows, width = half.shape
-    view = half.reshape(4, 2, 2, 2, rows // 32, width)
-    piece = reduce_plane(view, x, y, z).reshape(rows // 16, width)
-    return place(spread_plane(piece), shapes, row_split, spot)
-
-
-def sum_all(a, p, z):
-    rows = a.shape[0] // SUB
-    view = a.reshape(SUB, rows, a.shape[1])
-    total = take(view, p, 0).astype(f32)
-    for bits in range(1, SUB):
-        total = total + swap_wide(take(view, p ^ bits, 0), bits).astype(f32)
-    mine = total.astype(bf16)
-    total = mine.astype(f32)
-    for turn in (1, 2, 3):
-        total = total + turn_narrow(mine, turn).astype(f32)
-    return share_plane(across_groups(total.astype(bf16)), p)
-
-
-def share_plane(piece, p):
-    found = jnp.stack([piece] + [swap_wide(piece, bits) for bits in range(1, SUB)])
-    return jnp.take(found, jnp.arange(SUB) ^ p, axis=0)
+    )(spot, *parts)
+
+
+def arrange_kernel(spot, *refs):
+    parts, table, table_t = refs[:6], refs[6], refs[7]
+    for place, part in origins(spot[1], parts):
+        at = pl.ds(pl.multiple_of(place * 128, 128), 128)
+        table[:, at] = part[...]
+        table_t[at, :] = part[...].astype(f32).T.astype(bf16)
+
+
+def arrange(parts, spot):
+    return pl.pallas_call(
+        arrange_kernel,
+        out_shape=[
+            jax.ShapeDtypeStruct((COLS, D), bf16),
+            jax.ShapeDtypeStruct((D, COLS), bf16),
+        ],
+        in_specs=[pl.BlockSpec(memory_space=pltpu.SMEM)]
+        + [pl.BlockSpec(memory_space=pltpu.VMEM)] * 6,
+        out_specs=[pl.BlockSpec(memory_space=pltpu.VMEM)] * 2,
+        name="arrange",
+    )(spot, *parts)
+
+
+def order_kernel(spot, *refs):
+    out = refs[4]
+    for turn in range(4):
+        out[lax.rem(spot[0] - turn + 4, 4)] = refs[turn][...]
+
+
+def order_narrow(own, others, spot):
+    return pl.pallas_call(
+        order_kernel,
+        out_shape=jax.ShapeDtypeStruct((4, *own.shape), own.dtype),
+        in_specs=[pl.BlockSpec(memory_space=pltpu.SMEM)]
+        + [pl.BlockSpec(memory_space=pltpu.VMEM)] * 4,
+        out_specs=pl.BlockSpec(memory_space=pltpu.VMEM),
+        name="order",
+    )(spot, own, *others)
 
 
 def pair_probs(pixels, same, keys_row):
@@ -299,7 +377,7 @@
         lifted = probs * prob_grad
         centre = jnp.sum(lifted[PATCH_COLS : PATCH_COLS + VARS], axis=0, keepdims=True)
         score_grad = lifted - probs * centre
-        x_ref[i * HEAD_DIM : (i + 1) * HEAD_DIM, :] = dot_nt(grad_i, weighted).astype(bf16)
+        x_ref[:, i * COLS : (i + 1) * COLS] = dot_nt(grad_i, weighted).astype(bf16)
         sums.append(jnp.sum(score_grad * pixels_wide, axis=1, keepdims=True))
         term = probs * spread + score_grad * keys_col_ref[0, :, i : i + 1]
         pixel_grad = term if pixel_grad is None else pixel_grad + term
@@ -319,7 +397,7 @@
     return pl.pallas_call(
         variable_back_kernel,
         out_shape=[
-            jax.ShapeDtypeStruct((D, COLS), bf16),
+            jax.ShapeDtypeStruct((D // 2, 2 * COLS), bf16),
             jax.ShapeDtypeStruct((PAIRS, COLS, 2), f32),
             jax.ShapeDtypeStruct((COLS, rows), f32),
         ],
@@ -333,7 +411,7 @@
             pl.BlockSpec((rows, 128), lambda h: (0, h)),
         ],
         out_specs=[
-            pl.BlockSpec((128, COLS), lambda h: (h, 0)),
+            pl.BlockSpec((HEAD_DIM, 2 * COLS), lambda h: (h, 0)),
             pl.BlockSpec((1, COLS, 2), lambda h: (h, 0, 0)),
             pl.BlockSpec((COLS, rows), lambda h: (0, 0)),
         ],
@@ -518,148 +596,223 @@
     cotangent,
 ):
     rows = patches.shape[0]
-    wide, z = lax.axis_index("wide"), lax.axis_index("narrow")
-    p = wide % SUB
-    core, x, y = p & 1, (p >> 1) & 1, p >> 2
+    z, p = lax.axis_index("narrow"), lax.axis_index("wide") % SUB
+    core = p & 1
     spot = jnp.stack([z, p]).astype(jnp.int32)
     shard = D // 4
-
-    vectors = jnp.concatenate(
-        [
-            agg_query,
-            agg_out_bias,
-            norm_one_gain,
-            norm_one_bias,
-            attn_out_bias,
-            norm_two_gain,
-            norm_two_bias,
-            mlp_out_bias,
-            mlp_in_bias,
-        ]
-    ).reshape(-1, 128)
-    around = jnp.stack([vectors] + [turn_narrow(vectors, turn) for turn in (1, 2, 3)])
-    around = jnp.take(around, (z - jnp.arange(4)) % 4, axis=0).reshape(4, -1)
-    whole = [around[:, i * shard : (i + 1) * shard].reshape(D) for i in range(8)]
-    query_full = whole[0]
+    order = Order()
+    half = lambda a: columns_half(a, core)
+    other_half = lambda a: columns_half(a, 1 - core)
+
+    singles = (
+        agg_query,
+        agg_out_bias,
+        norm_one_gain,
+        norm_one_bias,
+        attn_out_bias,
+        norm_two_gain,
+        norm_two_bias,
+        mlp_out_bias,
+    )
+    at_row = lax.broadcasted_iota(jnp.int32, (8, shard), 0)
+    vectors = jnp.zeros((8, shard), bf16)
+    for i, single in enumerate(singles):
+        vectors = jnp.where(at_row == i, single[None, :], vectors)
+    vectors = jnp.concatenate([vectors, mlp_in_bias.reshape(4, shard)])
+    around = [turn_narrow(vectors, turn) for turn in (1, 2, 3)]
+    piece_a = pieces_of([agg_out_weight], p)
+    got_a = [turn_narrow(piece_a, turn) for turn in (1, 2, 3)]
+    piece_b = pieces_of([qkv_weight, attn_out_weight], p)
+    got_b = [turn_narrow(piece_b, turn) for turn in (1, 2, 3)]
+
+    line = jnp.arange(COLS, dtype=jnp.int32)
+    variable = jnp.where(line < PATCH_COLS, line // PIX, (line - PATCH_COLS) % VARS)
+    used = line < PATCH_COLS + VARS
+    same = ((variable[:, None] == variable[None, :]) & used[None, :]).astype(f32)
+    picks = variable[:, None] == jnp.arange(VARS, dtype=jnp.int32)[None, :]
+    chosen = jnp.sum(jnp.where(picks, var_ids[None, :], 0), axis=1)
+    source = jnp.where(line < PATCH_COLS, chosen * PIX + line % PIX, chosen + PATCH_COLS)
+    source = jnp.where(used, source, -1)
+    chooser = (source[:, None] == line[None, :]).astype(bf16)
+    embed_rows = jnp.concatenate(
+        [embed_weight, var_embed, jnp.zeros((COLS - PATCH_COLS - VARS, shard), bf16)]
+    )
+    value_part = lax.dynamic_slice_in_dim(value_weight, p * 128, 128, 1)
+    table_part = dot(embed_rows, value_part).astype(bf16)
+
+    around = order_narrow(vectors, order.hold(*around), spot)
+    whole = [around[:, i].reshape(D) for i in range(8)]
+    query_full = whole[0].astype(f32)
     agg_out_b, gain_one, bias_one, attn_out_b, gain_two, bias_two, mlp_out_b = [
         v.astype(f32) for v in whole[1:]
     ]
-    mlp_in_b = around[:, 8 * shard :].reshape(4 * D).astype(f32)
-    cot_there = swap_wide(cotangent, 1)
-
-    line = jnp.arange(COLS, dtype=jnp.int32)
-    variable = jnp.where(line < PATCH_COLS, line // PIX, (line - PATCH_COLS) % VARS)
-    same = (variable[:, None] == variable[None, :]) & (line[None, :] < PATCH_COLS + VARS)
-    same = same.astype(f32)
-    chosen = jnp.take(var_ids, variable)
-    source = jnp.where(line < PATCH_COLS, chosen * PIX + line % PIX, chosen + PATCH_COLS)
-    source = jnp.where(line < PATCH_COLS + VARS, source, -1)
-    chooser = (source[:, None] == line[None, :]).astype(bf16)
-    embed_rows = jnp.concatenate(
-        [embed_weight, var_embed, jnp.zeros((COLS - PATCH_COLS - VARS, shard), bf16)]
-    )
-    embed_rows = dot(chooser, embed_rows).astype(bf16)
-    key_query = jnp.sum(
-        key_weight.reshape(shard, HEADS, HEAD_DIM).astype(f32)
-        * query_full.reshape(1, HEADS, HEAD_DIM).astype(f32),
-        axis=-1,
+    mlp_in_b = around[:, 8:].reshape(4 * D).astype(f32)
+    head_of = jnp.arange(D, dtype=jnp.int32) // HEAD_DIM
+    heads_eye = (jnp.arange(HEADS, dtype=jnp.int32)[:, None] == head_of[None, :]).astype(f32)
+    query_rows = (heads_eye * query_full[None, :]).astype(bf16)
+    key_query_t = dot_nt(query_rows, key_weight).astype(bf16)
+    keys_part = dot_nt(key_query_t, embed_rows) * scale_by
+    keys_packed = jnp.concatenate(split_two(keys_part)).reshape(-1, 128)
+    packed = jnp.concatenate([table_part, keys_packed])
+    order.mark(packed)
+    got_packed = [turn_narrow(packed, turn) for turn in (1, 2, 3)]
+
+    full_patches = jnp.concatenate(
+        [
+            patches,
+            jnp.ones((rows, VARS), bf16),
+            jnp.zeros((rows, COLS - PATCH_COLS - VARS), bf16),
+        ],
+        axis=1,
+    )
+    pixels = lax.dot_general(
+        chooser, full_patches, (((0,), (1,)), ((), ())), preferred_element_type=f32
     ).astype(bf16)
-    keys_part = dot_nt(key_query.T, embed_rows) * scale_by
-    value_part = lax.dynamic_slice_in_dim(value_weight, p * 128, 128, 1)
-    table_part = dot(embed_rows, value_part).astype(bf16)
-    keys_t = keys_part
-    table_own = table_part.astype(f32)
-    for turn in (1, 2, 3):
-        keys_t = keys_t + turn_narrow(keys_part, turn)
-        table_own = table_own + turn_narrow(table_part, turn).astype(f32)
-    table_all = share_plane(table_own.astype(bf16), p)
-    table = table_all.transpose(1, 0, 2).reshape(COLS, D)
-    table_t = table_all.transpose(0, 2, 1).reshape(D, COLS)
-    keys_rows = keys_t.reshape(PAIRS, 2, COLS)
+    seg_row, seg_col, pad_col = segment_ids, segment_ids.T, pad_mask.T
+    cot_half, cot_got = half(cotangent), over_core(other_half(cotangent))
+
+    bundle_a = jnp.stack(order.hold(*got_a))
+    order.mark(bundle_a)
+    spread_a = Spread(bundle_a, order)
+    piece_c = order.hold(pieces_of([mlp_in_weight], p))
+    got_c = [turn_narrow(piece_c, turn) for turn in (1, 2, 3)]
+    spread_a.near_step()
+
+    got_packed = order.hold(*got_packed)
+    total = packed.astype(f32)
+    for part in got_packed:
+        total = total + part.astype(f32)
+    table_own = total[:COLS].astype(bf16)
+    order.mark(table_own)
+    keys_two = total[COLS:].reshape(2, HEADS, COLS)
+    keys_rows = (keys_two[0] + keys_two[1]).reshape(PAIRS, 2, COLS)
     keys_cols = keys_rows.transpose(0, 2, 1)
-
-    (agg_out_w,) = gather([agg_out_weight], p, spot)
-    qkv_w, attn_out_w = gather([qkv_weight, attn_out_weight], p, spot)
-    (mlp_in_w,) = gather([mlp_in_weight], p, spot)
-    (mlp_out_w,) = gather([mlp_out_weight], p, spot)
-
-    pixels = jnp.concatenate(
-        [
-            patches.T,
-            jnp.ones((VARS, rows), bf16),
-            jnp.zeros((COLS - PATCH_COLS - VARS, rows), bf16),
-        ]
-    )
+    spread_t = Spread(table_own, order)
+    spread_t.near_step()
+    spread_a.corner_step()
+    spread_t.corner_step()
+
+    bundle_b = jnp.stack(order.hold(*got_b))
+    order.mark(bundle_b)
+    spread_b = Spread(bundle_b, order)
+    piece_d = order.hold(pieces_of([mlp_out_weight], p))
+    got_d = [turn_narrow(piece_d, turn) for turn in (1, 2, 3)]
+    spread_b.near_step()
+    spread_t.last_step()
+    spread_a.last_step()
+    table, table_t = arrange(spread_t.parts(), spot)
     merged = variable_forward(pixels, same, keys_rows, table_t)
-    merged_there = swap_wide(merged, 1)
+    order.mark(merged)
+    merged_there = over_core(merged)
+    (agg_out_w,) = assemble([agg_out_weight], spread_a.parts(), spot)
     patch_state = dot(merged, agg_out_w) + agg_out_b
     unit_one, inverse_one = normalise(patch_state)
     normed = (unit_one * gain_one + bias_one).astype(bf16)
-    normed_there = swap_wide(normed, 1)
+    order.mark(normed)
+    normed_there = over_core(normed)
+
+    ke_part = dot(embed_rows, key_weight).astype(bf16)
+    got_ke = send_narrow(lambda at: lax.dynamic_slice_in_dim(ke_part, at * shard, shard, 1), z)
+
+    spread_b.corner_step()
+    bundle_c = jnp.stack(order.hold(*got_c))
+    order.mark(bundle_c)
+    spread_c = Spread(bundle_c, order)
+    spread_b.last_step()
+    spread_c.near_step()
+    qkv_w, attn_out_w = assemble([qkv_weight, attn_out_weight], spread_b.parts(), spot)
     project = dot(normed, qkv_w).astype(bf16)
-    seg_row, seg_col, pad_col = segment_ids, segment_ids.T, pad_mask.T
-    attended, logs = attention(project, seg_row, seg_col, pad_col)
-    attended_there = swap_wide(attended, 1)
+    order.mark(project)
+    spread_c.corner_step()
+    attended, logs = attention(order.hold(project), seg_row, seg_col, pad_col)
+    order.mark(attended)
+    attended_there = over_core(attended)
+    bundle_d = jnp.stack(order.hold(*got_d))
+    order.mark(bundle_d)
+    spread_d = Spread(bundle_d, order)
+    spread_c.last_step()
+    spread_d.near_step()
     residual = patch_state + dot(attended, attn_out_w) + attn_out_b
     unit_two, inverse_two = normalise(residual)
     normed_two = (unit_two * gain_two + bias_two).astype(bf16)
-    normed_two_there = swap_wide(normed_two, 1)
+    order.mark(normed_two)
+    normed_two_there = over_core(normed_two)
+    (mlp_in_w,) = assemble([mlp_in_weight], spread_c.parts(), spot)
     hidden_pre = dot(normed_two, mlp_in_w) + mlp_in_b
     hidden, slope = gelu_pair(hidden_pre)
     hidden, slope = hidden.astype(bf16), slope.astype(bf16)
-    result = (residual + dot(hidden, mlp_out_w) + mlp_out_b).astype(bf16)
+    order.mark(hidden)
+    hidden_there = over_core(hidden)
+    spread_d.corner_step()
+
+    def grad_of(own, there, own_half, got):
+        return (dot_tn(own, own_half) + dot_tn(there, got)).astype(bf16)
+
+    def blocks(a):
+        return a.reshape(4, 2, 2, a.shape[0] // 16, a.shape[1])
+
+    def add_held(pair):
+        total = add_two(*order.hold(*pair))
+        order.mark(total)
+        return total
+
+    def send_block(grad):
+        return send_narrow(lambda at: take(grad, at, 0), z)
+
+    def add_narrow(parts):
+        total = add_four(order.hold(*parts))
+        order.mark(total)
+        return total
 
     cot_float = cotangent.astype(f32)
-    cot_both = jnp.concatenate([cotangent, cot_there])
-    hidden_view = hidden.reshape(rows, 4, 2, D // 2)
-    hidden_got = swap_wide(take(hidden_view, 1 - core, 2), 1)
-    hidden_both = jnp.concatenate([take(hidden_view, core, 2), hidden_got]).reshape(2 * rows, -1)
-    grad_mlp_out = dot_tn(hidden_both, cot_both).astype(bf16)
-    (grad_mlp_out_w,) = reduce_grad(grad_mlp_out, [(D, D)], True, x, y, z, spot)
-
+    grad_d = blocks(grad_of(order.hold(hidden), hidden_there, cot_half, cot_got))
+    order.mark(grad_d)
+    grad_d = reduce_first(grad_d, p)
+    spread_d.last_step()
+    (mlp_out_w,) = assemble([mlp_out_weight], spread_d.parts(), spot)
     hidden_pre_grad = (dot_nt(cotangent, mlp_out_w) * slope.astype(f32)).astype(bf16)
-    pre_got = swap_wide(columns_half(hidden_pre_grad, 1 - core), 1)
-    pre_both = jnp.concatenate([columns_half(hidden_pre_grad, core), pre_got])
-    normed_two_both = jnp.concatenate([normed_two, normed_two_there])
-    grad_mlp_in = dot_tn(normed_two_both, pre_both).astype(bf16)
-    (grad_mlp_in_w,) = reduce_grad(grad_mlp_in, [(shard, 4 * D)], False, x, y, z, spot)
-
-    normed_two_grad = dot_nt(hidden_pre_grad, mlp_in_w)
+    order.mark(hidden_pre_grad)
+    pre_got = over_core(other_half(hidden_pre_grad))
+
+    normed_two_grad = dot_nt(order.hold(hidden_pre_grad), mlp_in_w)
     residual_grad = cot_float + normalise_back(normed_two_grad, gain_two, unit_two, inverse_two)
     branch_grad = residual_grad.astype(bf16)
-    branch_got = swap_wide(columns_half(branch_grad, 1 - core), 1)
-    branch_both = jnp.concatenate([columns_half(branch_grad, core), branch_got])
-    attended_both = jnp.concatenate([attended, attended_there])
-    grad_attn_out = dot_tn(attended_both, branch_both).astype(bf16)
-    attended_grad = dot_nt(branch_grad, attn_out_w).astype(bf16)
-    project_grad = attention_back(project, attended_grad, logs, seg_row, seg_col, pad_col)
-    project_got = swap_wide(columns_half(project_grad, 1 - core), 1)
-    project_both = jnp.concatenate([columns_half(project_grad, core), project_got])
-    normed_both = jnp.concatenate([normed, normed_there])
-    grad_qkv = dot_tn(normed_both, project_both).astype(bf16)
-    grad_qkv_w, grad_attn_out_w = reduce_grad(
-        jnp.concatenate([grad_qkv, grad_attn_out], axis=1),
-        [(shard, 3 * D), (shard, D)],
-        False,
-        x,
-        y,
-        z,
-        spot,
-    )
-
-    normed_grad = dot_nt(project_grad, qkv_w)
+    order.mark(branch_grad)
+    branch_got = over_core(other_half(branch_grad))
+    grad_c = blocks(
+        grad_of(normed_two, normed_two_there, order.hold(half(hidden_pre_grad)), pre_got)
+    )
+    order.mark(grad_c)
+    grad_c = reduce_first(grad_c, p)
+    attended_grad = dot_nt(order.hold(branch_grad), attn_out_w).astype(bf16)
+    order.mark(attended_grad)
+    grad_d = reduce_second(add_held(grad_d), p)
+    project_grad = attention_back(
+        project, order.hold(attended_grad), logs, seg_row, seg_col, pad_col
+    )
+    order.mark(project_grad)
+    project_got = over_core(other_half(project_grad))
+    normed_grad = dot_nt(order.hold(project_grad), qkv_w)
     state_grad = residual_grad + normalise_back(normed_grad, gain_one, unit_one, inverse_one)
     state_grad = state_grad.astype(bf16)
-    state_got = swap_wide(columns_half(state_grad, 1 - core), 1)
-    state_both = jnp.concatenate([columns_half(state_grad, core), state_got])
-    merged_both = jnp.concatenate([merged, merged_there])
-    grad_agg_out = dot_tn(merged_both, state_both).astype(bf16)
-    (grad_agg_out_w,) = reduce_grad(grad_agg_out, [(shard, D)], False, x, y, z, spot)
-    merged_grad = dot_nt(state_grad, agg_out_w).astype(bf16)
+    order.mark(state_grad)
+    state_got = over_core(other_half(state_grad))
+    grad_c = reduce_second(add_held(grad_c), p)
+    grad_b = jnp.concatenate(
+        [
+            grad_of(normed, normed_there, order.hold(half(project_grad)), project_got),
+            grad_of(attended, attended_there, half(branch_grad), branch_got),
+        ],
+        axis=1,
+    )
+    order.mark(grad_b)
+    grad_b = reduce_first(blocks(grad_b), p)
+    grad_d = send_block(add_held(grad_d))
+    merged_grad = dot_nt(order.hold(state_grad), agg_out_w).astype(bf16)
 
     cross, zed, pixel_grad = variable_back(pixels, same, keys_rows, keys_cols, table, merged_grad)
-    patches_grad = pixel_grad[:PATCH_COLS].T
-    zed_high, zed_low = split_two(zed.transpose(0, 2, 1).reshape(HEADS, COLS))
+    order.mark(cross)
+    zed_parts = split_two(zed.transpose(0, 2, 1).reshape(HEADS, COLS))
     column_sums = [
         jnp.sum(state_grad.astype(f32), axis=0),
         jnp.sum(normed_grad * unit_one, axis=0),
@@ -670,42 +823,92 @@
         jnp.sum(cot_float, axis=0),
         jnp.sum(hidden_pre_grad.astype(f32), axis=0),
     ]
-    small = jnp.concatenate(column_sums).astype(bf16).reshape(-1, COLS)
-    used = D + 2 * HEADS + small.shape[0]
-    padded = -(-used // 128) * 128
     small = jnp.concatenate(
-        [cross, zed_high, zed_low, small, jnp.zeros((padded - used, COLS), bf16)]
-    )
-    small = sum_all(small, p, z).reshape(padded, COLS)
-    cross = small[:D]
-    zed = small[D : D + HEADS].astype(f32) + small[D + HEADS : D + 2 * HEADS].astype(f32)
-    sums = small[D + 2 * HEADS : used].astype(f32)
+        [part.reshape(-1) for part in zed_parts] + [v.astype(bf16) for v in column_sums]
+    ).reshape(-1, 2 * COLS)
+    n_small = small.shape[0]
+    small = jnp.concatenate([small, jnp.zeros((16 * SUB - n_small, 2 * COLS), bf16)])
+    shared = jnp.concatenate(
+        [cross.reshape(SUB, HEAD_DIM, 2 * COLS), small.reshape(SUB, 16, 2 * COLS)], axis=1
+    )
+    shared = shared.reshape(2, 2, 2, 80, 2 * COLS)
+    shared_got = over_core(take(shared, 1 - core, 0))
+    grad_c = send_block(add_held(grad_c))
+    grad_a = grad_of(merged, merged_there, order.hold(half(state_grad)), state_got)
+    grad_a = grad_a.reshape(4, 2, 2, shard // 4, D // 2).transpose(1, 2, 0, 3, 4)
+    grad_a = grad_a.reshape(2, 2, shard, D // 2)
+    shared = add_two(take(shared, core, 0), shared_got)
+    grad_a = jnp.concatenate([grad_a, shared], axis=2)
+    order.mark(grad_a)
+    grad_a = reduce_first(grad_a, p)
+    grad_b = reduce_second(add_held(grad_b), p)
+    spread_d = Spread(add_narrow(grad_d), order)
+    result = (residual + dot(order.hold(hidden), mlp_out_w) + mlp_out_b).astype(bf16)
+    order.mark(result)
+    grad_a = reduce_second(add_held(grad_a), p)
+    spread_d.near_step()
+    spread_c = Spread(add_narrow(grad_c), order)
+    patches_grad = lax.dot_general(
+        order.hold(pixel_grad),
+        chooser.astype(f32),
+        (((0,), (1,)), ((), ())),
+        precision=lax.Precision.HIGHEST,
+        preferred_element_type=f32,
+    )[:, :PATCH_COLS]
+    order.mark(patches_grad)
+    grad_a = add_held(grad_a)
+    grad_a = send_narrow(
+        lambda at: jnp.concatenate(
+            [lax.dynamic_slice_in_dim(grad_a, at * 64, 64, 0), grad_a[shard:]]
+        ),
+        z,
+    )
+    grad_b = send_block(add_held(grad_b))
+    spread_c.near_step()
+    spread_d.corner_step()
+    spread_a = Spread(add_narrow(grad_a), order)
+    spread_c.corner_step()
+    spread_a.near_step()
+    spread_b = Spread(add_narrow(grad_b), order)
+    spread_d.last_step()
+    spread_a.corner_step()
+    spread_b.near_step()
+    spread_c.last_step()
+    (grad_mlp_out_w,) = place(spread_d.parts(), [(D, D)], spot)
+    order.mark(grad_mlp_out_w)
+    spread_a.last_step()
+    spread_b.corner_step()
+    (grad_mlp_in_w,) = place(spread_c.parts(), [(shard, 4 * D)], spot)
+    order.mark(grad_mlp_in_w)
+    grad_agg_out_w, cross, rest = place(spread_a.parts(), [(shard, D)], spot, shared=True)
+    order.mark(cross)
+
+    rest = rest.reshape(16 * SUB, 2 * COLS)
+    zed = rest[:16].reshape(2, HEADS, COLS)
+    zed = zed[0] + zed[1]
+    sums = rest[16:n_small].reshape(-1, COLS)
     own = lambda i: take(sums[4 * i : 4 * i + 4], z, 0)
     grad_mlp_in_b = lax.dynamic_slice_in_dim(sums[28:44], 4 * z, 4, 0).reshape(D)
-
     zed_both = split_two(zed)
-    grad_embed = dot(value_weight, cross).T + sum(
-        dot_nt(part.T, key_query) for part in zed_both
+    grad_embed = lax.dot_general(
+        cross, value_weight, (((0,), (1,)), ((), ())), preferred_element_type=f32
+    ) + (dot_tn(zed_both[0], key_query_t) + dot_tn(zed_both[1], key_query_t)) * scale_by
+    grad_value_w = lax.dot_general(
+        embed_rows, cross, (((0,), (1,)), ((), ())), preferred_element_type=f32
+    )
+    query_grad = sum(
+        lax.dot_general(embed_rows, part, (((0,), (1,)), ((), ())), preferred_element_type=f32)
+        for part in zed_both
     ) * scale_by
-    grad_embed = lax.dot_general(
-        chooser.astype(f32),
-        grad_embed,
-        (((0,), (0,)), ((), ())),
-        precision=lax.Precision.HIGHEST,
-        preferred_element_type=f32,
-    )
-    grad_value_w = dot_nt(embed_rows.T, cross)
-    query_grad = sum(dot_nt(embed_rows.T, part) for part in zed_both) * scale_by
-    grad_key_w = jnp.repeat(query_grad, HEAD_DIM, axis=1) * query_full.astype(f32)[None, :]
-    grad_query = jnp.sum(
-        jnp.repeat(query_grad, HEAD_DIM, axis=1) * key_weight.astype(f32), axis=0
-    )
-    grad_query = grad_query.astype(bf16).reshape(4, shard)
-    grad_agg_query = take(grad_query, z, 0).astype(f32)
-    for turn in (1, 2, 3):
-        grad_agg_query = grad_agg_query + turn_narrow(
-            take(grad_query, (z + turn) % 4, 0), turn
-        ).astype(f32)
+    grad_key_w = jnp.repeat(query_grad, HEAD_DIM, axis=1) * query_full[None, :]
+    ke_own = split_two(sum(part.astype(f32) for part in got_ke))
+    per_head = sum(dot(part, ke) for part in zed_both for ke in ke_own)
+    own_head = z * 4 + jnp.arange(shard, dtype=jnp.int32) // HEAD_DIM
+    mine = jnp.arange(HEADS, dtype=jnp.int32)[:, None] == own_head[None, :]
+    grad_agg_query = jnp.sum(jnp.where(mine, per_head, 0.0), axis=0) * scale_by
+
+    spread_b.last_step()
+    grad_qkv_w, grad_attn_out_w = place(spread_b.parts(), [(shard, 3 * D), (shard, D)], spot)
 
     return (
         result,

time: 775 us -> 526 us (0.68)
  waiting for transfers between devices: 248 us -> 109 us
  local copies, waits for them, and re-layouts: 143 us -> 62.5 us
  starting transfers between devices: 147 us -> 116 us
  matrix products: 78.5 us -> 102 us
  other arithmetic: 56.7 us -> 36 us
    ppermute x119 -> x64, waiting for transfers between devices: 168 us -> 79.7 us  [the longest x13 48.3 us: over_first(): return lax.ppermute(a, 'wide', wide_pairs(lambda i: 4 if i & 1 else 2))]
    ppermute x39 -> x33, waiting for transfers between devices: 80.3 us -> 29.8 us  [turn_narrow(): lax.ppermute(a, 'narrow', [(i, (i + by) % size) for i in range(size)])]
    ppermute x119 -> x64, starting transfers between devices: 79.9 us -> 33.1 us  [the longest x13 14.3 us: over_first(): return lax.ppermute(a, 'wide', wide_pairs(lambda i: 4 if i & 1 else 2))]
    unnamed x320 -> x222, local copies, waits for them, and re-layouts: 59.4 us -> 21.9 us
    select_n x5 -> x3, other arithmetic: 27.1 us -> 0.86 us  [the longest x1 0.85 us: per_device(): vectors = jnp.where(at_row == i, single[None, :], vectors)]
    dynamic_slice x16 -> x7, local copies, waits for them, and re-layouts: 22.7 us -> 4 us  [take(): return lax.dynamic_index_in_dim(a, at, axis, keepdims=False)]
    ppermute x39 -> x33, starting transfers between devices: 67.1 us -> 82.4 us  [turn_narrow(): lax.ppermute(a, 'narrow', [(i, (i + by) % size) for i in range(size)])]
    slice x20 -> x2, local copies, waits for them, and re-layouts: 11.4 us -> 0.02 us  [the longest x1 0.01 us: per_device(): table_own = total[:COLS].astype(bf16)]
  transfers between devices with their start and end apart: 158 -> 97, of which waited for: 43 -> 25; matrix products, arithmetic and copies ran while one was open for 27% -> 32% of each run, Pallas kernels for 6% -> 15%
where the time goes in v2:
time: 526 us; the launch traced here: 518 us
  starting transfers between devices  116 us (22%)
  waiting for transfers between devices  109 us (21%)
  matrix products  102 us (19%)
  Pallas kernels  89 us (17%)
  local copies, waits for them, and re-layouts  62.5 us (12%)
  other arithmetic  36 us (7%)
    ppermute x33, starting transfers between devices, turn_narrow(): lax.ppermute(a, 'narrow', [(i, (i + by) % size) for i in range(size)])  82.4 us
    ppermute x13, waiting for transfers between devices, over_first(): return lax.ppermute(a, 'wide', wide_pairs(lambda i: 4 if i & 1 else 2))  48.3 us
    dot_general x11, matrix products, dot(): return jnp.dot(a, b, preferred_element_type=f32)  33.7 us
    dot_general x7, matrix products, dot_nt(): lax.dot_general(a, b, (((1,), (1,)), ((), ())), preferred_element_type=f32)  31.6 us
    dot_general x12, matrix products, dot_tn(): lax.dot_general(a, b, (((0,), (0,)), ((), ())), preferred_element_type=f32)  30.7 us
    ppermute x33, waiting for transfers between devices, turn_narrow(): lax.ppermute(a, 'narrow', [(i, (i + by) % size) for i in range(size)])  29.8 us
    pallas_call x4, Pallas kernels, assemble(): pl.pallas_call(functools.partial(assemble_kernel, len(shards)), out_shape...  22.1 us
    unnamed x222, local copies, waits for them, and re-layouts  21.9 us
  transfers between devices with their start and end apart: 97, of which 25 were waited for; matrix products, arithmetic and copies ran while one was open for 32% of the time, Pallas kernels for 15%

profile of v2, /device:TPU:0, one launch (start us, length us, event | category | flops | bytes accessed | tf_op | source)
XLA Modules:
  0.0 517.5 jit_solution(5219817761537352710)
XLA Ops:
  2.4 3.1 collective-permute-start
  5.4 2.6 collective-permute-start.1
  16.8 2.8 collective-permute-start.8
  25.4 2.0 collective-permute-done.8
  28.6 10.4 %collective-permute-start.3 = (bf16[320,128]{1,0:T(8,128)(2,1)S(1)}, bf16[320,128]{1,0:T(8,128)(2,1)S(1)}, u32[]{:S(2)}, u32[]{:S(2)}) collective-permute-start(bf16[320,128]{1,0:T(8,128)(2,1)S(1)} %pad_maximum_fusion.20), channel_id=1, source_target_pairs={{0,1},{1,2},{2,3},{3,0},{4,5},{5,6},{6,7},{7,4},{8,9},{9,10},{10,1... | collective-permute-start | bytes 245768 | tf_op jit(solution)/shard_map/ppermute | solution.py:64
  39.0 2.4 collective-permute-start.5
  43.5 2.5 collective-permute-done.4
  50.5 3.3 collective-permute-done.12.refs_3_
  58.0 6.5 %collective-permute-start.26 = (bf16[32,4096]{1,0:T(8,128)(2,1)}, bf16[32,4096]{1,0:T(8,128)(2,1)}, u32[]{:S(2)}, u32[]{:S(2)}) collective-permute-start(bf16[32,4096]{1,0:T(8,128)(2,1)} %constant_dynamic-slice_fusion.24), channel_id=1, source_target_pairs={{0,1},{1,2},{2,3},{3,0},{4,5},{5,6},{6,7},{7,4},{8,9},{9,10},{10,1... | collective-permute-start | bytes 786440 | tf_op jit(solution)/shard_map/ppermute | solution.py:64
  69.0 3.1 collective-permute-done.20.refs_5_
  72.1 3.3 collective-permute-start.27
  77.0 2.3 arrange.1
  82.3 9.0 %variable_forward.1 = bf16[512,1024]{1,0:T(8,128)(2,1)S(1)} custom-call(bf16[256,512]{1,0:T(8,128)(2,1)S(1)} %copy-done.49, f32[256,256]{1,0:T(8,128)S(1)} %copy-done.36, f32[8,2,256]{2,1,0:T(2,128)S(1)} %add.478.keys_ref, bf16[1024,256]{1,0:T(8,128)(2,1)S(1)} %copy-done.48), custom_call_target="tpu_custom_call" | custom-call | flops 3221225472 | bytes 2097152 | tf_op jit(solution)/shard_map/variable_forward/pallas_call | solution.py:338
  91.7 3.1 assemble.4
  102.9 7.6 %collective-permute-done.25.refs_6_ = bf16[3,32,4096]{2,1,0:T(8,128)(2,1)} collective-permute-done((bf16[3,32,4096]{2,1,0:T(8,128)(2,1)S(1)}, bf16[3,32,4096]{2,1,0:T(8,128)(2,1)}, u32[]{:S(2)}, u32[]{:S(2)}) %collective-permute-start.25) | collective-permute-done | bytes 786464 | tf_op jit(solution)/shard_map/ppermute | solution.py:59
  117.7 2.2 collective-permute-start.36
  123.6 6.7 %assemble.5 = (bf16[1024,3072]{1,0:T(8,128)(2,1)}, bf16[1024,1024]{1,0:T(8,128)(2,1)S(1)}) custom-call(s32[2]{0:T(128)S(1)} %copy-done.41, bf16[256,3072]{1,0:T(8,128)(2,1)S(1)} %copy-done.17, bf16[256,1024]{1,0:T(8,128)(2,1)S(1)} %copy-done.29, bf16[3,32,4096]{2,1,0:T(8,128)(2,1)S(1)} %get-tuple-element.212.refs_2_, bf16[3,32,4096]{2,1,0:T(8,128)(2,1)S(1)} %copy-done.12, ...), custom_call_target="tpu_custom_call" | custom-call | bytes 16777216 | tf_op jit(solution)/shard_map/assemble/pallas_call | solution.py:165
  130.3 7.3 %convolution_convert_fusion.q_ref.k_ref.v_ref = bf16[512,3072]{1,0:T(8,128)(2,1)S(1)} fusion(bf16[512,1024]{1,0:T(8,128)(2,1)} %add_convert_fusion.14, bf16[1024,3072]{1,0:T(8,128)(2,1)} %get-tuple-element.218), kind=kOutput, calls=%fused_computation.13 | convolution fusion | flops 3222798336 | bytes 10485760 | tf_op jit(solution)/shard_map/dot_general | solution.py:30
  140.4 12.0 %attention.1 = (bf16[512,1024]{1,0:T(8,128)(2,1)S(1)}, f32[8,2,512]{2,1,0:T(2,128)S(1)}) custom-call(bf16[512,3072]{1,0:T(8,128)(2,1)S(1)} %convolution_convert_fusion.q_ref.k_ref.v_ref, bf16[512,3072]{1,0:T(8,128)(2,1)S(1)} %convolution_convert_fusion.q_ref.k_ref.v_ref, bf16[512,3072]{1,0:T(8,128)(2,1)S(1)} %convolution_convert_fusion.q_ref.k_ref.v_ref, ...), custom_call_target="tpu_custom_call" | custom-call | flops 2147483648 | bytes 4194304 | tf_op jit(solution)/shard_map/attention/pallas_call | solution.py:460
  159.0 5.7 %assemble.6 = bf16[1024,4096]{1,0:T(8,128)(2,1)} custom-call(s32[2]{0:T(128)S(1)} %copy-done.41, bf16[256,4096]{1,0:T(8,128)(2,1)S(1)} %copy-done.13, bf16[3,32,4096]{2,1,0:T(8,128)(2,1)S(1)} %copy-done.8, bf16[3,32,4096]{2,1,0:T(8,128)(2,1)S(1)} %copy-done.10, bf16[2,3,32,4096]{3,2,1,0:T(8,128)(2,1)} %collective-permute-done.31.refs_3_, ...), custom_call_target="tpu_custom_call" | custom-call | bytes 16777216 | tf_op jit(solution)/shard_map/assemble/pallas_call | solution.py:165
  164.7 10.7 %multiply_convert_fusion = (bf16[512,4096]{1,0:T(8,128)(2,1)}, f32[512,4096]{1,0:T(8,128)}) fusion(f32[4096]{0:T(1024)S(1)} %bitcast.298, bf16[512,1024]{1,0:T(8,128)(2,1)S(1)} %add_convert_fusion.13, bf16[1024,4096]{1,0:T(8,128)(2,1)} %assemble.6), kind=kOutput, calls=%fused_computation.10 | convolution fusion | flops 4307550208 | bytes 22036480 | tf_op jit(solution)/shard_map/dot_general | solution.py:30
  176.1 7.7 %collective-permute-done.38.refs_2_ = bf16[3,128,1024]{2,1,0:T(8,128)(2,1)S(1)} collective-permute-done((bf16[3,128,1024]{2,1,0:T(8,128)(2,1)S(1)}, bf16[3,128,1024]{2,1,0:T(8,128)(2,1)S(1)}, u32[]{:S(2)}, u32[]{:S(2)}) %collective-permute-start.38) | collective-permute-done | bytes 786464 | tf_op jit(solution)/shard_map/ppermute | solution.py:51
  188.0 18.6 %collective-permute-done.39.refs_3_ = bf16[2,3,128,1024]{3,2,1,0:T(8,128)(2,1)S(1)} collective-permute-done((bf16[2,3,128,1024]{3,2,1,0:T(8,128)(2,1)}, bf16[2,3,128,1024]{3,2,1,0:T(8,128)(2,1)S(1)}, u32[]{:S(2)}, u32[]{:S(2)}) %collective-permute-start.39) | collective-permute-done | bytes 1572896 | tf_op jit(solution)/shard_map/ppermute | solution.py:55
  206.7 4.7 fusion.20
  211.5 7.0 %add_convert_fusion.1 = bf16[4096,512]{1,0:T(8,128)(2,1)} fusion(f32[4096,512]{1,0:T(8,128)S(1)} %fusion.20, bf16[512,4096]{1,0:T(8,128)(2,1)} %collective-permute-done.40, bf16[512,512]{1,0:T(8,128)(2,1)} %collective-permute-done.41), kind=kOutput, calls=%fused_computation.9 | convolution fusion | flops 2151677952 | bytes 17301504 | tf_op jit(solution)/shard_map/dot_general | solution.py:38
  221.7 4.2 dynamic-slice_bitcast_fusion.4
  227.6 6.7 %assemble.7 = bf16[4096,1024]{1,0:T(8,128)(2,1)} custom-call(s32[2]{0:T(128)S(1)} %copy-done.41, bf16[1024,1024]{1,0:T(8,128)(2,1)S(1)} %copy-done.14, bf16[3,128,1024]{2,1,0:T(8,128)(2,1)S(1)} %copy-done.4, bf16[3,128,1024]{2,1,0:T(8,128)(2,1)S(1)} %copy-done.6, bf16[2,3,128,1024]{3,2,1,0:T(8,128)(2,1)S(1)} %collective-permute-done.39.refs_3_, ...), custom_call_target="tpu_custom_call" | custom-call | bytes 16777216 | tf_op jit(solution)/shard_map/assemble/pallas_call | solution.py:165
  234.3 12.9 %fusion.66 = (bf16[4096]{0:T(1024)(128)(2,1)}, bf16[512,4096]{1,0:T(8,128)(2,1)}) fusion(f32[512,4096]{1,0:T(8,128)} %get-tuple-element.465, f32[4096]{0:T(1024)S(1)} %bitcast.299, bf16[4096,1024]{1,0:T(8,128)(2,1)} %assemble.7, bf16[512,1024]{1,0:T(8,128)(2,1)S(1)} %copy-done.64), kind=kOutput, calls=%fused_computation.280 | convolution fusion | flops 4324323328 | bytes 22044672 | tf_op jit(solution)/shard_map/dot_general | solution.py:34
  247.3 9.1 %multiply_reduce_fusion = (bf16[1024]{0:T(1024)(128)(2,1)}, f32[512]{0:T(512)S(1)}, f32[512]{0:T(512)S(1)}, bf16[1024]{0:T(1024)(128)(2,1)}, f32[512,1024]{1,0:T(8,128)}) fusion(f32[512,1024]{1,0:T(8,128)S(1)} %copy-done.52, f32[512]{0:T(512)S(1)} %copy-done.84, f32[512]{0:T(512)S(1)} %broadcast_multiply_fusion.4, f32[1024]{0:T(1024)S(1)} %bitcast.294, ...), kind=kOutput, calls=%fused_computation.23 | convolution fusion | flops 4299682816 | bytes 16793600 | tf_op jit(solution)/shard_map/dot_general | solution.py:34
  256.4 2.9 constant_dynamic-slice_fusion.20
  261.7 2.4 fusion.67
  266.6 3.9 add_convert_fusion
  270.5 1.9 dynamic-slice_bitcast_fusion.2
  274.1 2.2 add_convert_fusion.5
  279.5 16.3 %attention_back.1 = bf16[512,3072]{1,0:T(8,128)(2,1)S(1)} custom-call(bf16[512,3072]{1,0:T(8,128)(2,1)S(1)} %copy-done.2, bf16[512,3072]{1,0:T(8,128)(2,1)S(1)} %copy-done.2, bf16[512,3072]{1,0:T(8,128)(2,1)S(1)} %copy-done.2, bf16[512,1024]{1,0:T(8,128)(2,1)S(1)} %convolution_convert_fusion.2.grad_ref, f32[8,2,512]{2,1,0:T(2,128)S(1)} %get-tuple-element.250.log_ref, ...), custom_call_target="tpu_custom_call" | custom-call | flops 5368709120 | bytes 8388608 | tf_op jit(solution)/shard_map/attention_back/pallas_call | solution.py:521
  297.4 6.2 %multiply_reduce_fusion.1 = (bf16[1024]{0:T(1024)(128)(2,1)S(1)}, f32[512]{0:T(512)S(1)}, f32[512]{0:T(512)S(1)}, bf16[1024]{0:T(1024)(128)(2,1)S(1)}, f32[512,1024]{1,0:T(8,128)S(1)}) fusion(f32[512]{0:T(512)S(1)} %add_rsqrt_fusion.1, f32[512]{0:T(512)S(1)} %broadcast_multiply_fusion.5, f32[512,1024]{1,0:T(8,128)S(1)} %copy-done.56, ...), kind=kOutput, calls=%fused_computation.24 | convolution fusion | flops 3226465280 | bytes 13651968 | tf_op jit(solution)/shard_map/dot_general | solution.py:34
  304.5 9.6 %collective-permute-done.49 = bf16[4,2,64,2048]{3,2,1,0:T(8,128)(2,1)S(1)} collective-permute-done((bf16[4,2,64,2048]{3,2,1,0:T(8,128)(2,1)}, bf16[4,2,64,2048]{3,2,1,0:T(8,128)(2,1)S(1)}, u32[]{:S(2)}, u32[]{:S(2)}) %collective-permute-start.49) | collective-permute-done | bytes 2097184 | tf_op jit(solution)/shard_map/ppermute | solution.py:55
  315.0 3.1 fusion.68
  319.6 3.6 add_convert_fusion.2
  323.2 2.7 pad_maximum_fusion
  325.9 2.6 add_convert_fusion.10
  330.4 14.2 %variable_back.1 = (bf16[512,512]{1,0:T(8,128)(2,1)S(1)}, f32[8,256,2]{2,1,0:T(8,128)S(1)}, f32[256,512]{1,0:T(8,128)S(1)}) custom-call(bf16[256,512]{1,0:T(8,128)(2,1)S(1)} %copy-done.50, f32[256,256]{1,0:T(8,128)S(1)} %copy-done.37, f32[8,2,256]{2,1,0:T(2,128)S(1)} %add.478.keys_ref, f32[8,256,2]{2,1,0:T(8,128)S(1)} %bitcast.247, ...), custom_call_target="tpu_custom_call" | custom-call | flops 5368709120 | bytes 2097152 | tf_op jit(solution)/shard_map/variable_back/pallas_call | solution.py:397
  348.6 2.8 dynamic-slice_bitcast_fusion
  353.5 2.3 collective-permute-start.55
  358.3 2.2 collective-permute-start.56
  360.6 2.0 add_convert_fusion.8
  362.9 14.6 %collective-permute-done.57 = bf16[4,2,64,2048]{3,2,1,0:T(8,128)(2,1)S(1)} collective-permute-done((bf16[4,2,64,2048]{3,2,1,0:T(8,128)(2,1)S(1)}, bf16[4,2,64,2048]{3,2,1,0:T(8,128)(2,1)S(1)}, u32[]{:S(2)}, u32[]{:S(2)}) %collective-permute-start.57) | collective-permute-done | bytes 2097184 | tf_op jit(solution)/shard_map/ppermute | solution.py:55
  382.3 7.8 %add_convert_fusion.7 = bf16[512,1024]{1,0:T(8,128)(2,1)} fusion(f32[512,1024]{1,0:T(8,128)S(1)} %copy-done.53, f32[1024]{0:T(1024)S(1)} %bitcast.300, bf16[512,4096]{1,0:T(8,128)(2,1)} %get-tuple-element.270, bf16[4096,1024]{1,0:T(8,128)(2,1)S(1)} %bitcast.260), kind=kOutput, calls=%fused_computation.22 | convolution fusion | flops 4296540160 | bytes 15732736 | tf_op jit(solution)/shard_map/dot_general | solution.py:30
  398.7 4.3 collective-permute-done.67
  403.2 7.8 %collective-permute-start.68 = (bf16[144,512]{1,0:T(8,128)(2,1)S(1)}, bf16[144,512]{1,0:T(8,128)(2,1)S(1)}, u32[]{:S(2)}, u32[]{:S(2)}) collective-permute-start(bf16[144,512]{1,0:T(8,128)(2,1)S(1)} %get-tuple-element.451), channel_id=1, source_target_pairs={{0,1},{1,2},{2,3},{3,0},{4,5},{5,6},{6,7},{7,4},{8,9},{9,10},{10,1... | collective-permute-start | bytes 442376 | tf_op jit(solution)/shard_map/ppermute | solution.py:64
  411.0 4.9 collective-permute-done.73
  415.9 1.9 collective-permute-start.70
  421.2 7.4 %collective-permute-done.70 = bf16[144,512]{1,0:T(8,128)(2,1)S(1)} collective-permute-done((bf16[144,512]{1,0:T(8,128)(2,1)S(1)}, bf16[144,512]{1,0:T(8,128)(2,1)S(1)}, u32[]{:S(2)}, u32[]{:S(2)}) %collective-permute-start.70) | collective-permute-done | bytes 147488 | tf_op jit(solution)/shard_map/ppermute | solution.py:64
  430.7 7.0 %collective-permute-start.80 = (bf16[64,2048]{1,0:T(8,128)(2,1)S(1)}, bf16[64,2048]{1,0:T(8,128)(2,1)S(1)}, u32[]{:S(2)}, u32[]{:S(2)}) collective-permute-start(bf16[64,2048]{1,0:T(8,128)(2,1)S(1)} %get-tuple-element.411), channel_id=1, source_target_pairs={{0,3},{1,0},{2,1},{3,2},{4,7},{5,4},{6,5},{7,6},{8,11},{9,8},{10,9... | collective-permute-start | bytes 786440 | tf_op jit(solution)/shard_map/ppermute | solution.py:64
  440.2 10.6 %collective-permute-done.79 = bf16[64,2048]{1,0:T(8,128)(2,1)S(1)} collective-permute-done((bf16[64,2048]{1,0:T(8,128)(2,1)S(1)}, bf16[64,2048]{1,0:T(8,128)(2,1)S(1)}, u32[]{:S(2)}, u32[]{:S(2)}) %collective-permute-start.79) | collective-permute-done | bytes 262176 | tf_op jit(solution)/shard_map/ppermute | solution.py:64
  458.3 6.1 %collective-permute-start.93 = (bf16[256,256]{1,0:T(8,128)(2,1)S(1)}, bf16[256,256]{1,0:T(8,128)(2,1)}, u32[]{:S(2)}, u32[]{:S(2)}) collective-permute-start(bf16[256,256]{1,0:T(8,128)(2,1)S(1)} %get-tuple-element.435), channel_id=1, source_target_pairs={{0,3},{1,0},{2,1},{3,2},{4,7},{5,4},{6,5},{7,6},{8,11},{9,8},{10,9... | collective-permute-start | bytes 393224 | tf_op jit(solution)/shard_map/ppermute | solution.py:64
  468.0 6.8 %collective-permute-start.91 = (bf16[256,256]{1,0:T(8,128)(2,1)}, bf16[256,256]{1,0:T(8,128)(2,1)}, u32[]{:S(2)}, u32[]{:S(2)}) collective-permute-start(bf16[256,256]{1,0:T(8,128)(2,1)} %get-tuple-element.434), channel_id=1, source_target_pairs={{0,1},{1,2},{2,3},{3,0},{4,5},{5,6},{6,7},{7,4},{8,9},{9,10},{10,1... | collective-permute-start | bytes 393224 | tf_op jit(solution)/shard_map/ppermute | solution.py:64
  474.7 2.8 collective-permute-done.92
  479.9 1.9 subtract_convert_fusion
  484.0 3.4 place.4
  488.2 3.3 place.5
  491.5 2.1 place.6
  509.2 2.6 copy.79
  514.5 2.8 place.7
  (547 shorter events, 156.2 us)
Async XLA Ops:
  2.4 14.4 %collective-permute-start = (bf16[12,256]{1,0:T(8,128)(2,1)S(1)}, bf16[12,256]{1,0:T(8,128)(2,1)S(1)}, u32[]{:S(2)}, u32[]{:S(2)}) collective-permute-start(bf16[12,256]{1,0:T(8,128)(2,1)S(1)} %pad_maximum_fusion.22.refs_0_), channel_id=1, source_target_pairs={{0,1},{1,2},{2,3},{3,0},{4,5},{5,6},{6,7},{7,4},{8,9},{9,10},{10,1... | collective-permute-start | bytes 18440 | tf_op jit(solution)/shard_map/ppermute | solution.py:64
  5.4 14.2 %collective-permute-start.1 = (bf16[12,256]{1,0:T(8,128)(2,1)S(1)}, bf16[12,256]{1,0:T(8,128)(2,1)S(1)}, u32[]{:S(2)}, u32[]{:S(2)}) collective-permute-start(bf16[12,256]{1,0:T(8,128)(2,1)S(1)} %pad_maximum_fusion.22.refs_0_), channel_id=1, source_target_pairs={{0,2},{1,3},{2,0},{3,1},{4,6},{5,7},{6,4},{7,5},{8,10},{9,11},{10,... | collective-permute-start | bytes 18440 | tf_op jit(solution)/shard_map/ppermute | solution.py:64
  8.0 12.2 %collective-permute-start.2 = (bf16[12,256]{1,0:T(8,128)(2,1)S(1)}, bf16[12,256]{1,0:T(8,128)(2,1)S(1)}, u32[]{:S(2)}, u32[]{:S(2)}) collective-permute-start(bf16[12,256]{1,0:T(8,128)(2,1)S(1)} %pad_maximum_fusion.22.refs_0_), channel_id=1, source_target_pairs={{0,3},{1,0},{2,1},{3,2},{4,7},{5,4},{6,5},{7,6},{8,11},{9,8},{10,9... | collective-permute-start | bytes 18440 | tf_op jit(solution)/shard_map/ppermute | solution.py:64
  10.2 15.2 %collective-permute-start.6 = (bf16[32,1024]{1,0:T(8,128)(2,1)S(1)}, bf16[32,1024]{1,0:T(8,128)(2,1)S(1)}, u32[]{:S(2)}, u32[]{:S(2)}) collective-permute-start(bf16[32,1024]{1,0:T(8,128)(2,1)S(1)} %constant_dynamic-slice_fusion.27), channel_id=1, source_target_pairs={{0,1},{1,2},{2,3},{3,0},{4,5},{5,6},{6,7},{7,4},{8,9},{9,10},{10,1... | collective-permute-start | bytes 196616 | tf_op jit(solution)/shard_map/ppermute | solution.py:64
  10.9 14.5 %collective-permute-start.7 = (bf16[32,1024]{1,0:T(8,128)(2,1)S(1)}, bf16[32,1024]{1,0:T(8,128)(2,1)S(1)}, u32[]{:S(2)}, u32[]{:S(2)}) collective-permute-start(bf16[32,1024]{1,0:T(8,128)(2,1)S(1)} %constant_dynamic-slice_fusion.27), channel_id=1, source_target_pairs={{0,2},{1,3},{2,0},{3,1},{4,6},{5,7},{6,4},{7,5},{8,10},{9,11},{10,... | collective-permute-start | bytes 196616 | tf_op jit(solution)/shard_map/ppermute | solution.py:64
  19.6 35.7 %collective-permute-start.15 = (bf16[32,4096]{1,0:T(8,128)(2,1)S(1)}, bf16[32,4096]{1,0:T(8,128)(2,1)S(1)}, u32[]{:S(2)}, u32[]{:S(2)}) collective-permute-start(bf16[32,4096]{1,0:T(8,128)(2,1)S(1)} %pad_maximum_fusion.13), channel_id=1, source_target_pairs={{0,1},{1,2},{2,3},{3,0},{4,5},{5,6},{6,7},{7,4},{8,9},{9,10},{10,1... | collective-permute-start | bytes 786440 | tf_op jit(solution)/shard_map/ppermute | solution.py:64
  20.3 35.0 %collective-permute-start.16 = (bf16[32,4096]{1,0:T(8,128)(2,1)S(1)}, bf16[32,4096]{1,0:T(8,128)(2,1)S(1)}, u32[]{:S(2)}, u32[]{:S(2)}) collective-permute-start(bf16[32,4096]{1,0:T(8,128)(2,1)S(1)} %pad_maximum_fusion.13), channel_id=1, source_target_pairs={{0,2},{1,3},{2,0},{3,1},{4,6},{5,7},{6,4},{7,5},{8,10},{9,11},{10,... | collective-permute-start | bytes 786440 | tf_op jit(solution)/shard_map/ppermute | solution.py:64
  27.4 11.6 %collective-permute-start.9 = (bf16[3,32,1024]{2,1,0:T(8,128)(2,1)S(1)}, bf16[3,32,1024]{2,1,0:T(8,128)(2,1)S(1)}, u32[]{:S(2)}, u32[]{:S(2)}) collective-permute-start(bf16[3,32,1024]{2,1,0:T(8,128)(2,1)S(1)} %get-tuple-element.199.refs_1_), channel_id=1, source_target_pairs={{0,4},{4,0},{8,12},{12,8},{16,20},{20,16},{24,28},{28,24},{1,5},{5... | collective-permute-start | bytes 589832 | tf_op jit(solution)/shard_map/ppermute | solution.py:51
  28.6 13.1 %collective-permute-start.3 = (bf16[320,128]{1,0:T(8,128)(2,1)S(1)}, bf16[320,128]{1,0:T(8,128)(2,1)S(1)}, u32[]{:S(2)}, u32[]{:S(2)}) collective-permute-start(bf16[320,128]{1,0:T(8,128)(2,1)S(1)} %pad_maximum_fusion.20), channel_id=1, source_target_pairs={{0,1},{1,2},{2,3},{3,0},{4,5},{5,6},{6,7},{7,4},{8,9},{9,10},{10,1... | collective-permute-start | bytes 245768 | tf_op jit(solution)/shard_map/ppermute | solution.py:64
  41.8 13.5 %collective-permute-start.17 = (bf16[32,4096]{1,0:T(8,128)(2,1)S(1)}, bf16[32,4096]{1,0:T(8,128)(2,1)S(1)}, u32[]{:S(2)}, u32[]{:S(2)}) collective-permute-start(bf16[32,4096]{1,0:T(8,128)(2,1)S(1)} %pad_maximum_fusion.13), channel_id=1, source_target_pairs={{0,3},{1,0},{2,1},{3,2},{4,7},{5,4},{6,5},{7,6},{8,11},{9,8},{10,9... | collective-permute-start | bytes 786440 | tf_op jit(solution)/shard_map/ppermute | solution.py:64
  55.4 11.3 %collective-permute-start.18 = (bf16[3,32,4096]{2,1,0:T(8,128)(2,1)S(1)}, bf16[3,32,4096]{2,1,0:T(8,128)(2,1)S(1)}, u32[]{:S(2)}, u32[]{:S(2)}) collective-permute-start(bf16[3,32,4096]{2,1,0:T(8,128)(2,1)S(1)} %get-tuple-element.212.refs_2_), channel_id=1, source_target_pairs={{0,4},{4,0},{8,12},{12,8},{16,20},{20,16},{24,28},{28,24},{1,5},{5... | collective-permute-start | bytes 2359304 | tf_op jit(solution)/shard_map/ppermute | solution.py:51
  58.0 41.0 %collective-permute-start.26 = (bf16[32,4096]{1,0:T(8,128)(2,1)}, bf16[32,4096]{1,0:T(8,128)(2,1)}, u32[]{:S(2)}, u32[]{:S(2)}) collective-permute-start(bf16[32,4096]{1,0:T(8,128)(2,1)} %constant_dynamic-slice_fusion.24), channel_id=1, source_target_pairs={{0,1},{1,2},{2,3},{3,0},{4,5},{5,6},{6,7},{7,4},{8,9},{9,10},{10,1... | collective-permute-start | bytes 786440 | tf_op jit(solution)/shard_map/ppermute | solution.py:64
  66.7 24.6 %collective-permute-start.21 = (bf16[2,3,32,1024]{3,2,1,0:T(8,128)(2,1)S(1)}, bf16[2,3,32,1024]{3,2,1,0:T(8,128)(2,1)}, u32[]{:S(2)}, u32[]{:S(2)}) collective-permute-start(bf16[2,3,32,1024]{3,2,1,0:T(8,128)(2,1)S(1)} %collective-permute-done.12.refs_3_), channel_id=1, source_target_pairs={{0,4},{4,0},{8,12},{12,8},{16,20},{20,16},{24,28},{28,24},{1,5},{5... | collective-permute-start | bytes 1179656 | tf_op jit(solution)/shard_map/ppermute | solution.py:51
  72.1 26.8 %collective-permute-start.27 = (bf16[32,4096]{1,0:T(8,128)(2,1)}, bf16[32,4096]{1,0:T(8,128)(2,1)}, u32[]{:S(2)}, u32[]{:S(2)}) collective-permute-start(bf16[32,4096]{1,0:T(8,128)(2,1)} %constant_dynamic-slice_fusion.24), channel_id=1, source_target_pairs={{0,2},{1,3},{2,0},{3,1},{4,6},{5,7},{6,4},{7,5},{8,10},{9,11},{10,... | collective-permute-start | bytes 786440 | tf_op jit(solution)/shard_map/ppermute | solution.py:64
  75.5 22.8 %collective-permute-start.23 = (bf16[2,3,32,4096]{3,2,1,0:T(8,128)(2,1)}, bf16[2,3,32,4096]{3,2,1,0:T(8,128)(2,1)S(1)}, u32[]{:S(2)}, u32[]{:S(2)}) collective-permute-start(bf16[2,3,32,4096]{3,2,1,0:T(8,128)(2,1)} %pad_maximum_fusion.2), channel_id=1, source_target_pairs={{0,8},{4,20},{8,0},{12,28},{16,24},{20,4},{24,16},{28,12},{1,9},{5... | collective-permute-start | bytes 4718600 | tf_op jit(solution)/shard_map/ppermute | solution.py:55
  77.0 14.7 %collective-permute-start.22 = (bf16[3,32,1024]{2,1,0:T(8,128)(2,1)}, bf16[3,32,1024]{2,1,0:T(8,128)(2,1)}, u32[]{:S(2)}, u32[]{:S(2)}) collective-permute-start(bf16[3,32,1024]{2,1,0:T(8,128)(2,1)} %copy-done.38), channel_id=1, source_target_pairs={{0,4},{4,0},{8,12},{12,8},{16,20},{20,16},{24,28},{28,24},{1,5},{5... | collective-permute-start | bytes 589832 | tf_op jit(solution)/shard_map/ppermute | solution.py:51
  98.4 12.2 %collective-permute-start.25 = (bf16[3,32,4096]{2,1,0:T(8,128)(2,1)S(1)}, bf16[3,32,4096]{2,1,0:T(8,128)(2,1)}, u32[]{:S(2)}, u32[]{:S(2)}) collective-permute-start(bf16[3,32,4096]{2,1,0:T(8,128)(2,1)S(1)} %slice_bitcast_fusion.2), channel_id=1, source_target_pairs={{0,16},{4,12},{8,24},{12,4},{16,0},{20,28},{24,8},{28,20},{1,17},{... | collective-permute-start | bytes 2359304 | tf_op jit(solution)/shard_map/ppermute | solution.py:59
  102.4 15.3 %collective-permute-start.24 = (bf16[2,3,32,4096]{3,2,1,0:T(8,128)(2,1)S(1)}, bf16[2,3,32,4096]{3,2,1,0:T(8,128)(2,1)}, u32[]{:S(2)}, u32[]{:S(2)}) collective-permute-start(bf16[2,3,32,4096]{3,2,1,0:T(8,128)(2,1)S(1)} %collective-permute-done.23.refs_4_), channel_id=1, source_target_pairs={{0,4},{4,0},{8,12},{12,8},{16,20},{20,16},{24,28},{28,24},{1,5},{5... | collective-permute-start | bytes 4718600 | tf_op jit(solution)/shard_map/ppermute | solution.py:51
  112.7 24.9 %collective-permute-start.31 = (bf16[2,3,32,4096]{3,2,1,0:T(8,128)(2,1)}, bf16[2,3,32,4096]{3,2,1,0:T(8,128)(2,1)}, u32[]{:S(2)}, u32[]{:S(2)}) collective-permute-start(bf16[2,3,32,4096]{3,2,1,0:T(8,128)(2,1)} %pad_maximum_fusion.3), channel_id=1, source_target_pairs={{0,8},{4,20},{8,0},{12,28},{16,24},{20,4},{24,16},{28,12},{1,9},{5... | collective-permute-start | bytes 4718600 | tf_op jit(solution)/shard_map/ppermute | solution.py:55
  115.4 37.1 %collective-permute-start.34 = (bf16[128,1024]{1,0:T(8,128)(2,1)S(1)}, bf16[128,1024]{1,0:T(8,128)(2,1)S(1)}, u32[]{:S(2)}, u32[]{:S(2)}) collective-permute-start(bf16[128,1024]{1,0:T(8,128)(2,1)S(1)} %constant_dynamic-slice_fusion.23), channel_id=1, source_target_pairs={{0,1},{1,2},{2,3},{3,0},{4,5},{5,6},{6,7},{7,4},{8,9},{9,10},{10,1... | collective-permute-start | bytes 786440 | tf_op jit(solution)/shard_map/ppermute | solution.py:64
  117.1 35.3 %collective-permute-start.35 = (bf16[128,1024]{1,0:T(8,128)(2,1)S(1)}, bf16[128,1024]{1,0:T(8,128)(2,1)S(1)}, u32[]{:S(2)}, u32[]{:S(2)}) collective-permute-start(bf16[128,1024]{1,0:T(8,128)(2,1)S(1)} %constant_dynamic-slice_fusion.23), channel_id=1, source_target_pairs={{0,2},{1,3},{2,0},{3,1},{4,6},{5,7},{6,4},{7,5},{8,10},{9,11},{10,... | collective-permute-start | bytes 786440 | tf_op jit(solution)/shard_map/ppermute | solution.py:64
  117.7 34.7 %collective-permute-start.36 = (bf16[128,1024]{1,0:T(8,128)(2,1)S(1)}, bf16[128,1024]{1,0:T(8,128)(2,1)S(1)}, u32[]{:S(2)}, u32[]{:S(2)}) collective-permute-start(bf16[128,1024]{1,0:T(8,128)(2,1)S(1)} %constant_dynamic-slice_fusion.23), channel_id=1, source_target_pairs={{0,3},{1,0},{2,1},{3,2},{4,7},{5,4},{6,5},{7,6},{8,11},{9,8},{10,9... | collective-permute-start | bytes 786440 | tf_op jit(solution)/shard_map/ppermute | solution.py:64
  139.4 18.0 %collective-permute-start.32 = (bf16[2,3,32,4096]{3,2,1,0:T(8,128)(2,1)}, bf16[2,3,32,4096]{3,2,1,0:T(8,128)(2,1)S(1)}, u32[]{:S(2)}, u32[]{:S(2)}) collective-permute-start(bf16[2,3,32,4096]{3,2,1,0:T(8,128)(2,1)} %collective-permute-done.31.refs_3_), channel_id=1, source_target_pairs={{0,4},{4,0},{8,12},{12,8},{16,20},{20,16},{24,28},{28,24},{1,5},{5... | collective-permute-start | bytes 4718600 | tf_op jit(solution)/shard_map/ppermute | solution.py:51
  139.5 16.2 %collective-permute-start.33 = (bf16[3,32,4096]{2,1,0:T(8,128)(2,1)S(1)}, bf16[3,32,4096]{2,1,0:T(8,128)(2,1)S(1)}, u32[]{:S(2)}, u32[]{:S(2)}) collective-permute-start(bf16[3,32,4096]{2,1,0:T(8,128)(2,1)S(1)} %slice_bitcast_fusion.1), channel_id=1, source_target_pairs={{0,16},{4,12},{8,24},{12,4},{16,0},{20,28},{24,8},{28,20},{1,17},{... | collective-permute-start | bytes 2359304 | tf_op jit(solution)/shard_map/ppermute | solution.py:59
  175.4 36.1 %collective-permute-start.40 = (bf16[512,4096]{1,0:T(8,128)(2,1)}, bf16[512,4096]{1,0:T(8,128)(2,1)}, u32[]{:S(2)}, u32[]{:S(2)}) collective-permute-start(bf16[512,4096]{1,0:T(8,128)(2,1)} %get-tuple-element.270), channel_id=1, source_target_pairs={{0,4},{4,0},{8,12},{12,8},{16,20},{20,16},{24,28},{28,24},{1,5},{5... | collective-permute-start | bytes 12582920 | tf_op jit(solution)/shard_map/ppermute | solution.py:51
  186.0 20.6 %collective-permute-start.39 = (bf16[2,3,128,1024]{3,2,1,0:T(8,128)(2,1)}, bf16[2,3,128,1024]{3,2,1,0:T(8,128)(2,1)S(1)}, u32[]{:S(2)}, u32[]{:S(2)}) collective-permute-start(bf16[2,3,128,1024]{3,2,1,0:T(8,128)(2,1)} %pad_maximum_fusion.4), channel_id=1, source_target_pairs={{0,8},{4,20},{8,0},{12,28},{16,24},{20,4},{24,16},{28,12},{1,9},{5... | collective-permute-start | bytes 4718600 | tf_op jit(solution)/shard_map/ppermute | solution.py:55
  187.8 23.7 %collective-permute-start.41 = (bf16[512,512]{1,0:T(8,128)(2,1)}, bf16[512,512]{1,0:T(8,128)(2,1)}, u32[]{:S(2)}, u32[]{:S(2)}) collective-permute-start(bf16[512,512]{1,0:T(8,128)(2,1)} %constant_dynamic-slice_fusion.22), channel_id=1, source_target_pairs={{0,4},{4,0},{8,12},{12,8},{16,20},{20,16},{24,28},{28,24},{1,5},{5... | collective-permute-start | bytes 1572872 | tf_op jit(solution)/shard_map/ppermute | solution.py:51
  206.6 21.0 %collective-permute-start.43 = (bf16[2,3,128,1024]{3,2,1,0:T(8,128)(2,1)S(1)}, bf16[2,3,128,1024]{3,2,1,0:T(8,128)(2,1)}, u32[]{:S(2)}, u32[]{:S(2)}) collective-permute-start(bf16[2,3,128,1024]{3,2,1,0:T(8,128)(2,1)S(1)} %collective-permute-done.39.refs_3_), channel_id=1, source_target_pairs={{0,4},{4,0},{8,12},{12,8},{16,20},{20,16},{24,28},{28,24},{1,5},{5... | collective-permute-start | bytes 4718600 | tf_op jit(solution)/shard_map/ppermute | solution.py:51
  206.7 12.2 %collective-permute-start.44 = (bf16[3,128,1024]{2,1,0:T(8,128)(2,1)S(1)}, bf16[3,128,1024]{2,1,0:T(8,128)(2,1)}, u32[]{:S(2)}, u32[]{:S(2)}) collective-permute-start(bf16[3,128,1024]{2,1,0:T(8,128)(2,1)S(1)} %slice_bitcast_fusion), channel_id=1, source_target_pairs={{0,16},{4,12},{8,24},{12,4},{16,0},{20,28},{24,8},{28,20},{1,17},{... | collective-permute-start | bytes 2359304 | tf_op jit(solution)/shard_map/ppermute | solution.py:59
  221.2 45.4 %collective-permute-start.46 = (bf16[512,1024]{1,0:T(8,128)(2,1)}, bf16[512,1024]{1,0:T(8,128)(2,1)}, u32[]{:S(2)}, u32[]{:S(2)}) collective-permute-start(bf16[512,1024]{1,0:T(8,128)(2,1)} %copy-done.68), channel_id=1, source_target_pairs={{0,4},{4,0},{8,12},{12,8},{16,20},{20,16},{24,28},{28,24},{1,5},{5... | collective-permute-start | bytes 3145736 | tf_op jit(solution)/shard_map/ppermute | solution.py:51
  221.5 43.4 %collective-permute-start.52 = (bf16[512,1024]{1,0:T(8,128)(2,1)S(1)}, bf16[512,1024]{1,0:T(8,128)(2,1)S(1)}, u32[]{:S(2)}, u32[]{:S(2)}) collective-permute-start(bf16[512,1024]{1,0:T(8,128)(2,1)S(1)} %get-tuple-element.221), channel_id=1, source_target_pairs={{0,4},{4,0},{8,12},{12,8},{16,20},{20,16},{24,28},{28,24},{1,5},{5... | collective-permute-start | bytes 3145736 | tf_op jit(solution)/shard_map/ppermute | solution.py:51
  225.9 48.3 %collective-permute-start.42 = (bf16[4,2,256,512]{3,2,1,0:T(8,128)(2,1)}, bf16[4,2,256,512]{3,2,1,0:T(8,128)(2,1)}, u32[]{:S(2)}, u32[]{:S(2)}) collective-permute-start(bf16[4,2,256,512]{3,2,1,0:T(8,128)(2,1)} %get-tuple-element.399), channel_id=1, source_target_pairs={{0,8},{4,20},{8,0},{12,28},{16,24},{20,4},{24,16},{28,12},{1,9},{5... | collective-permute-start | bytes 6291464 | tf_op jit(solution)/shard_map/ppermute | solution.py:55
  265.3 93.0 %collective-permute-start.59 = (bf16[512,1024]{1,0:T(8,128)(2,1)S(1)}, bf16[512,1024]{1,0:T(8,128)(2,1)}, u32[]{:S(2)}, u32[]{:S(2)}) collective-permute-start(bf16[512,1024]{1,0:T(8,128)(2,1)S(1)} %copy-done.19), channel_id=1, source_target_pairs={{0,4},{4,0},{8,12},{12,8},{16,20},{20,16},{24,28},{28,24},{1,5},{5... | collective-permute-start | bytes 3145736 | tf_op jit(solution)/shard_map/ppermute | solution.py:51
  265.4 54.3 %collective-permute-start.50 = (bf16[512,1024]{1,0:T(8,128)(2,1)}, bf16[512,1024]{1,0:T(8,128)(2,1)}, u32[]{:S(2)}, u32[]{:S(2)}) collective-permute-start(bf16[512,1024]{1,0:T(8,128)(2,1)} %add_convert_fusion.14), channel_id=1, source_target_pairs={{0,4},{4,0},{8,12},{12,8},{16,20},{20,16},{24,28},{28,24},{1,5},{5... | collective-permute-start | bytes 3145736 | tf_op jit(solution)/shard_map/ppermute | solution.py:51
  277.5 48.3 %collective-permute-start.48 = (bf16[4,256,512]{2,1,0:T(8,128)(2,1)}, bf16[4,256,512]{2,1,0:T(8,128)(2,1)}, u32[]{:S(2)}, u32[]{:S(2)}) collective-permute-start(bf16[4,256,512]{2,1,0:T(8,128)(2,1)} %get-tuple-element.407), channel_id=1, source_target_pairs={{0,16},{4,12},{8,24},{12,4},{16,0},{20,28},{24,8},{28,20},{1,17},{... | collective-permute-start | bytes 3145736 | tf_op jit(solution)/shard_map/ppermute | solution.py:59
  277.8 36.3 %collective-permute-start.49 = (bf16[4,2,64,2048]{3,2,1,0:T(8,128)(2,1)}, bf16[4,2,64,2048]{3,2,1,0:T(8,128)(2,1)S(1)}, u32[]{:S(2)}, u32[]{:S(2)}) collective-permute-start(bf16[4,2,64,2048]{3,2,1,0:T(8,128)(2,1)} %get-tuple-element.395), channel_id=1, source_target_pairs={{0,8},{4,20},{8,0},{12,28},{16,24},{20,4},{24,16},{28,12},{1,9},{5... | collective-permute-start | bytes 6291464 | tf_op jit(solution)/shard_map/ppermute | solution.py:55
  296.1 23.5 %collective-permute-start.51 = (bf16[512,1536]{1,0:T(8,128)(2,1)S(1)}, bf16[512,1536]{1,0:T(8,128)(2,1)}, u32[]{:S(2)}, u32[]{:S(2)}) collective-permute-start(bf16[512,1536]{1,0:T(8,128)(2,1)S(1)} %get-tuple-element.401), channel_id=1, source_target_pairs={{0,4},{4,0},{8,12},{12,8},{16,20},{20,16},{24,28},{28,24},{1,5},{5... | collective-permute-start | bytes 4718600 | tf_op jit(solution)/shard_map/ppermute | solution.py:51
  329.8 23.6 %collective-permute-start.58 = (bf16[4,64,2048]{2,1,0:T(8,128)(2,1)}, bf16[4,64,2048]{2,1,0:T(8,128)(2,1)}, u32[]{:S(2)}, u32[]{:S(2)}) collective-permute-start(bf16[4,64,2048]{2,1,0:T(8,128)(2,1)} %get-tuple-element.405), channel_id=1, source_target_pairs={{0,16},{4,12},{8,24},{12,4},{16,0},{20,28},{24,8},{28,20},{1,17},{... | collective-permute-start | bytes 3145736 | tf_op jit(solution)/shard_map/ppermute | solution.py:59
  351.4 26.1 %collective-permute-start.57 = (bf16[4,2,64,2048]{3,2,1,0:T(8,128)(2,1)S(1)}, bf16[4,2,64,2048]{3,2,1,0:T(8,128)(2,1)S(1)}, u32[]{:S(2)}, u32[]{:S(2)}) collective-permute-start(bf16[4,2,64,2048]{3,2,1,0:T(8,128)(2,1)S(1)} %get-tuple-element.393), channel_id=1, source_target_pairs={{0,8},{4,20},{8,0},{12,28},{16,24},{20,4},{24,16},{28,12},{1,9},{5... | collective-permute-start | bytes 6291464 | tf_op jit(solution)/shard_map/ppermute | solution.py:55
  353.2 26.6 %collective-permute-start.54 = (bf16[256,512]{1,0:T(8,128)(2,1)S(1)}, bf16[256,512]{1,0:T(8,128)(2,1)S(1)}, u32[]{:S(2)}, u32[]{:S(2)}) collective-permute-start(bf16[256,512]{1,0:T(8,128)(2,1)S(1)} %get-tuple-element.424), channel_id=1, source_target_pairs={{0,1},{1,2},{2,3},{3,0},{4,5},{5,6},{6,7},{7,4},{8,9},{9,10},{10,1... | collective-permute-start | bytes 786440 | tf_op jit(solution)/shard_map/ppermute | solution.py:64
  353.5 27.3 %collective-permute-start.55 = (bf16[256,512]{1,0:T(8,128)(2,1)S(1)}, bf16[256,512]{1,0:T(8,128)(2,1)S(1)}, u32[]{:S(2)}, u32[]{:S(2)}) collective-permute-start(bf16[256,512]{1,0:T(8,128)(2,1)S(1)} %get-tuple-element.423), channel_id=1, source_target_pairs={{0,2},{1,3},{2,0},{3,1},{4,6},{5,7},{6,4},{7,5},{8,10},{9,11},{10,... | collective-permute-start | bytes 786440 | tf_op jit(solution)/shard_map/ppermute | solution.py:64
  358.3 23.8 %collective-permute-start.56 = (bf16[256,512]{1,0:T(8,128)(2,1)S(1)}, bf16[256,512]{1,0:T(8,128)(2,1)S(1)}, u32[]{:S(2)}, u32[]{:S(2)}) collective-permute-start(bf16[256,512]{1,0:T(8,128)(2,1)S(1)} %get-tuple-element.422), channel_id=1, source_target_pairs={{0,3},{1,0},{2,1},{3,2},{4,7},{5,4},{6,5},{7,6},{8,11},{9,8},{10,9... | collective-permute-start | bytes 786440 | tf_op jit(solution)/shard_map/ppermute | solution.py:64
  360.5 33.7 %collective-permute-start.62 = (bf16[64,2048]{1,0:T(8,128)(2,1)S(1)}, bf16[64,2048]{1,0:T(8,128)(2,1)S(1)}, u32[]{:S(2)}, u32[]{:S(2)}) collective-permute-start(bf16[64,2048]{1,0:T(8,128)(2,1)S(1)} %get-tuple-element.420), channel_id=1, source_target_pairs={{0,1},{1,2},{2,3},{3,0},{4,5},{5,6},{6,7},{7,4},{8,9},{9,10},{10,1... | collective-permute-start | bytes 786440 | tf_op jit(solution)/shard_map/ppermute | solution.py:64
  377.5 19.8 %collective-permute-start.63 = (bf16[64,2048]{1,0:T(8,128)(2,1)S(1)}, bf16[64,2048]{1,0:T(8,128)(2,1)S(1)}, u32[]{:S(2)}, u32[]{:S(2)}) collective-permute-start(bf16[64,2048]{1,0:T(8,128)(2,1)S(1)} %get-tuple-element.419), channel_id=1, source_target_pairs={{0,2},{1,3},{2,0},{3,1},{4,6},{5,7},{6,4},{7,5},{8,10},{9,11},{10,... | collective-permute-start | bytes 786440 | tf_op jit(solution)/shard_map/ppermute | solution.py:64
  379.8 17.5 %collective-permute-start.64 = (bf16[64,2048]{1,0:T(8,128)(2,1)S(1)}, bf16[64,2048]{1,0:T(8,128)(2,1)S(1)}, u32[]{:S(2)}, u32[]{:S(2)}) collective-permute-start(bf16[64,2048]{1,0:T(8,128)(2,1)S(1)} %get-tuple-element.418), channel_id=1, source_target_pairs={{0,3},{1,0},{2,1},{3,2},{4,7},{5,4},{6,5},{7,6},{8,11},{9,8},{10,9... | collective-permute-start | bytes 786440 | tf_op jit(solution)/shard_map/ppermute | solution.py:64
  382.2 11.2 %collective-permute-start.65 = (bf16[256,512]{1,0:T(8,128)(2,1)S(1)}, bf16[256,512]{1,0:T(8,128)(2,1)S(1)}, u32[]{:S(2)}, u32[]{:S(2)}) collective-permute-start(bf16[256,512]{1,0:T(8,128)(2,1)S(1)} %add_convert_fusion.19.refs_0_), channel_id=1, source_target_pairs={{0,4},{4,0},{8,12},{12,8},{16,20},{20,16},{24,28},{28,24},{1,5},{5... | collective-permute-start | bytes 786440 | tf_op jit(solution)/shard_map/ppermute | solution.py:51
  392.0 11.0 %collective-permute-start.67 = (bf16[336,512]{1,0:T(8,128)(2,1)S(1)}, bf16[336,512]{1,0:T(8,128)(2,1)S(1)}, u32[]{:S(2)}, u32[]{:S(2)}) collective-permute-start(bf16[336,512]{1,0:T(8,128)(2,1)S(1)} %get-tuple-element.432), channel_id=1, source_target_pairs={{0,16},{4,12},{8,24},{12,4},{16,0},{20,28},{24,8},{28,20},{1,17},{... | collective-permute-start | bytes 1032200 | tf_op jit(solution)/shard_map/ppermute | solution.py:59
  393.4 22.5 %collective-permute-start.73 = (bf16[4,64,2048]{2,1,0:T(8,128)(2,1)S(1)}, bf16[4,64,2048]{2,1,0:T(8,128)(2,1)S(1)}, u32[]{:S(2)}, u32[]{:S(2)}) collective-permute-start(bf16[4,64,2048]{2,1,0:T(8,128)(2,1)S(1)} %get-tuple-element.403), channel_id=1, source_target_pairs={{0,16},{4,12},{8,24},{12,4},{16,0},{20,28},{24,8},{28,20},{1,17},{... | collective-permute-start | bytes 3145736 | tf_op jit(solution)/shard_map/ppermute | solution.py:59
  394.2 25.0 %collective-permute-start.71 = (bf16[2,256,512]{2,1,0:T(8,128)(2,1)S(1)}, bf16[2,256,512]{2,1,0:T(8,128)(2,1)S(1)}, u32[]{:S(2)}, u32[]{:S(2)}) collective-permute-start(bf16[2,256,512]{2,1,0:T(8,128)(2,1)S(1)} %pad_maximum_fusion.8), channel_id=1, source_target_pairs={{0,8},{4,20},{8,0},{12,28},{16,24},{20,4},{24,16},{28,12},{1,9},{5... | collective-permute-start | bytes 1572872 | tf_op jit(solution)/shard_map/ppermute | solution.py:55
  397.5 20.8 %collective-permute-start.72 = (bf16[64,2048]{1,0:T(8,128)(2,1)S(1)}, bf16[64,2048]{1,0:T(8,128)(2,1)S(1)}, u32[]{:S(2)}, u32[]{:S(2)}) collective-permute-start(bf16[64,2048]{1,0:T(8,128)(2,1)S(1)} %add_convert_fusion.18.refs_0_), channel_id=1, source_target_pairs={{0,4},{4,0},{8,12},{12,8},{16,20},{20,16},{24,28},{28,24},{1,5},{5... | collective-permute-start | bytes 786440 | tf_op jit(solution)/shard_map/ppermute | solution.py:51
  403.2 18.0 %collective-permute-start.68 = (bf16[144,512]{1,0:T(8,128)(2,1)S(1)}, bf16[144,512]{1,0:T(8,128)(2,1)S(1)}, u32[]{:S(2)}, u32[]{:S(2)}) collective-permute-start(bf16[144,512]{1,0:T(8,128)(2,1)S(1)} %get-tuple-element.451), channel_id=1, source_target_pairs={{0,1},{1,2},{2,3},{3,0},{4,5},{5,6},{6,7},{7,4},{8,9},{9,10},{10,1... | collective-permute-start | bytes 442376 | tf_op jit(solution)/shard_map/ppermute | solution.py:64
  415.9 12.7 %collective-permute-start.70 = (bf16[144,512]{1,0:T(8,128)(2,1)S(1)}, bf16[144,512]{1,0:T(8,128)(2,1)S(1)}, u32[]{:S(2)}, u32[]{:S(2)}) collective-permute-start(bf16[144,512]{1,0:T(8,128)(2,1)S(1)} %get-tuple-element.450), channel_id=1, source_target_pairs={{0,3},{1,0},{2,1},{3,2},{4,7},{5,4},{6,5},{7,6},{8,11},{9,8},{10,9... | collective-permute-start | bytes 442376 | tf_op jit(solution)/shard_map/ppermute | solution.py:64
  418.3 12.4 %collective-permute-start.75 = (bf16[2,64,2048]{2,1,0:T(8,128)(2,1)S(1)}, bf16[2,64,2048]{2,1,0:T(8,128)(2,1)S(1)}, u32[]{:S(2)}, u32[]{:S(2)}) collective-permute-start(bf16[2,64,2048]{2,1,0:T(8,128)(2,1)S(1)} %pad_maximum_fusion.9), channel_id=1, source_target_pairs={{0,8},{4,20},{8,0},{12,28},{16,24},{20,4},{24,16},{28,12},{1,9},{5... | collective-permute-start | bytes 1572872 | tf_op jit(solution)/shard_map/ppermute | solution.py:55
  419.9 32.7 %collective-permute-start.77 = (bf16[256,512]{1,0:T(8,128)(2,1)}, bf16[256,512]{1,0:T(8,128)(2,1)S(1)}, u32[]{:S(2)}, u32[]{:S(2)}) collective-permute-start(bf16[256,512]{1,0:T(8,128)(2,1)} %slice_bitcast_fusion.5), channel_id=1, source_target_pairs={{0,16},{4,12},{8,24},{12,4},{16,0},{20,28},{24,8},{28,20},{1,17},{... | collective-permute-start | bytes 786440 | tf_op jit(solution)/shard_map/ppermute | solution.py:59
  428.9 11.3 %collective-permute-start.78 = (bf16[64,2048]{1,0:T(8,128)(2,1)S(1)}, bf16[64,2048]{1,0:T(8,128)(2,1)S(1)}, u32[]{:S(2)}, u32[]{:S(2)}) collective-permute-start(bf16[64,2048]{1,0:T(8,128)(2,1)S(1)} %get-tuple-element.413), channel_id=1, source_target_pairs={{0,1},{1,2},{2,3},{3,0},{4,5},{5,6},{6,7},{7,4},{8,9},{9,10},{10,1... | collective-permute-start | bytes 786440 | tf_op jit(solution)/shard_map/ppermute | solution.py:64
  430.7 20.1 %collective-permute-start.79 = (bf16[64,2048]{1,0:T(8,128)(2,1)S(1)}, bf16[64,2048]{1,0:T(8,128)(2,1)S(1)}, u32[]{:S(2)}, u32[]{:S(2)}) collective-permute-start(bf16[64,2048]{1,0:T(8,128)(2,1)S(1)} %get-tuple-element.412), channel_id=1, source_target_pairs={{0,2},{1,3},{2,0},{3,1},{4,6},{5,7},{6,4},{7,5},{8,10},{9,11},{10,... | collective-permute-start | bytes 786440 | tf_op jit(solution)/shard_map/ppermute | solution.py:64
  430.7 20.1 %collective-permute-start.80 = (bf16[64,2048]{1,0:T(8,128)(2,1)S(1)}, bf16[64,2048]{1,0:T(8,128)(2,1)S(1)}, u32[]{:S(2)}, u32[]{:S(2)}) collective-permute-start(bf16[64,2048]{1,0:T(8,128)(2,1)S(1)} %get-tuple-element.411), channel_id=1, source_target_pairs={{0,3},{1,0},{2,1},{3,2},{4,7},{5,4},{6,5},{7,6},{8,11},{9,8},{10,9... | collective-permute-start | bytes 786440 | tf_op jit(solution)/shard_map/ppermute | solution.py:64
  439.2 13.4 %collective-permute-start.76 = (bf16[2,144,512]{2,1,0:T(8,128)(2,1)}, bf16[2,144,512]{2,1,0:T(8,128)(2,1)}, u32[]{:S(2)}, u32[]{:S(2)}) collective-permute-start(bf16[2,144,512]{2,1,0:T(8,128)(2,1)} %pad_maximum_fusion.12), channel_id=1, source_target_pairs={{0,8},{4,20},{8,0},{12,28},{16,24},{20,4},{24,16},{28,12},{1,9},{5... | collective-permute-start | bytes 884744 | tf_op jit(solution)/shard_map/ppermute | solution.py:55
  452.1 29.7 %collective-permute-start.83 = (bf16[2,256,512]{2,1,0:T(8,128)(2,1)S(1)}, bf16[2,256,512]{2,1,0:T(8,128)(2,1)}, u32[]{:S(2)}, u32[]{:S(2)}) collective-permute-start(bf16[2,256,512]{2,1,0:T(8,128)(2,1)S(1)} %collective-permute-done.71.refs_2_), channel_id=1, source_target_pairs={{0,4},{4,0},{8,12},{12,8},{16,20},{20,16},{24,28},{28,24},{1,5},{5... | collective-permute-start | bytes 1572872 | tf_op jit(solution)/shard_map/ppermute | solution.py:51
  455.8 31.6 %collective-permute-start.90 = (bf16[2,64,2048]{2,1,0:T(8,128)(2,1)}, bf16[2,64,2048]{2,1,0:T(8,128)(2,1)S(1)}, u32[]{:S(2)}, u32[]{:S(2)}) collective-permute-start(bf16[2,64,2048]{2,1,0:T(8,128)(2,1)} %pad_maximum_fusion.10), channel_id=1, source_target_pairs={{0,8},{4,20},{8,0},{12,28},{16,24},{20,4},{24,16},{28,12},{1,9},{5... | collective-permute-start | bytes 1572872 | tf_op jit(solution)/shard_map/ppermute | solution.py:55
  464.4 14.3 %collective-permute-start.85 = (bf16[64,2048]{1,0:T(8,128)(2,1)}, bf16[64,2048]{1,0:T(8,128)(2,1)}, u32[]{:S(2)}, u32[]{:S(2)}) collective-permute-start(bf16[64,2048]{1,0:T(8,128)(2,1)} %slice_bitcast_fusion.4), channel_id=1, source_target_pairs={{0,16},{4,12},{8,24},{12,4},{16,0},{20,28},{24,8},{28,20},{1,17},{... | collective-permute-start | bytes 786440 | tf_op jit(solution)/shard_map/ppermute | solution.py:59
  465.7 11.9 %collective-permute-start.92 = (bf16[256,256]{1,0:T(8,128)(2,1)}, bf16[256,256]{1,0:T(8,128)(2,1)}, u32[]{:S(2)}, u32[]{:S(2)}) collective-permute-start(bf16[256,256]{1,0:T(8,128)(2,1)} %get-tuple-element.436), channel_id=1, source_target_pairs={{0,2},{1,3},{2,0},{3,1},{4,6},{5,7},{6,4},{7,5},{8,10},{9,11},{10,... | collective-permute-start | bytes 393224 | tf_op jit(solution)/shard_map/ppermute | solution.py:64
  495.7 18.6 %collective-permute-start.94 = (bf16[2,64,2048]{2,1,0:T(8,128)(2,1)S(1)}, bf16[2,64,2048]{2,1,0:T(8,128)(2,1)S(1)}, u32[]{:S(2)}, u32[]{:S(2)}) collective-permute-start(bf16[2,64,2048]{2,1,0:T(8,128)(2,1)S(1)} %collective-permute-done.90.refs_2_), channel_id=1, source_target_pairs={{0,4},{4,0},{8,12},{12,8},{16,20},{20,16},{24,28},{28,24},{1,5},{5... | collective-permute-start | bytes 1572872 | tf_op jit(solution)/shard_map/ppermute | solution.py:51
  496.1 16.8 %collective-permute-start.95 = (bf16[64,2048]{1,0:T(8,128)(2,1)}, bf16[64,2048]{1,0:T(8,128)(2,1)S(1)}, u32[]{:S(2)}, u32[]{:S(2)}) collective-permute-start(bf16[64,2048]{1,0:T(8,128)(2,1)} %slice_bitcast_fusion.3), channel_id=1, source_target_pairs={{0,16},{4,12},{8,24},{12,4},{16,0},{20,28},{24,8},{28,20},{1,17},{... | collective-permute-start | bytes 786440 | tf_op jit(solution)/shard_map/ppermute | solution.py:59
  (138 other events, 1075.2 us)

commit v3 on v2

--- a/solution.py
+++ b/solution.py
@@ -26,6 +26,11 @@
 MB = 1 << 20
 
 
+def takes(microseconds):
+    flops = int(microseconds * 0.6 * 1e9)
+    return pl.CostEstimate(flops=flops, transcendentals=0, bytes_accessed=1)
+
+
 def dot(a, b):
     return jnp.dot(a, b, preferred_element_type=f32)
 
@@ -64,21 +69,45 @@
     return lax.ppermute(a, "narrow", [(i, (i + by) % size) for i in range(size)])
 
 
+def swap_narrow(a, bits):
+    size = lax.axis_size("narrow")
+    return lax.ppermute(a, "narrow", [(i, i ^ bits) for i in range(size)])
+
+
 def take(a, at, axis):
     return lax.dynamic_index_in_dim(a, at, axis, keepdims=False)
 
 
 class Order:
     def __init__(self):
-        self.last = None
+        self.pending = []
 
     def hold(self, *arrays):
-        if self.last is not None:
-            arrays = lax.optimization_barrier((*arrays, self.last))[:-1]
+        arrays = lax.optimization_barrier((*arrays, *self.pending))[: len(arrays)]
+        self.pending = [arrays[0]]
         return arrays[0] if len(arrays) == 1 else arrays
 
     def mark(self, array):
-        self.last = array
+        self.pending.append(array)
+
+
+class Narrow:
+    def __init__(self, own, order):
+        self.order = order
+        self.own = own
+        self.two = swap_narrow(own, 2)
+
+    def second_step(self):
+        self.two = self.order.hold(self.two)
+        both = jnp.stack([self.own, self.two])
+        self.order.mark(both)
+        self.others = swap_narrow(both, 1)
+
+    def bundle(self):
+        others = self.order.hold(self.others)
+        bundle = jnp.concatenate([self.two[None], others])
+        self.order.mark(bundle)
+        return bundle
 
 
 class Spread:
@@ -147,21 +176,21 @@
         rows = shard.shape[0]
         start(shard, full.at[pl.ds(pl.multiple_of(z * rows, rows), rows), :])
     for place, part in origins(p, parts):
-        for turn in range(1, 4):
-            origin = lax.rem(z - turn + 4, 4)
+        for i, bits in enumerate((2, 1, 3)):
+            origin = z ^ bits
             left = 0
             for full in fulls:
                 rows, width = full.shape[0] // 4, full.shape[1]
                 count = rows // SUB
                 at = pl.multiple_of(origin * rows + place * count, count)
-                start(part.at[turn - 1, :, left : left + width], full.at[pl.ds(at, count), :])
+                start(part.at[i, :, left : left + width], full.at[pl.ds(at, count), :])
                 left += width
     for copy in copies:
         copy.wait()
 
 
 def assemble(shards, parts, spot):
-    n_copies = len(shards) * 25
+    n_copies = 25 * len(shards)
     return pl.pallas_call(
         functools.partial(assemble_kernel, len(shards)),
         out_shape=[jax.ShapeDtypeStruct((4 * s.shape[0], s.shape[1]), s.dtype) for s in shards],
@@ -169,10 +198,8 @@
         + [pl.BlockSpec(memory_space=pl.ANY)] * (len(shards) + 6),
         out_specs=[pl.BlockSpec(memory_space=pltpu.VMEM)] * len(shards),
         scratch_shapes=[pltpu.SemaphoreType.DMA((n_copies,))],
-        compiler_params=pltpu.CompilerParams(vmem_limit_bytes=40 * MB),
-        cost_estimate=pl.CostEstimate(
-            flops=0, transcendentals=0, bytes_accessed=sum(16 * s.size for s in shards)
-        ),
+        compiler_params=pltpu.CompilerParams(vmem_limit_bytes=12 * MB),
+        cost_estimate=takes(3.5),
         name="assemble",
     )(spot, *shards, *parts)
 
@@ -187,40 +214,113 @@
     )
 
 
-def around_narrow(piece):
-    return jnp.stack([turn_narrow(piece, turn) for turn in (1, 2, 3)])
-
-
 def add_two(a, b):
     return (a.astype(f32) + b.astype(f32)).astype(bf16)
 
 
-def first_and_second(p):
-    core, x, y = p & 1, (p >> 1) & 1, p >> 2
-    return jnp.where(core == 0, x, y), jnp.where(core == 0, y, x)
-
-
-def reduce_first(grad, p):
-    first, _ = first_and_second(p)
-    axis = grad.ndim - 4
-    return take(grad, first, axis), over_first(take(grad, 1 - first, axis))
-
-
-def reduce_second(grad, p):
-    _, second = first_and_second(p)
-    axis = grad.ndim - 3
-    return take(grad, second, axis), over_second(take(grad, 1 - second, axis))
-
-
-def send_narrow(pick, z):
-    return [pick(z)] + [turn_narrow(pick((z + turn) % 4), turn) for turn in (1, 2, 3)]
-
-
-def add_four(parts):
-    total = parts[0].astype(f32)
-    for part in parts[1:]:
-        total = total + part.astype(f32)
-    return across_groups(total.astype(bf16))
+def pick_kernel(bits, grad, sent):
+    sent[...] = grad[...].reshape(sent.shape)
+
+
+def pick_first(grad, bit):
+    n, _, _, rows, width = grad.shape
+    return pl.pallas_call(
+        pick_kernel,
+        out_shape=jax.ShapeDtypeStruct((n, 2, rows, width), bf16),
+        grid_spec=pltpu.PrefetchScalarGridSpec(
+            num_scalar_prefetch=1,
+            grid=(n,),
+            in_specs=[pl.BlockSpec((1, 1, 2, rows, width), lambda i, b: (i, b[0], 0, 0, 0))],
+            out_specs=pl.BlockSpec((1, 2, rows, width), lambda i, b: (i, 0, 0, 0)),
+        ),
+        compiler_params=pltpu.CompilerParams(vmem_limit_bytes=5 * MB),
+        cost_estimate=takes(2.5),
+        name="pick_first",
+    )(bit[None], grad)
+
+
+def add_split_kernel(bits, kept_sent, got_sent, kept_kept, got_kept, sent, kept):
+    def total(a, b):
+        return (a[...].astype(f32).reshape(sent.shape) + b[...].astype(f32).reshape(sent.shape)).astype(bf16)
+
+    sent[...] = total(kept_sent, got_sent)
+    kept[...] = total(kept_kept, got_kept)
+
+
+def add_split(grad, got, first, bit):
+    n, _, _, rows, width = grad.shape
+    block = (1, 1, 1, rows, width)
+    got_block = (1, 1, rows, width)
+    out = jax.ShapeDtypeStruct((n, rows, width), bf16)
+    return pl.pallas_call(
+        add_split_kernel,
+        out_shape=[out, out],
+        grid_spec=pltpu.PrefetchScalarGridSpec(
+            num_scalar_prefetch=1,
+            grid=(n,),
+            in_specs=[
+                pl.BlockSpec(block, lambda i, b: (i, b[0], 1 - b[1], 0, 0)),
+                pl.BlockSpec(got_block, lambda i, b: (i, 1 - b[1], 0, 0)),
+                pl.BlockSpec(block, lambda i, b: (i, b[0], b[1], 0, 0)),
+                pl.BlockSpec(got_block, lambda i, b: (i, b[1], 0, 0)),
+            ],
+            out_specs=[pl.BlockSpec((1, rows, width), lambda i, b: (i, 0, 0))] * 2,
+        ),
+        compiler_params=pltpu.CompilerParams(vmem_limit_bytes=8 * MB),
+        cost_estimate=takes(2.5),
+        name="add_split",
+    )(jnp.stack([first, bit]), grad, got, grad, got)
+
+
+class Reduce:
+    def __init__(self, grad, p, z, order):
+        core, x, y = p & 1, (p >> 1) & 1, p >> 2
+        self.bits = [jnp.where(core == 0, x, y), jnp.where(core == 0, y, x), z & 1, z >> 1]
+        self.order, self.stage, self.kept = order, 0, grad
+        sent = pick_first(grad, 1 - self.bits[0])
+        order.mark(sent)
+        self.got = over_first(sent)
+
+    def step(self):
+        kept, got = self.kept, self.order.hold(self.got)
+        self.stage += 1
+        if self.stage == 4:
+            self.total = across_groups(add_two(kept[0], got[0]))
+            self.order.mark(self.total)
+            return
+        bit, first = self.bits[self.stage], jnp.zeros_like(self.bits[0])
+        if self.stage == 1:
+            first = self.bits[0]
+        else:
+            rows, width = kept.shape[1:]
+            kept = kept.reshape(-1, 1, 2, rows, width)
+            got = got.reshape(-1, 2, rows, width)
+        sent, self.kept = add_split(kept, got, first, bit)
+        self.order.mark(sent)
+        self.got = over_second(sent) if self.stage == 1 else swap_narrow(sent, self.stage - 1)
+
+
+class ReduceShared(Reduce):
+    def step(self):
+        if self.stage == 0:
+            return super().step()
+        total = add_two(self.kept, self.order.hold(self.got))
+        self.order.mark(total)
+        self.stage += 1
+        if self.stage == 4:
+            self.total = across_groups(total)
+            return
+        total = total.reshape(-1, total.shape[-1])
+        shape, axis = ((2, 2, 64, -1), 1) if self.stage == 2 else ((2, 64, -1), 0)
+        blocks, shared = total[:-80].reshape(shape), total[-80:]
+
+        def pick(bit):
+            return jnp.concatenate([take(blocks, bit, axis).reshape(-1, total.shape[-1]), shared])
+
+        sent = pick(1 - self.bits[self.stage])
+        self.order.mark(sent)
+        self.kept = pick(self.bits[self.stage])
+        self.got = swap_narrow(sent, self.stage - 1)
 
 
 def across_groups(a):
@@ -265,10 +365,8 @@
         in_specs=[pl.BlockSpec(memory_space=pltpu.SMEM)]
         + [pl.BlockSpec(memory_space=pltpu.VMEM)] * 6,
         out_specs=[pl.BlockSpec(memory_space=pltpu.VMEM)] * len(out_shape),
-        compiler_params=pltpu.CompilerParams(vmem_limit_bytes=40 * MB),
-        cost_estimate=pl.CostEstimate(
-            flops=0, transcendentals=0, bytes_accessed=sum(6 * s[0] * s[1] for s in shapes)
-        ),
+        compiler_params=pltpu.CompilerParams(vmem_limit_bytes=10 * MB),
+        cost_estimate=takes(3),
         name="place",
     )(spot, *parts)
 
@@ -295,10 +393,10 @@
     )(spot, *parts)
 
 
-def order_kernel(spot, *refs):
-    out = refs[4]
-    for turn in range(4):
-        out[lax.rem(spot[0] - turn + 4, 4)] = refs[turn][...]
+def order_kernel(spot, own, others, out):
+    out[spot[0]] = own[...]
+    for i, bits in enumerate((2, 1, 3)):
+        out[spot[0] ^ bits] = others[i]
 
 
 def order_narrow(own, others, spot):
@@ -306,10 +404,10 @@
         order_kernel,
         out_shape=jax.ShapeDtypeStruct((4, *own.shape), own.dtype),
         in_specs=[pl.BlockSpec(memory_space=pltpu.SMEM)]
-        + [pl.BlockSpec(memory_space=pltpu.VMEM)] * 4,
+        + [pl.BlockSpec(memory_space=pltpu.VMEM)] * 2,
         out_specs=pl.BlockSpec(memory_space=pltpu.VMEM),
         name="order",
-    )(spot, own, *others)
+    )(spot, own, others)
 
 
 def pair_probs(pixels, same, keys_row):
@@ -346,12 +444,8 @@
             pl.BlockSpec((128, COLS), lambda h: (h, 0)),
         ],
         out_specs=pl.BlockSpec((rows, 128), lambda h: (0, h)),
-        compiler_params=pltpu.CompilerParams(vmem_limit_bytes=40 * MB),
-        cost_estimate=pl.CostEstimate(
-            flops=6 * HEADS * rows * COLS * COLS,
-            transcendentals=HEADS * rows * COLS,
-            bytes_accessed=4 * rows * D,
-        ),
+        compiler_params=pltpu.CompilerParams(vmem_limit_bytes=8 * MB),
+        cost_estimate=takes(9),
         name="variable_forward",
     )(pixels, same, keys_rows, table_t)
 
@@ -415,12 +509,8 @@
             pl.BlockSpec((1, COLS, 2), lambda h: (h, 0, 0)),
             pl.BlockSpec((COLS, rows), lambda h: (0, 0)),
         ],
-        compiler_params=pltpu.CompilerParams(vmem_limit_bytes=40 * MB),
-        cost_estimate=pl.CostEstimate(
-            flops=10 * HEADS * rows * COLS * COLS,
-            transcendentals=HEADS * rows * COLS,
-            bytes_accessed=4 * rows * D,
-        ),
+        compiler_params=pltpu.CompilerParams(vmem_limit_bytes=10 * MB),
+        cost_estimate=takes(14.5),
         name="variable_back",
     )(pixels, same, keys_rows, keys_cols, table, grad)
 
@@ -474,10 +564,8 @@
         ],
         out_specs=[column(0), pl.BlockSpec((1, 2, rows), lambda h: (h, 0, 0))],
         scratch_shapes=[pltpu.VMEM((rows, rows), f32)],
-        compiler_params=pltpu.CompilerParams(vmem_limit_bytes=40 * MB),
-        cost_estimate=pl.CostEstimate(
-            flops=8 * rows * rows * D, transcendentals=HEADS * rows * rows, bytes_accessed=8 * rows * D
-        ),
+        compiler_params=pltpu.CompilerParams(vmem_limit_bytes=8 * MB),
+        cost_estimate=takes(12.5),
         name="attention",
     )(project, project, project, seg_row, seg_col, pad_col)
 
@@ -534,14 +622,145 @@
         ],
         out_specs=pl.BlockSpec((rows, 3 * D), lambda h: (0, 0)),
         scratch_shapes=[pltpu.VMEM((rows, rows), f32)],
-        compiler_params=pltpu.CompilerParams(vmem_limit_bytes=40 * MB),
-        cost_estimate=pl.CostEstimate(
-            flops=20 * rows * rows * D,
-            transcendentals=HEADS * rows * rows,
-            bytes_accessed=16 * rows * D,
-        ),
+        compiler_params=pltpu.CompilerParams(vmem_limit_bytes=14 * MB),
+        cost_estimate=takes(16.5),
         name="attention_back",
     )(project, project, project, grad, logs, seg_row, seg_col, pad_col)
+
+
+def mlp_in_kernel(rows_ref, weight, bias, hidden, slope):
+    value, change = gelu_pair(dot(rows_ref[...], weight[...]) + bias[...])
+    hidden[...] = value.astype(bf16)
+    slope[...] = change.astype(bf16)
+
+
+def mlp_in(rows_in, weight, bias):
+    rows, hidden = rows_in.shape[0], weight.shape[1]
+    block = 512
+    columns = lambda count: pl.BlockSpec((count, block), lambda i: (0, i))
+    return pl.pallas_call(
+        mlp_in_kernel,
+        out_shape=[jax.ShapeDtypeStruct((rows, hidden), bf16)] * 2,
+        grid=(hidden // block,),
+        in_specs=[pl.BlockSpec((rows, D), lambda i: (0, 0)), columns(D), columns(1)],
+        out_specs=[columns(rows)] * 2,
+        compiler_params=pltpu.CompilerParams(vmem_limit_bytes=14 * MB),
+        cost_estimate=takes(11),
+        name="mlp_in",
+    )(rows_in, weight, bias[None])
+
+
+def mlp_back_kernel(core, cot, w_out, w_in, slope, own, other, grad, sums):
+    step = pl.program_id(0)
+    pre = (dot_nt(cot[...], w_out[...]) * slope[...].astype(f32)).astype(bf16)
+    sums[0] = jnp.sum(pre.astype(f32), axis=0, keepdims=True)
+    part = dot_nt(pre, w_in[...])
+
+    @pl.when(step < 2)
+    def _():
+        other[...] = pre
+
+    @pl.when(step >= 2)
+    def _():
+        own[...] = pre
+
+    @pl.when(step == 0)
+    def _():
+        grad[...] = part
+
+    @pl.when(step > 0)
+    def _():
+        grad[...] += part
+
+
+def mlp_back(core, cot, w_out, w_in, slope):
+    rows, hidden = cot.shape[0], w_out.shape[0]
+    block = hidden // 4
+    at = lambda i, c: lax.rem(i + 2 - 2 * c[0], 4)
+    return pl.pallas_call(
+        mlp_back_kernel,
+        out_shape=[
+            jax.ShapeDtypeStruct((rows, hidden // 2), bf16),
+            jax.ShapeDtypeStruct((rows, hidden // 2), bf16),
+            jax.ShapeDtypeStruct((rows, D), f32),
+            jax.ShapeDtypeStruct((4, 1, block), f32),
+        ],
+        grid_spec=pltpu.PrefetchScalarGridSpec(
+            num_scalar_prefetch=1,
+            grid=(4,),
+            in_specs=[
+                pl.BlockSpec((rows, D), lambda i, c: (0, 0)),
+                pl.BlockSpec((block, D), lambda i, c: (at(i, c), 0)),
+                pl.BlockSpec((D, block), lambda i, c: (0, at(i, c))),
+                pl.BlockSpec((rows, block), lambda i, c: (0, at(i, c))),
+            ],
+            out_specs=[
+                pl.BlockSpec((rows, block), lambda i, c: (0, jnp.maximum(i - 2, 0))),
+                pl.BlockSpec((rows, block), lambda i, c: (0, jnp.minimum(i, 1))),
+                pl.BlockSpec((rows, D), lambda i, c: (0, 0)),
+                pl.BlockSpec((1, 1, block), lambda i, c: (at(i, c), 0, 0)),
+            ],
+        ),
+        compiler_params=pltpu.CompilerParams(vmem_limit_bytes=50 * MB),
+        cost_estimate=takes(15.5),
+        name="mlp_back",
+    )(core, cot, w_out, w_in, slope)
+
+
+def finish_kernel(
+    spot, cross, rest, value, embed_t, key_query, query, ke, embed_out, value_out, key_out, query_out, bias_out, *sums_out
+):
+    z = spot[0]
+    summed = cross[...]
+    zed = rest[0, :, :COLS] + rest[0, :, COLS:]
+    zed_both = split_two(zed)
+    embed_grad = dot(value[...], summed)
+    query_grad = 0.0
+    per_head = 0.0
+    for part in zed_both:
+        embed_grad += dot(key_query[...], part) * scale_by
+        query_grad += dot_nt(embed_t[...], part) * scale_by
+        per_head += dot_nt(part, ke[...]) * scale_by
+    embed_out[...] = embed_grad.T
+    value_out[...] = dot_nt(embed_t[...], summed)
+    head = lax.broadcasted_iota(jnp.int32, (HEADS, D), 0)
+    line = lax.broadcasted_iota(jnp.int32, (HEADS, D), 1)
+    eye = (head == line // HEAD_DIM).astype(bf16)
+    high, low = split_two(query_grad)
+    key_out[...] = (dot(high, eye) + dot(low, eye)) * query[...]
+    head = lax.broadcasted_iota(jnp.int32, per_head.shape, 0)
+    line = lax.broadcasted_iota(jnp.int32, per_head.shape, 1)
+    mine = head == z * 4 + line // HEAD_DIM
+    query_out[...] = jnp.sum(jnp.where(mine, per_head, 0.0), axis=0, keepdims=True)
+    column = pl.multiple_of((z & 1) * COLS, COLS)
+    for i, out in enumerate(sums_out):
+        at = 16 + 2 * i + (z >> 1)
+        out[...] = rest[at // 16, pl.ds(lax.rem(at, 16), 1), pl.ds(column, COLS)]
+    for i in range(2):
+        at = 16 + 14 + 2 * z + i
+        bias_out[pl.ds(i, 1), :] = rest[at // 16, pl.ds(lax.rem(at, 16), 1), :]
+
+
+def finish(spot, cross, rest, value, embed_t, key_query, query, ke):
+    shard = value.shape[0]
+    row = jax.ShapeDtypeStruct((1, shard), f32)
+    out_shape = [
+        jax.ShapeDtypeStruct((COLS, shard), f32),
+        jax.ShapeDtypeStruct((shard, D), f32),
+        jax.ShapeDtypeStruct((shard, D), f32),
+        row,
+        jax.ShapeDtypeStruct((2, 2 * COLS), f32),
+    ] + [row] * 7
+    return pl.pallas_call(
+        finish_kernel,
+        out_shape=out_shape,
+        in_specs=[pl.BlockSpec(memory_space=pltpu.SMEM)]
+        + [pl.BlockSpec(memory_space=pltpu.VMEM)] * 7,
+        out_specs=[pl.BlockSpec(memory_space=pltpu.VMEM)] * len(out_shape),
+        compiler_params=pltpu.CompilerParams(vmem_limit_bytes=12 * MB),
+        cost_estimate=takes(3),
+        name="finish",
+    )(spot, cross, rest, value, embed_t, key_query, query[None], ke)
 
 
 def normalise(values):
@@ -619,11 +838,11 @@
     for i, single in enumerate(singles):
         vectors = jnp.where(at_row == i, single[None, :], vectors)
     vectors = jnp.concatenate([vectors, mlp_in_bias.reshape(4, shard)])
-    around = [turn_narrow(vectors, turn) for turn in (1, 2, 3)]
-    piece_a = pieces_of([agg_out_weight], p)
-    got_a = [turn_narrow(piece_a, turn) for turn in (1, 2, 3)]
-    piece_b = pieces_of([qkv_weight, attn_out_weight], p)
-    got_b = [turn_narrow(piece_b, turn) for turn in (1, 2, 3)]
+    narrow_v = Narrow(vectors, order)
+    narrow_a = Narrow(pieces_of([agg_out_weight], p), order)
+    narrow_b = Narrow(pieces_of([qkv_weight, attn_out_weight], p), order)
+    narrow_v.second_step()
+    narrow_a.second_step()
 
     line = jnp.arange(COLS, dtype=jnp.int32)
     variable = jnp.where(line < PATCH_COLS, line // PIX, (line - PATCH_COLS) % VARS)
@@ -640,7 +859,7 @@
     value_part = lax.dynamic_slice_in_dim(value_weight, p * 128, 128, 1)
     table_part = dot(embed_rows, value_part).astype(bf16)
 
-    around = order_narrow(vectors, order.hold(*around), spot)
+    around = order_narrow(vectors, narrow_v.bundle(), spot)
     whole = [around[:, i].reshape(D) for i in range(8)]
     query_full = whole[0].astype(f32)
     agg_out_b, gain_one, bias_one, attn_out_b, gain_two, bias_two, mlp_out_b = [
@@ -671,13 +890,9 @@
     seg_row, seg_col, pad_col = segment_ids, segment_ids.T, pad_mask.T
     cot_half, cot_got = half(cotangent), over_core(other_half(cotangent))
 
-    bundle_a = jnp.stack(order.hold(*got_a))
-    order.mark(bundle_a)
-    spread_a = Spread(bundle_a, order)
-    piece_c = order.hold(pieces_of([mlp_in_weight], p))
-    got_c = [turn_narrow(piece_c, turn) for turn in (1, 2, 3)]
+    spread_a = Spread(narrow_a.bundle(), order)
+    narrow_b.second_step()
     spread_a.near_step()
-
     got_packed = order.hold(*got_packed)
     total = packed.astype(f32)
     for part in got_packed:
@@ -691,59 +906,53 @@
     spread_t.near_step()
     spread_a.corner_step()
     spread_t.corner_step()
-
-    bundle_b = jnp.stack(order.hold(*got_b))
-    order.mark(bundle_b)
-    spread_b = Spread(bundle_b, order)
-    piece_d = order.hold(pieces_of([mlp_out_weight], p))
-    got_d = [turn_narrow(piece_d, turn) for turn in (1, 2, 3)]
+    spread_b = Spread(narrow_b.bundle(), order)
+    narrow_c = Narrow(order.hold(pieces_of([mlp_in_weight], p)), order)
     spread_b.near_step()
     spread_t.last_step()
     spread_a.last_step()
     table, table_t = arrange(spread_t.parts(), spot)
     merged = variable_forward(pixels, same, keys_rows, table_t)
     order.mark(merged)
+    (agg_out_w,) = assemble([agg_out_weight], spread_a.parts(), spot)
     merged_there = over_core(merged)
-    (agg_out_w,) = assemble([agg_out_weight], spread_a.parts(), spot)
     patch_state = dot(merged, agg_out_w) + agg_out_b
     unit_one, inverse_one = normalise(patch_state)
     normed = (unit_one * gain_one + bias_one).astype(bf16)
     order.mark(normed)
+    narrow_c.second_step()
+    spread_b.corner_step()
+    merged_there = order.hold(merged_there)
+    spread_b.last_step()
     normed_there = over_core(normed)
-
-    ke_part = dot(embed_rows, key_weight).astype(bf16)
-    got_ke = send_narrow(lambda at: lax.dynamic_slice_in_dim(ke_part, at * shard, shard, 1), z)
-
-    spread_b.corner_step()
-    bundle_c = jnp.stack(order.hold(*got_c))
-    order.mark(bundle_c)
-    spread_c = Spread(bundle_c, order)
-    spread_b.last_step()
+    spread_c = Spread(narrow_c.bundle(), order)
+    narrow_d = Narrow(order.hold(pieces_of([mlp_out_weight], p)), order)
     spread_c.near_step()
     qkv_w, attn_out_w = assemble([qkv_weight, attn_out_weight], spread_b.parts(), spot)
-    project = dot(normed, qkv_w).astype(bf16)
+    project = dot(order.hold(normed), qkv_w).astype(bf16)
     order.mark(project)
-    spread_c.corner_step()
+    narrow_d.second_step()
+    normed_there = order.hold(normed_there)
     attended, logs = attention(order.hold(project), seg_row, seg_col, pad_col)
     order.mark(attended)
+    spread_c.corner_step()
     attended_there = over_core(attended)
-    bundle_d = jnp.stack(order.hold(*got_d))
-    order.mark(bundle_d)
-    spread_d = Spread(bundle_d, order)
-    spread_c.last_step()
-    spread_d.near_step()
-    residual = patch_state + dot(attended, attn_out_w) + attn_out_b
+    spread_d = Spread(narrow_d.bundle(), order)
+    residual = patch_state + dot(order.hold(attended), attn_out_w) + attn_out_b
     unit_two, inverse_two = normalise(residual)
     normed_two = (unit_two * gain_two + bias_two).astype(bf16)
     order.mark(normed_two)
+    spread_c.last_step()
+    spread_d.near_step()
     normed_two_there = over_core(normed_two)
     (mlp_in_w,) = assemble([mlp_in_weight], spread_c.parts(), spot)
-    hidden_pre = dot(normed_two, mlp_in_w) + mlp_in_b
-    hidden, slope = gelu_pair(hidden_pre)
-    hidden, slope = hidden.astype(bf16), slope.astype(bf16)
+    attended_there, normed_two_there = order.hold(attended_there, normed_two_there)
+    hidden, slope = mlp_in(order.hold(normed_two), mlp_in_w, mlp_in_b)
     order.mark(hidden)
     hidden_there = over_core(hidden)
     spread_d.corner_step()
+    spread_d.last_step()
+    (mlp_out_w,) = assemble([mlp_out_weight], spread_d.parts(), spot)
 
     def grad_of(own, there, own_half, got):
         return (dot_tn(own, own_half) + dot_tn(there, got)).astype(bf16)
@@ -751,67 +960,68 @@
     def blocks(a):
         return a.reshape(4, 2, 2, a.shape[0] // 16, a.shape[1])
 
-    def add_held(pair):
-        total = add_two(*order.hold(*pair))
-        order.mark(total)
-        return total
-
-    def send_block(grad):
-        return send_narrow(lambda at: take(grad, at, 0), z)
-
-    def add_narrow(parts):
-        total = add_four(order.hold(*parts))
-        order.mark(total)
-        return total
-
     cot_float = cotangent.astype(f32)
-    grad_d = blocks(grad_of(order.hold(hidden), hidden_there, cot_half, cot_got))
+    pre_half, pre_other, normed_two_grad, pre_sums = mlp_back(
+        core[None], order.hold(cotangent), mlp_out_w, mlp_in_w, slope
+    )
+    order.mark(pre_other)
+    pre_got = over_core(pre_other)
+    grad_d = blocks(grad_of(*order.hold(hidden, hidden_there), cot_half, cot_got))
     order.mark(grad_d)
-    grad_d = reduce_first(grad_d, p)
-    spread_d.last_step()
-    (mlp_out_w,) = assemble([mlp_out_weight], spread_d.parts(), spot)
-    hidden_pre_grad = (dot_nt(cotangent, mlp_out_w) * slope.astype(f32)).astype(bf16)
-    order.mark(hidden_pre_grad)
-    pre_got = over_core(other_half(hidden_pre_grad))
-
-    normed_two_grad = dot_nt(order.hold(hidden_pre_grad), mlp_in_w)
-    residual_grad = cot_float + normalise_back(normed_two_grad, gain_two, unit_two, inverse_two)
+    reduce_d = Reduce(grad_d, p, z, order)
+    ke_part = lax.dot_general(
+        key_weight, embed_rows, (((0,), (1,)), ((), ())), preferred_element_type=f32
+    ).astype(bf16)
+    ke_part = order.hold(ke_part).reshape(2, 2, shard, COLS)
+    ke_kept, ke_got = take(ke_part, z & 1, 1), swap_narrow(take(ke_part, 1 - (z & 1), 1), 1)
+    residual_grad = cot_float + normalise_back(
+        order.hold(normed_two_grad), gain_two, unit_two, inverse_two
+    )
     branch_grad = residual_grad.astype(bf16)
     order.mark(branch_grad)
     branch_got = over_core(other_half(branch_grad))
-    grad_c = blocks(
-        grad_of(normed_two, normed_two_there, order.hold(half(hidden_pre_grad)), pre_got)
+    grad_c = grad_of(normed_two, normed_two_there, *order.hold(pre_half, pre_got))
+    order.mark(grad_c)
+    grad_c = jnp.concatenate(
+        [grad_c, grad_of(attended, attended_there, *order.hold(half(branch_grad), branch_got))],
+        axis=1,
     )
     order.mark(grad_c)
-    grad_c = reduce_first(grad_c, p)
+    reduce_c = Reduce(blocks(grad_c), p, z, order)
     attended_grad = dot_nt(order.hold(branch_grad), attn_out_w).astype(bf16)
     order.mark(attended_grad)
-    grad_d = reduce_second(add_held(grad_d), p)
-    project_grad = attention_back(
-        project, order.hold(attended_grad), logs, seg_row, seg_col, pad_col
-    )
-    order.mark(project_grad)
-    project_got = over_core(other_half(project_grad))
+    reduce_d.step()
+    ke_two = add_two(ke_kept, order.hold(ke_got))
+    order.mark(ke_two)
+    ke_got = swap_narrow(take(ke_two, 1 - (z >> 1), 0), 2)
+    attended_grad = order.hold(attended_grad)
+    project_grad = attention_back(project, attended_grad, logs, seg_row, seg_col, pad_col)
+    project_other = other_half(project_grad)
+    order.mark(project_other)
+    project_got = over_core(project_other)
+    reduce_d.step()
+    ke_own = add_two(take(ke_two, z >> 1, 0), order.hold(ke_got))
+    order.mark(ke_own)
     normed_grad = dot_nt(order.hold(project_grad), qkv_w)
     state_grad = residual_grad + normalise_back(normed_grad, gain_one, unit_one, inverse_one)
     state_grad = state_grad.astype(bf16)
     order.mark(state_grad)
+    grad_b = grad_of(normed, normed_there, *order.hold(half(project_grad), project_got))
+    order.mark(grad_b)
+    reduce_b = Reduce(blocks(grad_b), p, z, order)
     state_got = over_core(other_half(state_grad))
-    grad_c = reduce_second(add_held(grad_c), p)
-    grad_b = jnp.concatenate(
-        [
-            grad_of(normed, normed_there, order.hold(half(project_grad)), project_got),
-            grad_of(attended, attended_there, half(branch_grad), branch_got),
-        ],
-        axis=1,
-    )
-    order.mark(grad_b)
-    grad_b = reduce_first(blocks(grad_b), p)
-    grad_d = send_block(add_held(grad_d))
     merged_grad = dot_nt(order.hold(state_grad), agg_out_w).astype(bf16)
-
+    order.mark(merged_grad)
+    reduce_d.step()
+    reduce_c.step()
+    merged_grad = order.hold(merged_grad)
     cross, zed, pixel_grad = variable_back(pixels, same, keys_rows, keys_cols, table, merged_grad)
     order.mark(cross)
+    reduce_d.step()
+    spread_d = Spread(reduce_d.total, order)
+    reduce_c.step()
+    grad_a = grad_of(merged, merged_there, *order.hold(half(state_grad), state_got))
+    order.mark(grad_a)
     zed_parts = split_two(zed.transpose(0, 2, 1).reshape(HEADS, COLS))
     column_sums = [
         jnp.sum(state_grad.astype(f32), axis=0),
@@ -821,33 +1031,38 @@
         jnp.sum(normed_two_grad * unit_two, axis=0),
         jnp.sum(normed_two_grad, axis=0),
         jnp.sum(cot_float, axis=0),
-        jnp.sum(hidden_pre_grad.astype(f32), axis=0),
+        pre_sums.reshape(-1),
     ]
-    small = jnp.concatenate(
-        [part.reshape(-1) for part in zed_parts] + [v.astype(bf16) for v in column_sums]
-    ).reshape(-1, 2 * COLS)
-    n_small = small.shape[0]
-    small = jnp.concatenate([small, jnp.zeros((16 * SUB - n_small, 2 * COLS), bf16)])
+    sums = jnp.concatenate([v.astype(bf16) for v in column_sums]).reshape(-1, 2 * COLS)
+    filler = jnp.zeros((16 * (SUB - 1) - sums.shape[0], 2 * COLS), bf16)
+    small = jnp.concatenate([jnp.concatenate(zed_parts, axis=1), sums, filler])
     shared = jnp.concatenate(
         [cross.reshape(SUB, HEAD_DIM, 2 * COLS), small.reshape(SUB, 16, 2 * COLS)], axis=1
     )
     shared = shared.reshape(2, 2, 2, 80, 2 * COLS)
+    order.mark(shared)
     shared_got = over_core(take(shared, 1 - core, 0))
-    grad_c = send_block(add_held(grad_c))
-    grad_a = grad_of(merged, merged_there, order.hold(half(state_grad)), state_got)
     grad_a = grad_a.reshape(4, 2, 2, shard // 4, D // 2).transpose(1, 2, 0, 3, 4)
     grad_a = grad_a.reshape(2, 2, shard, D // 2)
-    shared = add_two(take(shared, core, 0), shared_got)
+    shared = add_two(take(shared, core, 0), order.hold(shared_got))
     grad_a = jnp.concatenate([grad_a, shared], axis=2)
     order.mark(grad_a)
-    grad_a = reduce_first(grad_a, p)
-    grad_b = reduce_second(add_held(grad_b), p)
-    spread_d = Spread(add_narrow(grad_d), order)
+    reduce_a = ReduceShared(grad_a[None], p, z, order)
+    reduce_b.step()
+    spread_d.near_step()
+    reduce_c.step()
     result = (residual + dot(order.hold(hidden), mlp_out_w) + mlp_out_b).astype(bf16)
     order.mark(result)
-    grad_a = reduce_second(add_held(grad_a), p)
-    spread_d.near_step()
-    spread_c = Spread(add_narrow(grad_c), order)
+    reduce_a.step()
+    reduce_b.step()
+    reduce_c.step()
+    spread_c = Spread(reduce_c.total, order)
+    spread_d.corner_step()
+    reduce_a.step()
+    spread_c.near_step()
+    reduce_b.step()
+    reduce_a.step()
+    spread_d.last_step()
     patches_grad = lax.dot_general(
         order.hold(pixel_grad),
         chooser.astype(f32),
@@ -856,59 +1071,32 @@
         preferred_element_type=f32,
     )[:, :PATCH_COLS]
     order.mark(patches_grad)
-    grad_a = add_held(grad_a)
-    grad_a = send_narrow(
-        lambda at: jnp.concatenate(
-            [lax.dynamic_slice_in_dim(grad_a, at * 64, 64, 0), grad_a[shard:]]
-        ),
-        z,
-    )
-    grad_b = send_block(add_held(grad_b))
-    spread_c.near_step()
-    spread_d.corner_step()
-    spread_a = Spread(add_narrow(grad_a), order)
+    reduce_a.step()
+    spread_a = Spread(reduce_a.total, order)
+    reduce_b.step()
+    spread_b = Spread(reduce_b.total, order)
+    spread_a.near_step()
+    spread_b.near_step()
     spread_c.corner_step()
-    spread_a.near_step()
-    spread_b = Spread(add_narrow(grad_b), order)
-    spread_d.last_step()
-    spread_a.corner_step()
-    spread_b.near_step()
-    spread_c.last_step()
     (grad_mlp_out_w,) = place(spread_d.parts(), [(D, D)], spot)
     order.mark(grad_mlp_out_w)
+    spread_a.corner_step()
+    spread_b.corner_step()
+    spread_c.last_step()
     spread_a.last_step()
-    spread_b.corner_step()
-    (grad_mlp_in_w,) = place(spread_c.parts(), [(shard, 4 * D)], spot)
+    grad_mlp_in_w, grad_attn_out_w = place(spread_c.parts(), [(shard, 4 * D), (shard, D)], spot)
     order.mark(grad_mlp_in_w)
+    spread_b.last_step()
     grad_agg_out_w, cross, rest = place(spread_a.parts(), [(shard, D)], spot, shared=True)
     order.mark(cross)
-
-    rest = rest.reshape(16 * SUB, 2 * COLS)
-    zed = rest[:16].reshape(2, HEADS, COLS)
-    zed = zed[0] + zed[1]
-    sums = rest[16:n_small].reshape(-1, COLS)
-    own = lambda i: take(sums[4 * i : 4 * i + 4], z, 0)
-    grad_mlp_in_b = lax.dynamic_slice_in_dim(sums[28:44], 4 * z, 4, 0).reshape(D)
-    zed_both = split_two(zed)
-    grad_embed = lax.dot_general(
-        cross, value_weight, (((0,), (1,)), ((), ())), preferred_element_type=f32
-    ) + (dot_tn(zed_both[0], key_query_t) + dot_tn(zed_both[1], key_query_t)) * scale_by
-    grad_value_w = lax.dot_general(
-        embed_rows, cross, (((0,), (1,)), ((), ())), preferred_element_type=f32
+    (grad_qkv_w,) = place(spread_b.parts(), [(shard, 3 * D)], spot)
+
+    finished = finish(
+        spot, cross, rest, value_weight, embed_rows.T, key_query_t.T, query_full, ke_own
     )
-    query_grad = sum(
-        lax.dot_general(embed_rows, part, (((0,), (1,)), ((), ())), preferred_element_type=f32)
-        for part in zed_both
-    ) * scale_by
-    grad_key_w = jnp.repeat(query_grad, HEAD_DIM, axis=1) * query_full[None, :]
-    ke_own = split_two(sum(part.astype(f32) for part in got_ke))
-    per_head = sum(dot(part, ke) for part in zed_both for ke in ke_own)
-    own_head = z * 4 + jnp.arange(shard, dtype=jnp.int32) // HEAD_DIM
-    mine = jnp.arange(HEADS, dtype=jnp.int32)[:, None] == own_head[None, :]
-    grad_agg_query = jnp.sum(jnp.where(mine, per_head, 0.0), axis=0) * scale_by
-
-    spread_b.last_step()
-    grad_qkv_w, grad_attn_out_w = place(spread_b.parts(), [(shard, 3 * D), (shard, D)], spot)
+    grad_embed, grad_value_w, grad_key_w, grad_agg_query, grad_mlp_in_b = finished[:5]
+    grad_agg_query, grad_mlp_in_b = grad_agg_query.reshape(shard), grad_mlp_in_b.reshape(D)
+    own = lambda i: finished[5 + i].reshape(shard)
 
     return (
         result,

time: 526 us -> 455 us (0.87)
  starting transfers between devices: 116 us -> 62.5 us
  Pallas kernels: 89 us -> 136 us
  matrix products: 102 us -> 60.9 us
  waiting for transfers between devices: 109 us -> 99.1 us
  local copies, waits for them, and re-layouts: 62.5 us -> 54.2 us
    ppermute x33 -> x3, starting transfers between devices: 82.4 us -> 4.43 us  [turn_narrow(): lax.ppermute(a, 'narrow', [(i, (i + by) % size) for i in range(size)])]
    pallas_call x0 -> x17, Pallas kernels: none -> 55.7 us  [the longest x10 17.5 us: add_split(): pl.pallas_call(add_split_kernel, out_shape=[out, out], grid_spec=pltpu.Pr...]
    ppermute x0 -> x20, waiting for transfers between devices: none -> 38.8 us  [swap_narrow(): return lax.ppermute(a, 'narrow', [(i, i ^ bits) for i in range(size)])]
    ppermute x13, waiting for transfers between devices: 48.3 us -> 12.6 us  [over_first(): return lax.ppermute(a, 'wide', wide_pairs(lambda i: 4 if i & 1 else 2))]
    ppermute x33 -> x3, waiting for transfers between devices: 29.8 us -> 2.83 us  [turn_narrow(): lax.ppermute(a, 'narrow', [(i, (i + by) % size) for i in range(size)])]
    ppermute x0 -> x20, starting transfers between devices: none -> 25 us  [swap_narrow(): return lax.ppermute(a, 'narrow', [(i, i ^ bits) for i in range(size)])]
    dot_general x7 -> x5, matrix products: 31.6 us -> 7.1 us  [dot_nt(): lax.dot_general(a, b, (((1,), (1,)), ((), ())), preferred_element_type=f32)]
    ppermute x13, waiting for transfers between devices: 21.1 us -> 43.3 us  [over_second(): return lax.ppermute(a, 'wide', wide_pairs(lambda i: 2 if i & 1 else 4))]
  transfers between devices with their start and end apart: 97 -> 87, of which waited for: 25 -> 29; matrix products, arithmetic and copies ran while one was open for 32% -> 27% of each run, Pallas kernels for 15% -> 30%
where the time goes in v3:
time: 455 us; the launch traced here: 449 us
  Pallas kernels  136 us (30%)
  waiting for transfers between devices  99.1 us (22%)
  starting transfers between devices  62.5 us (14%)
  matrix products  60.9 us (13%)
  local copies, waits for them, and re-layouts  54.2 us (12%)
  other arithmetic  34.2 us (8%)
    ppermute x13, waiting for transfers between devices, over_second(): return lax.ppermute(a, 'wide', wide_pairs(lambda i: 2 if i & 1 else 4))  43.3 us
    ppermute x20, waiting for transfers between devices, swap_narrow(): return lax.ppermute(a, 'narrow', [(i, i ^ bits) for i in range(size)])  38.8 us
    dot_general x10, matrix products, dot_tn(): lax.dot_general(a, b, (((0,), (0,)), ((), ())), preferred_element_type=f32)  31.8 us
    unnamed x268, local copies, waits for them, and re-layouts  27.8 us
    ppermute x20, starting transfers between devices, swap_narrow(): return lax.ppermute(a, 'narrow', [(i, i ^ bits) for i in range(size)])  25 us
    ppermute x13, starting transfers between devices, over_first(): return lax.ppermute(a, 'wide', wide_pairs(lambda i: 4 if i & 1 else 2))  17.6 us
    pallas_call x10, Pallas kernels, add_split(): pl.pallas_call(add_split_kernel, out_shape=[out, out], grid_spec=pltpu.Pr...  17.5 us
    dot_general x5, matrix products, dot(): return jnp.dot(a, b, preferred_element_type=f32)  16.8 us
  transfers between devices with their start and end apart: 87, of which 29 were waited for; matrix products, arithmetic and copies ran while one was open for 27% of the time, Pallas kernels for 30%

profile of v3, /device:TPU:0, one launch (start us, length us, event | category | flops | bytes accessed | tf_op | source)
XLA Modules:
  0.0 449.3 jit_solution(5422926328199193636)
XLA Ops:
  1.6 4.0 collective-permute-start.2
  9.2 3.0 collective-permute-start.8
  15.9 2.0 convolution_convert_fusion.4.pixels_ref
  21.8 2.2 collective-permute-done.1
  29.9 3.0 collective-permute-start.4
  43.8 2.3 collective-permute-done.10.refs_2_
  46.1 4.1 collective-permute-done.14
  58.3 2.3 collective-permute-done.17.refs_5_
  62.1 2.3 arrange.1
  66.4 9.1 %variable_forward.1 = bf16[512,1024]{1,0:T(8,128)(2,1)S(1)} custom-call(bf16[256,512]{1,0:T(8,128)(2,1)S(1)} %copy-done.58, f32[256,256]{1,0:T(8,128)S(1)} %and_convert_fusion.same_ref, f32[8,2,256]{2,1,0:T(2,128)S(1)} %add.266.keys_ref, bf16[1024,256]{1,0:T(8,128)(2,1)S(1)} %copy-done.51), custom_call_target="tpu_custom_call" | custom-call | flops 5400000000 | bytes 1 | tf_op jit(solution)/shard_map/variable_forward/pallas_call | solution.py:436
  76.2 3.1 assemble.4
  85.2 10.9 %collective-permute-done.23.refs_6_ = bf16[3,32,4096]{2,1,0:T(8,128)(2,1)} collective-permute-done((bf16[3,32,4096]{2,1,0:T(8,128)(2,1)S(1)}, bf16[3,32,4096]{2,1,0:T(8,128)(2,1)}, u32[]{:S(2)}, u32[]{:S(2)}) %collective-permute-start.23) | collective-permute-done | bytes 786464 | tf_op jit(solution)/shard_map/ppermute | solution.py:64
  96.1 2.0 collective-permute-done.26
  107.2 4.1 assemble.5
  111.4 3.7 convolution_convert_fusion.q_ref.k_ref.v_ref
  115.1 3.5 collective-permute-done.29
  118.7 12.5 %attention.1 = (bf16[512,1024]{1,0:T(8,128)(2,1)}, f32[8,2,512]{2,1,0:T(2,128)S(1)}) custom-call(bf16[512,3072]{1,0:T(8,128)(2,1)S(1)} %convolution_convert_fusion.q_ref.k_ref.v_ref, bf16[512,3072]{1,0:T(8,128)(2,1)S(1)} %convolution_convert_fusion.q_ref.k_ref.v_ref, bf16[512,3072]{1,0:T(8,128)(2,1)S(1)} %convolution_convert_fusion.q_ref.k_ref.v_ref, ...), custom_call_target="tpu_custom_call" | custom-call | flops 7500000256 | bytes 1 | tf_op jit(solution)/shard_map/attention/pallas_call | solution.py:550
  134.8 2.9 fusion.44
  140.4 4.9 %collective-permute-done.35.refs_5_ = bf16[3,32,4096]{2,1,0:T(8,128)(2,1)} collective-permute-done((bf16[3,32,4096]{2,1,0:T(8,128)(2,1)S(1)}, bf16[3,32,4096]{2,1,0:T(8,128)(2,1)}, u32[]{:S(2)}, u32[]{:S(2)}) %collective-permute-start.35) | collective-permute-done | bytes 786464 | tf_op jit(solution)/shard_map/ppermute | solution.py:64
  149.8 3.5 assemble.6.weight.w_in
  153.4 12.8 %mlp_in.1 = (bf16[512,4096]{1,0:T(8,128)(2,1)}, bf16[512,4096]{1,0:T(8,128)(2,1)S(1)}) custom-call(bf16[512,1024]{1,0:T(8,128)(2,1)} %add_convert_fusion.7.rows_ref, bf16[1024,4096]{1,0:T(8,128)(2,1)S(1)} %assemble.6.weight.w_in, f32[1,4096]{1,0:T(1,128)S(1)} %reshape.439.bias), custom_call_target="tpu_custom_call" | custom-call | flops 6600000000 | bytes 1 | tf_op jit(solution)/shard_map/mlp_in/pallas_call | solution.py:641
  166.2 2.0 copy-done.64
  172.4 9.7 %collective-permute-done.40.refs_5_ = bf16[3,128,1024]{2,1,0:T(8,128)(2,1)} collective-permute-done((bf16[3,128,1024]{2,1,0:T(8,128)(2,1)}, bf16[3,128,1024]{2,1,0:T(8,128)(2,1)}, u32[]{:S(2)}, u32[]{:S(2)}) %collective-permute-start.40) | collective-permute-done | bytes 786464 | tf_op jit(solution)/shard_map/ppermute | solution.py:64
  183.6 2.1 fusion
  190.8 3.0 assemble.7.w_out
  193.8 3.3 copy-done.5
  197.2 15.3 %mlp_back.1 = (bf16[512,2048]{1,0:T(8,128)(2,1)S(1)}, bf16[512,2048]{1,0:T(8,128)(2,1)}, f32[512,1024]{1,0:T(8,128)}, f32[4,1,1024]{2,1,0:T(1,128)S(1)}) custom-call(s32[1]{0:T(128)} %bitcast.38.core, bf16[512,1024]{1,0:T(8,128)(2,1)S(1)} %copy-done.7, bf16[4096,1024]{1,0:T(8,128)(2,1)} %copy-done.5, bf16[1024,4096]{1,0:T(8,128)(2,1)} %copy-done.6, ...), custom_call_target="tpu_custom_call" | custom-call | flops 9299999744 | bytes 1 | tf_op jit(solution)/shard_map/mlp_back/pallas_call | solution.py:680
  213.8 4.7 %fusion.45 = f32[4096,512]{1,0:T(8,128)S(1)} fusion(bf16[512,4096]{1,0:T(8,128)(2,1)} %collective-permute-done.43, bf16[512,512]{1,0:T(8,128)(2,1)} %collective-permute-done.44), kind=kOutput, calls=%fused_computation.212 | convolution fusion | flops 2147483648 | bytes 13107200 | tf_op jit(solution)/shard_map/dot_general | solution.py:43
  218.5 4.9 %add_convert_fusion.1 = bf16[4096,512]{1,0:T(8,128)(2,1)S(1)} fusion(f32[4096,512]{1,0:T(8,128)S(1)} %fusion.45, bf16[512,4096]{1,0:T(8,128)(2,1)} %get-tuple-element.337, bf16[512,1024]{1,0:T(8,128)(2,1)S(1)} %copy-done.7, s32[]{:T(128)S(6)} %select_n.204), kind=kOutput, calls=%fused_computation.1 | convolution fusion | flops 2151677952 | bytes 17301508 | tf_op jit(solution)/shard_map/dot_general | solution.py:43
  223.4 3.1 pick_first.4
  228.0 2.0 copy.72
  230.0 3.8 multiply_reduce_fusion
  237.3 2.0 collective-permute-start.49
  239.3 4.5 fusion.46
  243.8 5.9 %add_convert_fusion = bf16[1024,2048]{1,0:T(8,128)(2,1)} fusion(f32[1024,2048]{1,0:T(8,128)S(1)} %fusion.46, bf16[512,1024]{1,0:T(8,128)(2,1)} %add_convert_fusion.7.rows_ref, bf16[512,2048]{1,0:T(8,128)(2,1)S(1)} %copy-done.61), kind=kOutput, calls=%fused_computation | convolution fusion | flops 2151677952 | bytes 15728640 | tf_op jit(solution)/shard_map/dot_general | solution.py:43
  253.6 2.6 pad_maximum_fusion
  256.3 2.3 pick_first.5
  265.5 16.5 %attention_back.1 = bf16[512,3072]{1,0:T(8,128)(2,1)S(1)} custom-call(bf16[512,3072]{1,0:T(8,128)(2,1)S(1)} %copy-done.66, bf16[512,3072]{1,0:T(8,128)(2,1)S(1)} %copy-done.66, bf16[512,3072]{1,0:T(8,128)(2,1)S(1)} %copy-done.66, bf16[512,1024]{1,0:T(8,128)(2,1)S(1)} %convolution_convert_fusion.2.grad_ref, f32[8,2,512]{2,1,0:T(2,128)S(1)} %get-tuple-element.305.log_ref, ...), custom_call_target="tpu_custom_call" | custom-call | flops 9900000256 | bytes 1 | tf_op jit(solution)/shard_map/attention_back/pallas_call | solution.py:609
  283.9 5.8 %collective-permute-done.48 = bf16[4,256,512]{2,1,0:T(8,128)(2,1)S(1)} collective-permute-done((bf16[4,256,512]{2,1,0:T(8,128)(2,1)S(1)}, bf16[4,256,512]{2,1,0:T(8,128)(2,1)S(1)}, u32[]{:S(2)}, u32[]{:S(2)}) %collective-permute-start.48) | collective-permute-done | bytes 1048608 | tf_op jit(solution)/shard_map/ppermute | solution.py:64
  292.2 4.0 multiply_reduce_fusion.1
  299.9 3.4 fusion.48
  308.5 2.3 add_split.12
  310.9 2.3 collective-permute-start.54
  313.2 4.4 add_split.13
  320.6 14.2 %variable_back.1 = (bf16[512,512]{1,0:T(8,128)(2,1)S(1)}, f32[8,256,2]{2,1,0:T(8,128)S(1)}, f32[256,512]{1,0:T(8,128)S(1)}) custom-call(bf16[256,512]{1,0:T(8,128)(2,1)S(1)} %copy-done.59, f32[256,256]{1,0:T(8,128)S(1)} %copy-done.29, f32[8,2,256]{2,1,0:T(2,128)S(1)} %add.266.keys_ref, f32[8,256,2]{2,1,0:T(8,128)S(1)} %bitcast.202, ...), custom_call_target="tpu_custom_call" | custom-call | flops 8700000256 | bytes 1 | tf_op jit(solution)/shard_map/variable_back/pallas_call | solution.py:491
  337.4 2.2 copy.77
  345.1 5.1 %collective-permute-done.53 = bf16[4,64,2560]{2,1,0:T(8,128)(2,1)} collective-permute-done((bf16[4,64,2560]{2,1,0:T(8,128)(2,1)}, bf16[4,64,2560]{2,1,0:T(8,128)(2,1)}, u32[]{:S(2)}, u32[]{:S(2)}) %collective-permute-start.53) | collective-permute-done | bytes 1310752 | tf_op jit(solution)/shard_map/ppermute | solution.py:64
  351.6 2.0 add_split.14
  358.8 3.2 add_split.15
  363.8 5.0 %collective-permute-done.55 = bf16[2,64,2560]{2,1,0:T(8,128)(2,1)S(1)} collective-permute-done((bf16[2,64,2560]{2,1,0:T(8,128)(2,1)S(1)}, bf16[2,64,2560]{2,1,0:T(8,128)(2,1)S(1)}, u32[]{:S(2)}, u32[]{:S(2)}) %collective-permute-start.55) | collective-permute-done | bytes 655392 | tf_op jit(solution)/shard_map/ppermute | solution.py:74
  370.4 7.8 %add_convert_fusion.3 = bf16[512,1024]{1,0:T(8,128)(2,1)} fusion(f32[512,1024]{1,0:T(8,128)S(1)} %copy-done.69, bf16[512,4096]{1,0:T(8,128)(2,1)} %get-tuple-element.337, bf16[4096,1024]{1,0:T(8,128)(2,1)S(1)} %bitcast.195, f32[1024]{0:T(1024)S(1)} %bitcast.276), kind=kOutput, calls=%fused_computation.5 | convolution fusion | flops 4296540160 | bytes 15732736 | tf_op jit(solution)/shard_map/dot_general | solution.py:35
  382.3 2.3 collective-permute-done.61
  388.1 2.2 collective-permute-start.75
  390.4 2.7 collective-permute-done.67
  393.7 3.8 collective-permute-done.66
  398.3 2.4 collective-permute-start.69
  401.9 13.1 %collective-permute-done.69 = bf16[144,512]{1,0:T(8,128)(2,1)S(1)} collective-permute-done((bf16[144,512]{1,0:T(8,128)(2,1)S(1)}, bf16[144,512]{1,0:T(8,128)(2,1)S(1)}, u32[]{:S(2)}, u32[]{:S(2)}) %collective-permute-start.69) | collective-permute-done | bytes 147488 | tf_op jit(solution)/shard_map/ppermute | solution.py:74
  419.2 2.8 place.4
  422.0 2.6 collective-permute-done.72.refs_2_
  424.6 6.4 %collective-permute-done.80.refs_2_ = bf16[2,64,1536]{2,1,0:T(8,128)(2,1)S(1)} collective-permute-done((bf16[2,64,1536]{2,1,0:T(8,128)(2,1)S(1)}, bf16[2,64,1536]{2,1,0:T(8,128)(2,1)S(1)}, u32[]{:S(2)}, u32[]{:S(2)}) %collective-permute-start.80) | collective-permute-done | bytes 393248 | tf_op jit(solution)/shard_map/ppermute | solution.py:60
  433.4 3.0 collective-permute-done.78.refs_4_
  436.9 3.2 place.5
  441.9 2.7 finish.1
  446.6 2.4 place.7
  (561 shorter events, 148.9 us)
Async XLA Ops:
  1.6 19.7 %collective-permute-start.2 = (bf16[32,1024]{1,0:T(8,128)(2,1)S(1)}, bf16[32,1024]{1,0:T(8,128)(2,1)S(1)}, u32[]{:S(2)}, u32[]{:S(2)}) collective-permute-start(bf16[32,1024]{1,0:T(8,128)(2,1)S(1)} %constant_dynamic-slice_fusion.13), channel_id=1, source_target_pairs={{0,2},{1,3},{2,0},{3,1},{4,6},{5,7},{6,4},{7,5},{8,10},{9,11},{10,... | collective-permute-start | bytes 196616 | tf_op jit(solution)/shard_map/ppermute | solution.py:74
  7.2 12.4 %collective-permute-start = (bf16[12,256]{1,0:T(8,128)(2,1)S(1)}, bf16[12,256]{1,0:T(8,128)(2,1)S(1)}, u32[]{:S(2)}, u32[]{:S(2)}) collective-permute-start(bf16[12,256]{1,0:T(8,128)(2,1)S(1)} %get-tuple-element.455.own), channel_id=1, source_target_pairs={{0,2},{1,3},{2,0},{3,1},{4,6},{5,7},{6,4},{7,5},{8,10},{9,11},{10,... | collective-permute-start | bytes 18440 | tf_op jit(solution)/shard_map/ppermute | solution.py:74
  9.2 24.3 %collective-permute-start.8 = (bf16[32,4096]{1,0:T(8,128)(2,1)S(1)}, bf16[32,4096]{1,0:T(8,128)(2,1)S(1)}, u32[]{:S(2)}, u32[]{:S(2)}) collective-permute-start(bf16[32,4096]{1,0:T(8,128)(2,1)S(1)} %get-tuple-element.441), channel_id=1, source_target_pairs={{0,2},{1,3},{2,0},{3,1},{4,6},{5,7},{6,4},{7,5},{8,10},{9,11},{10,... | collective-permute-start | bytes 786440 | tf_op jit(solution)/shard_map/ppermute | solution.py:74
  21.3 12.1 %collective-permute-start.6 = (bf16[2,32,1024]{2,1,0:T(8,128)(2,1)S(1)}, bf16[2,32,1024]{2,1,0:T(8,128)(2,1)S(1)}, u32[]{:S(2)}, u32[]{:S(2)}) collective-permute-start(bf16[2,32,1024]{2,1,0:T(8,128)(2,1)S(1)} %pad_maximum_fusion.23), channel_id=1, source_target_pairs={{0,1},{1,0},{2,3},{3,2},{4,5},{5,4},{6,7},{7,6},{8,9},{9,8},{10,11... | collective-permute-start | bytes 393224 | tf_op jit(solution)/shard_map/ppermute | solution.py:74
  28.9 7.9 %collective-permute-start.3 = (bf16[320,128]{1,0:T(8,128)(2,1)S(1)}, bf16[320,128]{1,0:T(8,128)(2,1)S(1)}, u32[]{:S(2)}, u32[]{:S(2)}) collective-permute-start(bf16[320,128]{1,0:T(8,128)(2,1)S(1)} %pad_maximum_fusion.25), channel_id=1, source_target_pairs={{0,1},{1,2},{2,3},{3,0},{4,5},{5,6},{6,7},{7,4},{8,9},{9,10},{10,1... | collective-permute-start | bytes 245768 | tf_op jit(solution)/shard_map/ppermute | solution.py:69
  29.9 8.7 %collective-permute-start.4 = (bf16[320,128]{1,0:T(8,128)(2,1)S(1)}, bf16[320,128]{1,0:T(8,128)(2,1)S(1)}, u32[]{:S(2)}, u32[]{:S(2)}) collective-permute-start(bf16[320,128]{1,0:T(8,128)(2,1)S(1)} %pad_maximum_fusion.25), channel_id=1, source_target_pairs={{0,2},{1,3},{2,0},{3,1},{4,6},{5,7},{6,4},{7,5},{8,10},{9,11},{10,... | collective-permute-start | bytes 245768 | tf_op jit(solution)/shard_map/ppermute | solution.py:69
  33.5 16.7 %collective-permute-start.14 = (bf16[2,32,4096]{2,1,0:T(8,128)(2,1)S(1)}, bf16[2,32,4096]{2,1,0:T(8,128)(2,1)S(1)}, u32[]{:S(2)}, u32[]{:S(2)}) collective-permute-start(bf16[2,32,4096]{2,1,0:T(8,128)(2,1)S(1)} %pad_maximum_fusion.10), channel_id=1, source_target_pairs={{0,1},{1,0},{2,3},{3,2},{4,5},{5,4},{6,7},{7,6},{8,9},{9,8},{10,11... | collective-permute-start | bytes 1572872 | tf_op jit(solution)/shard_map/ppermute | solution.py:74
  35.3 7.8 %collective-permute-start.11 = (bf16[2,3,32,1024]{3,2,1,0:T(8,128)(2,1)S(1)}, bf16[2,3,32,1024]{3,2,1,0:T(8,128)(2,1)S(1)}, u32[]{:S(2)}, u32[]{:S(2)}) collective-permute-start(bf16[2,3,32,1024]{3,2,1,0:T(8,128)(2,1)S(1)} %pad_maximum_fusion.14), channel_id=1, source_target_pairs={{0,8},{4,20},{8,0},{12,28},{16,24},{20,4},{24,16},{28,12},{1,9},{5... | collective-permute-start | bytes 1179656 | tf_op jit(solution)/shard_map/ppermute | solution.py:60
  57.9 18.2 %collective-permute-start.18 = (bf16[2,3,32,1024]{3,2,1,0:T(8,128)(2,1)S(1)}, bf16[2,3,32,1024]{3,2,1,0:T(8,128)(2,1)}, u32[]{:S(2)}, u32[]{:S(2)}) collective-permute-start(bf16[2,3,32,1024]{3,2,1,0:T(8,128)(2,1)S(1)} %collective-permute-done.11.refs_3_), channel_id=1, source_target_pairs={{0,4},{4,0},{8,12},{12,8},{16,20},{20,16},{24,28},{28,24},{1,5},{5... | collective-permute-start | bytes 1179656 | tf_op jit(solution)/shard_map/ppermute | solution.py:56
  58.2 24.6 %collective-permute-start.21 = (bf16[32,4096]{1,0:T(8,128)(2,1)}, bf16[32,4096]{1,0:T(8,128)(2,1)}, u32[]{:S(2)}, u32[]{:S(2)}) collective-permute-start(bf16[32,4096]{1,0:T(8,128)(2,1)} %constant_dynamic-slice_fusion.10), channel_id=1, source_target_pairs={{0,2},{1,3},{2,0},{3,1},{4,6},{5,7},{6,4},{7,5},{8,10},{9,11},{10,... | collective-permute-start | bytes 786440 | tf_op jit(solution)/shard_map/ppermute | solution.py:74
  60.6 23.3 %collective-permute-start.20 = (bf16[2,3,32,4096]{3,2,1,0:T(8,128)(2,1)}, bf16[2,3,32,4096]{3,2,1,0:T(8,128)(2,1)S(1)}, u32[]{:S(2)}, u32[]{:S(2)}) collective-permute-start(bf16[2,3,32,4096]{3,2,1,0:T(8,128)(2,1)} %pad_maximum_fusion.1), channel_id=1, source_target_pairs={{0,8},{4,20},{8,0},{12,28},{16,24},{20,4},{24,16},{28,12},{1,9},{5... | collective-permute-start | bytes 4718600 | tf_op jit(solution)/shard_map/ppermute | solution.py:60
  62.1 14.1 %collective-permute-start.19 = (bf16[3,32,1024]{2,1,0:T(8,128)(2,1)S(1)}, bf16[3,32,1024]{2,1,0:T(8,128)(2,1)}, u32[]{:S(2)}, u32[]{:S(2)}) collective-permute-start(bf16[3,32,1024]{2,1,0:T(8,128)(2,1)S(1)} %collective-permute-done.17.refs_5_), channel_id=1, source_target_pairs={{0,4},{4,0},{8,12},{12,8},{16,20},{20,16},{24,28},{28,24},{1,5},{5... | collective-permute-start | bytes 589832 | tf_op jit(solution)/shard_map/ppermute | solution.py:56
  75.6 9.6 %collective-permute-start.24 = (bf16[512,1024]{1,0:T(8,128)(2,1)S(1)}, bf16[512,1024]{1,0:T(8,128)(2,1)S(1)}, u32[]{:S(2)}, u32[]{:S(2)}) collective-permute-start(bf16[512,1024]{1,0:T(8,128)(2,1)S(1)} %variable_forward.1), channel_id=1, source_target_pairs={{0,4},{4,0},{8,12},{12,8},{16,20},{20,16},{24,28},{28,24},{1,5},{5... | collective-permute-start | bytes 3145736 | tf_op jit(solution)/shard_map/ppermute | solution.py:56
  83.9 12.2 %collective-permute-start.23 = (bf16[3,32,4096]{2,1,0:T(8,128)(2,1)S(1)}, bf16[3,32,4096]{2,1,0:T(8,128)(2,1)}, u32[]{:S(2)}, u32[]{:S(2)}) collective-permute-start(bf16[3,32,4096]{2,1,0:T(8,128)(2,1)S(1)} %slice_bitcast_fusion.2), channel_id=1, source_target_pairs={{0,16},{4,12},{8,24},{12,4},{16,0},{20,28},{24,8},{28,20},{1,17},{... | collective-permute-start | bytes 2359304 | tf_op jit(solution)/shard_map/ppermute | solution.py:64
  84.5 13.6 %collective-permute-start.26 = (bf16[2,32,4096]{2,1,0:T(8,128)(2,1)S(1)}, bf16[2,32,4096]{2,1,0:T(8,128)(2,1)S(1)}, u32[]{:S(2)}, u32[]{:S(2)}) collective-permute-start(bf16[2,32,4096]{2,1,0:T(8,128)(2,1)S(1)} %pad_maximum_fusion.11), channel_id=1, source_target_pairs={{0,1},{1,0},{2,3},{3,2},{4,5},{5,4},{6,7},{7,6},{8,9},{9,8},{10,11... | collective-permute-start | bytes 1572872 | tf_op jit(solution)/shard_map/ppermute | solution.py:74
  85.2 22.0 %collective-permute-start.22 = (bf16[2,3,32,4096]{3,2,1,0:T(8,128)(2,1)S(1)}, bf16[2,3,32,4096]{3,2,1,0:T(8,128)(2,1)}, u32[]{:S(2)}, u32[]{:S(2)}) collective-permute-start(bf16[2,3,32,4096]{3,2,1,0:T(8,128)(2,1)S(1)} %collective-permute-done.20.refs_4_), channel_id=1, source_target_pairs={{0,4},{4,0},{8,12},{12,8},{16,20},{20,16},{24,28},{28,24},{1,5},{5... | collective-permute-start | bytes 4718600 | tf_op jit(solution)/shard_map/ppermute | solution.py:56
  100.1 7.1 %collective-permute-start.25 = (bf16[3,32,4096]{2,1,0:T(8,128)(2,1)}, bf16[3,32,4096]{2,1,0:T(8,128)(2,1)}, u32[]{:S(2)}, u32[]{:S(2)}) collective-permute-start(bf16[3,32,4096]{2,1,0:T(8,128)(2,1)} %collective-permute-done.23.refs_6_), channel_id=1, source_target_pairs={{0,4},{4,0},{8,12},{12,8},{16,20},{20,16},{24,28},{28,24},{1,5},{5... | collective-permute-start | bytes 2359304 | tf_op jit(solution)/shard_map/ppermute | solution.py:56
  103.4 15.3 %collective-permute-start.28 = (bf16[512,1024]{1,0:T(8,128)(2,1)}, bf16[512,1024]{1,0:T(8,128)(2,1)S(1)}, u32[]{:S(2)}, u32[]{:S(2)}) collective-permute-start(bf16[512,1024]{1,0:T(8,128)(2,1)} %add_convert_fusion.8), channel_id=1, source_target_pairs={{0,4},{4,0},{8,12},{12,8},{16,20},{20,16},{24,28},{28,24},{1,5},{5... | collective-permute-start | bytes 3145736 | tf_op jit(solution)/shard_map/ppermute | solution.py:56
  103.5 15.1 %collective-permute-start.29 = (bf16[128,1024]{1,0:T(8,128)(2,1)S(1)}, bf16[128,1024]{1,0:T(8,128)(2,1)S(1)}, u32[]{:S(2)}, u32[]{:S(2)}) collective-permute-start(bf16[128,1024]{1,0:T(8,128)(2,1)S(1)} %constant_dynamic-slice_fusion.9), channel_id=1, source_target_pairs={{0,2},{1,3},{2,0},{3,1},{4,6},{5,7},{6,4},{7,5},{8,10},{9,11},{10,... | collective-permute-start | bytes 786440 | tf_op jit(solution)/shard_map/ppermute | solution.py:74
  106.3 25.1 %collective-permute-start.31 = (bf16[2,3,32,4096]{3,2,1,0:T(8,128)(2,1)S(1)}, bf16[2,3,32,4096]{3,2,1,0:T(8,128)(2,1)}, u32[]{:S(2)}, u32[]{:S(2)}) collective-permute-start(bf16[2,3,32,4096]{3,2,1,0:T(8,128)(2,1)S(1)} %pad_maximum_fusion.2), channel_id=1, source_target_pairs={{0,8},{4,20},{8,0},{12,28},{16,24},{20,4},{24,16},{28,12},{1,9},{5... | collective-permute-start | bytes 4718600 | tf_op jit(solution)/shard_map/ppermute | solution.py:60
  118.6 15.2 %collective-permute-start.30 = (bf16[2,128,1024]{2,1,0:T(8,128)(2,1)S(1)}, bf16[2,128,1024]{2,1,0:T(8,128)(2,1)S(1)}, u32[]{:S(2)}, u32[]{:S(2)}) collective-permute-start(bf16[2,128,1024]{2,1,0:T(8,128)(2,1)S(1)} %pad_maximum_fusion.12), channel_id=1, source_target_pairs={{0,1},{1,0},{2,3},{3,2},{4,5},{5,4},{6,7},{7,6},{8,9},{9,8},{10,11... | collective-permute-start | bytes 1572872 | tf_op jit(solution)/shard_map/ppermute | solution.py:74
  131.3 18.5 %collective-permute-start.32 = (bf16[512,1024]{1,0:T(8,128)(2,1)}, bf16[512,1024]{1,0:T(8,128)(2,1)}, u32[]{:S(2)}, u32[]{:S(2)}) collective-permute-start(bf16[512,1024]{1,0:T(8,128)(2,1)} %get-tuple-element.264), channel_id=1, source_target_pairs={{0,4},{4,0},{8,12},{12,8},{16,20},{20,16},{24,28},{28,24},{1,5},{5... | collective-permute-start | bytes 3145736 | tf_op jit(solution)/shard_map/ppermute | solution.py:56
  131.4 18.4 %collective-permute-start.34 = (bf16[2,3,32,4096]{3,2,1,0:T(8,128)(2,1)}, bf16[2,3,32,4096]{3,2,1,0:T(8,128)(2,1)}, u32[]{:S(2)}, u32[]{:S(2)}) collective-permute-start(bf16[2,3,32,4096]{3,2,1,0:T(8,128)(2,1)} %collective-permute-done.31.refs_3_), channel_id=1, source_target_pairs={{0,4},{4,0},{8,12},{12,8},{16,20},{20,16},{24,28},{28,24},{1,5},{5... | collective-permute-start | bytes 4718600 | tf_op jit(solution)/shard_map/ppermute | solution.py:56
  133.1 12.2 %collective-permute-start.35 = (bf16[3,32,4096]{2,1,0:T(8,128)(2,1)S(1)}, bf16[3,32,4096]{2,1,0:T(8,128)(2,1)}, u32[]{:S(2)}, u32[]{:S(2)}) collective-permute-start(bf16[3,32,4096]{2,1,0:T(8,128)(2,1)S(1)} %slice_bitcast_fusion.1), channel_id=1, source_target_pairs={{0,16},{4,12},{8,24},{12,4},{16,0},{20,28},{24,8},{28,20},{1,17},{... | collective-permute-start | bytes 2359304 | tf_op jit(solution)/shard_map/ppermute | solution.py:64
  139.8 10.0 %collective-permute-start.33 = (bf16[512,1024]{1,0:T(8,128)(2,1)}, bf16[512,1024]{1,0:T(8,128)(2,1)}, u32[]{:S(2)}, u32[]{:S(2)}) collective-permute-start(bf16[512,1024]{1,0:T(8,128)(2,1)} %add_convert_fusion.7.rows_ref), channel_id=1, source_target_pairs={{0,4},{4,0},{8,12},{12,8},{16,20},{20,16},{24,28},{28,24},{1,5},{5... | collective-permute-start | bytes 3145736 | tf_op jit(solution)/shard_map/ppermute | solution.py:56
  148.4 20.4 %collective-permute-start.38 = (bf16[2,3,128,1024]{3,2,1,0:T(8,128)(2,1)S(1)}, bf16[2,3,128,1024]{3,2,1,0:T(8,128)(2,1)S(1)}, u32[]{:S(2)}, u32[]{:S(2)}) collective-permute-start(bf16[2,3,128,1024]{3,2,1,0:T(8,128)(2,1)S(1)} %pad_maximum_fusion.3), channel_id=1, source_target_pairs={{0,8},{4,20},{8,0},{12,28},{16,24},{20,4},{24,16},{28,12},{1,9},{5... | collective-permute-start | bytes 4718600 | tf_op jit(solution)/shard_map/ppermute | solution.py:60
  168.2 45.5 %collective-permute-start.43 = (bf16[512,4096]{1,0:T(8,128)(2,1)}, bf16[512,4096]{1,0:T(8,128)(2,1)}, u32[]{:S(2)}, u32[]{:S(2)}) collective-permute-start(bf16[512,4096]{1,0:T(8,128)(2,1)} %get-tuple-element.337), channel_id=1, source_target_pairs={{0,4},{4,0},{8,12},{12,8},{16,20},{20,16},{24,28},{28,24},{1,5},{5... | collective-permute-start | bytes 12582920 | tf_op jit(solution)/shard_map/ppermute | solution.py:56
  169.8 12.3 %collective-permute-start.40 = (bf16[3,128,1024]{2,1,0:T(8,128)(2,1)}, bf16[3,128,1024]{2,1,0:T(8,128)(2,1)}, u32[]{:S(2)}, u32[]{:S(2)}) collective-permute-start(bf16[3,128,1024]{2,1,0:T(8,128)(2,1)} %slice_bitcast_fusion), channel_id=1, source_target_pairs={{0,16},{4,12},{8,24},{12,4},{16,0},{20,28},{24,8},{28,20},{1,17},{... | collective-permute-start | bytes 2359304 | tf_op jit(solution)/shard_map/ppermute | solution.py:64
  170.4 16.6 %collective-permute-start.39 = (bf16[2,3,128,1024]{3,2,1,0:T(8,128)(2,1)S(1)}, bf16[2,3,128,1024]{3,2,1,0:T(8,128)(2,1)}, u32[]{:S(2)}, u32[]{:S(2)}) collective-permute-start(bf16[2,3,128,1024]{3,2,1,0:T(8,128)(2,1)S(1)} %collective-permute-done.38.refs_3_), channel_id=1, source_target_pairs={{0,4},{4,0},{8,12},{12,8},{16,20},{20,16},{24,28},{28,24},{1,5},{5... | collective-permute-start | bytes 4718600 | tf_op jit(solution)/shard_map/ppermute | solution.py:56
  171.3 42.4 %collective-permute-start.44 = (bf16[512,512]{1,0:T(8,128)(2,1)}, bf16[512,512]{1,0:T(8,128)(2,1)}, u32[]{:S(2)}, u32[]{:S(2)}) collective-permute-start(bf16[512,512]{1,0:T(8,128)(2,1)} %constant_dynamic-slice_fusion.8), channel_id=1, source_target_pairs={{0,4},{4,0},{8,12},{12,8},{16,20},{20,16},{24,28},{28,24},{1,5},{5... | collective-permute-start | bytes 1572872 | tf_op jit(solution)/shard_map/ppermute | solution.py:56
  212.5 26.8 %collective-permute-start.42 = (bf16[512,2048]{1,0:T(8,128)(2,1)}, bf16[512,2048]{1,0:T(8,128)(2,1)}, u32[]{:S(2)}, u32[]{:S(2)}) collective-permute-start(bf16[512,2048]{1,0:T(8,128)(2,1)} %get-tuple-element.288), channel_id=1, source_target_pairs={{0,4},{4,0},{8,12},{12,8},{16,20},{20,16},{24,28},{28,24},{1,5},{5... | collective-permute-start | bytes 6291464 | tf_op jit(solution)/shard_map/ppermute | solution.py:56
  226.5 35.0 %collective-permute-start.47 = (bf16[4,2,256,512]{3,2,1,0:T(8,128)(2,1)}, bf16[4,2,256,512]{3,2,1,0:T(8,128)(2,1)S(1)}, u32[]{:S(2)}, u32[]{:S(2)}) collective-permute-start(bf16[4,2,256,512]{3,2,1,0:T(8,128)(2,1)} %pick_first.4), channel_id=1, source_target_pairs={{0,8},{4,20},{8,0},{12,28},{16,24},{20,4},{24,16},{28,12},{1,9},{5... | collective-permute-start | bytes 6291464 | tf_op jit(solution)/shard_map/ppermute | solution.py:60
  235.6 14.1 %collective-permute-start.45 = (bf16[512,512]{1,0:T(8,128)(2,1)S(1)}, bf16[512,512]{1,0:T(8,128)(2,1)S(1)}, u32[]{:S(2)}, u32[]{:S(2)}) collective-permute-start(bf16[512,512]{1,0:T(8,128)(2,1)S(1)} %get-tuple-element.430), channel_id=1, source_target_pairs={{0,4},{4,0},{8,12},{12,8},{16,20},{20,16},{24,28},{28,24},{1,5},{5... | collective-permute-start | bytes 1572872 | tf_op jit(solution)/shard_map/ppermute | solution.py:56
  237.3 26.9 %collective-permute-start.49 = (bf16[2,256,256]{2,1,0:T(8,128)(2,1)}, bf16[2,256,256]{2,1,0:T(8,128)(2,1)}, u32[]{:S(2)}, u32[]{:S(2)}) collective-permute-start(bf16[2,256,256]{2,1,0:T(8,128)(2,1)} %dynamic-slice_bitcast_fusion), channel_id=1, source_target_pairs={{0,1},{1,0},{2,3},{3,2},{4,5},{5,4},{6,7},{7,6},{8,9},{9,8},{10,11... | collective-permute-start | bytes 786440 | tf_op jit(solution)/shard_map/ppermute | solution.py:74
  259.6 53.6 %collective-permute-start.46 = (bf16[4,2,64,2560]{3,2,1,0:T(8,128)(2,1)}, bf16[4,2,64,2560]{3,2,1,0:T(8,128)(2,1)}, u32[]{:S(2)}, u32[]{:S(2)}) collective-permute-start(bf16[4,2,64,2560]{3,2,1,0:T(8,128)(2,1)} %pick_first.5), channel_id=1, source_target_pairs={{0,8},{4,20},{8,0},{12,28},{16,24},{20,4},{24,16},{28,12},{1,9},{5... | collective-permute-start | bytes 7864328 | tf_op jit(solution)/shard_map/ppermute | solution.py:60
  263.5 26.2 %collective-permute-start.48 = (bf16[4,256,512]{2,1,0:T(8,128)(2,1)S(1)}, bf16[4,256,512]{2,1,0:T(8,128)(2,1)S(1)}, u32[]{:S(2)}, u32[]{:S(2)}) collective-permute-start(bf16[4,256,512]{2,1,0:T(8,128)(2,1)S(1)} %get-tuple-element.302), channel_id=1, source_target_pairs={{0,16},{4,12},{8,24},{12,4},{16,0},{20,28},{24,8},{28,20},{1,17},{... | collective-permute-start | bytes 3145736 | tf_op jit(solution)/shard_map/ppermute | solution.py:64
  265.3 26.8 %collective-permute-start.51 = (bf16[256,256]{1,0:T(8,128)(2,1)S(1)}, bf16[256,256]{1,0:T(8,128)(2,1)S(1)}, u32[]{:S(2)}, u32[]{:S(2)}) collective-permute-start(bf16[256,256]{1,0:T(8,128)(2,1)S(1)} %dynamic-slice_bitcast_fusion.1), channel_id=1, source_target_pairs={{0,2},{1,3},{2,0},{3,1},{4,6},{5,7},{6,4},{7,5},{8,10},{9,11},{10,... | collective-permute-start | bytes 393224 | tf_op jit(solution)/shard_map/ppermute | solution.py:74
  283.9 16.0 %collective-permute-start.52 = (bf16[512,1536]{1,0:T(8,128)(2,1)}, bf16[512,1536]{1,0:T(8,128)(2,1)}, u32[]{:S(2)}, u32[]{:S(2)}) collective-permute-start(bf16[512,1536]{1,0:T(8,128)(2,1)} %get-tuple-element.426), channel_id=1, source_target_pairs={{0,4},{4,0},{8,12},{12,8},{16,20},{20,16},{24,28},{28,24},{1,5},{5... | collective-permute-start | bytes 4718600 | tf_op jit(solution)/shard_map/ppermute | solution.py:56
  292.0 16.4 %collective-permute-start.50 = (bf16[2,256,512]{2,1,0:T(8,128)(2,1)}, bf16[2,256,512]{2,1,0:T(8,128)(2,1)}, u32[]{:S(2)}, u32[]{:S(2)}) collective-permute-start(bf16[2,256,512]{2,1,0:T(8,128)(2,1)} %get-tuple-element.307), channel_id=1, source_target_pairs={{0,1},{1,0},{2,3},{3,2},{4,5},{5,4},{6,7},{7,6},{8,9},{9,8},{10,11... | collective-permute-start | bytes 1572872 | tf_op jit(solution)/shard_map/ppermute | solution.py:74
  299.1 54.6 %collective-permute-start.59 = (bf16[512,512]{1,0:T(8,128)(2,1)}, bf16[512,512]{1,0:T(8,128)(2,1)}, u32[]{:S(2)}, u32[]{:S(2)}) collective-permute-start(bf16[512,512]{1,0:T(8,128)(2,1)} %get-tuple-element.427), channel_id=1, source_target_pairs={{0,4},{4,0},{8,12},{12,8},{16,20},{20,16},{24,28},{28,24},{1,5},{5... | collective-permute-start | bytes 1572872 | tf_op jit(solution)/shard_map/ppermute | solution.py:56
  310.9 32.7 %collective-permute-start.54 = (bf16[1,256,512]{2,1,0:T(8,128)(2,1)}, bf16[1,256,512]{2,1,0:T(8,128)(2,1)}, u32[]{:S(2)}, u32[]{:S(2)}) collective-permute-start(bf16[1,256,512]{2,1,0:T(8,128)(2,1)} %get-tuple-element.315), channel_id=1, source_target_pairs={{0,2},{1,3},{2,0},{3,1},{4,6},{5,7},{6,4},{7,5},{8,10},{9,11},{10,... | collective-permute-start | bytes 786440 | tf_op jit(solution)/shard_map/ppermute | solution.py:74
  318.6 31.7 %collective-permute-start.53 = (bf16[4,64,2560]{2,1,0:T(8,128)(2,1)}, bf16[4,64,2560]{2,1,0:T(8,128)(2,1)}, u32[]{:S(2)}, u32[]{:S(2)}) collective-permute-start(bf16[4,64,2560]{2,1,0:T(8,128)(2,1)} %get-tuple-element.318), channel_id=1, source_target_pairs={{0,16},{4,12},{8,24},{12,4},{16,0},{20,28},{24,8},{28,20},{1,17},{... | collective-permute-start | bytes 3932168 | tf_op jit(solution)/shard_map/ppermute | solution.py:64
  319.1 39.7 %collective-permute-start.57 = (bf16[4,2,64,1536]{3,2,1,0:T(8,128)(2,1)}, bf16[4,2,64,1536]{3,2,1,0:T(8,128)(2,1)}, u32[]{:S(2)}, u32[]{:S(2)}) collective-permute-start(bf16[4,2,64,1536]{3,2,1,0:T(8,128)(2,1)} %pick_first.6), channel_id=1, source_target_pairs={{0,8},{4,20},{8,0},{12,28},{16,24},{20,4},{24,16},{28,12},{1,9},{5... | collective-permute-start | bytes 4718600 | tf_op jit(solution)/shard_map/ppermute | solution.py:60
  343.5 12.9 %collective-permute-start.58 = (bf16[2,2,80,512]{3,2,1,0:T(8,128)(2,1)S(1)}, bf16[2,2,80,512]{3,2,1,0:T(8,128)(2,1)S(1)}, u32[]{:S(2)}, u32[]{:S(2)}) collective-permute-start(bf16[2,2,80,512]{3,2,1,0:T(8,128)(2,1)S(1)} %fusion.5), channel_id=1, source_target_pairs={{0,4},{4,0},{8,12},{12,8},{16,20},{20,16},{24,28},{28,24},{1,5},{5... | collective-permute-start | bytes 983048 | tf_op jit(solution)/shard_map/ppermute | solution.py:56
  344.6 18.0 %collective-permute-start.56 = (bf16[256,512]{1,0:T(8,128)(2,1)S(1)}, bf16[256,512]{1,0:T(8,128)(2,1)S(1)}, u32[]{:S(2)}, u32[]{:S(2)}) collective-permute-start(bf16[256,512]{1,0:T(8,128)(2,1)S(1)} %bitcast.204), channel_id=1, source_target_pairs={{0,4},{4,0},{8,12},{12,8},{16,20},{20,16},{24,28},{28,24},{1,5},{5... | collective-permute-start | bytes 786440 | tf_op jit(solution)/shard_map/ppermute | solution.py:56
  353.6 15.1 %collective-permute-start.55 = (bf16[2,64,2560]{2,1,0:T(8,128)(2,1)S(1)}, bf16[2,64,2560]{2,1,0:T(8,128)(2,1)S(1)}, u32[]{:S(2)}, u32[]{:S(2)}) collective-permute-start(bf16[2,64,2560]{2,1,0:T(8,128)(2,1)S(1)} %get-tuple-element.325), channel_id=1, source_target_pairs={{0,1},{1,0},{2,3},{3,2},{4,5},{5,4},{6,7},{7,6},{8,9},{9,8},{10,11... | collective-permute-start | bytes 1966088 | tf_op jit(solution)/shard_map/ppermute | solution.py:74
  357.1 21.0 %collective-permute-start.63 = (bf16[1,2,336,512]{3,2,1,0:T(8,128)(2,1)S(1)}, bf16[1,2,336,512]{3,2,1,0:T(8,128)(2,1)S(1)}, u32[]{:S(2)}, u32[]{:S(2)}) collective-permute-start(bf16[1,2,336,512]{3,2,1,0:T(8,128)(2,1)S(1)} %pick_first.7), channel_id=1, source_target_pairs={{0,8},{4,20},{8,0},{12,28},{16,24},{20,4},{24,16},{28,12},{1,9},{5... | collective-permute-start | bytes 2064392 | tf_op jit(solution)/shard_map/ppermute | solution.py:60
  362.0 17.6 %collective-permute-start.62 = (bf16[4,64,1536]{2,1,0:T(8,128)(2,1)S(1)}, bf16[4,64,1536]{2,1,0:T(8,128)(2,1)S(1)}, u32[]{:S(2)}, u32[]{:S(2)}) collective-permute-start(bf16[4,64,1536]{2,1,0:T(8,128)(2,1)S(1)} %get-tuple-element.332), channel_id=1, source_target_pairs={{0,16},{4,12},{8,24},{12,4},{16,0},{20,28},{24,8},{28,20},{1,17},{... | collective-permute-start | bytes 2359304 | tf_op jit(solution)/shard_map/ppermute | solution.py:64
  362.7 22.3 %collective-permute-start.60 = (bf16[2,256,512]{2,1,0:T(8,128)(2,1)S(1)}, bf16[2,256,512]{2,1,0:T(8,128)(2,1)S(1)}, u32[]{:S(2)}, u32[]{:S(2)}) collective-permute-start(bf16[2,256,512]{2,1,0:T(8,128)(2,1)S(1)} %pad_maximum_fusion.13), channel_id=1, source_target_pairs={{0,8},{4,20},{8,0},{12,28},{16,24},{20,4},{24,16},{28,12},{1,9},{5... | collective-permute-start | bytes 1572872 | tf_op jit(solution)/shard_map/ppermute | solution.py:60
  369.5 15.2 %collective-permute-start.61 = (bf16[1,64,2560]{2,1,0:T(8,128)(2,1)S(1)}, bf16[1,64,2560]{2,1,0:T(8,128)(2,1)S(1)}, u32[]{:S(2)}, u32[]{:S(2)}) collective-permute-start(bf16[1,64,2560]{2,1,0:T(8,128)(2,1)S(1)} %get-tuple-element.336), channel_id=1, source_target_pairs={{0,2},{1,3},{2,0},{3,1},{4,6},{5,7},{6,4},{7,5},{8,10},{9,11},{10,... | collective-permute-start | bytes 983048 | tf_op jit(solution)/shard_map/ppermute | solution.py:74
  378.8 7.3 %collective-permute-start.65 = (bf16[1,336,512]{2,1,0:T(8,128)(2,1)S(1)}, bf16[1,336,512]{2,1,0:T(8,128)(2,1)S(1)}, u32[]{:S(2)}, u32[]{:S(2)}) collective-permute-start(bf16[1,336,512]{2,1,0:T(8,128)(2,1)S(1)} %get-tuple-element.340), channel_id=1, source_target_pairs={{0,16},{4,12},{8,24},{12,4},{16,0},{20,28},{24,8},{28,20},{1,17},{... | collective-permute-start | bytes 1032200 | tf_op jit(solution)/shard_map/ppermute | solution.py:64
  380.6 12.4 %collective-permute-start.67 = (bf16[2,64,1536]{2,1,0:T(8,128)(2,1)S(1)}, bf16[2,64,1536]{2,1,0:T(8,128)(2,1)S(1)}, u32[]{:S(2)}, u32[]{:S(2)}) collective-permute-start(bf16[2,64,1536]{2,1,0:T(8,128)(2,1)S(1)} %get-tuple-element.343), channel_id=1, source_target_pairs={{0,1},{1,0},{2,3},{3,2},{4,5},{5,4},{6,7},{7,6},{8,9},{9,8},{10,11... | collective-permute-start | bytes 1179656 | tf_op jit(solution)/shard_map/ppermute | solution.py:74
  385.0 15.7 %collective-permute-start.64 = (bf16[256,512]{1,0:T(8,128)(2,1)S(1)}, bf16[256,512]{1,0:T(8,128)(2,1)S(1)}, u32[]{:S(2)}, u32[]{:S(2)}) collective-permute-start(bf16[256,512]{1,0:T(8,128)(2,1)S(1)} %slice_bitcast_fusion.4), channel_id=1, source_target_pairs={{0,16},{4,12},{8,24},{12,4},{16,0},{20,28},{24,8},{28,20},{1,17},{... | collective-permute-start | bytes 786440 | tf_op jit(solution)/shard_map/ppermute | solution.py:64
  386.4 11.2 %collective-permute-start.66 = (bf16[208,512]{1,0:T(8,128)(2,1)S(1)}, bf16[208,512]{1,0:T(8,128)(2,1)S(1)}, u32[]{:S(2)}, u32[]{:S(2)}) collective-permute-start(bf16[208,512]{1,0:T(8,128)(2,1)S(1)} %pad_maximum_fusion.19), channel_id=1, source_target_pairs={{0,1},{1,0},{2,3},{3,2},{4,5},{5,4},{6,7},{7,6},{8,9},{9,8},{10,11... | collective-permute-start | bytes 638984 | tf_op jit(solution)/shard_map/ppermute | solution.py:74
  388.1 30.6 %collective-permute-start.75 = (bf16[2,64,2560]{2,1,0:T(8,128)(2,1)S(1)}, bf16[2,64,2560]{2,1,0:T(8,128)(2,1)S(1)}, u32[]{:S(2)}, u32[]{:S(2)}) collective-permute-start(bf16[2,64,2560]{2,1,0:T(8,128)(2,1)S(1)} %pad_maximum_fusion.9), channel_id=1, source_target_pairs={{0,8},{4,20},{8,0},{12,28},{16,24},{20,4},{24,16},{28,12},{1,9},{5... | collective-permute-start | bytes 1966088 | tf_op jit(solution)/shard_map/ppermute | solution.py:60
  397.6 17.5 %collective-permute-start.71 = (bf16[1,64,1536]{2,1,0:T(8,128)(2,1)S(1)}, bf16[1,64,1536]{2,1,0:T(8,128)(2,1)S(1)}, u32[]{:S(2)}, u32[]{:S(2)}) collective-permute-start(bf16[1,64,1536]{2,1,0:T(8,128)(2,1)S(1)} %get-tuple-element.352), channel_id=1, source_target_pairs={{0,2},{1,3},{2,0},{3,1},{4,6},{5,7},{6,4},{7,5},{8,10},{9,11},{10,... | collective-permute-start | bytes 589832 | tf_op jit(solution)/shard_map/ppermute | solution.py:74
  398.3 16.7 %collective-permute-start.69 = (bf16[144,512]{1,0:T(8,128)(2,1)S(1)}, bf16[144,512]{1,0:T(8,128)(2,1)S(1)}, u32[]{:S(2)}, u32[]{:S(2)}) collective-permute-start(bf16[144,512]{1,0:T(8,128)(2,1)S(1)} %pad_maximum_fusion.22), channel_id=1, source_target_pairs={{0,2},{1,3},{2,0},{3,1},{4,6},{5,7},{6,4},{7,5},{8,10},{9,11},{10,... | collective-permute-start | bytes 442376 | tf_op jit(solution)/shard_map/ppermute | solution.py:74
  416.5 8.1 %collective-permute-start.72 = (bf16[2,144,512]{2,1,0:T(8,128)(2,1)S(1)}, bf16[2,144,512]{2,1,0:T(8,128)(2,1)S(1)}, u32[]{:S(2)}, u32[]{:S(2)}) collective-permute-start(bf16[2,144,512]{2,1,0:T(8,128)(2,1)S(1)} %pad_maximum_fusion.16), channel_id=1, source_target_pairs={{0,8},{4,20},{8,0},{12,28},{16,24},{20,4},{24,16},{28,12},{1,9},{5... | collective-permute-start | bytes 884744 | tf_op jit(solution)/shard_map/ppermute | solution.py:60
  417.3 13.7 %collective-permute-start.80 = (bf16[2,64,1536]{2,1,0:T(8,128)(2,1)S(1)}, bf16[2,64,1536]{2,1,0:T(8,128)(2,1)S(1)}, u32[]{:S(2)}, u32[]{:S(2)}) collective-permute-start(bf16[2,64,1536]{2,1,0:T(8,128)(2,1)S(1)} %pad_maximum_fusion.15), channel_id=1, source_target_pairs={{0,8},{4,20},{8,0},{12,28},{16,24},{20,4},{24,16},{28,12},{1,9},{5... | collective-permute-start | bytes 1179656 | tf_op jit(solution)/shard_map/ppermute | solution.py:60
  418.8 18.1 %collective-permute-start.83 = (bf16[2,64,2560]{2,1,0:T(8,128)(2,1)S(1)}, bf16[2,64,2560]{2,1,0:T(8,128)(2,1)S(1)}, u32[]{:S(2)}, u32[]{:S(2)}) collective-permute-start(bf16[2,64,2560]{2,1,0:T(8,128)(2,1)S(1)} %collective-permute-done.75.refs_2_), channel_id=1, source_target_pairs={{0,4},{4,0},{8,12},{12,8},{16,20},{20,16},{24,28},{28,24},{1,5},{5... | collective-permute-start | bytes 1966088 | tf_op jit(solution)/shard_map/ppermute | solution.py:56
  418.9 12.2 %collective-permute-start.79 = (bf16[64,2560]{1,0:T(8,128)(2,1)S(1)}, bf16[64,2560]{1,0:T(8,128)(2,1)S(1)}, u32[]{:S(2)}, u32[]{:S(2)}) collective-permute-start(bf16[64,2560]{1,0:T(8,128)(2,1)S(1)} %slice_bitcast_fusion.3), channel_id=1, source_target_pairs={{0,16},{4,12},{8,24},{12,4},{16,0},{20,28},{24,8},{28,20},{1,17},{... | collective-permute-start | bytes 983048 | tf_op jit(solution)/shard_map/ppermute | solution.py:64
  431.2 9.0 %collective-permute-start.77 = (bf16[2,144,512]{2,1,0:T(8,128)(2,1)S(1)}, bf16[2,144,512]{2,1,0:T(8,128)(2,1)S(1)}, u32[]{:S(2)}, u32[]{:S(2)}) collective-permute-start(bf16[2,144,512]{2,1,0:T(8,128)(2,1)S(1)} %collective-permute-done.72.refs_2_), channel_id=1, source_target_pairs={{0,4},{4,0},{8,12},{12,8},{16,20},{20,16},{24,28},{28,24},{1,5},{5... | collective-permute-start | bytes 884744 | tf_op jit(solution)/shard_map/ppermute | solution.py:56
  432.0 8.1 %collective-permute-start.82 = (bf16[64,1536]{1,0:T(8,128)(2,1)S(1)}, bf16[64,1536]{1,0:T(8,128)(2,1)S(1)}, u32[]{:S(2)}, u32[]{:S(2)}) collective-permute-start(bf16[64,1536]{1,0:T(8,128)(2,1)S(1)} %slice_bitcast_fusion.5), channel_id=1, source_target_pairs={{0,16},{4,12},{8,24},{12,4},{16,0},{20,28},{24,8},{28,20},{1,17},{... | collective-permute-start | bytes 589832 | tf_op jit(solution)/shard_map/ppermute | solution.py:64
  436.4 10.2 %collective-permute-start.85 = (bf16[2,64,1536]{2,1,0:T(8,128)(2,1)S(1)}, bf16[2,64,1536]{2,1,0:T(8,128)(2,1)S(1)}, u32[]{:S(2)}, u32[]{:S(2)}) collective-permute-start(bf16[2,64,1536]{2,1,0:T(8,128)(2,1)S(1)} %collective-permute-done.80.refs_2_), channel_id=1, source_target_pairs={{0,4},{4,0},{8,12},{12,8},{16,20},{20,16},{24,28},{28,24},{1,5},{5... | collective-permute-start | bytes 1179656 | tf_op jit(solution)/shard_map/ppermute | solution.py:56
  (152 other events, 1251.9 us)

commit v4 on v3

--- a/solution.py
+++ b/solution.py
@@ -27,7 +27,7 @@
 
 
 def takes(microseconds):
-    flops = int(microseconds * 0.6 * 1e9)
+    flops = int(microseconds * 1.3 * 1e9)
     return pl.CostEstimate(flops=flops, transcendentals=0, bytes_accessed=1)
 
 
@@ -75,7 +75,11 @@
 
 
 def take(a, at, axis):
-    return lax.dynamic_index_in_dim(a, at, axis, keepdims=False)
+    return lax.dynamic_index_in_dim(a, at, axis, keepdims=False, allow_negative_indices=False)
+
+
+def rows_from(a, start, count, axis):
+    return lax.dynamic_slice_in_dim(a, start, count, axis, allow_negative_indices=False)
 
 
 class Order:
@@ -89,6 +93,37 @@
 
     def mark(self, array):
         self.pending.append(array)
+
+
+class Where:
+    def __init__(self, order):
+        z, p = lax.axis_index("narrow"), lax.axis_index("wide") % SUB
+        core, x, y = p & 1, (p >> 1) & 1, p >> 2
+        first, second = jnp.where(core == 0, x, y), jnp.where(core == 0, y, x)
+        low, high = z & 1, z >> 1
+        zero = jnp.zeros_like(z)
+        plain = {
+            "core": core,
+            "other_core": 1 - core,
+            "low": low,
+            "other_low": 1 - low,
+            "high": high,
+            "other_high": 1 - high,
+            "piece_row": p * (D // 4 // SUB),
+            "long_piece_row": p * (D // SUB),
+            "half_column": core * (D // 2),
+            "other_half_column": (1 - core) * (D // 2),
+            "wide_half_column": core * (3 * D // 2),
+            "other_wide_half_column": (1 - core) * (3 * D // 2),
+            "spot": jnp.stack([z, p]),
+            "core_alone": core[None],
+            "unsent": (1 - first)[None],
+            "second_step": jnp.stack([first, second]),
+            "third_step": jnp.stack([zero, low]),
+            "fourth_step": jnp.stack([zero, high]),
+        }
+        for name, value in zip(plain, order.hold(*plain.values())):
+            setattr(self, name, value)
 
 
 class Narrow:
@@ -103,9 +138,9 @@
         self.order.mark(both)
         self.others = swap_narrow(both, 1)
 
-    def bundle(self):
+    def bundle(self, *more):
         others = self.order.hold(self.others)
-        bundle = jnp.concatenate([self.two[None], others])
+        bundle = jnp.concatenate([self.two[None], others, *more])
         self.order.mark(bundle)
         return bundle
 
@@ -204,14 +239,14 @@
     )(spot, *shards, *parts)
 
 
-def pieces_of(shards, p):
-    return jnp.concatenate(
-        [
-            lax.dynamic_slice_in_dim(s, p * (s.shape[0] // SUB), s.shape[0] // SUB, 0)
-            for s in shards
-        ],
-        axis=1,
-    )
+def pieces_of(shards, start):
+    rows = shards[0].shape[0] // SUB
+    return jnp.concatenate([rows_from(shard, start, rows, 0) for shard in shards], axis=1)
+
+
+def beside(a):
+    rows = a.shape[0] // 4
+    return jnp.concatenate([a[i * rows : (i + 1) * rows] for i in range(4)], axis=1)
 
 
 def add_two(a, b):
@@ -222,7 +257,7 @@
     sent[...] = grad[...].reshape(sent.shape)
 
 
-def pick_first(grad, bit):
+def pick_first(grad, bits):
     n, _, _, rows, width = grad.shape
     return pl.pallas_call(
         pick_kernel,
@@ -236,7 +271,7 @@
         compiler_params=pltpu.CompilerParams(vmem_limit_bytes=5 * MB),
         cost_estimate=takes(2.5),
         name="pick_first",
-    )(bit[None], grad)
+    )(bits, grad)
 
 
 def add_split_kernel(bits, kept_sent, got_sent, kept_kept, got_kept, sent, kept):
@@ -247,7 +282,7 @@
     kept[...] = total(kept_kept, got_kept)
 
 
-def add_split(grad, got, first, bit):
+def add_split(grad, got, bits):
     n, _, _, rows, width = grad.shape
     block = (1, 1, 1, rows, width)
     got_block = (1, 1, rows, width)
@@ -269,15 +304,13 @@
         compiler_params=pltpu.CompilerParams(vmem_limit_bytes=8 * MB),
         cost_estimate=takes(2.5),
         name="add_split",
-    )(jnp.stack([first, bit]), grad, got, grad, got)
+    )(bits, grad, got, grad, got)
 
 
 class Reduce:
-    def __init__(self, grad, p, z, order):
-        core, x, y = p & 1, (p >> 1) & 1, p >> 2
-        self.bits = [jnp.where(core == 0, x, y), jnp.where(core == 0, y, x), z & 1, z >> 1]
-        self.order, self.stage, self.kept = order, 0, grad
-        sent = pick_first(grad, 1 - self.bits[0])
+    def __init__(self, grad, where, order):
+        self.where, self.order, self.stage, self.kept = where, order, 0, grad
+        sent = pick_first(grad, where.unsent)
         order.mark(sent)
         self.got = over_first(sent)
 
@@ -288,14 +321,13 @@
             self.total = across_groups(add_two(kept[0], got[0]))
             self.order.mark(self.total)
             return
-        bit, first = self.bits[self.stage], jnp.zeros_like(self.bits[0])
-        if self.stage == 1:
-            first = self.bits[0]
-        else:
+        if self.stage > 1:
             rows, width = kept.shape[1:]
             kept = kept.reshape(-1, 1, 2, rows, width)
             got = got.reshape(-1, 2, rows, width)
-        sent, self.kept = add_split(kept, got, first, bit)
+        where = self.where
+        bits = (where.second_step, where.third_step, where.fourth_step)[self.stage - 1]
+        sent, self.kept = add_split(kept, got, bits)
         self.order.mark(sent)
         self.got = over_second(sent) if self.stage == 1 else swap_narrow(sent, self.stage - 1)
 
@@ -317,9 +349,11 @@
         def pick(bit):
             return jnp.concatenate([take(blocks, bit, axis).reshape(-1, total.shape[-1]), shared])
 
-        sent = pick(1 - self.bits[self.stage])
+        where = self.where
+        own, other = (where.low, where.other_low) if self.stage == 2 else (where.high, where.other_high)
+        sent = pick(other)
         self.order.mark(sent)
-        self.kept = pick(self.bits[self.stage])
+        self.kept = pick(own)
         self.got = swap_narrow(sent, self.stage - 1)
 
 
@@ -375,8 +409,9 @@
     parts, table, table_t = refs[:6], refs[6], refs[7]
     for place, part in origins(spot[1], parts):
         at = pl.ds(pl.multiple_of(place * 128, 128), 128)
-        table[:, at] = part[...]
-        table_t[at, :] = part[...].astype(f32).T.astype(bf16)
+        rows = jnp.concatenate([part[3, :, i * COLS : (i + 1) * COLS] for i in range(4)], axis=0)
+        table_t[at, :] = rows
+        table[:, at] = rows.astype(f32).T.astype(bf16)
 
 
 def arrange(parts, spot):
@@ -451,15 +486,20 @@
 
 
 def variable_back_kernel(
-    pixels_ref, same_ref, keys_ref, keys_col_ref, table_ref, grad_ref, x_ref, zed_ref, pixel_ref
+    pixels_ref, same_ref, keys_ref, keys_col_ref, table_ref, grad_ref, x_ref, zed_ref, pixel_ref, zed_columns
 ):
     step = pl.program_id(0)
+
+    @pl.when(step == 0)
+    def _():
+        zed_columns[...] = jnp.zeros_like(zed_columns)
+
     pixels = pixels_ref[...]
     pixels_wide = pixels.astype(f32)
     same = same_ref[...]
     same_low = same.astype(bf16)
     grad_t = grad_ref[...].astype(f32).T.astype(bf16)
-    sums = []
+    line = lax.broadcasted_iota(jnp.int32, zed_columns.shape, 1)
     pixel_grad = None
     for i in range(2):
         probs = pair_probs(pixels, same, keys_ref[0, i : i + 1, :])
@@ -472,10 +512,10 @@
         centre = jnp.sum(lifted[PATCH_COLS : PATCH_COLS + VARS], axis=0, keepdims=True)
         score_grad = lifted - probs * centre
         x_ref[:, i * COLS : (i + 1) * COLS] = dot_nt(grad_i, weighted).astype(bf16)
-        sums.append(jnp.sum(score_grad * pixels_wide, axis=1, keepdims=True))
+        sums = jnp.sum(score_grad * pixels_wide, axis=1, keepdims=True)
+        zed_columns[...] += jnp.where(line == 2 * step + i, sums, 0.0)
         term = probs * spread + score_grad * keys_col_ref[0, :, i : i + 1]
         pixel_grad = term if pixel_grad is None else pixel_grad + term
-    zed_ref[0] = jnp.concatenate(sums, axis=1)
 
     @pl.when(step == 0)
     def _():
@@ -484,6 +524,10 @@
     @pl.when(step > 0)
     def _():
         pixel_ref[...] += pixel_grad
+
+    @pl.when(step == PAIRS - 1)
+    def _():
+        zed_ref[...] = zed_columns[...].T[:HEADS]
 
 
 def variable_back(pixels, same, keys_rows, keys_cols, table, grad):
@@ -492,7 +536,7 @@
         variable_back_kernel,
         out_shape=[
             jax.ShapeDtypeStruct((D // 2, 2 * COLS), bf16),
-            jax.ShapeDtypeStruct((PAIRS, COLS, 2), f32),
+            jax.ShapeDtypeStruct((HEADS, COLS), f32),
             jax.ShapeDtypeStruct((COLS, rows), f32),
         ],
         grid=(PAIRS,),
@@ -506,11 +550,12 @@
         ],
         out_specs=[
             pl.BlockSpec((HEAD_DIM, 2 * COLS), lambda h: (h, 0)),
-            pl.BlockSpec((1, COLS, 2), lambda h: (h, 0, 0)),
+            pl.BlockSpec((HEADS, COLS), lambda h: (0, 0)),
             pl.BlockSpec((COLS, rows), lambda h: (0, 0)),
         ],
+        scratch_shapes=[pltpu.VMEM((COLS, 128), f32)],
         compiler_params=pltpu.CompilerParams(vmem_limit_bytes=10 * MB),
-        cost_estimate=takes(14.5),
+        cost_estimate=takes(1),
         name="variable_back",
     )(pixels, same, keys_rows, keys_cols, table, grad)
 
@@ -701,7 +746,7 @@
                 pl.BlockSpec((1, 1, block), lambda i, c: (at(i, c), 0, 0)),
             ],
         ),
-        compiler_params=pltpu.CompilerParams(vmem_limit_bytes=50 * MB),
+        compiler_params=pltpu.CompilerParams(vmem_limit_bytes=24 * MB),
         cost_estimate=takes(15.5),
         name="mlp_back",
     )(core, cot, w_out, w_in, slope)
@@ -784,11 +829,6 @@
     return values * below, below + values * density
 
 
-def columns_half(a, core):
-    span = a.shape[1] // 2
-    return lax.dynamic_slice_in_dim(a, core * span, span, 1)
-
-
 def per_device(
     patches,
     var_ids,
@@ -815,13 +855,19 @@
     cotangent,
 ):
     rows = patches.shape[0]
-    z, p = lax.axis_index("narrow"), lax.axis_index("wide") % SUB
-    core = p & 1
-    spot = jnp.stack([z, p]).astype(jnp.int32)
     shard = D // 4
     order = Order()
-    half = lambda a: columns_half(a, core)
-    other_half = lambda a: columns_half(a, 1 - core)
+    where = Where(order)
+    spot = where.spot
+
+    def half(a):
+        span = a.shape[1] // 2
+        return rows_from(a, where.half_column if span == D // 2 else where.wide_half_column, span, 1)
+
+    def other_half(a):
+        span = a.shape[1] // 2
+        start = where.other_half_column if span == D // 2 else where.other_wide_half_column
+        return rows_from(a, start, span, 1)
 
     singles = (
         agg_query,
@@ -839,10 +885,11 @@
         vectors = jnp.where(at_row == i, single[None, :], vectors)
     vectors = jnp.concatenate([vectors, mlp_in_bias.reshape(4, shard)])
     narrow_v = Narrow(vectors, order)
-    narrow_a = Narrow(pieces_of([agg_out_weight], p), order)
-    narrow_b = Narrow(pieces_of([qkv_weight, attn_out_weight], p), order)
+    narrow_a = Narrow(pieces_of([agg_out_weight], where.piece_row), order)
+    narrow_b = Narrow(pieces_of([qkv_weight, attn_out_weight], where.piece_row), order)
     narrow_v.second_step()
     narrow_a.second_step()
+    narrow_b.second_step()
 
     line = jnp.arange(COLS, dtype=jnp.int32)
     variable = jnp.where(line < PATCH_COLS, line // PIX, (line - PATCH_COLS) % VARS)
@@ -856,8 +903,11 @@
     embed_rows = jnp.concatenate(
         [embed_weight, var_embed, jnp.zeros((COLS - PATCH_COLS - VARS, shard), bf16)]
     )
-    value_part = lax.dynamic_slice_in_dim(value_weight, p * 128, 128, 1)
-    table_part = dot(embed_rows, value_part).astype(bf16)
+    value_part = rows_from(value_weight, where.long_piece_row, 128, 1)
+    table_part = lax.dot_general(
+        value_part, embed_rows, (((0,), (1,)), ((), ())), preferred_element_type=f32
+    )
+    table_part = beside(table_part.astype(bf16))
 
     around = order_narrow(vectors, narrow_v.bundle(), spot)
     whole = [around[:, i].reshape(D) for i in range(8)]
@@ -871,10 +921,18 @@
     query_rows = (heads_eye * query_full[None, :]).astype(bf16)
     key_query_t = dot_nt(query_rows, key_weight).astype(bf16)
     keys_part = dot_nt(key_query_t, embed_rows) * scale_by
-    keys_packed = jnp.concatenate(split_two(keys_part)).reshape(-1, 128)
-    packed = jnp.concatenate([table_part, keys_packed])
+    packed = jnp.concatenate([table_part, beside(jnp.concatenate(split_two(keys_part)))])
     order.mark(packed)
     got_packed = [turn_narrow(packed, turn) for turn in (1, 2, 3)]
+
+    same, chooser = order.hold(same, chooser)
+    agg_out_b, gain_one, bias_one, attn_out_b, gain_two, bias_two, mlp_out_b, mlp_in_b = order.hold(
+        agg_out_b, gain_one, bias_one, attn_out_b, gain_two, bias_two, mlp_out_b, mlp_in_b
+    )
+    piece_c = pieces_of([mlp_in_weight], where.piece_row)
+    piece_d = pieces_of([mlp_out_weight], where.long_piece_row)
+    order.mark(piece_c)
+    order.mark(piece_d)
 
     full_patches = jnp.concatenate(
         [
@@ -887,47 +945,45 @@
     pixels = lax.dot_general(
         chooser, full_patches, (((0,), (1,)), ((), ())), preferred_element_type=f32
     ).astype(bf16)
-    seg_row, seg_col, pad_col = segment_ids, segment_ids.T, pad_mask.T
-    cot_half, cot_got = half(cotangent), over_core(other_half(cotangent))
-
-    spread_a = Spread(narrow_a.bundle(), order)
-    narrow_b.second_step()
-    spread_a.near_step()
+    seg_row, seg_col, pad_col = order.hold(segment_ids, segment_ids.T, pad_mask.T)
+    pixels = order.hold(pixels)
+    cot_half, cot_other = order.hold(half(cotangent), other_half(cotangent))
+    cot_got = over_core(cot_other)
+
     got_packed = order.hold(*got_packed)
     total = packed.astype(f32)
     for part in got_packed:
         total = total + part.astype(f32)
-    table_own = total[:COLS].astype(bf16)
+    table_own = total[:32].astype(bf16)
     order.mark(table_own)
-    keys_two = total[COLS:].reshape(2, HEADS, COLS)
-    keys_rows = (keys_two[0] + keys_two[1]).reshape(PAIRS, 2, COLS)
+    keys_two = jnp.concatenate([total[32:, i * COLS : (i + 1) * COLS] for i in range(4)])
+    keys_rows = (keys_two[:HEADS] + keys_two[HEADS:]).reshape(PAIRS, 2, COLS)
     keys_cols = keys_rows.transpose(0, 2, 1)
-    spread_t = Spread(table_own, order)
-    spread_t.near_step()
+    spread_a = Spread(narrow_a.bundle(table_own[None]), order)
+    spread_b = Spread(narrow_b.bundle(), order)
+    narrow_c = Narrow(order.hold(piece_c), order)
+    spread_a.near_step()
     spread_a.corner_step()
-    spread_t.corner_step()
-    spread_b = Spread(narrow_b.bundle(), order)
-    narrow_c = Narrow(order.hold(pieces_of([mlp_in_weight], p)), order)
     spread_b.near_step()
-    spread_t.last_step()
     spread_a.last_step()
-    table, table_t = arrange(spread_t.parts(), spot)
-    merged = variable_forward(pixels, same, keys_rows, table_t)
+    parts_a = spread_a.parts()
+    table, table_t = arrange(parts_a, spot)
+    narrow_c.second_step()
+    spread_b.corner_step()
+    merged = variable_forward(pixels, same, keys_rows, order.hold(table_t))
     order.mark(merged)
-    (agg_out_w,) = assemble([agg_out_weight], spread_a.parts(), spot)
     merged_there = over_core(merged)
+    (agg_out_w,) = assemble([agg_out_weight], parts_a, spot)
     patch_state = dot(merged, agg_out_w) + agg_out_b
     unit_one, inverse_one = normalise(patch_state)
     normed = (unit_one * gain_one + bias_one).astype(bf16)
     order.mark(normed)
-    narrow_c.second_step()
-    spread_b.corner_step()
     merged_there = order.hold(merged_there)
+    spread_c = Spread(narrow_c.bundle(), order)
+    narrow_d = Narrow(order.hold(piece_d), order)
     spread_b.last_step()
+    spread_c.near_step()
     normed_there = over_core(normed)
-    spread_c = Spread(narrow_c.bundle(), order)
-    narrow_d = Narrow(order.hold(pieces_of([mlp_out_weight], p)), order)
-    spread_c.near_step()
     qkv_w, attn_out_w = assemble([qkv_weight, attn_out_weight], spread_b.parts(), spot)
     project = dot(order.hold(normed), qkv_w).astype(bf16)
     order.mark(project)
@@ -936,14 +992,14 @@
     attended, logs = attention(order.hold(project), seg_row, seg_col, pad_col)
     order.mark(attended)
     spread_c.corner_step()
+    spread_d = Spread(narrow_d.bundle(), order)
     attended_there = over_core(attended)
-    spread_d = Spread(narrow_d.bundle(), order)
     residual = patch_state + dot(order.hold(attended), attn_out_w) + attn_out_b
     unit_two, inverse_two = normalise(residual)
     normed_two = (unit_two * gain_two + bias_two).astype(bf16)
     order.mark(normed_two)
+    spread_d.near_step()
     spread_c.last_step()
-    spread_d.near_step()
     normed_two_there = over_core(normed_two)
     (mlp_in_w,) = assemble([mlp_in_weight], spread_c.parts(), spot)
     attended_there, normed_two_there = order.hold(attended_there, normed_two_there)
@@ -951,29 +1007,29 @@
     order.mark(hidden)
     hidden_there = over_core(hidden)
     spread_d.corner_step()
+
+    def grad_of(own, there, own_half, got):
+        return (dot_tn(own, own_half) + dot_tn(there, got)).astype(bf16)
+
+    def blocks(a):
+        return a.reshape(4, 2, 2, a.shape[0] // 16, a.shape[1])
+
+    cot_float = cotangent.astype(f32)
     spread_d.last_step()
     (mlp_out_w,) = assemble([mlp_out_weight], spread_d.parts(), spot)
-
-    def grad_of(own, there, own_half, got):
-        return (dot_tn(own, own_half) + dot_tn(there, got)).astype(bf16)
-
-    def blocks(a):
-        return a.reshape(4, 2, 2, a.shape[0] // 16, a.shape[1])
-
-    cot_float = cotangent.astype(f32)
     pre_half, pre_other, normed_two_grad, pre_sums = mlp_back(
-        core[None], order.hold(cotangent), mlp_out_w, mlp_in_w, slope
+        where.core_alone, order.hold(cotangent), mlp_out_w, mlp_in_w, slope
     )
     order.mark(pre_other)
-    pre_got = over_core(pre_other)
     grad_d = blocks(grad_of(*order.hold(hidden, hidden_there), cot_half, cot_got))
     order.mark(grad_d)
-    reduce_d = Reduce(grad_d, p, z, order)
+    reduce_d = Reduce(grad_d, where, order)
+    pre_got = over_core(pre_other)
     ke_part = lax.dot_general(
         key_weight, embed_rows, (((0,), (1,)), ((), ())), preferred_element_type=f32
     ).astype(bf16)
     ke_part = order.hold(ke_part).reshape(2, 2, shard, COLS)
-    ke_kept, ke_got = take(ke_part, z & 1, 1), swap_narrow(take(ke_part, 1 - (z & 1), 1), 1)
+    ke_kept, ke_got = take(ke_part, where.low, 1), swap_narrow(take(ke_part, where.other_low, 1), 1)
     residual_grad = cot_float + normalise_back(
         order.hold(normed_two_grad), gain_two, unit_two, inverse_two
     )
@@ -987,42 +1043,44 @@
         axis=1,
     )
     order.mark(grad_c)
-    reduce_c = Reduce(blocks(grad_c), p, z, order)
+    reduce_c = Reduce(blocks(grad_c), where, order)
     attended_grad = dot_nt(order.hold(branch_grad), attn_out_w).astype(bf16)
     order.mark(attended_grad)
     reduce_d.step()
     ke_two = add_two(ke_kept, order.hold(ke_got))
     order.mark(ke_two)
-    ke_got = swap_narrow(take(ke_two, 1 - (z >> 1), 0), 2)
+    ke_got = swap_narrow(take(ke_two, where.other_high, 0), 2)
     attended_grad = order.hold(attended_grad)
     project_grad = attention_back(project, attended_grad, logs, seg_row, seg_col, pad_col)
-    project_other = other_half(project_grad)
+    order.mark(project_grad)
+    reduce_d.step()
+    project_other = other_half(order.hold(project_grad))
     order.mark(project_other)
     project_got = over_core(project_other)
-    reduce_d.step()
-    ke_own = add_two(take(ke_two, z >> 1, 0), order.hold(ke_got))
+    reduce_c.step()
+    ke_own = add_two(take(ke_two, where.high, 0), order.hold(ke_got))
     order.mark(ke_own)
+    grad_b = grad_of(normed, normed_there, *order.hold(half(project_grad), project_got))
+    order.mark(grad_b)
+    reduce_b = Reduce(blocks(grad_b), where, order)
     normed_grad = dot_nt(order.hold(project_grad), qkv_w)
     state_grad = residual_grad + normalise_back(normed_grad, gain_one, unit_one, inverse_one)
     state_grad = state_grad.astype(bf16)
     order.mark(state_grad)
-    grad_b = grad_of(normed, normed_there, *order.hold(half(project_grad), project_got))
-    order.mark(grad_b)
-    reduce_b = Reduce(blocks(grad_b), p, z, order)
     state_got = over_core(other_half(state_grad))
+    reduce_d.step()
     merged_grad = dot_nt(order.hold(state_grad), agg_out_w).astype(bf16)
     order.mark(merged_grad)
-    reduce_d.step()
-    reduce_c.step()
     merged_grad = order.hold(merged_grad)
     cross, zed, pixel_grad = variable_back(pixels, same, keys_rows, keys_cols, table, merged_grad)
     order.mark(cross)
+    reduce_c.step()
     reduce_d.step()
     spread_d = Spread(reduce_d.total, order)
-    reduce_c.step()
+    reduce_b.step()
     grad_a = grad_of(merged, merged_there, *order.hold(half(state_grad), state_got))
     order.mark(grad_a)
-    zed_parts = split_two(zed.transpose(0, 2, 1).reshape(HEADS, COLS))
+    zed_parts = split_two(zed)
     column_sums = [
         jnp.sum(state_grad.astype(f32), axis=0),
         jnp.sum(normed_grad * unit_one, axis=0),
@@ -1041,18 +1099,15 @@
     )
     shared = shared.reshape(2, 2, 2, 80, 2 * COLS)
     order.mark(shared)
-    shared_got = over_core(take(shared, 1 - core, 0))
+    shared_got = over_core(take(shared, where.other_core, 0))
     grad_a = grad_a.reshape(4, 2, 2, shard // 4, D // 2).transpose(1, 2, 0, 3, 4)
     grad_a = grad_a.reshape(2, 2, shard, D // 2)
-    shared = add_two(take(shared, core, 0), order.hold(shared_got))
+    shared = add_two(take(shared, where.core, 0), order.hold(shared_got))
     grad_a = jnp.concatenate([grad_a, shared], axis=2)
     order.mark(grad_a)
-    reduce_a = ReduceShared(grad_a[None], p, z, order)
-    reduce_b.step()
+    reduce_a = ReduceShared(grad_a[None], where, order)
     spread_d.near_step()
     reduce_c.step()
-    result = (residual + dot(order.hold(hidden), mlp_out_w) + mlp_out_b).astype(bf16)
-    order.mark(result)
     reduce_a.step()
     reduce_b.step()
     reduce_c.step()
@@ -1060,9 +1115,11 @@
     spread_d.corner_step()
     reduce_a.step()
     spread_c.near_step()
+    reduce_a.step()
     reduce_b.step()
-    reduce_a.step()
     spread_d.last_step()
+    result = (residual + dot(order.hold(hidden), mlp_out_w) + mlp_out_b).astype(bf16)
+    order.mark(result)
     patches_grad = lax.dot_general(
         order.hold(pixel_grad),
         chooser.astype(f32),

time: 455 us -> 430 us (0.945)
  Pallas kernels: 136 us -> 123 us
  matrix products: 60.9 us -> 48.5 us
  waiting for transfers between devices: 99.1 us -> 111 us
  other arithmetic: 34.2 us -> 27.7 us
  local copies, waits for them, and re-layouts: 54.2 us -> 48.8 us
    ppermute x13 -> x12, waiting for transfers between devices: 12.6 us -> 28.9 us  [over_first(): return lax.ppermute(a, 'wide', wide_pairs(lambda i: 4 if i & 1 else 2))]
    ppermute x13 -> x12, waiting for transfers between devices: 43.3 us -> 35.4 us  [over_second(): return lax.ppermute(a, 'wide', wide_pairs(lambda i: 2 if i & 1 else 4))]
    dot_general x10, matrix products: 31.8 us -> 24 us  [dot_tn(): lax.dot_general(a, b, (((0,), (0,)), ((), ())), preferred_element_type=f32)]
    ppermute x13 -> x12, starting transfers between devices: 7.79 us -> 14.2 us  [over_second(): return lax.ppermute(a, 'wide', wide_pairs(lambda i: 2 if i & 1 else 4))]
    dynamic_slice x10 -> x11, local copies, waits for them, and re-layouts: 9.63 us -> 14.7 us  [the longest x10 14.6 us: rows_from(): lax.dynamic_slice_in_dim(a, start, count, axis, allow_negative_indices=Fa...]
    dot_general x5 -> x4, matrix products: 16.8 us -> 12 us  [dot(): return jnp.dot(a, b, preferred_element_type=f32)]
    unnamed x268 -> x255, local copies, waits for them, and re-layouts: 27.8 us -> 23.1 us
    ppermute x13 -> x12, starting transfers between devices: 17.6 us -> 14.2 us  [over_first(): return lax.ppermute(a, 'wide', wide_pairs(lambda i: 4 if i & 1 else 2))]
  transfers between devices with their start and end apart: 87 -> 82, of which waited for: 29 -> 31; matrix products, arithmetic and copies ran while one was open for 27% -> 24% of each run, Pallas kernels for 30% -> 28%
where the time goes in v4:
time: 430 us; the launch traced here: 425 us
  Pallas kernels  123 us (29%)
  waiting for transfers between devices  111 us (26%)
  starting transfers between devices  63.5 us (15%)
  local copies, waits for them, and re-layouts  48.8 us (11%)
  matrix products  48.5 us (11%)
  other arithmetic  27.7 us (6%)
    ppermute x20, waiting for transfers between devices, swap_narrow(): return lax.ppermute(a, 'narrow', [(i, i ^ bits) for i in range(size)])  40.9 us
    ppermute x12, waiting for transfers between devices, over_second(): return lax.ppermute(a, 'wide', wide_pairs(lambda i: 2 if i & 1 else 4))  35.4 us
    ppermute x12, waiting for transfers between devices, over_first(): return lax.ppermute(a, 'wide', wide_pairs(lambda i: 4 if i & 1 else 2))  28.9 us
    ppermute x20, starting transfers between devices, swap_narrow(): return lax.ppermute(a, 'narrow', [(i, i ^ bits) for i in range(size)])  24.8 us
    dot_general x10, matrix products, dot_tn(): lax.dot_general(a, b, (((0,), (0,)), ((), ())), preferred_element_type=f32)  24 us
    unnamed x255, local copies, waits for them, and re-layouts  23.1 us
    pallas_call x1, Pallas kernels, attention_back(): pl.pallas_call(attention_back_kernel, out_shape=jax.ShapeDtypeStruct((row...  16.5 us
    dynamic_slice x10, local copies, waits for them, and re-layouts, rows_from(): lax.dynamic_slice_in_dim(a, start, count, axis, allow_negative_indices=Fa...  14.6 us
  transfers between devices with their start and end apart: 82, of which 31 were waited for; matrix products, arithmetic and copies ran while one was open for 24% of the time, Pallas kernels for 28%

profile of v4, /device:TPU:0, one launch (start us, length us, event | category | flops | bytes accessed | tf_op | source)
XLA Modules:
  0.0 424.9 jit_solution(7428453184269267241)
XLA Ops:
  3.4 4.1 collective-permute-start.2
  10.1 3.0 collective-permute-start
  17.3 1.8 constant_dynamic-slice_fusion.10
  31.7 1.8 collective-permute-start.4
  36.9 2.0 convolution_convert_fusion.4.pixels_ref
  42.4 8.7 %collective-permute-done.9 = bf16[2,32,4096]{2,1,0:T(8,128)(2,1)S(1)} collective-permute-done((bf16[2,32,4096]{2,1,0:T(8,128)(2,1)S(1)}, bf16[2,32,4096]{2,1,0:T(8,128)(2,1)S(1)}, u32[]{:S(2)}, u32[]{:S(2)}) %collective-permute-start.9) | collective-permute-done | bytes 524320 | tf_op jit(solution)/shard_map/ppermute | solution.py:74
  52.9 7.7 %collective-permute-done.10.refs_2_.refs_3_ = bf16[2,4,32,1024]{3,2,1,0:T(8,128)(2,1)S(1)} collective-permute-done((bf16[2,4,32,1024]{3,2,1,0:T(8,128)(2,1)S(1)}, bf16[2,4,32,1024]{3,2,1,0:T(8,128)(2,1)S(1)}, u32[]{:S(2)}, u32[]{:S(2)}) %collective-permute-start.10) | collective-permute-done | bytes 524320 | tf_op jit(solution)/shard_map/ppermute | solution.py:60
  65.2 7.7 %collective-permute-done.12.refs_4_.refs_5_ = bf16[4,32,1024]{2,1,0:T(8,128)(2,1)S(1)} collective-permute-done((bf16[4,32,1024]{2,1,0:T(8,128)(2,1)S(1)}, bf16[4,32,1024]{2,1,0:T(8,128)(2,1)S(1)}, u32[]{:S(2)}, u32[]{:S(2)}) %collective-permute-start.12) | collective-permute-done | bytes 262176 | tf_op jit(solution)/shard_map/ppermute | solution.py:64
  74.6 5.9 %collective-permute-done.16 = bf16[32,4096]{1,0:T(8,128)(2,1)} collective-permute-done((bf16[32,4096]{1,0:T(8,128)(2,1)}, bf16[32,4096]{1,0:T(8,128)(2,1)}, u32[]{:S(2)}, u32[]{:S(2)}) %collective-permute-start.16) | collective-permute-done | bytes 262176 | tf_op jit(solution)/shard_map/ppermute | solution.py:74
  80.5 1.9 pad_maximum_fusion.12
  82.4 2.6 arrange.1
  88.1 3.7 assemble.4
  91.8 1.8 slice_bitcast_fusion.2
  94.3 9.1 %variable_forward.1 = bf16[512,1024]{1,0:T(8,128)(2,1)S(1)} custom-call(bf16[256,512]{1,0:T(8,128)(2,1)S(1)} %copy-done.60, f32[256,256]{1,0:T(8,128)S(1)} %copy-done.32, f32[8,2,256]{2,1,0:T(2,128)S(1)} %add.206.keys_ref, bf16[1024,256]{1,0:T(8,128)(2,1)S(1)} %copy-done.53), custom_call_target="tpu_custom_call" | custom-call | flops 11699999744 | bytes 1 | tf_op jit(solution)/shard_map/variable_forward/pallas_call | solution.py:471
  107.0 2.7 fusion.38
  111.7 1.9 collective-permute-start.24
  116.2 4.1 assemble.5
  120.3 3.7 convolution_convert_fusion.q_ref.k_ref.v_ref
  124.0 2.8 collective-permute-done.24
  127.0 12.0 %attention.1 = (bf16[512,1024]{1,0:T(8,128)(2,1)S(1)}, f32[8,2,512]{2,1,0:T(2,128)S(1)}) custom-call(bf16[512,3072]{1,0:T(8,128)(2,1)S(1)} %convolution_convert_fusion.q_ref.k_ref.v_ref, bf16[512,3072]{1,0:T(8,128)(2,1)S(1)} %convolution_convert_fusion.q_ref.k_ref.v_ref, bf16[512,3072]{1,0:T(8,128)(2,1)S(1)} %convolution_convert_fusion.q_ref.k_ref.v_ref, ...), custom_call_target="tpu_custom_call" | custom-call | flops 16250000384 | bytes 1 | tf_op jit(solution)/shard_map/attention/pallas_call | solution.py:595
  145.5 6.9 %collective-permute-done.30.refs_5_ = bf16[3,32,4096]{2,1,0:T(8,128)(2,1)S(1)} collective-permute-done((bf16[3,32,4096]{2,1,0:T(8,128)(2,1)S(1)}, bf16[3,32,4096]{2,1,0:T(8,128)(2,1)S(1)}, u32[]{:S(2)}, u32[]{:S(2)}) %collective-permute-start.30) | collective-permute-done | bytes 786464 | tf_op jit(solution)/shard_map/ppermute | solution.py:64
  154.6 2.3 assemble.6.weight.w_in
  157.9 10.0 %mlp_in.1 = (bf16[512,4096]{1,0:T(8,128)(2,1)S(1)}, bf16[512,4096]{1,0:T(8,128)(2,1)S(1)}) custom-call(bf16[512,1024]{1,0:T(8,128)(2,1)S(1)} %add_convert_fusion.7.rows_ref, bf16[1024,4096]{1,0:T(8,128)(2,1)S(1)} %assemble.6.weight.w_in, f32[1,4096]{1,0:T(1,128)S(1)} %bitcast.211), custom_call_target="tpu_custom_call" | custom-call | flops 14300000256 | bytes 1 | tf_op jit(solution)/shard_map/mlp_in/pallas_call | solution.py:686
  167.9 3.3 copy-done.59
  171.3 2.0 collective-permute-done.34.refs_3_
  174.6 10.8 %collective-permute-done.36.refs_5_ = bf16[3,128,1024]{2,1,0:T(8,128)(2,1)S(1)} collective-permute-done((bf16[3,128,1024]{2,1,0:T(8,128)(2,1)S(1)}, bf16[3,128,1024]{2,1,0:T(8,128)(2,1)S(1)}, u32[]{:S(2)}, u32[]{:S(2)}) %collective-permute-start.36) | collective-permute-done | bytes 786464 | tf_op jit(solution)/shard_map/ppermute | solution.py:64
  189.3 13.0 %mlp_back.1 = (bf16[512,2048]{1,0:T(8,128)(2,1)S(1)}, bf16[512,2048]{1,0:T(8,128)(2,1)}, f32[512,1024]{1,0:T(8,128)S(1)}, f32[4,1,1024]{2,1,0:T(1,128)S(1)}) custom-call(s32[1]{0:T(128)} %bitcast.3.core, bf16[512,1024]{1,0:T(8,128)(2,1)S(1)} %copy-done.8, bf16[4096,1024]{1,0:T(8,128)(2,1)S(1)} %assemble.7.w_out, bf16[1024,4096]{1,0:T(8,128)(2,1)S(1)} %bitcast.244, ...), custom_call_target="tpu_custom_call" | custom-call | flops 20149999616 | bytes 1 | tf_op jit(solution)/shard_map/mlp_back/pallas_call | solution.py:725
  202.8 5.1 %fusion.48 = f32[4096,512]{1,0:T(8,128)S(1)} fusion(bf16[512,4096]{1,0:T(8,128)(2,1)} %collective-permute-done.33, bf16[512,512]{1,0:T(8,128)(2,1)} %collective-permute-done.38), kind=kOutput, calls=%fused_computation.213 | convolution fusion | flops 2147483648 | bytes 13107200 | tf_op jit(solution)/shard_map/dot_general | solution.py:43
  208.0 2.6 add_convert_fusion.1
  210.7 3.0 pick_first.4
  215.5 2.1 copy.71
  217.5 2.6 multiply_reduce_fusion
  220.2 2.2 fusion.41
  224.9 4.2 fusion.49
  229.1 2.6 add_convert_fusion
  234.1 2.3 pick_first.5
  240.1 3.1 add_split.10
  246.3 16.5 %attention_back.1 = bf16[512,3072]{1,0:T(8,128)(2,1)S(1)} custom-call(bf16[512,3072]{1,0:T(8,128)(2,1)S(1)} %copy-done.70, bf16[512,3072]{1,0:T(8,128)(2,1)S(1)} %copy-done.70, bf16[512,3072]{1,0:T(8,128)(2,1)S(1)} %copy-done.70, bf16[512,1024]{1,0:T(8,128)(2,1)S(1)} %convolution_convert_fusion.2.grad_ref, f32[8,2,512]{2,1,0:T(2,128)S(1)} %get-tuple-element.354.log_ref, ...), custom_call_target="tpu_custom_call" | custom-call | flops 21450000384 | bytes 1 | tf_op jit(solution)/shard_map/attention_back/pallas_call | solution.py:654
  262.8 6.6 %collective-permute-done.42 = bf16[4,256,512]{2,1,0:T(8,128)(2,1)S(1)} collective-permute-done((bf16[4,256,512]{2,1,0:T(8,128)(2,1)S(1)}, bf16[4,256,512]{2,1,0:T(8,128)(2,1)S(1)}, u32[]{:S(2)}, u32[]{:S(2)}) %collective-permute-start.42) | collective-permute-done | bytes 1048608 | tf_op jit(solution)/shard_map/ppermute | solution.py:64
  270.9 2.3 constant_dynamic-slice_fusion.4
  276.0 2.5 constant_dynamic-slice_fusion.5
  280.5 2.5 copy-done.5
  286.0 3.4 fusion.51
  289.4 1.8 add_convert_fusion.2
  295.0 4.0 multiply_reduce_fusion.1
  305.1 14.6 %variable_back.1 = (bf16[512,512]{1,0:T(8,128)(2,1)S(1)}, f32[16,256]{1,0:T(8,128)S(1)}, f32[256,512]{1,0:T(8,128)S(1)}) custom-call(bf16[256,512]{1,0:T(8,128)(2,1)S(1)} %copy-done.61, f32[256,256]{1,0:T(8,128)S(1)} %copy-done.33, f32[8,2,256]{2,1,0:T(2,128)S(1)} %add.206.keys_ref, f32[8,256,2]{2,1,0:T(8,128)S(1)} %bitcast.195, ...), custom_call_target="tpu_custom_call" | custom-call | flops 1300000000 | bytes 1 | tf_op jit(solution)/shard_map/variable_back/pallas_call | solution.py:535
  328.5 3.1 add_split.15
  331.6 1.9 fusion.52
  338.1 5.2 %collective-permute-done.55 = bf16[2,64,2560]{2,1,0:T(8,128)(2,1)S(1)} collective-permute-done((bf16[2,64,2560]{2,1,0:T(8,128)(2,1)S(1)}, bf16[2,64,2560]{2,1,0:T(8,128)(2,1)S(1)}, u32[]{:S(2)}, u32[]{:S(2)}) %collective-permute-start.55) | collective-permute-done | bytes 655392 | tf_op jit(solution)/shard_map/ppermute | solution.py:74
  345.4 7.3 %collective-permute-done.58.got_sent.got_kept = bf16[1,2,336,512]{3,2,1,0:T(8,128)(2,1)S(1)} collective-permute-done((bf16[1,2,336,512]{3,2,1,0:T(8,128)(2,1)S(1)}, bf16[1,2,336,512]{3,2,1,0:T(8,128)(2,1)S(1)}, u32[]{:S(2)}, u32[]{:S(2)}) %collective-permute-start.58) | collective-permute-done | bytes 688160 | tf_op jit(solution)/shard_map/ppermute | solution.py:60
  358.2 2.6 collective-permute-done.56
  361.0 2.4 collective-permute-done.54.refs_2_
  367.1 6.6 %collective-permute-done.62 = bf16[208,512]{1,0:T(8,128)(2,1)S(1)} collective-permute-done((bf16[208,512]{1,0:T(8,128)(2,1)S(1)}, bf16[208,512]{1,0:T(8,128)(2,1)S(1)}, u32[]{:S(2)}, u32[]{:S(2)}) %collective-permute-start.62) | collective-permute-done | bytes 213024 | tf_op jit(solution)/shard_map/ppermute | solution.py:74
  374.7 2.9 collective-permute-start.66
  377.7 5.5 %add_convert_fusion.3 = bf16[512,1024]{1,0:T(8,128)(2,1)} fusion(f32[512,1024]{1,0:T(8,128)S(1)} %copy-done.73, bf16[512,4096]{1,0:T(8,128)(2,1)S(1)} %copy-done.7, bf16[4096,1024]{1,0:T(8,128)(2,1)S(1)} %bitcast.242, f32[1024]{0:T(1024)S(1)} %bitcast.281), kind=kOutput, calls=%fused_computation.5 | convolution fusion | flops 4296540160 | bytes 15732736 | tf_op jit(solution)/shard_map/dot_general | solution.py:35
  384.3 3.0 collective-permute-done.64
  387.5 4.0 collective-permute-done.66
  395.7 2.8 place.4
  400.3 6.4 %collective-permute-done.75.refs_2_ = bf16[2,64,1536]{2,1,0:T(8,128)(2,1)S(1)} collective-permute-done((bf16[2,64,1536]{2,1,0:T(8,128)(2,1)S(1)}, bf16[2,64,1536]{2,1,0:T(8,128)(2,1)S(1)}, u32[]{:S(2)}, u32[]{:S(2)}) %collective-permute-start.75) | collective-permute-done | bytes 393248 | tf_op jit(solution)/shard_map/ppermute | solution.py:60
  407.5 2.0 collective-permute-start.77
  409.6 2.5 collective-permute-done.73.refs_4_
  412.6 3.2 place.5
  417.6 2.7 finish.1
  422.2 2.4 place.7
  (532 shorter events, 134.3 us)
Async XLA Ops:
  3.4 23.1 %collective-permute-start.2 = (bf16[32,4096]{1,0:T(8,128)(2,1)S(1)}, bf16[32,4096]{1,0:T(8,128)(2,1)S(1)}, u32[]{:S(2)}, u32[]{:S(2)}) collective-permute-start(bf16[32,4096]{1,0:T(8,128)(2,1)S(1)} %get-tuple-element.499), channel_id=1, source_target_pairs={{0,2},{1,3},{2,0},{3,1},{4,6},{5,7},{6,4},{7,5},{8,10},{9,11},{10,... | collective-permute-start | bytes 786440 | tf_op jit(solution)/shard_map/ppermute | solution.py:74
  8.4 17.0 %collective-permute-start.3 = (bf16[32,1024]{1,0:T(8,128)(2,1)S(1)}, bf16[32,1024]{1,0:T(8,128)(2,1)S(1)}, u32[]{:S(2)}, u32[]{:S(2)}) collective-permute-start(bf16[32,1024]{1,0:T(8,128)(2,1)S(1)} %constant_dynamic-slice_fusion.12), channel_id=1, source_target_pairs={{0,2},{1,3},{2,0},{3,1},{4,6},{5,7},{6,4},{7,5},{8,10},{9,11},{10,... | collective-permute-start | bytes 196616 | tf_op jit(solution)/shard_map/ppermute | solution.py:74
  10.1 13.6 %collective-permute-start = (bf16[12,256]{1,0:T(8,128)(2,1)S(1)}, bf16[12,256]{1,0:T(8,128)(2,1)S(1)}, u32[]{:S(2)}, u32[]{:S(2)}) collective-permute-start(bf16[12,256]{1,0:T(8,128)(2,1)S(1)} %get-tuple-element.523.own), channel_id=1, source_target_pairs={{0,2},{1,3},{2,0},{3,1},{4,6},{5,7},{6,4},{7,5},{8,10},{9,11},{10,... | collective-permute-start | bytes 18440 | tf_op jit(solution)/shard_map/ppermute | solution.py:74
  26.0 15.3 %collective-permute-start.7 = (bf16[2,32,1024]{2,1,0:T(8,128)(2,1)}, bf16[2,32,1024]{2,1,0:T(8,128)(2,1)}, u32[]{:S(2)}, u32[]{:S(2)}) collective-permute-start(bf16[2,32,1024]{2,1,0:T(8,128)(2,1)} %pad_maximum_fusion.23), channel_id=1, source_target_pairs={{0,1},{1,0},{2,3},{3,2},{4,5},{5,4},{6,7},{7,6},{8,9},{9,8},{10,11... | collective-permute-start | bytes 393224 | tf_op jit(solution)/shard_map/ppermute | solution.py:74
  31.7 7.8 %collective-permute-start.4 = (bf16[40,1024]{1,0:T(8,128)(2,1)S(1)}, bf16[40,1024]{1,0:T(8,128)(2,1)S(1)}, u32[]{:S(2)}, u32[]{:S(2)}) collective-permute-start(bf16[40,1024]{1,0:T(8,128)(2,1)S(1)} %maximum_maximum_fusion.2), channel_id=1, source_target_pairs={{0,1},{1,2},{2,3},{3,0},{4,5},{5,6},{6,7},{7,4},{8,9},{9,10},{10,1... | collective-permute-start | bytes 245768 | tf_op jit(solution)/shard_map/ppermute | solution.py:69
  33.5 6.3 %collective-permute-start.5 = (bf16[40,1024]{1,0:T(8,128)(2,1)S(1)}, bf16[40,1024]{1,0:T(8,128)(2,1)S(1)}, u32[]{:S(2)}, u32[]{:S(2)}) collective-permute-start(bf16[40,1024]{1,0:T(8,128)(2,1)S(1)} %maximum_maximum_fusion.2), channel_id=1, source_target_pairs={{0,2},{1,3},{2,0},{3,1},{4,6},{5,7},{6,4},{7,5},{8,10},{9,11},{10,... | collective-permute-start | bytes 245768 | tf_op jit(solution)/shard_map/ppermute | solution.py:69
  34.8 6.4 %collective-permute-start.6 = (bf16[40,1024]{1,0:T(8,128)(2,1)S(1)}, bf16[40,1024]{1,0:T(8,128)(2,1)S(1)}, u32[]{:S(2)}, u32[]{:S(2)}) collective-permute-start(bf16[40,1024]{1,0:T(8,128)(2,1)S(1)} %maximum_maximum_fusion.2), channel_id=1, source_target_pairs={{0,3},{1,0},{2,1},{3,2},{4,7},{5,4},{6,5},{7,6},{8,11},{9,8},{10,9... | collective-permute-start | bytes 245768 | tf_op jit(solution)/shard_map/ppermute | solution.py:69
  36.0 15.1 %collective-permute-start.9 = (bf16[2,32,4096]{2,1,0:T(8,128)(2,1)S(1)}, bf16[2,32,4096]{2,1,0:T(8,128)(2,1)S(1)}, u32[]{:S(2)}, u32[]{:S(2)}) collective-permute-start(bf16[2,32,4096]{2,1,0:T(8,128)(2,1)S(1)} %pad_maximum_fusion.10), channel_id=1, source_target_pairs={{0,1},{1,0},{2,3},{3,2},{4,5},{5,4},{6,7},{7,6},{8,9},{9,8},{10,11... | collective-permute-start | bytes 1572872 | tf_op jit(solution)/shard_map/ppermute | solution.py:74
  42.3 9.0 %collective-permute-start.8 = (bf16[4,32,1024]{2,1,0:T(8,128)(2,1)S(1)}, bf16[4,32,1024]{2,1,0:T(8,128)(2,1)S(1)}, u32[]{:S(2)}, u32[]{:S(2)}) collective-permute-start(bf16[4,32,1024]{2,1,0:T(8,128)(2,1)S(1)} %get-tuple-element.268.refs_0_.refs_1_), channel_id=1, source_target_pairs={{0,4},{4,0},{8,12},{12,8},{16,20},{20,16},{24,28},{28,24},{1,5},{5... | collective-permute-start | bytes 786440 | tf_op jit(solution)/shard_map/ppermute | solution.py:56
  51.2 9.4 %collective-permute-start.13 = (bf16[3,32,4096]{2,1,0:T(8,128)(2,1)S(1)}, bf16[3,32,4096]{2,1,0:T(8,128)(2,1)S(1)}, u32[]{:S(2)}, u32[]{:S(2)}) collective-permute-start(bf16[3,32,4096]{2,1,0:T(8,128)(2,1)S(1)} %get-tuple-element.285.refs_2_), channel_id=1, source_target_pairs={{0,4},{4,0},{8,12},{12,8},{16,20},{20,16},{24,28},{28,24},{1,5},{5... | collective-permute-start | bytes 2359304 | tf_op jit(solution)/shard_map/ppermute | solution.py:56
  51.4 9.2 %collective-permute-start.10 = (bf16[2,4,32,1024]{3,2,1,0:T(8,128)(2,1)S(1)}, bf16[2,4,32,1024]{3,2,1,0:T(8,128)(2,1)S(1)}, u32[]{:S(2)}, u32[]{:S(2)}) collective-permute-start(bf16[2,4,32,1024]{3,2,1,0:T(8,128)(2,1)S(1)} %pad_maximum_fusion.11), channel_id=1, source_target_pairs={{0,8},{4,20},{8,0},{12,28},{16,24},{20,4},{24,16},{28,12},{1,9},{5... | collective-permute-start | bytes 1572872 | tf_op jit(solution)/shard_map/ppermute | solution.py:60
  62.1 29.7 %collective-permute-start.15 = (bf16[2,3,32,4096]{3,2,1,0:T(8,128)(2,1)}, bf16[2,3,32,4096]{3,2,1,0:T(8,128)(2,1)}, u32[]{:S(2)}, u32[]{:S(2)}) collective-permute-start(bf16[2,3,32,4096]{3,2,1,0:T(8,128)(2,1)} %pad_maximum_fusion.1), channel_id=1, source_target_pairs={{0,8},{4,20},{8,0},{12,28},{16,24},{20,4},{24,16},{28,12},{1,9},{5... | collective-permute-start | bytes 4718600 | tf_op jit(solution)/shard_map/ppermute | solution.py:60
  63.6 9.2 %collective-permute-start.12 = (bf16[4,32,1024]{2,1,0:T(8,128)(2,1)S(1)}, bf16[4,32,1024]{2,1,0:T(8,128)(2,1)S(1)}, u32[]{:S(2)}, u32[]{:S(2)}) collective-permute-start(bf16[4,32,1024]{2,1,0:T(8,128)(2,1)S(1)} %slice_bitcast_fusion.5), channel_id=1, source_target_pairs={{0,16},{4,12},{8,24},{12,4},{16,0},{20,28},{24,8},{28,20},{1,17},{... | collective-permute-start | bytes 786440 | tf_op jit(solution)/shard_map/ppermute | solution.py:64
  64.9 9.6 %collective-permute-start.11 = (bf16[2,4,32,1024]{3,2,1,0:T(8,128)(2,1)S(1)}, bf16[2,4,32,1024]{3,2,1,0:T(8,128)(2,1)S(1)}, u32[]{:S(2)}, u32[]{:S(2)}) collective-permute-start(bf16[2,4,32,1024]{3,2,1,0:T(8,128)(2,1)S(1)} %collective-permute-done.10.refs_2_.refs_3_), channel_id=1, source_target_pairs={{0,4},{4,0},{8,12},{12,8},{16,20},{20,16},{24,28},{28,24},{1,5},{5... | collective-permute-start | bytes 1572872 | tf_op jit(solution)/shard_map/ppermute | solution.py:56
  64.9 15.6 %collective-permute-start.16 = (bf16[32,4096]{1,0:T(8,128)(2,1)}, bf16[32,4096]{1,0:T(8,128)(2,1)}, u32[]{:S(2)}, u32[]{:S(2)}) collective-permute-start(bf16[32,4096]{1,0:T(8,128)(2,1)} %constant_dynamic-slice_fusion.11), channel_id=1, source_target_pairs={{0,2},{1,3},{2,0},{3,1},{4,6},{5,7},{6,4},{7,5},{8,10},{9,11},{10,... | collective-permute-start | bytes 786440 | tf_op jit(solution)/shard_map/ppermute | solution.py:74
  82.3 24.6 %collective-permute-start.19 = (bf16[2,32,4096]{2,1,0:T(8,128)(2,1)}, bf16[2,32,4096]{2,1,0:T(8,128)(2,1)}, u32[]{:S(2)}, u32[]{:S(2)}) collective-permute-start(bf16[2,32,4096]{2,1,0:T(8,128)(2,1)} %pad_maximum_fusion.12), channel_id=1, source_target_pairs={{0,1},{1,0},{2,3},{3,2},{4,5},{5,4},{6,7},{7,6},{8,9},{9,8},{10,11... | collective-permute-start | bytes 1572872 | tf_op jit(solution)/shard_map/ppermute | solution.py:74
  93.6 22.6 %collective-permute-start.17 = (bf16[2,3,32,4096]{3,2,1,0:T(8,128)(2,1)}, bf16[2,3,32,4096]{3,2,1,0:T(8,128)(2,1)}, u32[]{:S(2)}, u32[]{:S(2)}) collective-permute-start(bf16[2,3,32,4096]{3,2,1,0:T(8,128)(2,1)} %collective-permute-done.15.refs_4_), channel_id=1, source_target_pairs={{0,4},{4,0},{8,12},{12,8},{16,20},{20,16},{24,28},{28,24},{1,5},{5... | collective-permute-start | bytes 4718600 | tf_op jit(solution)/shard_map/ppermute | solution.py:56
  93.7 16.5 %collective-permute-start.18 = (bf16[3,32,4096]{2,1,0:T(8,128)(2,1)S(1)}, bf16[3,32,4096]{2,1,0:T(8,128)(2,1)}, u32[]{:S(2)}, u32[]{:S(2)}) collective-permute-start(bf16[3,32,4096]{2,1,0:T(8,128)(2,1)S(1)} %slice_bitcast_fusion.2), channel_id=1, source_target_pairs={{0,16},{4,12},{8,24},{12,4},{16,0},{20,28},{24,8},{28,20},{1,17},{... | collective-permute-start | bytes 2359304 | tf_op jit(solution)/shard_map/ppermute | solution.py:64
  111.4 15.6 %collective-permute-start.23 = (bf16[512,1024]{1,0:T(8,128)(2,1)}, bf16[512,1024]{1,0:T(8,128)(2,1)S(1)}, u32[]{:S(2)}, u32[]{:S(2)}) collective-permute-start(bf16[512,1024]{1,0:T(8,128)(2,1)} %add_convert_fusion.8), channel_id=1, source_target_pairs={{0,4},{4,0},{8,12},{12,8},{16,20},{20,16},{24,28},{28,24},{1,5},{5... | collective-permute-start | bytes 3145736 | tf_op jit(solution)/shard_map/ppermute | solution.py:56
  111.7 15.1 %collective-permute-start.24 = (bf16[128,1024]{1,0:T(8,128)(2,1)}, bf16[128,1024]{1,0:T(8,128)(2,1)S(1)}, u32[]{:S(2)}, u32[]{:S(2)}) collective-permute-start(bf16[128,1024]{1,0:T(8,128)(2,1)} %constant_dynamic-slice_fusion.10), channel_id=1, source_target_pairs={{0,2},{1,3},{2,0},{3,1},{4,6},{5,7},{6,4},{7,5},{8,10},{9,11},{10,... | collective-permute-start | bytes 786440 | tf_op jit(solution)/shard_map/ppermute | solution.py:74
  115.1 24.0 %collective-permute-start.26 = (bf16[2,3,32,4096]{3,2,1,0:T(8,128)(2,1)S(1)}, bf16[2,3,32,4096]{3,2,1,0:T(8,128)(2,1)S(1)}, u32[]{:S(2)}, u32[]{:S(2)}) collective-permute-start(bf16[2,3,32,4096]{3,2,1,0:T(8,128)(2,1)S(1)} %pad_maximum_fusion.2), channel_id=1, source_target_pairs={{0,8},{4,20},{8,0},{12,28},{16,24},{20,4},{24,16},{28,12},{1,9},{5... | collective-permute-start | bytes 4718600 | tf_op jit(solution)/shard_map/ppermute | solution.py:60
  126.9 13.3 %collective-permute-start.25 = (bf16[2,128,1024]{2,1,0:T(8,128)(2,1)S(1)}, bf16[2,128,1024]{2,1,0:T(8,128)(2,1)S(1)}, u32[]{:S(2)}, u32[]{:S(2)}) collective-permute-start(bf16[2,128,1024]{2,1,0:T(8,128)(2,1)S(1)} %pad_maximum_fusion.13), channel_id=1, source_target_pairs={{0,1},{1,0},{2,3},{3,2},{4,5},{5,4},{6,7},{7,6},{8,9},{9,8},{10,11... | collective-permute-start | bytes 1572872 | tf_op jit(solution)/shard_map/ppermute | solution.py:74
  140.3 12.1 %collective-permute-start.30 = (bf16[3,32,4096]{2,1,0:T(8,128)(2,1)S(1)}, bf16[3,32,4096]{2,1,0:T(8,128)(2,1)S(1)}, u32[]{:S(2)}, u32[]{:S(2)}) collective-permute-start(bf16[3,32,4096]{2,1,0:T(8,128)(2,1)S(1)} %slice_bitcast_fusion.1), channel_id=1, source_target_pairs={{0,16},{4,12},{8,24},{12,4},{16,0},{20,28},{24,8},{28,20},{1,17},{... | collective-permute-start | bytes 2359304 | tf_op jit(solution)/shard_map/ppermute | solution.py:64
  141.6 13.0 %collective-permute-start.29 = (bf16[2,3,32,4096]{3,2,1,0:T(8,128)(2,1)S(1)}, bf16[2,3,32,4096]{3,2,1,0:T(8,128)(2,1)S(1)}, u32[]{:S(2)}, u32[]{:S(2)}) collective-permute-start(bf16[2,3,32,4096]{3,2,1,0:T(8,128)(2,1)S(1)} %collective-permute-done.26.refs_3_), channel_id=1, source_target_pairs={{0,4},{4,0},{8,12},{12,8},{16,20},{20,16},{24,28},{28,24},{1,5},{5... | collective-permute-start | bytes 4718600 | tf_op jit(solution)/shard_map/ppermute | solution.py:56
  152.9 20.4 %collective-permute-start.34 = (bf16[2,3,128,1024]{3,2,1,0:T(8,128)(2,1)S(1)}, bf16[2,3,128,1024]{3,2,1,0:T(8,128)(2,1)S(1)}, u32[]{:S(2)}, u32[]{:S(2)}) collective-permute-start(bf16[2,3,128,1024]{3,2,1,0:T(8,128)(2,1)S(1)} %pad_maximum_fusion.3), channel_id=1, source_target_pairs={{0,8},{4,20},{8,0},{12,28},{16,24},{20,4},{24,16},{28,12},{1,9},{5... | collective-permute-start | bytes 4718600 | tf_op jit(solution)/shard_map/ppermute | solution.py:60
  171.2 31.6 %collective-permute-start.33 = (bf16[512,4096]{1,0:T(8,128)(2,1)S(1)}, bf16[512,4096]{1,0:T(8,128)(2,1)}, u32[]{:S(2)}, u32[]{:S(2)}) collective-permute-start(bf16[512,4096]{1,0:T(8,128)(2,1)S(1)} %get-tuple-element.408), channel_id=1, source_target_pairs={{0,4},{4,0},{8,12},{12,8},{16,20},{20,16},{24,28},{28,24},{1,5},{5... | collective-permute-start | bytes 12582920 | tf_op jit(solution)/shard_map/ppermute | solution.py:56
  173.3 12.1 %collective-permute-start.36 = (bf16[3,128,1024]{2,1,0:T(8,128)(2,1)S(1)}, bf16[3,128,1024]{2,1,0:T(8,128)(2,1)S(1)}, u32[]{:S(2)}, u32[]{:S(2)}) collective-permute-start(bf16[3,128,1024]{2,1,0:T(8,128)(2,1)S(1)} %slice_bitcast_fusion), channel_id=1, source_target_pairs={{0,16},{4,12},{8,24},{12,4},{16,0},{20,28},{24,8},{28,20},{1,17},{... | collective-permute-start | bytes 2359304 | tf_op jit(solution)/shard_map/ppermute | solution.py:64
  174.6 12.5 %collective-permute-start.35 = (bf16[2,3,128,1024]{3,2,1,0:T(8,128)(2,1)S(1)}, bf16[2,3,128,1024]{3,2,1,0:T(8,128)(2,1)S(1)}, u32[]{:S(2)}, u32[]{:S(2)}) collective-permute-start(bf16[2,3,128,1024]{3,2,1,0:T(8,128)(2,1)S(1)} %collective-permute-done.34.refs_3_), channel_id=1, source_target_pairs={{0,4},{4,0},{8,12},{12,8},{16,20},{20,16},{24,28},{28,24},{1,5},{5... | collective-permute-start | bytes 4718600 | tf_op jit(solution)/shard_map/ppermute | solution.py:56
  186.6 16.2 %collective-permute-start.38 = (bf16[512,512]{1,0:T(8,128)(2,1)S(1)}, bf16[512,512]{1,0:T(8,128)(2,1)}, u32[]{:S(2)}, u32[]{:S(2)}) collective-permute-start(bf16[512,512]{1,0:T(8,128)(2,1)S(1)} %copy-done.95), channel_id=1, source_target_pairs={{0,4},{4,0},{8,12},{12,8},{16,20},{20,16},{24,28},{28,24},{1,5},{5... | collective-permute-start | bytes 1572872 | tf_op jit(solution)/shard_map/ppermute | solution.py:56
  202.3 22.5 %collective-permute-start.41 = (bf16[512,2048]{1,0:T(8,128)(2,1)}, bf16[512,2048]{1,0:T(8,128)(2,1)}, u32[]{:S(2)}, u32[]{:S(2)}) collective-permute-start(bf16[512,2048]{1,0:T(8,128)(2,1)} %get-tuple-element.332), channel_id=1, source_target_pairs={{0,4},{4,0},{8,12},{12,8},{16,20},{20,16},{24,28},{28,24},{1,5},{5... | collective-permute-start | bytes 6291464 | tf_op jit(solution)/shard_map/ppermute | solution.py:56
  213.7 26.4 %collective-permute-start.39 = (bf16[4,2,256,512]{3,2,1,0:T(8,128)(2,1)}, bf16[4,2,256,512]{3,2,1,0:T(8,128)(2,1)}, u32[]{:S(2)}, u32[]{:S(2)}) collective-permute-start(bf16[4,2,256,512]{3,2,1,0:T(8,128)(2,1)} %pick_first.4), channel_id=1, source_target_pairs={{0,8},{4,20},{8,0},{12,28},{16,24},{20,4},{24,16},{28,12},{1,9},{5... | collective-permute-start | bytes 6291464 | tf_op jit(solution)/shard_map/ppermute | solution.py:60
  222.9 8.8 %collective-permute-start.40 = (bf16[512,512]{1,0:T(8,128)(2,1)S(1)}, bf16[512,512]{1,0:T(8,128)(2,1)S(1)}, u32[]{:S(2)}, u32[]{:S(2)}) collective-permute-start(bf16[512,512]{1,0:T(8,128)(2,1)S(1)} %get-tuple-element.484), channel_id=1, source_target_pairs={{0,4},{4,0},{8,12},{12,8},{16,20},{20,16},{24,28},{28,24},{1,5},{5... | collective-permute-start | bytes 1572872 | tf_op jit(solution)/shard_map/ppermute | solution.py:56
  224.1 20.4 %collective-permute-start.43 = (bf16[2,256,256]{2,1,0:T(8,128)(2,1)}, bf16[2,256,256]{2,1,0:T(8,128)(2,1)}, u32[]{:S(2)}, u32[]{:S(2)}) collective-permute-start(bf16[2,256,256]{2,1,0:T(8,128)(2,1)} %dynamic-slice_bitcast_fusion), channel_id=1, source_target_pairs={{0,1},{1,0},{2,3},{3,2},{4,5},{5,4},{6,7},{7,6},{8,9},{9,8},{10,11... | collective-permute-start | bytes 786440 | tf_op jit(solution)/shard_map/ppermute | solution.py:74
  237.4 43.1 %collective-permute-start.47 = (bf16[4,2,64,2560]{3,2,1,0:T(8,128)(2,1)}, bf16[4,2,64,2560]{3,2,1,0:T(8,128)(2,1)S(1)}, u32[]{:S(2)}, u32[]{:S(2)}) collective-permute-start(bf16[4,2,64,2560]{3,2,1,0:T(8,128)(2,1)} %pick_first.5), channel_id=1, source_target_pairs={{0,8},{4,20},{8,0},{12,28},{16,24},{20,4},{24,16},{28,12},{1,9},{5... | collective-permute-start | bytes 7864328 | tf_op jit(solution)/shard_map/ppermute | solution.py:60
  243.2 26.2 %collective-permute-start.42 = (bf16[4,256,512]{2,1,0:T(8,128)(2,1)S(1)}, bf16[4,256,512]{2,1,0:T(8,128)(2,1)S(1)}, u32[]{:S(2)}, u32[]{:S(2)}) collective-permute-start(bf16[4,256,512]{2,1,0:T(8,128)(2,1)S(1)} %get-tuple-element.349), channel_id=1, source_target_pairs={{0,16},{4,12},{8,24},{12,4},{16,0},{20,28},{24,8},{28,20},{1,17},{... | collective-permute-start | bytes 3145736 | tf_op jit(solution)/shard_map/ppermute | solution.py:64
  273.2 12.8 %collective-permute-start.45 = (bf16[512,1536]{1,0:T(8,128)(2,1)}, bf16[512,1536]{1,0:T(8,128)(2,1)}, u32[]{:S(2)}, u32[]{:S(2)}) collective-permute-start(bf16[512,1536]{1,0:T(8,128)(2,1)} %constant_dynamic-slice_fusion.4), channel_id=1, source_target_pairs={{0,4},{4,0},{8,12},{12,8},{16,20},{20,16},{24,28},{28,24},{1,5},{5... | collective-permute-start | bytes 4718600 | tf_op jit(solution)/shard_map/ppermute | solution.py:56
  274.7 11.2 %collective-permute-start.46 = (bf16[256,256]{1,0:T(8,128)(2,1)S(1)}, bf16[256,256]{1,0:T(8,128)(2,1)S(1)}, u32[]{:S(2)}, u32[]{:S(2)}) collective-permute-start(bf16[256,256]{1,0:T(8,128)(2,1)S(1)} %dynamic-slice_bitcast_fusion.1), channel_id=1, source_target_pairs={{0,2},{1,3},{2,0},{3,1},{4,6},{5,7},{6,4},{7,5},{8,10},{9,11},{10,... | collective-permute-start | bytes 393224 | tf_op jit(solution)/shard_map/ppermute | solution.py:74
  278.5 21.4 %collective-permute-start.44 = (bf16[2,256,512]{2,1,0:T(8,128)(2,1)}, bf16[2,256,512]{2,1,0:T(8,128)(2,1)S(1)}, u32[]{:S(2)}, u32[]{:S(2)}) collective-permute-start(bf16[2,256,512]{2,1,0:T(8,128)(2,1)} %get-tuple-element.357), channel_id=1, source_target_pairs={{0,1},{1,0},{2,3},{3,2},{4,5},{5,4},{6,7},{7,6},{8,9},{9,8},{10,11... | collective-permute-start | bytes 1572872 | tf_op jit(solution)/shard_map/ppermute | solution.py:74
  285.3 35.9 %collective-permute-start.49 = (bf16[4,64,2560]{2,1,0:T(8,128)(2,1)S(1)}, bf16[4,64,2560]{2,1,0:T(8,128)(2,1)S(1)}, u32[]{:S(2)}, u32[]{:S(2)}) collective-permute-start(bf16[4,64,2560]{2,1,0:T(8,128)(2,1)S(1)} %get-tuple-element.363), channel_id=1, source_target_pairs={{0,16},{4,12},{8,24},{12,4},{16,0},{20,28},{24,8},{28,20},{1,17},{... | collective-permute-start | bytes 3932168 | tf_op jit(solution)/shard_map/ppermute | solution.py:64
  300.8 26.6 %collective-permute-start.48 = (bf16[1,256,512]{2,1,0:T(8,128)(2,1)S(1)}, bf16[1,256,512]{2,1,0:T(8,128)(2,1)}, u32[]{:S(2)}, u32[]{:S(2)}) collective-permute-start(bf16[1,256,512]{2,1,0:T(8,128)(2,1)S(1)} %get-tuple-element.371), channel_id=1, source_target_pairs={{0,2},{1,3},{2,0},{3,1},{4,6},{5,7},{6,4},{7,5},{8,10},{9,11},{10,... | collective-permute-start | bytes 786440 | tf_op jit(solution)/shard_map/ppermute | solution.py:74
  302.4 26.1 %collective-permute-start.53 = (bf16[4,2,64,1536]{3,2,1,0:T(8,128)(2,1)S(1)}, bf16[4,2,64,1536]{3,2,1,0:T(8,128)(2,1)}, u32[]{:S(2)}, u32[]{:S(2)}) collective-permute-start(bf16[4,2,64,1536]{3,2,1,0:T(8,128)(2,1)S(1)} %pick_first.6), channel_id=1, source_target_pairs={{0,8},{4,20},{8,0},{12,28},{16,24},{20,4},{24,16},{28,12},{1,9},{5... | collective-permute-start | bytes 4718600 | tf_op jit(solution)/shard_map/ppermute | solution.py:60
  322.2 9.4 %collective-permute-start.52 = (bf16[512,512]{1,0:T(8,128)(2,1)}, bf16[512,512]{1,0:T(8,128)(2,1)}, u32[]{:S(2)}, u32[]{:S(2)}) collective-permute-start(bf16[512,512]{1,0:T(8,128)(2,1)} %get-tuple-element.481), channel_id=1, source_target_pairs={{0,4},{4,0},{8,12},{12,8},{16,20},{20,16},{24,28},{28,24},{1,5},{5... | collective-permute-start | bytes 1572872 | tf_op jit(solution)/shard_map/ppermute | solution.py:56
  322.5 11.9 %collective-permute-start.51 = (bf16[2,2,80,512]{3,2,1,0:T(8,128)(2,1)S(1)}, bf16[2,2,80,512]{3,2,1,0:T(8,128)(2,1)S(1)}, u32[]{:S(2)}, u32[]{:S(2)}) collective-permute-start(bf16[2,2,80,512]{3,2,1,0:T(8,128)(2,1)S(1)} %fusion.4), channel_id=1, source_target_pairs={{0,4},{4,0},{8,12},{12,8},{16,20},{20,16},{24,28},{28,24},{1,5},{5... | collective-permute-start | bytes 983048 | tf_op jit(solution)/shard_map/ppermute | solution.py:56
  326.6 16.7 %collective-permute-start.55 = (bf16[2,64,2560]{2,1,0:T(8,128)(2,1)S(1)}, bf16[2,64,2560]{2,1,0:T(8,128)(2,1)S(1)}, u32[]{:S(2)}, u32[]{:S(2)}) collective-permute-start(bf16[2,64,2560]{2,1,0:T(8,128)(2,1)S(1)} %get-tuple-element.378), channel_id=1, source_target_pairs={{0,1},{1,0},{2,3},{3,2},{4,5},{5,4},{6,7},{7,6},{8,9},{9,8},{10,11... | collective-permute-start | bytes 1966088 | tf_op jit(solution)/shard_map/ppermute | solution.py:74
  328.4 8.5 %collective-permute-start.50 = (bf16[256,512]{1,0:T(8,128)(2,1)S(1)}, bf16[256,512]{1,0:T(8,128)(2,1)S(1)}, u32[]{:S(2)}, u32[]{:S(2)}) collective-permute-start(bf16[256,512]{1,0:T(8,128)(2,1)S(1)} %bitcast.196), channel_id=1, source_target_pairs={{0,4},{4,0},{8,12},{12,8},{16,20},{20,16},{24,28},{28,24},{1,5},{5... | collective-permute-start | bytes 786440 | tf_op jit(solution)/shard_map/ppermute | solution.py:56
  334.7 18.0 %collective-permute-start.58 = (bf16[1,2,336,512]{3,2,1,0:T(8,128)(2,1)S(1)}, bf16[1,2,336,512]{3,2,1,0:T(8,128)(2,1)S(1)}, u32[]{:S(2)}, u32[]{:S(2)}) collective-permute-start(bf16[1,2,336,512]{3,2,1,0:T(8,128)(2,1)S(1)} %pick_first.7), channel_id=1, source_target_pairs={{0,8},{4,20},{8,0},{12,28},{16,24},{20,4},{24,16},{28,12},{1,9},{5... | collective-permute-start | bytes 2064392 | tf_op jit(solution)/shard_map/ppermute | solution.py:60
  335.5 20.4 %collective-permute-start.57 = (bf16[4,64,1536]{2,1,0:T(8,128)(2,1)S(1)}, bf16[4,64,1536]{2,1,0:T(8,128)(2,1)S(1)}, u32[]{:S(2)}, u32[]{:S(2)}) collective-permute-start(bf16[4,64,1536]{2,1,0:T(8,128)(2,1)S(1)} %get-tuple-element.384), channel_id=1, source_target_pairs={{0,16},{4,12},{8,24},{12,4},{16,0},{20,28},{24,8},{28,20},{1,17},{... | collective-permute-start | bytes 2359304 | tf_op jit(solution)/shard_map/ppermute | solution.py:64
  336.9 26.5 %collective-permute-start.54 = (bf16[2,256,512]{2,1,0:T(8,128)(2,1)S(1)}, bf16[2,256,512]{2,1,0:T(8,128)(2,1)S(1)}, u32[]{:S(2)}, u32[]{:S(2)}) collective-permute-start(bf16[2,256,512]{2,1,0:T(8,128)(2,1)S(1)} %pad_maximum_fusion.14), channel_id=1, source_target_pairs={{0,8},{4,20},{8,0},{12,28},{16,24},{20,4},{24,16},{28,12},{1,9},{5... | collective-permute-start | bytes 1572872 | tf_op jit(solution)/shard_map/ppermute | solution.py:60
  344.0 16.9 %collective-permute-start.56 = (bf16[1,64,2560]{2,1,0:T(8,128)(2,1)S(1)}, bf16[1,64,2560]{2,1,0:T(8,128)(2,1)S(1)}, u32[]{:S(2)}, u32[]{:S(2)}) collective-permute-start(bf16[1,64,2560]{2,1,0:T(8,128)(2,1)S(1)} %get-tuple-element.391), channel_id=1, source_target_pairs={{0,2},{1,3},{2,0},{3,1},{4,6},{5,7},{6,4},{7,5},{8,10},{9,11},{10,... | collective-permute-start | bytes 983048 | tf_op jit(solution)/shard_map/ppermute | solution.py:74
  353.4 11.3 %collective-permute-start.61 = (bf16[1,336,512]{2,1,0:T(8,128)(2,1)S(1)}, bf16[1,336,512]{2,1,0:T(8,128)(2,1)S(1)}, u32[]{:S(2)}, u32[]{:S(2)}) collective-permute-start(bf16[1,336,512]{2,1,0:T(8,128)(2,1)S(1)} %get-tuple-element.393), channel_id=1, source_target_pairs={{0,16},{4,12},{8,24},{12,4},{16,0},{20,28},{24,8},{28,20},{1,17},{... | collective-permute-start | bytes 1032200 | tf_op jit(solution)/shard_map/ppermute | solution.py:64
  357.0 17.0 %collective-permute-start.60 = (bf16[2,64,1536]{2,1,0:T(8,128)(2,1)S(1)}, bf16[2,64,1536]{2,1,0:T(8,128)(2,1)S(1)}, u32[]{:S(2)}, u32[]{:S(2)}) collective-permute-start(bf16[2,64,1536]{2,1,0:T(8,128)(2,1)S(1)} %get-tuple-element.396), channel_id=1, source_target_pairs={{0,1},{1,0},{2,3},{3,2},{4,5},{5,4},{6,7},{7,6},{8,9},{9,8},{10,11... | collective-permute-start | bytes 1179656 | tf_op jit(solution)/shard_map/ppermute | solution.py:74
  363.4 14.2 %collective-permute-start.59 = (bf16[256,512]{1,0:T(8,128)(2,1)S(1)}, bf16[256,512]{1,0:T(8,128)(2,1)S(1)}, u32[]{:S(2)}, u32[]{:S(2)}) collective-permute-start(bf16[256,512]{1,0:T(8,128)(2,1)S(1)} %slice_bitcast_fusion.4), channel_id=1, source_target_pairs={{0,16},{4,12},{8,24},{12,4},{16,0},{20,28},{24,8},{28,20},{1,17},{... | collective-permute-start | bytes 786440 | tf_op jit(solution)/shard_map/ppermute | solution.py:64
  364.9 8.8 %collective-permute-start.62 = (bf16[208,512]{1,0:T(8,128)(2,1)S(1)}, bf16[208,512]{1,0:T(8,128)(2,1)S(1)}, u32[]{:S(2)}, u32[]{:S(2)}) collective-permute-start(bf16[208,512]{1,0:T(8,128)(2,1)S(1)} %pad_maximum_fusion.20), channel_id=1, source_target_pairs={{0,1},{1,0},{2,3},{3,2},{4,5},{5,4},{6,7},{7,6},{8,9},{9,8},{10,11... | collective-permute-start | bytes 638984 | tf_op jit(solution)/shard_map/ppermute | solution.py:74
  365.9 28.5 %collective-permute-start.70 = (bf16[2,64,2560]{2,1,0:T(8,128)(2,1)S(1)}, bf16[2,64,2560]{2,1,0:T(8,128)(2,1)S(1)}, u32[]{:S(2)}, u32[]{:S(2)}) collective-permute-start(bf16[2,64,2560]{2,1,0:T(8,128)(2,1)S(1)} %pad_maximum_fusion.9), channel_id=1, source_target_pairs={{0,8},{4,20},{8,0},{12,28},{16,24},{20,4},{24,16},{28,12},{1,9},{5... | collective-permute-start | bytes 1966088 | tf_op jit(solution)/shard_map/ppermute | solution.py:60
  373.9 13.4 %collective-permute-start.64 = (bf16[144,512]{1,0:T(8,128)(2,1)S(1)}, bf16[144,512]{1,0:T(8,128)(2,1)S(1)}, u32[]{:S(2)}, u32[]{:S(2)}) collective-permute-start(bf16[144,512]{1,0:T(8,128)(2,1)S(1)} %pad_maximum_fusion.22), channel_id=1, source_target_pairs={{0,2},{1,3},{2,0},{3,1},{4,6},{5,7},{6,4},{7,5},{8,10},{9,11},{10,... | collective-permute-start | bytes 442376 | tf_op jit(solution)/shard_map/ppermute | solution.py:74
  374.7 16.8 %collective-permute-start.66 = (bf16[1,64,1536]{2,1,0:T(8,128)(2,1)S(1)}, bf16[1,64,1536]{2,1,0:T(8,128)(2,1)S(1)}, u32[]{:S(2)}, u32[]{:S(2)}) collective-permute-start(bf16[1,64,1536]{2,1,0:T(8,128)(2,1)S(1)} %get-tuple-element.406), channel_id=1, source_target_pairs={{0,2},{1,3},{2,0},{3,1},{4,6},{5,7},{6,4},{7,5},{8,10},{9,11},{10,... | collective-permute-start | bytes 589832 | tf_op jit(solution)/shard_map/ppermute | solution.py:74
  392.2 8.1 %collective-permute-start.67 = (bf16[2,144,512]{2,1,0:T(8,128)(2,1)S(1)}, bf16[2,144,512]{2,1,0:T(8,128)(2,1)S(1)}, u32[]{:S(2)}, u32[]{:S(2)}) collective-permute-start(bf16[2,144,512]{2,1,0:T(8,128)(2,1)S(1)} %pad_maximum_fusion.16), channel_id=1, source_target_pairs={{0,8},{4,20},{8,0},{12,28},{16,24},{20,4},{24,16},{28,12},{1,9},{5... | collective-permute-start | bytes 884744 | tf_op jit(solution)/shard_map/ppermute | solution.py:60
  393.1 13.7 %collective-permute-start.75 = (bf16[2,64,1536]{2,1,0:T(8,128)(2,1)S(1)}, bf16[2,64,1536]{2,1,0:T(8,128)(2,1)S(1)}, u32[]{:S(2)}, u32[]{:S(2)}) collective-permute-start(bf16[2,64,1536]{2,1,0:T(8,128)(2,1)S(1)} %pad_maximum_fusion.15), channel_id=1, source_target_pairs={{0,8},{4,20},{8,0},{12,28},{16,24},{20,4},{24,16},{28,12},{1,9},{5... | collective-permute-start | bytes 1179656 | tf_op jit(solution)/shard_map/ppermute | solution.py:60
  394.5 18.1 %collective-permute-start.78 = (bf16[2,64,2560]{2,1,0:T(8,128)(2,1)S(1)}, bf16[2,64,2560]{2,1,0:T(8,128)(2,1)S(1)}, u32[]{:S(2)}, u32[]{:S(2)}) collective-permute-start(bf16[2,64,2560]{2,1,0:T(8,128)(2,1)S(1)} %collective-permute-done.70.refs_2_), channel_id=1, source_target_pairs={{0,4},{4,0},{8,12},{12,8},{16,20},{20,16},{24,28},{28,24},{1,5},{5... | collective-permute-start | bytes 1966088 | tf_op jit(solution)/shard_map/ppermute | solution.py:56
  394.6 12.2 %collective-permute-start.74 = (bf16[64,2560]{1,0:T(8,128)(2,1)S(1)}, bf16[64,2560]{1,0:T(8,128)(2,1)S(1)}, u32[]{:S(2)}, u32[]{:S(2)}) collective-permute-start(bf16[64,2560]{1,0:T(8,128)(2,1)S(1)} %slice_bitcast_fusion.3), channel_id=1, source_target_pairs={{0,16},{4,12},{8,24},{12,4},{16,0},{20,28},{24,8},{28,20},{1,17},{... | collective-permute-start | bytes 983048 | tf_op jit(solution)/shard_map/ppermute | solution.py:64
  407.3 8.6 %collective-permute-start.72 = (bf16[2,144,512]{2,1,0:T(8,128)(2,1)S(1)}, bf16[2,144,512]{2,1,0:T(8,128)(2,1)S(1)}, u32[]{:S(2)}, u32[]{:S(2)}) collective-permute-start(bf16[2,144,512]{2,1,0:T(8,128)(2,1)S(1)} %collective-permute-done.67.refs_2_), channel_id=1, source_target_pairs={{0,4},{4,0},{8,12},{12,8},{16,20},{20,16},{24,28},{28,24},{1,5},{5... | collective-permute-start | bytes 884744 | tf_op jit(solution)/shard_map/ppermute | solution.py:56
  407.5 8.3 %collective-permute-start.77 = (bf16[64,1536]{1,0:T(8,128)(2,1)S(1)}, bf16[64,1536]{1,0:T(8,128)(2,1)S(1)}, u32[]{:S(2)}, u32[]{:S(2)}) collective-permute-start(bf16[64,1536]{1,0:T(8,128)(2,1)S(1)} %slice_bitcast_fusion.6), channel_id=1, source_target_pairs={{0,16},{4,12},{8,24},{12,4},{16,0},{20,28},{24,8},{28,20},{1,17},{... | collective-permute-start | bytes 589832 | tf_op jit(solution)/shard_map/ppermute | solution.py:64
  412.0 10.2 %collective-permute-start.80 = (bf16[2,64,1536]{2,1,0:T(8,128)(2,1)S(1)}, bf16[2,64,1536]{2,1,0:T(8,128)(2,1)S(1)}, u32[]{:S(2)}, u32[]{:S(2)}) collective-permute-start(bf16[2,64,1536]{2,1,0:T(8,128)(2,1)S(1)} %collective-permute-done.75.refs_2_), channel_id=1, source_target_pairs={{0,4},{4,0},{8,12},{12,8},{16,20},{20,16},{24,28},{28,24},{1,5},{5... | collective-permute-start | bytes 1179656 | tf_op jit(solution)/shard_map/ppermute | solution.py:56
  415.8 6.4 %collective-permute-start.81 = (bf16[64,1536]{1,0:T(8,128)(2,1)S(1)}, bf16[64,1536]{1,0:T(8,128)(2,1)S(1)}, u32[]{:S(2)}, u32[]{:S(2)}) collective-permute-start(bf16[64,1536]{1,0:T(8,128)(2,1)S(1)} %collective-permute-done.77.refs_4_), channel_id=1, source_target_pairs={{0,4},{4,0},{8,12},{12,8},{16,20},{20,16},{24,28},{28,24},{1,5},{5... | collective-permute-start | bytes 589832 | tf_op jit(solution)/shard_map/ppermute | solution.py:56
  (140 other events, 1254.3 us)

commit v5 on v4

--- a/solution.py
+++ b/solution.py
@@ -27,7 +27,7 @@
 
 
 def takes(microseconds):
-    flops = int(microseconds * 1.3 * 1e9)
+    flops = int(microseconds * 1.8 * 1e9)
     return pl.CostEstimate(flops=flops, transcendentals=0, bytes_accessed=1)
 
 
@@ -480,7 +480,7 @@
         ],
         out_specs=pl.BlockSpec((rows, 128), lambda h: (0, h)),
         compiler_params=pltpu.CompilerParams(vmem_limit_bytes=8 * MB),
-        cost_estimate=takes(9),
+        cost_estimate=takes(4),
         name="variable_forward",
     )(pixels, same, keys_rows, table_t)
 
@@ -968,12 +968,15 @@
     spread_a.last_step()
     parts_a = spread_a.parts()
     table, table_t = arrange(parts_a, spot)
+    (agg_out_w,) = assemble([agg_out_weight], parts_a, spot)
+    order.mark(table_t)
+    order.mark(agg_out_w)
     narrow_c.second_step()
     spread_b.corner_step()
     merged = variable_forward(pixels, same, keys_rows, order.hold(table_t))
     order.mark(merged)
     merged_there = over_core(merged)
-    (agg_out_w,) = assemble([agg_out_weight], parts_a, spot)
+    spread_b.last_step()
     patch_state = dot(merged, agg_out_w) + agg_out_b
     unit_one, inverse_one = normalise(patch_state)
     normed = (unit_one * gain_one + bias_one).astype(bf16)
@@ -981,7 +984,6 @@
     merged_there = order.hold(merged_there)
     spread_c = Spread(narrow_c.bundle(), order)
     narrow_d = Narrow(order.hold(piece_d), order)
-    spread_b.last_step()
     spread_c.near_step()
     normed_there = over_core(normed)
     qkv_w, attn_out_w = assemble([qkv_weight, attn_out_weight], spread_b.parts(), spot)
@@ -1052,11 +1054,10 @@
     ke_got = swap_narrow(take(ke_two, where.other_high, 0), 2)
     attended_grad = order.hold(attended_grad)
     project_grad = attention_back(project, attended_grad, logs, seg_row, seg_col, pad_col)
-    order.mark(project_grad)
-    reduce_d.step()
-    project_other = other_half(order.hold(project_grad))
+    project_other = other_half(project_grad)
     order.mark(project_other)
     project_got = over_core(project_other)
+    reduce_d.step()
     reduce_c.step()
     ke_own = add_two(take(ke_two, where.high, 0), order.hold(ke_got))
     order.mark(ke_own)
@@ -1071,12 +1072,13 @@
     reduce_d.step()
     merged_grad = dot_nt(order.hold(state_grad), agg_out_w).astype(bf16)
     order.mark(merged_grad)
+    reduce_c.step()
     merged_grad = order.hold(merged_grad)
     cross, zed, pixel_grad = variable_back(pixels, same, keys_rows, keys_cols, table, merged_grad)
     order.mark(cross)
-    reduce_c.step()
     reduce_d.step()
     spread_d = Spread(reduce_d.total, order)
+    reduce_c.step()
     reduce_b.step()
     grad_a = grad_of(merged, merged_there, *order.hold(half(state_grad), state_got))
     order.mark(grad_a)
@@ -1107,19 +1109,21 @@
     order.mark(grad_a)
     reduce_a = ReduceShared(grad_a[None], where, order)
     spread_d.near_step()
-    reduce_c.step()
-    reduce_a.step()
     reduce_b.step()
     reduce_c.step()
     spread_c = Spread(reduce_c.total, order)
+    reduce_a.step()
     spread_d.corner_step()
+    reduce_b.step()
     reduce_a.step()
+    result = (residual + dot(order.hold(hidden), mlp_out_w) + mlp_out_b).astype(bf16)
+    order.mark(result)
+    reduce_b.step()
+    spread_b = Spread(reduce_b.total, order)
     spread_c.near_step()
     reduce_a.step()
-    reduce_b.step()
     spread_d.last_step()
-    result = (residual + dot(order.hold(hidden), mlp_out_w) + mlp_out_b).astype(bf16)
-    order.mark(result)
+    spread_b.near_step()
     patches_grad = lax.dot_general(
         order.hold(pixel_grad),
         chooser.astype(f32),
@@ -1130,24 +1134,20 @@
     order.mark(patches_grad)
     reduce_a.step()
     spread_a = Spread(reduce_a.total, order)
-    reduce_b.step()
-    spread_b = Spread(reduce_b.total, order)
+    spread_c.corner_step()
     spread_a.near_step()
-    spread_b.near_step()
-    spread_c.corner_step()
+    spread_b.corner_step()
     (grad_mlp_out_w,) = place(spread_d.parts(), [(D, D)], spot)
     order.mark(grad_mlp_out_w)
+    spread_c.last_step()
     spread_a.corner_step()
-    spread_b.corner_step()
-    spread_c.last_step()
-    spread_a.last_step()
+    spread_b.last_step()
     grad_mlp_in_w, grad_attn_out_w = place(spread_c.parts(), [(shard, 4 * D), (shard, D)], spot)
     order.mark(grad_mlp_in_w)
-    spread_b.last_step()
+    spread_a.last_step()
+    (grad_qkv_w,) = place(spread_b.parts(), [(shard, 3 * D)], spot)
+    order.mark(grad_qkv_w)
     grad_agg_out_w, cross, rest = place(spread_a.parts(), [(shard, D)], spot, shared=True)
-    order.mark(cross)
-    (grad_qkv_w,) = place(spread_b.parts(), [(shard, 3 * D)], spot)
-
     finished = finish(
         spot, cross, rest, value_weight, embed_rows.T, key_query_t.T, query_full, ke_own
     )

time: 430 us -> 414 us (0.963)
  waiting for transfers between devices: 111 us -> 98.2 us
  local copies, waits for them, and re-layouts: 48.8 us -> 40.1 us
  Pallas kernels: 123 us -> 128 us
    ppermute x20, waiting for transfers between devices: 40.9 us -> 30.7 us  [swap_narrow(): return lax.ppermute(a, 'narrow', [(i, i ^ bits) for i in range(size)])]
    ppermute x12, waiting for transfers between devices: 28.9 us -> 21.5 us  [over_first(): return lax.ppermute(a, 'wide', wide_pairs(lambda i: 4 if i & 1 else 2))]
    ppermute x12, waiting for transfers between devices: 35.4 us -> 40.7 us  [over_second(): return lax.ppermute(a, 'wide', wide_pairs(lambda i: 2 if i & 1 else 4))]
    unnamed x255, local copies, waits for them, and re-layouts: 23.1 us -> 18.1 us
    dynamic_slice x10 -> x9, local copies, waits for them, and re-layouts: 14.6 us -> 13.3 us  [rows_from(): lax.dynamic_slice_in_dim(a, start, count, axis, allow_negative_indices=Fa...]
  transfers between devices with their start and end apart: 82 -> 82, of which waited for: 31 -> 30; matrix products, arithmetic and copies ran while one was open for 24% -> 23% of each run, Pallas kernels for 28% -> 30%
where the time goes in v5:
time: 414 us; the launch traced here: 409 us
  Pallas kernels  128 us (31%)
  waiting for transfers between devices  98.2 us (24%)
  starting transfers between devices  63.9 us (15%)
  matrix products  50.6 us (12%)
  local copies, waits for them, and re-layouts  40.1 us (10%)
  other arithmetic  25.5 us (6%)
    ppermute x12, waiting for transfers between devices, over_second(): return lax.ppermute(a, 'wide', wide_pairs(lambda i: 2 if i & 1 else 4))  40.7 us
    ppermute x20, waiting for transfers between devices, swap_narrow(): return lax.ppermute(a, 'narrow', [(i, i ^ bits) for i in range(size)])  30.7 us
    dot_general x10, matrix products, dot_tn(): lax.dot_general(a, b, (((0,), (0,)), ((), ())), preferred_element_type=f32)  24 us
    ppermute x20, starting transfers between devices, swap_narrow(): return lax.ppermute(a, 'narrow', [(i, i ^ bits) for i in range(size)])  21.7 us
    ppermute x12, waiting for transfers between devices, over_first(): return lax.ppermute(a, 'wide', wide_pairs(lambda i: 4 if i & 1 else 2))  21.5 us
    unnamed x255, local copies, waits for them, and re-layouts  18.1 us
    pallas_call x10, Pallas kernels, add_split(): pl.pallas_call(add_split_kernel, out_shape=[out, out], grid_spec=pltpu.Pr...  17.2 us
    pallas_call x1, Pallas kernels, attention_back(): pl.pallas_call(attention_back_kernel, out_shape=jax.ShapeDtypeStruct((row...  16.5 us
  transfers between devices with their start and end apart: 82, of which 30 were waited for; matrix products, arithmetic and copies ran while one was open for 23% of the time, Pallas kernels for 30%

profile of v5, /device:TPU:0, one launch (start us, length us, event | category | flops | bytes accessed | tf_op | source)
XLA Modules:
  0.0 409.2 jit_solution(17229063030111091267)
XLA Ops:
  3.4 4.1 %collective-permute-start.2 = (bf16[32,4096]{1,0:T(8,128)(2,1)S(1)}, bf16[32,4096]{1,0:T(8,128)(2,1)S(1)}, u32[]{:S(2)}, u32[]{:S(2)}) collective-permute-start(bf16[32,4096]{1,0:T(8,128)(2,1)S(1)} %get-tuple-element.499), channel_id=1, source_target_pairs={{0,2},{1,3},{2,0},{3,1},{4,6},{5,7},{6,4},{7,5},{8,10},{9,11},{10,... | collective-permute-start | bytes 786440 | tf_op jit(solution)/shard_map/ppermute | solution.py:74
  10.1 3.0 collective-permute-start
  17.3 1.8 constant_dynamic-slice_fusion.10
  19.0 1.8 constant_dynamic-slice_fusion.11
  31.8 1.8 collective-permute-start.4
  36.9 2.0 convolution_convert_fusion.4.pixels_ref
  42.4 8.7 %collective-permute-done.9 = bf16[2,32,4096]{2,1,0:T(8,128)(2,1)S(1)} collective-permute-done((bf16[2,32,4096]{2,1,0:T(8,128)(2,1)S(1)}, bf16[2,32,4096]{2,1,0:T(8,128)(2,1)S(1)}, u32[]{:S(2)}, u32[]{:S(2)}) %collective-permute-start.9) | collective-permute-done | bytes 524320 | tf_op jit(solution)/shard_map/ppermute | solution.py:74
  52.9 7.7 %collective-permute-done.10.refs_2_.refs_3_ = bf16[2,4,32,1024]{3,2,1,0:T(8,128)(2,1)S(1)} collective-permute-done((bf16[2,4,32,1024]{3,2,1,0:T(8,128)(2,1)S(1)}, bf16[2,4,32,1024]{3,2,1,0:T(8,128)(2,1)S(1)}, u32[]{:S(2)}, u32[]{:S(2)}) %collective-permute-start.10) | collective-permute-done | bytes 524320 | tf_op jit(solution)/shard_map/ppermute | solution.py:60
  69.9 3.7 assemble.4
  75.0 2.6 arrange.1
  77.6 5.1 %collective-permute-done.16 = bf16[32,4096]{1,0:T(8,128)(2,1)} collective-permute-done((bf16[32,4096]{1,0:T(8,128)(2,1)}, bf16[32,4096]{1,0:T(8,128)(2,1)}, u32[]{:S(2)}, u32[]{:S(2)}) %collective-permute-start.16) | collective-permute-done | bytes 262176 | tf_op jit(solution)/shard_map/ppermute | solution.py:74
  86.9 9.0 %variable_forward.1 = bf16[512,1024]{1,0:T(8,128)(2,1)S(1)} custom-call(bf16[256,512]{1,0:T(8,128)(2,1)S(1)} %copy-done.50, f32[256,256]{1,0:T(8,128)S(1)} %copy-done.25, f32[8,2,256]{2,1,0:T(2,128)S(1)} %add.206.keys_ref, bf16[1024,256]{1,0:T(8,128)(2,1)S(1)} %copy-done.43), custom_call_target="tpu_custom_call" | custom-call | flops 7200000000 | bytes 1 | tf_op jit(solution)/shard_map/variable_forward/pallas_call | solution.py:471
  99.8 2.4 fusion.38
  106.9 1.7 collective-permute-start.26
  108.7 4.1 assemble.5
  112.8 3.7 convolution_convert_fusion.q_ref.k_ref.v_ref
  116.5 2.8 collective-permute-done.24
  119.5 12.0 %attention.1 = (bf16[512,1024]{1,0:T(8,128)(2,1)S(1)}, f32[8,2,512]{2,1,0:T(2,128)S(1)}) custom-call(bf16[512,3072]{1,0:T(8,128)(2,1)S(1)} %convolution_convert_fusion.q_ref.k_ref.v_ref, bf16[512,3072]{1,0:T(8,128)(2,1)S(1)} %convolution_convert_fusion.q_ref.k_ref.v_ref, bf16[512,3072]{1,0:T(8,128)(2,1)S(1)} %convolution_convert_fusion.q_ref.k_ref.v_ref, ...), custom_call_target="tpu_custom_call" | custom-call | flops 22499999744 | bytes 1 | tf_op jit(solution)/shard_map/attention/pallas_call | solution.py:595
  133.1 1.8 collective-permute-start.30
  137.9 7.3 %collective-permute-done.30.refs_5_ = bf16[3,32,4096]{2,1,0:T(8,128)(2,1)S(1)} collective-permute-done((bf16[3,32,4096]{2,1,0:T(8,128)(2,1)S(1)}, bf16[3,32,4096]{2,1,0:T(8,128)(2,1)S(1)}, u32[]{:S(2)}, u32[]{:S(2)}) %collective-permute-start.30) | collective-permute-done | bytes 786464 | tf_op jit(solution)/shard_map/ppermute | solution.py:64
  147.5 2.3 assemble.6.weight.w_in
  149.9 10.0 %mlp_in.1 = (bf16[512,4096]{1,0:T(8,128)(2,1)S(1)}, bf16[512,4096]{1,0:T(8,128)(2,1)S(1)}) custom-call(bf16[512,1024]{1,0:T(8,128)(2,1)S(1)} %add_convert_fusion.7.rows_ref, bf16[1024,4096]{1,0:T(8,128)(2,1)S(1)} %assemble.6.weight.w_in, f32[1,4096]{1,0:T(1,128)S(1)} %bitcast.213), custom_call_target="tpu_custom_call" | custom-call | flops 19800000512 | bytes 1 | tf_op jit(solution)/shard_map/mlp_in/pallas_call | solution.py:686
  159.8 3.2 copy-done.57
  163.0 2.6 collective-permute-done.33.refs_3_
  165.7 1.8 collective-permute-start.35
  167.9 9.8 %collective-permute-done.35.refs_5_ = bf16[3,128,1024]{2,1,0:T(8,128)(2,1)S(1)} collective-permute-done((bf16[3,128,1024]{2,1,0:T(8,128)(2,1)S(1)}, bf16[3,128,1024]{2,1,0:T(8,128)(2,1)S(1)}, u32[]{:S(2)}, u32[]{:S(2)}) %collective-permute-start.35) | collective-permute-done | bytes 786464 | tf_op jit(solution)/shard_map/ppermute | solution.py:64
  181.6 13.0 %mlp_back.1 = (bf16[512,2048]{1,0:T(8,128)(2,1)S(1)}, bf16[512,2048]{1,0:T(8,128)(2,1)}, f32[512,1024]{1,0:T(8,128)S(1)}, f32[4,1,1024]{2,1,0:T(1,128)S(1)}) custom-call(s32[1]{0:T(128)} %bitcast.3.core, bf16[512,1024]{1,0:T(8,128)(2,1)S(1)} %copy-done.7, bf16[4096,1024]{1,0:T(8,128)(2,1)S(1)} %assemble.7.w_out, bf16[1024,4096]{1,0:T(8,128)(2,1)S(1)} %bitcast.246, ...), custom_call_target="tpu_custom_call" | custom-call | flops 27900000256 | bytes 1 | tf_op jit(solution)/shard_map/mlp_back/pallas_call | solution.py:725
  195.1 5.1 %fusion.48 = f32[4096,512]{1,0:T(8,128)S(1)} fusion(bf16[512,4096]{1,0:T(8,128)(2,1)} %collective-permute-done.37, bf16[512,512]{1,0:T(8,128)(2,1)} %collective-permute-done.38), kind=kOutput, calls=%fused_computation.213 | convolution fusion | flops 2147483648 | bytes 13107200 | tf_op jit(solution)/shard_map/dot_general | solution.py:43
  200.3 2.6 add_convert_fusion.1
  203.0 3.0 pick_first.4
  207.5 2.1 copy.71
  209.7 2.6 multiply_reduce_fusion
  212.3 2.3 fusion.41
  216.9 4.2 %fusion.49 = f32[1024,2048]{1,0:T(8,128)S(1)} fusion(bf16[512,1024]{1,0:T(8,128)(2,1)S(1)} %copy-done.112, bf16[512,2048]{1,0:T(8,128)(2,1)} %collective-permute-done.40), kind=kOutput, calls=%fused_computation.214 | convolution fusion | flops 2147483648 | bytes 11534336 | tf_op jit(solution)/shard_map/dot_general | solution.py:43
  221.2 2.6 add_convert_fusion
  226.2 2.3 pick_first.5
  232.4 4.2 %add_split.10 = (bf16[4,256,512]{2,1,0:T(8,128)(2,1)}, bf16[4,256,512]{2,1,0:T(8,128)(2,1)S(1)}) custom-call(s32[2]{0:T(128)S(1)} %get-tuple-element.317.bits, bf16[4,2,2,256,512]{4,3,2,1,0:T(8,128)(2,1)S(1)} %bitcast.186, bf16[4,2,256,512]{3,2,1,0:T(8,128)(2,1)} %collective-permute-done.42.got_sent.got_kept, bf16[4,2,2,256,512]{4,3,2,1,0:T(8,128)(2,1)S(1)} %bitcast.187, ...), custom_call_target="tpu_custom_call" | custom-call | flops 4499999744 | bytes 1 | tf_op jit(solution)/shard_map/add_split/pallas_call | solution.py:290
  237.6 1.7 collective-permute-start.46
  240.0 16.5 %attention_back.1 = bf16[512,3072]{1,0:T(8,128)(2,1)S(1)} custom-call(bf16[512,3072]{1,0:T(8,128)(2,1)S(1)} %copy-done.62, bf16[512,3072]{1,0:T(8,128)(2,1)S(1)} %copy-done.62, bf16[512,3072]{1,0:T(8,128)(2,1)S(1)} %copy-done.62, bf16[512,1024]{1,0:T(8,128)(2,1)S(1)} %convolution_convert_fusion.2.grad_ref, f32[8,2,512]{2,1,0:T(2,128)S(1)} %get-tuple-element.350.log_ref, ...), custom_call_target="tpu_custom_call" | custom-call | flops 29699999744 | bytes 1 | tf_op jit(solution)/shard_map/attention_back/pallas_call | solution.py:654
  256.6 3.3 constant_dynamic-slice_fusion.4
  261.3 2.6 collective-permute-done.46
  267.2 5.5 %collective-permute-done.45.got_sent.got_kept = bf16[4,2,64,2560]{3,2,1,0:T(8,128)(2,1)} collective-permute-done((bf16[4,2,64,2560]{3,2,1,0:T(8,128)(2,1)}, bf16[4,2,64,2560]{3,2,1,0:T(8,128)(2,1)}, u32[]{:S(2)}, u32[]{:S(2)}) %collective-permute-start.45) | collective-permute-done | bytes 2621472 | tf_op jit(solution)/shard_map/ppermute | solution.py:60
  272.7 4.4 %add_split.12 = (bf16[4,64,2560]{2,1,0:T(8,128)(2,1)}, bf16[4,64,2560]{2,1,0:T(8,128)(2,1)S(1)}) custom-call(s32[2]{0:T(128)S(1)} %get-tuple-element.317.bits, bf16[4,2,2,64,2560]{4,3,2,1,0:T(8,128)(2,1)S(1)} %bitcast.191, bf16[4,2,64,2560]{3,2,1,0:T(8,128)(2,1)} %collective-permute-done.45.got_sent.got_kept, bf16[4,2,2,64,2560]{4,3,2,1,0:T(8,128)(2,1)S(1)} %bitcast.192, ...), custom_call_target="tpu_custom_call" | custom-call | flops 4499999744 | bytes 1 | tf_op jit(solution)/shard_map/add_split/pallas_call | solution.py:290
  279.7 3.4 fusion.51
  283.1 2.0 add_convert_fusion.2
  285.2 1.9 pick_first.6
  288.9 4.0 multiply_reduce_fusion.1
  297.7 3.3 convolution_convert_fusion.1.grad_ref
  303.0 14.5 %variable_back.1 = (bf16[512,512]{1,0:T(8,128)(2,1)S(1)}, f32[16,256]{1,0:T(8,128)S(1)}, f32[256,512]{1,0:T(8,128)S(1)}) custom-call(bf16[256,512]{1,0:T(8,128)(2,1)S(1)} %copy-done.51, f32[256,256]{1,0:T(8,128)S(1)} %copy-done.26, f32[8,2,256]{2,1,0:T(2,128)S(1)} %add.206.keys_ref, f32[8,256,2]{2,1,0:T(8,128)S(1)} %bitcast.197, ...), custom_call_target="tpu_custom_call" | custom-call | flops 1800000000 | bytes 1 | tf_op jit(solution)/shard_map/variable_back/pallas_call | solution.py:535
  319.4 2.6 collective-permute-done.51
  323.9 3.1 add_split.16
  328.1 1.8 fusion.52
  333.3 11.6 %collective-permute-done.56 = bf16[4,64,1536]{2,1,0:T(8,128)(2,1)S(1)} collective-permute-done((bf16[4,64,1536]{2,1,0:T(8,128)(2,1)S(1)}, bf16[4,64,1536]{2,1,0:T(8,128)(2,1)S(1)}, u32[]{:S(2)}, u32[]{:S(2)}) %collective-permute-start.56) | collective-permute-done | bytes 786464 | tf_op jit(solution)/shard_map/ppermute | solution.py:64
  348.7 2.4 collective-permute-done.60.refs_2_
  355.9 1.9 collective-permute-start.61
  359.5 5.5 %add_convert_fusion.3 = bf16[512,1024]{1,0:T(8,128)(2,1)} fusion(f32[512,1024]{1,0:T(8,128)S(1)} %copy-done.65, bf16[512,4096]{1,0:T(8,128)(2,1)S(1)} %copy-done.3, bf16[4096,1024]{1,0:T(8,128)(2,1)S(1)} %bitcast.244, f32[1024]{0:T(1024)S(1)} %bitcast.284), kind=kOutput, calls=%fused_computation.5 | convolution fusion | flops 4296540160 | bytes 15732736 | tf_op jit(solution)/shard_map/dot_general | solution.py:35
  365.0 2.3 collective-permute-done.61
  371.3 7.0 %collective-permute-done.66 = bf16[144,512]{1,0:T(8,128)(2,1)S(1)} collective-permute-done((bf16[144,512]{1,0:T(8,128)(2,1)S(1)}, bf16[144,512]{1,0:T(8,128)(2,1)S(1)}, u32[]{:S(2)}, u32[]{:S(2)}) %collective-permute-start.66) | collective-permute-done | bytes 147488 | tf_op jit(solution)/shard_map/ppermute | solution.py:74
  383.0 2.8 place.4
  385.9 3.1 collective-permute-done.70.refs_4_
  391.3 3.6 collective-permute-done.78.refs_4_
  396.4 3.3 place.5
  400.2 2.4 place.6
  404.3 2.7 finish.1
  (532 shorter events, 126.3 us)
Async XLA Ops:
  3.4 23.2 %collective-permute-start.2 = (bf16[32,4096]{1,0:T(8,128)(2,1)S(1)}, bf16[32,4096]{1,0:T(8,128)(2,1)S(1)}, u32[]{:S(2)}, u32[]{:S(2)}) collective-permute-start(bf16[32,4096]{1,0:T(8,128)(2,1)S(1)} %get-tuple-element.499), channel_id=1, source_target_pairs={{0,2},{1,3},{2,0},{3,1},{4,6},{5,7},{6,4},{7,5},{8,10},{9,11},{10,... | collective-permute-start | bytes 786440 | tf_op jit(solution)/shard_map/ppermute | solution.py:74
  8.4 17.1 %collective-permute-start.3 = (bf16[32,1024]{1,0:T(8,128)(2,1)S(1)}, bf16[32,1024]{1,0:T(8,128)(2,1)S(1)}, u32[]{:S(2)}, u32[]{:S(2)}) collective-permute-start(bf16[32,1024]{1,0:T(8,128)(2,1)S(1)} %constant_dynamic-slice_fusion.12), channel_id=1, source_target_pairs={{0,2},{1,3},{2,0},{3,1},{4,6},{5,7},{6,4},{7,5},{8,10},{9,11},{10,... | collective-permute-start | bytes 196616 | tf_op jit(solution)/shard_map/ppermute | solution.py:74
  10.1 13.7 %collective-permute-start = (bf16[12,256]{1,0:T(8,128)(2,1)S(1)}, bf16[12,256]{1,0:T(8,128)(2,1)S(1)}, u32[]{:S(2)}, u32[]{:S(2)}) collective-permute-start(bf16[12,256]{1,0:T(8,128)(2,1)S(1)} %get-tuple-element.523.own), channel_id=1, source_target_pairs={{0,2},{1,3},{2,0},{3,1},{4,6},{5,7},{6,4},{7,5},{8,10},{9,11},{10,... | collective-permute-start | bytes 18440 | tf_op jit(solution)/shard_map/ppermute | solution.py:74
  26.1 15.2 %collective-permute-start.7 = (bf16[2,32,1024]{2,1,0:T(8,128)(2,1)}, bf16[2,32,1024]{2,1,0:T(8,128)(2,1)}, u32[]{:S(2)}, u32[]{:S(2)}) collective-permute-start(bf16[2,32,1024]{2,1,0:T(8,128)(2,1)} %pad_maximum_fusion.23), channel_id=1, source_target_pairs={{0,1},{1,0},{2,3},{3,2},{4,5},{5,4},{6,7},{7,6},{8,9},{9,8},{10,11... | collective-permute-start | bytes 393224 | tf_op jit(solution)/shard_map/ppermute | solution.py:74
  31.8 7.8 %collective-permute-start.4 = (bf16[40,1024]{1,0:T(8,128)(2,1)S(1)}, bf16[40,1024]{1,0:T(8,128)(2,1)S(1)}, u32[]{:S(2)}, u32[]{:S(2)}) collective-permute-start(bf16[40,1024]{1,0:T(8,128)(2,1)S(1)} %maximum_maximum_fusion.2), channel_id=1, source_target_pairs={{0,1},{1,2},{2,3},{3,0},{4,5},{5,6},{6,7},{7,4},{8,9},{9,10},{10,1... | collective-permute-start | bytes 245768 | tf_op jit(solution)/shard_map/ppermute | solution.py:69
  36.0 15.1 %collective-permute-start.9 = (bf16[2,32,4096]{2,1,0:T(8,128)(2,1)S(1)}, bf16[2,32,4096]{2,1,0:T(8,128)(2,1)S(1)}, u32[]{:S(2)}, u32[]{:S(2)}) collective-permute-start(bf16[2,32,4096]{2,1,0:T(8,128)(2,1)S(1)} %pad_maximum_fusion.10), channel_id=1, source_target_pairs={{0,1},{1,0},{2,3},{3,2},{4,5},{5,4},{6,7},{7,6},{8,9},{9,8},{10,11... | collective-permute-start | bytes 1572872 | tf_op jit(solution)/shard_map/ppermute | solution.py:74
  42.3 9.0 %collective-permute-start.8 = (bf16[4,32,1024]{2,1,0:T(8,128)(2,1)S(1)}, bf16[4,32,1024]{2,1,0:T(8,128)(2,1)S(1)}, u32[]{:S(2)}, u32[]{:S(2)}) collective-permute-start(bf16[4,32,1024]{2,1,0:T(8,128)(2,1)S(1)} %get-tuple-element.267.refs_0_.refs_1_), channel_id=1, source_target_pairs={{0,4},{4,0},{8,12},{12,8},{16,20},{20,16},{24,28},{28,24},{1,5},{5... | collective-permute-start | bytes 786440 | tf_op jit(solution)/shard_map/ppermute | solution.py:56
  51.2 11.0 %collective-permute-start.13 = (bf16[3,32,4096]{2,1,0:T(8,128)(2,1)S(1)}, bf16[3,32,4096]{2,1,0:T(8,128)(2,1)S(1)}, u32[]{:S(2)}, u32[]{:S(2)}) collective-permute-start(bf16[3,32,4096]{2,1,0:T(8,128)(2,1)S(1)} %get-tuple-element.284.refs_2_), channel_id=1, source_target_pairs={{0,4},{4,0},{8,12},{12,8},{16,20},{20,16},{24,28},{28,24},{1,5},{5... | collective-permute-start | bytes 2359304 | tf_op jit(solution)/shard_map/ppermute | solution.py:56
  51.4 9.2 %collective-permute-start.10 = (bf16[2,4,32,1024]{3,2,1,0:T(8,128)(2,1)S(1)}, bf16[2,4,32,1024]{3,2,1,0:T(8,128)(2,1)S(1)}, u32[]{:S(2)}, u32[]{:S(2)}) collective-permute-start(bf16[2,4,32,1024]{3,2,1,0:T(8,128)(2,1)S(1)} %pad_maximum_fusion.11), channel_id=1, source_target_pairs={{0,8},{4,20},{8,0},{12,28},{16,24},{20,4},{24,16},{28,12},{1,9},{5... | collective-permute-start | bytes 1572872 | tf_op jit(solution)/shard_map/ppermute | solution.py:60
  60.6 8.1 %collective-permute-start.11 = (bf16[2,4,32,1024]{3,2,1,0:T(8,128)(2,1)S(1)}, bf16[2,4,32,1024]{3,2,1,0:T(8,128)(2,1)S(1)}, u32[]{:S(2)}, u32[]{:S(2)}) collective-permute-start(bf16[2,4,32,1024]{3,2,1,0:T(8,128)(2,1)S(1)} %collective-permute-done.10.refs_2_.refs_3_), channel_id=1, source_target_pairs={{0,4},{4,0},{8,12},{12,8},{16,20},{20,16},{24,28},{28,24},{1,5},{5... | collective-permute-start | bytes 1572872 | tf_op jit(solution)/shard_map/ppermute | solution.py:56
  64.4 20.7 %collective-permute-start.15 = (bf16[2,3,32,4096]{3,2,1,0:T(8,128)(2,1)}, bf16[2,3,32,4096]{3,2,1,0:T(8,128)(2,1)}, u32[]{:S(2)}, u32[]{:S(2)}) collective-permute-start(bf16[2,3,32,4096]{3,2,1,0:T(8,128)(2,1)} %pad_maximum_fusion.1), channel_id=1, source_target_pairs={{0,8},{4,20},{8,0},{12,28},{16,24},{20,4},{24,16},{28,12},{1,9},{5... | collective-permute-start | bytes 4718600 | tf_op jit(solution)/shard_map/ppermute | solution.py:60
  67.2 15.5 %collective-permute-start.16 = (bf16[32,4096]{1,0:T(8,128)(2,1)}, bf16[32,4096]{1,0:T(8,128)(2,1)}, u32[]{:S(2)}, u32[]{:S(2)}) collective-permute-start(bf16[32,4096]{1,0:T(8,128)(2,1)} %constant_dynamic-slice_fusion.11), channel_id=1, source_target_pairs={{0,2},{1,3},{2,0},{3,1},{4,6},{5,7},{6,4},{7,5},{8,10},{9,11},{10,... | collective-permute-start | bytes 786440 | tf_op jit(solution)/shard_map/ppermute | solution.py:74
  83.6 16.2 %collective-permute-start.20 = (bf16[2,32,4096]{2,1,0:T(8,128)(2,1)S(1)}, bf16[2,32,4096]{2,1,0:T(8,128)(2,1)S(1)}, u32[]{:S(2)}, u32[]{:S(2)}) collective-permute-start(bf16[2,32,4096]{2,1,0:T(8,128)(2,1)S(1)} %pad_maximum_fusion.12), channel_id=1, source_target_pairs={{0,1},{1,0},{2,3},{3,2},{4,5},{5,4},{6,7},{7,6},{8,9},{9,8},{10,11... | collective-permute-start | bytes 1572872 | tf_op jit(solution)/shard_map/ppermute | solution.py:74
  86.4 13.4 %collective-permute-start.18 = (bf16[3,32,4096]{2,1,0:T(8,128)(2,1)S(1)}, bf16[3,32,4096]{2,1,0:T(8,128)(2,1)}, u32[]{:S(2)}, u32[]{:S(2)}) collective-permute-start(bf16[3,32,4096]{2,1,0:T(8,128)(2,1)S(1)} %slice_bitcast_fusion.2), channel_id=1, source_target_pairs={{0,16},{4,12},{8,24},{12,4},{16,0},{20,28},{24,8},{28,20},{1,17},{... | collective-permute-start | bytes 2359304 | tf_op jit(solution)/shard_map/ppermute | solution.py:64
  97.4 11.3 %collective-permute-start.17 = (bf16[2,3,32,4096]{3,2,1,0:T(8,128)(2,1)}, bf16[2,3,32,4096]{3,2,1,0:T(8,128)(2,1)}, u32[]{:S(2)}, u32[]{:S(2)}) collective-permute-start(bf16[2,3,32,4096]{3,2,1,0:T(8,128)(2,1)} %collective-permute-done.15.refs_4_), channel_id=1, source_target_pairs={{0,4},{4,0},{8,12},{12,8},{16,20},{20,16},{24,28},{28,24},{1,5},{5... | collective-permute-start | bytes 4718600 | tf_op jit(solution)/shard_map/ppermute | solution.py:56
  103.9 15.6 %collective-permute-start.23 = (bf16[512,1024]{1,0:T(8,128)(2,1)}, bf16[512,1024]{1,0:T(8,128)(2,1)S(1)}, u32[]{:S(2)}, u32[]{:S(2)}) collective-permute-start(bf16[512,1024]{1,0:T(8,128)(2,1)} %add_convert_fusion.8), channel_id=1, source_target_pairs={{0,4},{4,0},{8,12},{12,8},{16,20},{20,16},{24,28},{28,24},{1,5},{5... | collective-permute-start | bytes 3145736 | tf_op jit(solution)/shard_map/ppermute | solution.py:56
  104.0 15.4 %collective-permute-start.24 = (bf16[128,1024]{1,0:T(8,128)(2,1)}, bf16[128,1024]{1,0:T(8,128)(2,1)S(1)}, u32[]{:S(2)}, u32[]{:S(2)}) collective-permute-start(bf16[128,1024]{1,0:T(8,128)(2,1)} %constant_dynamic-slice_fusion.10), channel_id=1, source_target_pairs={{0,2},{1,3},{2,0},{3,1},{4,6},{5,7},{6,4},{7,5},{8,10},{9,11},{10,... | collective-permute-start | bytes 786440 | tf_op jit(solution)/shard_map/ppermute | solution.py:74
  106.9 24.7 %collective-permute-start.26 = (bf16[2,3,32,4096]{3,2,1,0:T(8,128)(2,1)S(1)}, bf16[2,3,32,4096]{3,2,1,0:T(8,128)(2,1)S(1)}, u32[]{:S(2)}, u32[]{:S(2)}) collective-permute-start(bf16[2,3,32,4096]{3,2,1,0:T(8,128)(2,1)S(1)} %pad_maximum_fusion.2), channel_id=1, source_target_pairs={{0,8},{4,20},{8,0},{12,28},{16,24},{20,4},{24,16},{28,12},{1,9},{5... | collective-permute-start | bytes 4718600 | tf_op jit(solution)/shard_map/ppermute | solution.py:60
  119.4 13.5 %collective-permute-start.25 = (bf16[2,128,1024]{2,1,0:T(8,128)(2,1)S(1)}, bf16[2,128,1024]{2,1,0:T(8,128)(2,1)S(1)}, u32[]{:S(2)}, u32[]{:S(2)}) collective-permute-start(bf16[2,128,1024]{2,1,0:T(8,128)(2,1)S(1)} %pad_maximum_fusion.13), channel_id=1, source_target_pairs={{0,1},{1,0},{2,3},{3,2},{4,5},{5,4},{6,7},{7,6},{8,9},{9,8},{10,11... | collective-permute-start | bytes 1572872 | tf_op jit(solution)/shard_map/ppermute | solution.py:74
  131.6 15.9 %collective-permute-start.27 = (bf16[512,1024]{1,0:T(8,128)(2,1)S(1)}, bf16[512,1024]{1,0:T(8,128)(2,1)S(1)}, u32[]{:S(2)}, u32[]{:S(2)}) collective-permute-start(bf16[512,1024]{1,0:T(8,128)(2,1)S(1)} %get-tuple-element.300), channel_id=1, source_target_pairs={{0,4},{4,0},{8,12},{12,8},{16,20},{20,16},{24,28},{28,24},{1,5},{5... | collective-permute-start | bytes 3145736 | tf_op jit(solution)/shard_map/ppermute | solution.py:56
  133.1 12.1 %collective-permute-start.30 = (bf16[3,32,4096]{2,1,0:T(8,128)(2,1)S(1)}, bf16[3,32,4096]{2,1,0:T(8,128)(2,1)S(1)}, u32[]{:S(2)}, u32[]{:S(2)}) collective-permute-start(bf16[3,32,4096]{2,1,0:T(8,128)(2,1)S(1)} %slice_bitcast_fusion.1), channel_id=1, source_target_pairs={{0,16},{4,12},{8,24},{12,4},{16,0},{20,28},{24,8},{28,20},{1,17},{... | collective-permute-start | bytes 2359304 | tf_op jit(solution)/shard_map/ppermute | solution.py:64
  134.9 11.8 %collective-permute-start.29 = (bf16[2,3,32,4096]{3,2,1,0:T(8,128)(2,1)S(1)}, bf16[2,3,32,4096]{3,2,1,0:T(8,128)(2,1)S(1)}, u32[]{:S(2)}, u32[]{:S(2)}) collective-permute-start(bf16[2,3,32,4096]{3,2,1,0:T(8,128)(2,1)S(1)} %collective-permute-done.26.refs_3_), channel_id=1, source_target_pairs={{0,4},{4,0},{8,12},{12,8},{16,20},{20,16},{24,28},{28,24},{1,5},{5... | collective-permute-start | bytes 4718600 | tf_op jit(solution)/shard_map/ppermute | solution.py:56
  137.2 10.3 %collective-permute-start.28 = (bf16[512,1024]{1,0:T(8,128)(2,1)S(1)}, bf16[512,1024]{1,0:T(8,128)(2,1)S(1)}, u32[]{:S(2)}, u32[]{:S(2)}) collective-permute-start(bf16[512,1024]{1,0:T(8,128)(2,1)S(1)} %add_convert_fusion.7.rows_ref), channel_id=1, source_target_pairs={{0,4},{4,0},{8,12},{12,8},{16,20},{20,16},{24,28},{28,24},{1,5},{5... | collective-permute-start | bytes 3145736 | tf_op jit(solution)/shard_map/ppermute | solution.py:56
  145.2 20.4 %collective-permute-start.33 = (bf16[2,3,128,1024]{3,2,1,0:T(8,128)(2,1)S(1)}, bf16[2,3,128,1024]{3,2,1,0:T(8,128)(2,1)S(1)}, u32[]{:S(2)}, u32[]{:S(2)}) collective-permute-start(bf16[2,3,128,1024]{3,2,1,0:T(8,128)(2,1)S(1)} %pad_maximum_fusion.3), channel_id=1, source_target_pairs={{0,8},{4,20},{8,0},{12,28},{16,24},{20,4},{24,16},{28,12},{1,9},{5... | collective-permute-start | bytes 4718600 | tf_op jit(solution)/shard_map/ppermute | solution.py:60
  165.7 12.1 %collective-permute-start.35 = (bf16[3,128,1024]{2,1,0:T(8,128)(2,1)S(1)}, bf16[3,128,1024]{2,1,0:T(8,128)(2,1)S(1)}, u32[]{:S(2)}, u32[]{:S(2)}) collective-permute-start(bf16[3,128,1024]{2,1,0:T(8,128)(2,1)S(1)} %slice_bitcast_fusion), channel_id=1, source_target_pairs={{0,16},{4,12},{8,24},{12,4},{16,0},{20,28},{24,8},{28,20},{1,17},{... | collective-permute-start | bytes 2359304 | tf_op jit(solution)/shard_map/ppermute | solution.py:64
  167.4 12.0 %collective-permute-start.34 = (bf16[2,3,128,1024]{3,2,1,0:T(8,128)(2,1)S(1)}, bf16[2,3,128,1024]{3,2,1,0:T(8,128)(2,1)S(1)}, u32[]{:S(2)}, u32[]{:S(2)}) collective-permute-start(bf16[2,3,128,1024]{3,2,1,0:T(8,128)(2,1)S(1)} %collective-permute-done.33.refs_3_), channel_id=1, source_target_pairs={{0,4},{4,0},{8,12},{12,8},{16,20},{20,16},{24,28},{28,24},{1,5},{5... | collective-permute-start | bytes 4718600 | tf_op jit(solution)/shard_map/ppermute | solution.py:56
  167.4 27.7 %collective-permute-start.37 = (bf16[512,4096]{1,0:T(8,128)(2,1)S(1)}, bf16[512,4096]{1,0:T(8,128)(2,1)}, u32[]{:S(2)}, u32[]{:S(2)}) collective-permute-start(bf16[512,4096]{1,0:T(8,128)(2,1)S(1)} %get-tuple-element.403), channel_id=1, source_target_pairs={{0,4},{4,0},{8,12},{12,8},{16,20},{20,16},{24,28},{28,24},{1,5},{5... | collective-permute-start | bytes 12582920 | tf_op jit(solution)/shard_map/ppermute | solution.py:56
  178.9 16.2 %collective-permute-start.38 = (bf16[512,512]{1,0:T(8,128)(2,1)S(1)}, bf16[512,512]{1,0:T(8,128)(2,1)}, u32[]{:S(2)}, u32[]{:S(2)}) collective-permute-start(bf16[512,512]{1,0:T(8,128)(2,1)S(1)} %copy-done.91), channel_id=1, source_target_pairs={{0,4},{4,0},{8,12},{12,8},{16,20},{20,16},{24,28},{28,24},{1,5},{5... | collective-permute-start | bytes 1572872 | tf_op jit(solution)/shard_map/ppermute | solution.py:56
  194.6 22.3 %collective-permute-start.40 = (bf16[512,2048]{1,0:T(8,128)(2,1)}, bf16[512,2048]{1,0:T(8,128)(2,1)}, u32[]{:S(2)}, u32[]{:S(2)}) collective-permute-start(bf16[512,2048]{1,0:T(8,128)(2,1)} %get-tuple-element.330), channel_id=1, source_target_pairs={{0,4},{4,0},{8,12},{12,8},{16,20},{20,16},{24,28},{28,24},{1,5},{5... | collective-permute-start | bytes 6291464 | tf_op jit(solution)/shard_map/ppermute | solution.py:56
  206.0 26.4 %collective-permute-start.42 = (bf16[4,2,256,512]{3,2,1,0:T(8,128)(2,1)}, bf16[4,2,256,512]{3,2,1,0:T(8,128)(2,1)}, u32[]{:S(2)}, u32[]{:S(2)}) collective-permute-start(bf16[4,2,256,512]{3,2,1,0:T(8,128)(2,1)} %pick_first.4), channel_id=1, source_target_pairs={{0,8},{4,20},{8,0},{12,28},{16,24},{20,4},{24,16},{28,12},{1,9},{5... | collective-permute-start | bytes 6291464 | tf_op jit(solution)/shard_map/ppermute | solution.py:60
  215.2 8.6 %collective-permute-start.39 = (bf16[512,512]{1,0:T(8,128)(2,1)S(1)}, bf16[512,512]{1,0:T(8,128)(2,1)S(1)}, u32[]{:S(2)}, u32[]{:S(2)}) collective-permute-start(bf16[512,512]{1,0:T(8,128)(2,1)S(1)} %get-tuple-element.484), channel_id=1, source_target_pairs={{0,4},{4,0},{8,12},{12,8},{16,20},{20,16},{24,28},{28,24},{1,5},{5... | collective-permute-start | bytes 1572872 | tf_op jit(solution)/shard_map/ppermute | solution.py:56
  215.7 23.6 %collective-permute-start.41 = (bf16[2,256,256]{2,1,0:T(8,128)(2,1)S(1)}, bf16[2,256,256]{2,1,0:T(8,128)(2,1)S(1)}, u32[]{:S(2)}, u32[]{:S(2)}) collective-permute-start(bf16[2,256,256]{2,1,0:T(8,128)(2,1)S(1)} %dynamic-slice_bitcast_fusion), channel_id=1, source_target_pairs={{0,1},{1,0},{2,3},{3,2},{4,5},{5,4},{6,7},{7,6},{8,9},{9,8},{10,11... | collective-permute-start | bytes 786440 | tf_op jit(solution)/shard_map/ppermute | solution.py:74
  229.5 43.2 %collective-permute-start.45 = (bf16[4,2,64,2560]{3,2,1,0:T(8,128)(2,1)}, bf16[4,2,64,2560]{3,2,1,0:T(8,128)(2,1)}, u32[]{:S(2)}, u32[]{:S(2)}) collective-permute-start(bf16[4,2,64,2560]{3,2,1,0:T(8,128)(2,1)} %pick_first.5), channel_id=1, source_target_pairs={{0,8},{4,20},{8,0},{12,28},{16,24},{20,4},{24,16},{28,12},{1,9},{5... | collective-permute-start | bytes 7864328 | tf_op jit(solution)/shard_map/ppermute | solution.py:60
  237.6 26.3 %collective-permute-start.46 = (bf16[4,256,512]{2,1,0:T(8,128)(2,1)}, bf16[4,256,512]{2,1,0:T(8,128)(2,1)S(1)}, u32[]{:S(2)}, u32[]{:S(2)}) collective-permute-start(bf16[4,256,512]{2,1,0:T(8,128)(2,1)} %get-tuple-element.346), channel_id=1, source_target_pairs={{0,16},{4,12},{8,24},{12,4},{16,0},{20,28},{24,8},{28,20},{1,17},{... | collective-permute-start | bytes 3145736 | tf_op jit(solution)/shard_map/ppermute | solution.py:64
  259.9 19.7 %collective-permute-start.43 = (bf16[512,1536]{1,0:T(8,128)(2,1)}, bf16[512,1536]{1,0:T(8,128)(2,1)}, u32[]{:S(2)}, u32[]{:S(2)}) collective-permute-start(bf16[512,1536]{1,0:T(8,128)(2,1)} %get-tuple-element.479), channel_id=1, source_target_pairs={{0,4},{4,0},{8,12},{12,8},{16,20},{20,16},{24,28},{28,24},{1,5},{5... | collective-permute-start | bytes 4718600 | tf_op jit(solution)/shard_map/ppermute | solution.py:56
  260.5 19.1 %collective-permute-start.44 = (bf16[256,256]{1,0:T(8,128)(2,1)S(1)}, bf16[256,256]{1,0:T(8,128)(2,1)S(1)}, u32[]{:S(2)}, u32[]{:S(2)}) collective-permute-start(bf16[256,256]{1,0:T(8,128)(2,1)S(1)} %dynamic-slice_bitcast_fusion.1), channel_id=1, source_target_pairs={{0,2},{1,3},{2,0},{3,1},{4,6},{5,7},{6,4},{7,5},{8,10},{9,11},{10,... | collective-permute-start | bytes 393224 | tf_op jit(solution)/shard_map/ppermute | solution.py:74
  266.0 27.8 %collective-permute-start.50 = (bf16[2,256,512]{2,1,0:T(8,128)(2,1)S(1)}, bf16[2,256,512]{2,1,0:T(8,128)(2,1)S(1)}, u32[]{:S(2)}, u32[]{:S(2)}) collective-permute-start(bf16[2,256,512]{2,1,0:T(8,128)(2,1)S(1)} %get-tuple-element.357), channel_id=1, source_target_pairs={{0,1},{1,0},{2,3},{3,2},{4,5},{5,4},{6,7},{7,6},{8,9},{9,8},{10,11... | collective-permute-start | bytes 1572872 | tf_op jit(solution)/shard_map/ppermute | solution.py:74
  278.2 22.8 %collective-permute-start.49 = (bf16[4,64,2560]{2,1,0:T(8,128)(2,1)}, bf16[4,64,2560]{2,1,0:T(8,128)(2,1)S(1)}, u32[]{:S(2)}, u32[]{:S(2)}) collective-permute-start(bf16[4,64,2560]{2,1,0:T(8,128)(2,1)} %get-tuple-element.359), channel_id=1, source_target_pairs={{0,16},{4,12},{8,24},{12,4},{16,0},{20,28},{24,8},{28,20},{1,17},{... | collective-permute-start | bytes 3932168 | tf_op jit(solution)/shard_map/ppermute | solution.py:64
  294.4 23.2 %collective-permute-start.52 = (bf16[1,256,512]{2,1,0:T(8,128)(2,1)S(1)}, bf16[1,256,512]{2,1,0:T(8,128)(2,1)}, u32[]{:S(2)}, u32[]{:S(2)}) collective-permute-start(bf16[1,256,512]{2,1,0:T(8,128)(2,1)S(1)} %get-tuple-element.369), channel_id=1, source_target_pairs={{0,2},{1,3},{2,0},{3,1},{4,6},{5,7},{6,4},{7,5},{8,10},{9,11},{10,... | collective-permute-start | bytes 786440 | tf_op jit(solution)/shard_map/ppermute | solution.py:74
  295.1 27.7 %collective-permute-start.48 = (bf16[4,2,64,1536]{3,2,1,0:T(8,128)(2,1)}, bf16[4,2,64,1536]{3,2,1,0:T(8,128)(2,1)}, u32[]{:S(2)}, u32[]{:S(2)}) collective-permute-start(bf16[4,2,64,1536]{3,2,1,0:T(8,128)(2,1)} %pick_first.6), channel_id=1, source_target_pairs={{0,8},{4,20},{8,0},{12,28},{16,24},{20,4},{24,16},{28,12},{1,9},{5... | collective-permute-start | bytes 4718600 | tf_op jit(solution)/shard_map/ppermute | solution.py:60
  297.6 30.5 %collective-permute-start.47 = (bf16[512,512]{1,0:T(8,128)(2,1)}, bf16[512,512]{1,0:T(8,128)(2,1)}, u32[]{:S(2)}, u32[]{:S(2)}) collective-permute-start(bf16[512,512]{1,0:T(8,128)(2,1)} %get-tuple-element.481), channel_id=1, source_target_pairs={{0,4},{4,0},{8,12},{12,8},{16,20},{20,16},{24,28},{28,24},{1,5},{5... | collective-permute-start | bytes 1572872 | tf_op jit(solution)/shard_map/ppermute | solution.py:56
  302.0 20.0 %collective-permute-start.51 = (bf16[2,64,2560]{2,1,0:T(8,128)(2,1)S(1)}, bf16[2,64,2560]{2,1,0:T(8,128)(2,1)S(1)}, u32[]{:S(2)}, u32[]{:S(2)}) collective-permute-start(bf16[2,64,2560]{2,1,0:T(8,128)(2,1)S(1)} %get-tuple-element.372), channel_id=1, source_target_pairs={{0,1},{1,0},{2,3},{3,2},{4,5},{5,4},{6,7},{7,6},{8,9},{9,8},{10,11... | collective-permute-start | bytes 1966088 | tf_op jit(solution)/shard_map/ppermute | solution.py:74
  317.7 12.9 %collective-permute-start.53 = (bf16[2,2,80,512]{3,2,1,0:T(8,128)(2,1)S(1)}, bf16[2,2,80,512]{3,2,1,0:T(8,128)(2,1)S(1)}, u32[]{:S(2)}, u32[]{:S(2)}) collective-permute-start(bf16[2,2,80,512]{3,2,1,0:T(8,128)(2,1)S(1)} %fusion.6), channel_id=1, source_target_pairs={{0,4},{4,0},{8,12},{12,8},{16,20},{20,16},{24,28},{28,24},{1,5},{5... | collective-permute-start | bytes 983048 | tf_op jit(solution)/shard_map/ppermute | solution.py:56
  319.1 13.0 %collective-permute-start.57 = (bf16[256,512]{1,0:T(8,128)(2,1)S(1)}, bf16[256,512]{1,0:T(8,128)(2,1)S(1)}, u32[]{:S(2)}, u32[]{:S(2)}) collective-permute-start(bf16[256,512]{1,0:T(8,128)(2,1)S(1)} %bitcast.198), channel_id=1, source_target_pairs={{0,4},{4,0},{8,12},{12,8},{16,20},{20,16},{24,28},{28,24},{1,5},{5... | collective-permute-start | bytes 786440 | tf_op jit(solution)/shard_map/ppermute | solution.py:56
  322.7 24.5 %collective-permute-start.55 = (bf16[1,64,2560]{2,1,0:T(8,128)(2,1)S(1)}, bf16[1,64,2560]{2,1,0:T(8,128)(2,1)S(1)}, u32[]{:S(2)}, u32[]{:S(2)}) collective-permute-start(bf16[1,64,2560]{2,1,0:T(8,128)(2,1)S(1)} %get-tuple-element.380), channel_id=1, source_target_pairs={{0,2},{1,3},{2,0},{3,1},{4,6},{5,7},{6,4},{7,5},{8,10},{9,11},{10,... | collective-permute-start | bytes 983048 | tf_op jit(solution)/shard_map/ppermute | solution.py:74
  327.0 17.9 %collective-permute-start.56 = (bf16[4,64,1536]{2,1,0:T(8,128)(2,1)S(1)}, bf16[4,64,1536]{2,1,0:T(8,128)(2,1)S(1)}, u32[]{:S(2)}, u32[]{:S(2)}) collective-permute-start(bf16[4,64,1536]{2,1,0:T(8,128)(2,1)S(1)} %get-tuple-element.382), channel_id=1, source_target_pairs={{0,16},{4,12},{8,24},{12,4},{16,0},{20,28},{24,8},{28,20},{1,17},{... | collective-permute-start | bytes 2359304 | tf_op jit(solution)/shard_map/ppermute | solution.py:64
  331.1 16.3 %collective-permute-start.54 = (bf16[1,2,336,512]{3,2,1,0:T(8,128)(2,1)S(1)}, bf16[1,2,336,512]{3,2,1,0:T(8,128)(2,1)S(1)}, u32[]{:S(2)}, u32[]{:S(2)}) collective-permute-start(bf16[1,2,336,512]{3,2,1,0:T(8,128)(2,1)S(1)} %pick_first.7), channel_id=1, source_target_pairs={{0,8},{4,20},{8,0},{12,28},{16,24},{20,4},{24,16},{28,12},{1,9},{5... | collective-permute-start | bytes 2064392 | tf_op jit(solution)/shard_map/ppermute | solution.py:60
  332.2 19.0 %collective-permute-start.60 = (bf16[2,256,512]{2,1,0:T(8,128)(2,1)S(1)}, bf16[2,256,512]{2,1,0:T(8,128)(2,1)S(1)}, u32[]{:S(2)}, u32[]{:S(2)}) collective-permute-start(bf16[2,256,512]{2,1,0:T(8,128)(2,1)S(1)} %pad_maximum_fusion.14), channel_id=1, source_target_pairs={{0,8},{4,20},{8,0},{12,28},{16,24},{20,4},{24,16},{28,12},{1,9},{5... | collective-permute-start | bytes 1572872 | tf_op jit(solution)/shard_map/ppermute | solution.py:60
  345.9 8.2 %collective-permute-start.59 = (bf16[2,64,1536]{2,1,0:T(8,128)(2,1)S(1)}, bf16[2,64,1536]{2,1,0:T(8,128)(2,1)S(1)}, u32[]{:S(2)}, u32[]{:S(2)}) collective-permute-start(bf16[2,64,1536]{2,1,0:T(8,128)(2,1)S(1)} %get-tuple-element.392), channel_id=1, source_target_pairs={{0,1},{1,0},{2,3},{3,2},{4,5},{5,4},{6,7},{7,6},{8,9},{9,8},{10,11... | collective-permute-start | bytes 1179656 | tf_op jit(solution)/shard_map/ppermute | solution.py:74
  347.3 20.1 %collective-permute-start.65 = (bf16[64,2560]{1,0:T(8,128)(2,1)S(1)}, bf16[64,2560]{1,0:T(8,128)(2,1)S(1)}, u32[]{:S(2)}, u32[]{:S(2)}) collective-permute-start(bf16[64,2560]{1,0:T(8,128)(2,1)S(1)} %bitcast.195), channel_id=1, source_target_pairs={{0,4},{4,0},{8,12},{12,8},{16,20},{20,16},{24,28},{28,24},{1,5},{5... | collective-permute-start | bytes 983048 | tf_op jit(solution)/shard_map/ppermute | solution.py:56
  348.1 7.6 %collective-permute-start.58 = (bf16[1,336,512]{2,1,0:T(8,128)(2,1)S(1)}, bf16[1,336,512]{2,1,0:T(8,128)(2,1)S(1)}, u32[]{:S(2)}, u32[]{:S(2)}) collective-permute-start(bf16[1,336,512]{2,1,0:T(8,128)(2,1)S(1)} %get-tuple-element.396), channel_id=1, source_target_pairs={{0,16},{4,12},{8,24},{12,4},{16,0},{20,28},{24,8},{28,20},{1,17},{... | collective-permute-start | bytes 1032200 | tf_op jit(solution)/shard_map/ppermute | solution.py:64
  351.2 31.9 %collective-permute-start.71 = (bf16[2,256,512]{2,1,0:T(8,128)(2,1)S(1)}, bf16[2,256,512]{2,1,0:T(8,128)(2,1)S(1)}, u32[]{:S(2)}, u32[]{:S(2)}) collective-permute-start(bf16[2,256,512]{2,1,0:T(8,128)(2,1)S(1)} %collective-permute-done.60.refs_2_), channel_id=1, source_target_pairs={{0,4},{4,0},{8,12},{12,8},{16,20},{20,16},{24,28},{28,24},{1,5},{5... | collective-permute-start | bytes 1572872 | tf_op jit(solution)/shard_map/ppermute | solution.py:56
  352.4 16.7 %collective-permute-start.63 = (bf16[256,512]{1,0:T(8,128)(2,1)S(1)}, bf16[256,512]{1,0:T(8,128)(2,1)S(1)}, u32[]{:S(2)}, u32[]{:S(2)}) collective-permute-start(bf16[256,512]{1,0:T(8,128)(2,1)S(1)} %slice_bitcast_fusion.4), channel_id=1, source_target_pairs={{0,16},{4,12},{8,24},{12,4},{16,0},{20,28},{24,8},{28,20},{1,17},{... | collective-permute-start | bytes 786440 | tf_op jit(solution)/shard_map/ppermute | solution.py:64
  355.9 11.4 %collective-permute-start.61 = (bf16[1,64,1536]{2,1,0:T(8,128)(2,1)S(1)}, bf16[1,64,1536]{2,1,0:T(8,128)(2,1)S(1)}, u32[]{:S(2)}, u32[]{:S(2)}) collective-permute-start(bf16[1,64,1536]{2,1,0:T(8,128)(2,1)S(1)} %get-tuple-element.400), channel_id=1, source_target_pairs={{0,2},{1,3},{2,0},{3,1},{4,6},{5,7},{6,4},{7,5},{8,10},{9,11},{10,... | collective-permute-start | bytes 589832 | tf_op jit(solution)/shard_map/ppermute | solution.py:74
  357.8 10.4 %collective-permute-start.64 = (bf16[208,512]{1,0:T(8,128)(2,1)S(1)}, bf16[208,512]{1,0:T(8,128)(2,1)S(1)}, u32[]{:S(2)}, u32[]{:S(2)}) collective-permute-start(bf16[208,512]{1,0:T(8,128)(2,1)S(1)} %pad_maximum_fusion.20), channel_id=1, source_target_pairs={{0,1},{1,0},{2,3},{3,2},{4,5},{5,4},{6,7},{7,6},{8,9},{9,8},{10,11... | collective-permute-start | bytes 638984 | tf_op jit(solution)/shard_map/ppermute | solution.py:74
  367.5 10.9 %collective-permute-start.68 = (bf16[2,64,2560]{2,1,0:T(8,128)(2,1)S(1)}, bf16[2,64,2560]{2,1,0:T(8,128)(2,1)S(1)}, u32[]{:S(2)}, u32[]{:S(2)}) collective-permute-start(bf16[2,64,2560]{2,1,0:T(8,128)(2,1)S(1)} %pad_maximum_fusion.9), channel_id=1, source_target_pairs={{0,8},{4,20},{8,0},{12,28},{16,24},{20,4},{24,16},{28,12},{1,9},{5... | collective-permute-start | bytes 1966088 | tf_op jit(solution)/shard_map/ppermute | solution.py:60
  368.3 10.0 %collective-permute-start.66 = (bf16[144,512]{1,0:T(8,128)(2,1)S(1)}, bf16[144,512]{1,0:T(8,128)(2,1)S(1)}, u32[]{:S(2)}, u32[]{:S(2)}) collective-permute-start(bf16[144,512]{1,0:T(8,128)(2,1)S(1)} %pad_maximum_fusion.22), channel_id=1, source_target_pairs={{0,2},{1,3},{2,0},{3,1},{4,6},{5,7},{6,4},{7,5},{8,10},{9,11},{10,... | collective-permute-start | bytes 442376 | tf_op jit(solution)/shard_map/ppermute | solution.py:74
  369.1 13.9 %collective-permute-start.72 = (bf16[256,512]{1,0:T(8,128)(2,1)S(1)}, bf16[256,512]{1,0:T(8,128)(2,1)S(1)}, u32[]{:S(2)}, u32[]{:S(2)}) collective-permute-start(bf16[256,512]{1,0:T(8,128)(2,1)S(1)} %collective-permute-done.63.refs_4_), channel_id=1, source_target_pairs={{0,4},{4,0},{8,12},{12,8},{16,20},{20,16},{24,28},{28,24},{1,5},{5... | collective-permute-start | bytes 786440 | tf_op jit(solution)/shard_map/ppermute | solution.py:56
  369.1 13.2 %collective-permute-start.73 = (bf16[2,64,1536]{2,1,0:T(8,128)(2,1)S(1)}, bf16[2,64,1536]{2,1,0:T(8,128)(2,1)S(1)}, u32[]{:S(2)}, u32[]{:S(2)}) collective-permute-start(bf16[2,64,1536]{2,1,0:T(8,128)(2,1)S(1)} %pad_maximum_fusion.15), channel_id=1, source_target_pairs={{0,8},{4,20},{8,0},{12,28},{16,24},{20,4},{24,16},{28,12},{1,9},{5... | collective-permute-start | bytes 1179656 | tf_op jit(solution)/shard_map/ppermute | solution.py:60
  378.5 17.9 %collective-permute-start.76 = (bf16[2,64,2560]{2,1,0:T(8,128)(2,1)S(1)}, bf16[2,64,2560]{2,1,0:T(8,128)(2,1)S(1)}, u32[]{:S(2)}, u32[]{:S(2)}) collective-permute-start(bf16[2,64,2560]{2,1,0:T(8,128)(2,1)S(1)} %collective-permute-done.68.refs_2_), channel_id=1, source_target_pairs={{0,4},{4,0},{8,12},{12,8},{16,20},{20,16},{24,28},{28,24},{1,5},{5... | collective-permute-start | bytes 1966088 | tf_op jit(solution)/shard_map/ppermute | solution.py:56
  379.7 9.3 %collective-permute-start.70 = (bf16[64,2560]{1,0:T(8,128)(2,1)S(1)}, bf16[64,2560]{1,0:T(8,128)(2,1)S(1)}, u32[]{:S(2)}, u32[]{:S(2)}) collective-permute-start(bf16[64,2560]{1,0:T(8,128)(2,1)S(1)} %slice_bitcast_fusion.3), channel_id=1, source_target_pairs={{0,16},{4,12},{8,24},{12,4},{16,0},{20,28},{24,8},{28,20},{1,17},{... | collective-permute-start | bytes 983048 | tf_op jit(solution)/shard_map/ppermute | solution.py:64
  382.4 8.4 %collective-permute-start.69 = (bf16[2,144,512]{2,1,0:T(8,128)(2,1)S(1)}, bf16[2,144,512]{2,1,0:T(8,128)(2,1)S(1)}, u32[]{:S(2)}, u32[]{:S(2)}) collective-permute-start(bf16[2,144,512]{2,1,0:T(8,128)(2,1)S(1)} %pad_maximum_fusion.16), channel_id=1, source_target_pairs={{0,8},{4,20},{8,0},{12,28},{16,24},{20,4},{24,16},{28,12},{1,9},{5... | collective-permute-start | bytes 884744 | tf_op jit(solution)/shard_map/ppermute | solution.py:60
  390.7 9.4 %collective-permute-start.80 = (bf16[2,64,1536]{2,1,0:T(8,128)(2,1)S(1)}, bf16[2,64,1536]{2,1,0:T(8,128)(2,1)S(1)}, u32[]{:S(2)}, u32[]{:S(2)}) collective-permute-start(bf16[2,64,1536]{2,1,0:T(8,128)(2,1)S(1)} %collective-permute-done.73.refs_2_), channel_id=1, source_target_pairs={{0,4},{4,0},{8,12},{12,8},{16,20},{20,16},{24,28},{28,24},{1,5},{5... | collective-permute-start | bytes 1179656 | tf_op jit(solution)/shard_map/ppermute | solution.py:56
  390.7 11.9 %collective-permute-start.74 = (bf16[2,144,512]{2,1,0:T(8,128)(2,1)S(1)}, bf16[2,144,512]{2,1,0:T(8,128)(2,1)S(1)}, u32[]{:S(2)}, u32[]{:S(2)}) collective-permute-start(bf16[2,144,512]{2,1,0:T(8,128)(2,1)S(1)} %collective-permute-done.69.refs_2_), channel_id=1, source_target_pairs={{0,4},{4,0},{8,12},{12,8},{16,20},{20,16},{24,28},{28,24},{1,5},{5... | collective-permute-start | bytes 884744 | tf_op jit(solution)/shard_map/ppermute | solution.py:56
  (140 other events, 1298.9 us)

commit v6 on v5

--- a/solution.py
+++ b/solution.py
@@ -1000,6 +1000,11 @@
     unit_two, inverse_two = normalise(residual)
     normed_two = (unit_two * gain_two + bias_two).astype(bf16)
     order.mark(normed_two)
+    ke_part = lax.dot_general(
+        key_weight, embed_rows, (((0,), (1,)), ((), ())), preferred_element_type=f32
+    ).astype(bf16)
+    order.mark(ke_part)
+    order.mark(keys_cols)
     spread_d.near_step()
     spread_c.last_step()
     normed_two_there = over_core(normed_two)
@@ -1027,9 +1032,6 @@
     order.mark(grad_d)
     reduce_d = Reduce(grad_d, where, order)
     pre_got = over_core(pre_other)
-    ke_part = lax.dot_general(
-        key_weight, embed_rows, (((0,), (1,)), ((), ())), preferred_element_type=f32
-    ).astype(bf16)
     ke_part = order.hold(ke_part).reshape(2, 2, shard, COLS)
     ke_kept, ke_got = take(ke_part, where.low, 1), swap_narrow(take(ke_part, where.other_low, 1), 1)
     residual_grad = cot_float + normalise_back(
@@ -1058,6 +1060,10 @@
     order.mark(project_other)
     project_got = over_core(project_other)
     reduce_d.step()
+    late = order.hold(normed_two_grad)
+    sums_two = [jnp.sum(late * unit_two, axis=0), jnp.sum(late, axis=0)]
+    order.mark(sums_two[0])
+    order.mark(sums_two[1])
     reduce_c.step()
     ke_own = add_two(take(ke_two, where.high, 0), order.hold(ke_got))
     order.mark(ke_own)
@@ -1088,8 +1094,7 @@
         jnp.sum(normed_grad * unit_one, axis=0),
         jnp.sum(normed_grad, axis=0),
         jnp.sum(branch_grad.astype(f32), axis=0),
-        jnp.sum(normed_two_grad * unit_two, axis=0),
-        jnp.sum(normed_two_grad, axis=0),
+        *sums_two,
         jnp.sum(cot_float, axis=0),
         pre_sums.reshape(-1),
     ]
@@ -1108,14 +1113,14 @@
     grad_a = jnp.concatenate([grad_a, shared], axis=2)
     order.mark(grad_a)
     reduce_a = ReduceShared(grad_a[None], where, order)
-    spread_d.near_step()
     reduce_b.step()
     reduce_c.step()
     spread_c = Spread(reduce_c.total, order)
     reduce_a.step()
-    spread_d.corner_step()
+    spread_d.near_step()
     reduce_b.step()
     reduce_a.step()
+    spread_d.corner_step()
     result = (residual + dot(order.hold(hidden), mlp_out_w) + mlp_out_b).astype(bf16)
     order.mark(result)
     reduce_b.step()

time: 414 us -> 414 us (level)
  waiting for transfers between devices: 98.2 us -> 93.2 us
  starting transfers between devices: 63.9 us -> 68.8 us
    unnamed x255 -> x233, local copies, waits for them, and re-layouts: 18.1 us -> 11.3 us
    ppermute x20, starting transfers between devices: 21.7 us -> 26.8 us  [swap_narrow(): return lax.ppermute(a, 'narrow', [(i, i ^ bits) for i in range(size)])]
    ppermute x12, waiting for transfers between devices: 40.7 us -> 36.5 us  [over_second(): return lax.ppermute(a, 'wide', wide_pairs(lambda i: 2 if i & 1 else 4))]
  transfers between devices with their start and end apart: 82 -> 82, of which waited for: 30 -> 27; matrix products, arithmetic and copies ran while one was open for 23% -> 25% of each run, Pallas kernels for 30% -> 30%
where the time goes in v6:
time: 414 us; the launch traced here: 409 us
  Pallas kernels  126 us (30%)
  waiting for transfers between devices  93.2 us (23%)
  starting transfers between devices  68.8 us (17%)
  matrix products  52.8 us (13%)
  local copies, waits for them, and re-layouts  36.1 us (9%)
  other arithmetic  28.5 us (7%)
    ppermute x12, waiting for transfers between devices, over_second(): return lax.ppermute(a, 'wide', wide_pairs(lambda i: 2 if i & 1 else 4))  36.5 us
    ppermute x20, waiting for transfers between devices, swap_narrow(): return lax.ppermute(a, 'narrow', [(i, i ^ bits) for i in range(size)])  29.5 us
    ppermute x20, starting transfers between devices, swap_narrow(): return lax.ppermute(a, 'narrow', [(i, i ^ bits) for i in range(size)])  26.8 us
    dot_general x10, matrix products, dot_tn(): lax.dot_general(a, b, (((0,), (0,)), ((), ())), preferred_element_type=f32)  25.1 us
    ppermute x12, waiting for transfers between devices, over_first(): return lax.ppermute(a, 'wide', wide_pairs(lambda i: 4 if i & 1 else 2))  21 us
    ppermute x12, starting transfers between devices, over_second(): return lax.ppermute(a, 'wide', wide_pairs(lambda i: 2 if i & 1 else 4))  18 us
    pallas_call x1, Pallas kernels, attention_back(): pl.pallas_call(attention_back_kernel, out_shape=jax.ShapeDtypeStruct((row...  16.5 us
    pallas_call x10, Pallas kernels, add_split(): pl.pallas_call(add_split_kernel, out_shape=[out, out], grid_spec=pltpu.Pr...  16.1 us
  transfers between devices with their start and end apart: 82, of which 27 were waited for; matrix products, arithmetic and copies ran while one was open for 25% of the time, Pallas kernels for 30%

profile of v6, /device:TPU:0, one launch (start us, length us, event | category | flops | bytes accessed | tf_op | source)
XLA Modules:
  0.0 409.0 jit_solution(6877690057862984159)
XLA Ops:
  3.4 4.1 %collective-permute-start.2 = (bf16[32,4096]{1,0:T(8,128)(2,1)S(1)}, bf16[32,4096]{1,0:T(8,128)(2,1)S(1)}, u32[]{:S(2)}, u32[]{:S(2)}) collective-permute-start(bf16[32,4096]{1,0:T(8,128)(2,1)S(1)} %get-tuple-element.501), channel_id=1, source_target_pairs={{0,2},{1,3},{2,0},{3,1},{4,6},{5,7},{6,4},{7,5},{8,10},{9,11},{10,... | collective-permute-start | bytes 786440 | tf_op jit(solution)/shard_map/ppermute | solution.py:74
  10.1 3.0 collective-permute-start
  19.0 1.8 constant_dynamic-slice_fusion.11
  31.7 1.8 collective-permute-start.4
  36.9 2.0 convolution_convert_fusion.4.pixels_ref
  42.4 8.7 %collective-permute-done.9 = bf16[2,32,4096]{2,1,0:T(8,128)(2,1)S(1)} collective-permute-done((bf16[2,32,4096]{2,1,0:T(8,128)(2,1)S(1)}, bf16[2,32,4096]{2,1,0:T(8,128)(2,1)S(1)}, u32[]{:S(2)}, u32[]{:S(2)}) %collective-permute-start.9) | collective-permute-done | bytes 524320 | tf_op jit(solution)/shard_map/ppermute | solution.py:74
  53.0 7.7 %collective-permute-done.10.refs_2_.refs_3_ = bf16[2,4,32,1024]{3,2,1,0:T(8,128)(2,1)S(1)} collective-permute-done((bf16[2,4,32,1024]{3,2,1,0:T(8,128)(2,1)S(1)}, bf16[2,4,32,1024]{3,2,1,0:T(8,128)(2,1)S(1)}, u32[]{:S(2)}, u32[]{:S(2)}) %collective-permute-start.10) | collective-permute-done | bytes 524320 | tf_op jit(solution)/shard_map/ppermute | solution.py:60
  69.9 3.7 assemble.4
  74.9 2.6 arrange.1
  77.5 5.1 %collective-permute-done.16 = bf16[32,4096]{1,0:T(8,128)(2,1)} collective-permute-done((bf16[32,4096]{1,0:T(8,128)(2,1)}, bf16[32,4096]{1,0:T(8,128)(2,1)}, u32[]{:S(2)}, u32[]{:S(2)}) %collective-permute-start.16) | collective-permute-done | bytes 262176 | tf_op jit(solution)/shard_map/ppermute | solution.py:74
  86.9 9.0 %variable_forward.1 = bf16[512,1024]{1,0:T(8,128)(2,1)S(1)} custom-call(bf16[256,512]{1,0:T(8,128)(2,1)S(1)} %copy-done.44, f32[256,256]{1,0:T(8,128)S(1)} %copy-done.21, f32[8,2,256]{2,1,0:T(2,128)S(1)} %add.206.keys_ref, bf16[1024,256]{1,0:T(8,128)(2,1)S(1)} %copy-done.39), custom_call_target="tpu_custom_call" | custom-call | flops 7200000000 | bytes 1 | tf_op jit(solution)/shard_map/variable_forward/pallas_call | solution.py:471
  99.8 2.4 fusion.38
  108.7 4.1 assemble.5
  112.9 3.7 convolution_convert_fusion.q_ref.k_ref.v_ref
  116.6 2.8 collective-permute-done.24
  119.5 12.5 %attention.1 = (bf16[512,1024]{1,0:T(8,128)(2,1)}, f32[8,2,512]{2,1,0:T(2,128)S(1)}) custom-call(bf16[512,3072]{1,0:T(8,128)(2,1)S(1)} %convolution_convert_fusion.q_ref.k_ref.v_ref, bf16[512,3072]{1,0:T(8,128)(2,1)S(1)} %convolution_convert_fusion.q_ref.k_ref.v_ref, bf16[512,3072]{1,0:T(8,128)(2,1)S(1)} %convolution_convert_fusion.q_ref.k_ref.v_ref, ...), custom_call_target="tpu_custom_call" | custom-call | flops 22499999744 | bytes 1 | tf_op jit(solution)/shard_map/attention/pallas_call | solution.py:595
  132.1 2.2 slice_bitcast_fusion.1
  137.6 2.7 fusion.48
  150.8 3.4 assemble.6.weight.w_in
  154.3 10.0 %mlp_in.1 = (bf16[512,4096]{1,0:T(8,128)(2,1)S(1)}, bf16[512,4096]{1,0:T(8,128)(2,1)S(1)}) custom-call(bf16[512,1024]{1,0:T(8,128)(2,1)S(1)} %add_convert_fusion.7.rows_ref, bf16[1024,4096]{1,0:T(8,128)(2,1)S(1)} %assemble.6.weight.w_in, f32[1,4096]{1,0:T(1,128)S(1)} %bitcast.210), custom_call_target="tpu_custom_call" | custom-call | flops 19800000512 | bytes 1 | tf_op jit(solution)/shard_map/mlp_in/pallas_call | solution.py:686
  164.3 2.0 copy-done.57
  166.3 2.4 collective-permute-done.34.refs_3_
  170.9 9.9 %collective-permute-done.36.refs_5_ = bf16[3,128,1024]{2,1,0:T(8,128)(2,1)S(1)} collective-permute-done((bf16[3,128,1024]{2,1,0:T(8,128)(2,1)S(1)}, bf16[3,128,1024]{2,1,0:T(8,128)(2,1)S(1)}, u32[]{:S(2)}, u32[]{:S(2)}) %collective-permute-start.36) | collective-permute-done | bytes 786464 | tf_op jit(solution)/shard_map/ppermute | solution.py:64
  183.1 3.0 assemble.7.w_out
  186.1 13.0 %mlp_back.1 = (bf16[512,2048]{1,0:T(8,128)(2,1)S(1)}, bf16[512,2048]{1,0:T(8,128)(2,1)}, f32[512,1024]{1,0:T(8,128)S(1)}, f32[4,1,1024]{2,1,0:T(1,128)S(1)}) custom-call(s32[1]{0:T(128)} %bitcast.3.core, bf16[512,1024]{1,0:T(8,128)(2,1)S(1)} %copy-done.6, bf16[4096,1024]{1,0:T(8,128)(2,1)S(1)} %assemble.7.w_out, bf16[1024,4096]{1,0:T(8,128)(2,1)S(1)} %bitcast.241, ...), custom_call_target="tpu_custom_call" | custom-call | flops 27900000256 | bytes 1 | tf_op jit(solution)/shard_map/mlp_back/pallas_call | solution.py:725
  199.6 5.1 %fusion.49 = f32[4096,512]{1,0:T(8,128)S(1)} fusion(bf16[512,4096]{1,0:T(8,128)(2,1)} %collective-permute-done.33, bf16[512,512]{1,0:T(8,128)(2,1)S(1)} %collective-permute-done.38), kind=kOutput, calls=%fused_computation.214 | convolution fusion | flops 2147483648 | bytes 13107200 | tf_op jit(solution)/shard_map/dot_general | solution.py:43
  204.7 2.6 add_convert_fusion.1
  207.4 3.0 pick_first.4
  212.0 2.1 copy.72
  214.1 2.4 multiply_reduce_fusion.7
  216.5 2.2 fusion.42
  220.5 2.0 collective-permute-start.43
  222.4 4.5 %fusion.50 = f32[1024,2048]{1,0:T(8,128)S(1)} fusion(bf16[512,1024]{1,0:T(8,128)(2,1)} %collective-permute-done.28, bf16[512,2048]{1,0:T(8,128)(2,1)} %collective-permute-done.41), kind=kOutput, calls=%fused_computation.215 | convolution fusion | flops 2147483648 | bytes 11534336 | tf_op jit(solution)/shard_map/dot_general | solution.py:43
  226.9 2.6 add_convert_fusion
  229.6 2.0 fusion.51
  231.6 2.0 add_convert_fusion.6
  236.9 3.4 add_split.10
  242.8 16.5 %attention_back.1 = bf16[512,3072]{1,0:T(8,128)(2,1)S(1)} custom-call(bf16[512,3072]{1,0:T(8,128)(2,1)S(1)} %copy-done.56, bf16[512,3072]{1,0:T(8,128)(2,1)S(1)} %copy-done.56, bf16[512,3072]{1,0:T(8,128)(2,1)S(1)} %copy-done.56, bf16[512,1024]{1,0:T(8,128)(2,1)S(1)} %convolution_convert_fusion.2.grad_ref, f32[8,2,512]{2,1,0:T(2,128)S(1)} %get-tuple-element.354.log_ref, ...), custom_call_target="tpu_custom_call" | custom-call | flops 29699999744 | bytes 1 | tf_op jit(solution)/shard_map/attention_back/pallas_call | solution.py:654
  259.3 1.8 constant_dynamic-slice_fusion.4
  262.9 3.6 collective-permute-done.42
  269.5 7.8 %collective-permute-done.47.got_sent.got_kept = bf16[4,2,64,2560]{3,2,1,0:T(8,128)(2,1)S(1)} collective-permute-done((bf16[4,2,64,2560]{3,2,1,0:T(8,128)(2,1)S(1)}, bf16[4,2,64,2560]{3,2,1,0:T(8,128)(2,1)S(1)}, u32[]{:S(2)}, u32[]{:S(2)}) %collective-permute-start.47) | collective-permute-done | bytes 2621472 | tf_op jit(solution)/shard_map/ppermute | solution.py:60
  277.2 2.3 add_split.12
  281.0 1.8 fusion.52
  282.8 1.9 add_convert_fusion.2
  286.9 4.0 multiply_reduce_fusion
  296.9 3.3 convolution_convert_fusion.1.grad_ref
  300.3 2.0 add_split.14
  302.9 14.6 %variable_back.1 = (bf16[512,512]{1,0:T(8,128)(2,1)S(1)}, f32[16,256]{1,0:T(8,128)S(1)}, f32[256,512]{1,0:T(8,128)S(1)}) custom-call(bf16[256,512]{1,0:T(8,128)(2,1)S(1)} %copy-done.45, f32[256,256]{1,0:T(8,128)S(1)} %copy-done.22, f32[8,2,256]{2,1,0:T(2,128)S(1)} %add.206.keys_ref, f32[8,256,2]{2,1,0:T(8,128)S(1)} %bitcast.195, ...), custom_call_target="tpu_custom_call" | custom-call | flops 1800000000 | bytes 1 | tf_op jit(solution)/shard_map/variable_back/pallas_call | solution.py:535
  322.7 3.1 add_split.16
  326.8 1.8 fusion.53
  330.9 12.7 %collective-permute-done.57 = bf16[4,64,1536]{2,1,0:T(8,128)(2,1)S(1)} collective-permute-done((bf16[4,64,1536]{2,1,0:T(8,128)(2,1)S(1)}, bf16[4,64,1536]{2,1,0:T(8,128)(2,1)S(1)}, u32[]{:S(2)}, u32[]{:S(2)}) %collective-permute-start.57) | collective-permute-done | bytes 786464 | tf_op jit(solution)/shard_map/ppermute | solution.py:64
  348.5 4.3 %collective-permute-done.60 = bf16[2,64,1536]{2,1,0:T(8,128)(2,1)S(1)} collective-permute-done((bf16[2,64,1536]{2,1,0:T(8,128)(2,1)S(1)}, bf16[2,64,1536]{2,1,0:T(8,128)(2,1)S(1)}, u32[]{:S(2)}, u32[]{:S(2)}) %collective-permute-start.60) | collective-permute-done | bytes 393248 | tf_op jit(solution)/shard_map/ppermute | solution.py:74
  353.4 2.6 collective-permute-start.61
  360.5 5.5 %add_convert_fusion.3 = bf16[512,1024]{1,0:T(8,128)(2,1)} fusion(f32[512,1024]{1,0:T(8,128)S(1)} %copy-done.62, bf16[512,4096]{1,0:T(8,128)(2,1)S(1)} %copy-done.3, bf16[4096,1024]{1,0:T(8,128)(2,1)S(1)} %bitcast.239, f32[1024]{0:T(1024)S(1)} %bitcast.279), kind=kOutput, calls=%fused_computation.5 | convolution fusion | flops 4296540160 | bytes 15732736 | tf_op jit(solution)/shard_map/dot_general | solution.py:35
  367.3 2.0 collective-permute-start.66
  371.1 6.1 %collective-permute-done.66 = bf16[144,512]{1,0:T(8,128)(2,1)S(1)} collective-permute-done((bf16[144,512]{1,0:T(8,128)(2,1)S(1)}, bf16[144,512]{1,0:T(8,128)(2,1)S(1)}, u32[]{:S(2)}, u32[]{:S(2)}) %collective-permute-start.66) | collective-permute-done | bytes 147488 | tf_op jit(solution)/shard_map/ppermute | solution.py:74
  382.0 2.8 place.4
  384.8 3.2 collective-permute-done.70.refs_4_
  388.2 2.3 collective-permute-start.78
  391.0 3.1 collective-permute-done.78.refs_4_
  394.1 2.0 collective-permute-start.75
  396.2 3.3 place.5
  399.9 2.4 place.6
  404.1 2.7 finish.1
  (510 shorter events, 129.1 us)
Async XLA Ops:
  3.4 23.1 %collective-permute-start.2 = (bf16[32,4096]{1,0:T(8,128)(2,1)S(1)}, bf16[32,4096]{1,0:T(8,128)(2,1)S(1)}, u32[]{:S(2)}, u32[]{:S(2)}) collective-permute-start(bf16[32,4096]{1,0:T(8,128)(2,1)S(1)} %get-tuple-element.501), channel_id=1, source_target_pairs={{0,2},{1,3},{2,0},{3,1},{4,6},{5,7},{6,4},{7,5},{8,10},{9,11},{10,... | collective-permute-start | bytes 786440 | tf_op jit(solution)/shard_map/ppermute | solution.py:74
  8.4 17.0 %collective-permute-start.3 = (bf16[32,1024]{1,0:T(8,128)(2,1)S(1)}, bf16[32,1024]{1,0:T(8,128)(2,1)S(1)}, u32[]{:S(2)}, u32[]{:S(2)}) collective-permute-start(bf16[32,1024]{1,0:T(8,128)(2,1)S(1)} %constant_dynamic-slice_fusion.12), channel_id=1, source_target_pairs={{0,2},{1,3},{2,0},{3,1},{4,6},{5,7},{6,4},{7,5},{8,10},{9,11},{10,... | collective-permute-start | bytes 196616 | tf_op jit(solution)/shard_map/ppermute | solution.py:74
  10.1 13.6 %collective-permute-start = (bf16[12,256]{1,0:T(8,128)(2,1)S(1)}, bf16[12,256]{1,0:T(8,128)(2,1)S(1)}, u32[]{:S(2)}, u32[]{:S(2)}) collective-permute-start(bf16[12,256]{1,0:T(8,128)(2,1)S(1)} %get-tuple-element.525.own), channel_id=1, source_target_pairs={{0,2},{1,3},{2,0},{3,1},{4,6},{5,7},{6,4},{7,5},{8,10},{9,11},{10,... | collective-permute-start | bytes 18440 | tf_op jit(solution)/shard_map/ppermute | solution.py:74
  26.0 15.3 %collective-permute-start.7 = (bf16[2,32,1024]{2,1,0:T(8,128)(2,1)}, bf16[2,32,1024]{2,1,0:T(8,128)(2,1)}, u32[]{:S(2)}, u32[]{:S(2)}) collective-permute-start(bf16[2,32,1024]{2,1,0:T(8,128)(2,1)} %pad_maximum_fusion.23), channel_id=1, source_target_pairs={{0,1},{1,0},{2,3},{3,2},{4,5},{5,4},{6,7},{7,6},{8,9},{9,8},{10,11... | collective-permute-start | bytes 393224 | tf_op jit(solution)/shard_map/ppermute | solution.py:74
  36.0 15.1 %collective-permute-start.9 = (bf16[2,32,4096]{2,1,0:T(8,128)(2,1)S(1)}, bf16[2,32,4096]{2,1,0:T(8,128)(2,1)S(1)}, u32[]{:S(2)}, u32[]{:S(2)}) collective-permute-start(bf16[2,32,4096]{2,1,0:T(8,128)(2,1)S(1)} %pad_maximum_fusion.10), channel_id=1, source_target_pairs={{0,1},{1,0},{2,3},{3,2},{4,5},{5,4},{6,7},{7,6},{8,9},{9,8},{10,11... | collective-permute-start | bytes 1572872 | tf_op jit(solution)/shard_map/ppermute | solution.py:74
  42.3 9.0 %collective-permute-start.8 = (bf16[4,32,1024]{2,1,0:T(8,128)(2,1)S(1)}, bf16[4,32,1024]{2,1,0:T(8,128)(2,1)S(1)}, u32[]{:S(2)}, u32[]{:S(2)}) collective-permute-start(bf16[4,32,1024]{2,1,0:T(8,128)(2,1)S(1)} %get-tuple-element.268.refs_0_.refs_1_), channel_id=1, source_target_pairs={{0,4},{4,0},{8,12},{12,8},{16,20},{20,16},{24,28},{28,24},{1,5},{5... | collective-permute-start | bytes 786440 | tf_op jit(solution)/shard_map/ppermute | solution.py:56
  51.2 11.0 %collective-permute-start.13 = (bf16[3,32,4096]{2,1,0:T(8,128)(2,1)S(1)}, bf16[3,32,4096]{2,1,0:T(8,128)(2,1)S(1)}, u32[]{:S(2)}, u32[]{:S(2)}) collective-permute-start(bf16[3,32,4096]{2,1,0:T(8,128)(2,1)S(1)} %get-tuple-element.285.refs_2_), channel_id=1, source_target_pairs={{0,4},{4,0},{8,12},{12,8},{16,20},{20,16},{24,28},{28,24},{1,5},{5... | collective-permute-start | bytes 2359304 | tf_op jit(solution)/shard_map/ppermute | solution.py:56
  51.4 9.2 %collective-permute-start.10 = (bf16[2,4,32,1024]{3,2,1,0:T(8,128)(2,1)S(1)}, bf16[2,4,32,1024]{3,2,1,0:T(8,128)(2,1)S(1)}, u32[]{:S(2)}, u32[]{:S(2)}) collective-permute-start(bf16[2,4,32,1024]{3,2,1,0:T(8,128)(2,1)S(1)} %pad_maximum_fusion.11), channel_id=1, source_target_pairs={{0,8},{4,20},{8,0},{12,28},{16,24},{20,4},{24,16},{28,12},{1,9},{5... | collective-permute-start | bytes 1572872 | tf_op jit(solution)/shard_map/ppermute | solution.py:60
  60.6 8.1 %collective-permute-start.11 = (bf16[2,4,32,1024]{3,2,1,0:T(8,128)(2,1)S(1)}, bf16[2,4,32,1024]{3,2,1,0:T(8,128)(2,1)S(1)}, u32[]{:S(2)}, u32[]{:S(2)}) collective-permute-start(bf16[2,4,32,1024]{3,2,1,0:T(8,128)(2,1)S(1)} %collective-permute-done.10.refs_2_.refs_3_), channel_id=1, source_target_pairs={{0,4},{4,0},{8,12},{12,8},{16,20},{20,16},{24,28},{28,24},{1,5},{5... | collective-permute-start | bytes 1572872 | tf_op jit(solution)/shard_map/ppermute | solution.py:56
  64.4 20.7 %collective-permute-start.15 = (bf16[2,3,32,4096]{3,2,1,0:T(8,128)(2,1)}, bf16[2,3,32,4096]{3,2,1,0:T(8,128)(2,1)}, u32[]{:S(2)}, u32[]{:S(2)}) collective-permute-start(bf16[2,3,32,4096]{3,2,1,0:T(8,128)(2,1)} %pad_maximum_fusion.1), channel_id=1, source_target_pairs={{0,8},{4,20},{8,0},{12,28},{16,24},{20,4},{24,16},{28,12},{1,9},{5... | collective-permute-start | bytes 4718600 | tf_op jit(solution)/shard_map/ppermute | solution.py:60
  67.2 15.5 %collective-permute-start.16 = (bf16[32,4096]{1,0:T(8,128)(2,1)}, bf16[32,4096]{1,0:T(8,128)(2,1)}, u32[]{:S(2)}, u32[]{:S(2)}) collective-permute-start(bf16[32,4096]{1,0:T(8,128)(2,1)} %constant_dynamic-slice_fusion.11), channel_id=1, source_target_pairs={{0,2},{1,3},{2,0},{3,1},{4,6},{5,7},{6,4},{7,5},{8,10},{9,11},{10,... | collective-permute-start | bytes 786440 | tf_op jit(solution)/shard_map/ppermute | solution.py:74
  83.6 16.2 %collective-permute-start.20 = (bf16[2,32,4096]{2,1,0:T(8,128)(2,1)S(1)}, bf16[2,32,4096]{2,1,0:T(8,128)(2,1)S(1)}, u32[]{:S(2)}, u32[]{:S(2)}) collective-permute-start(bf16[2,32,4096]{2,1,0:T(8,128)(2,1)S(1)} %pad_maximum_fusion.12), channel_id=1, source_target_pairs={{0,1},{1,0},{2,3},{3,2},{4,5},{5,4},{6,7},{7,6},{8,9},{9,8},{10,11... | collective-permute-start | bytes 1572872 | tf_op jit(solution)/shard_map/ppermute | solution.py:74
  86.4 13.4 %collective-permute-start.18 = (bf16[3,32,4096]{2,1,0:T(8,128)(2,1)S(1)}, bf16[3,32,4096]{2,1,0:T(8,128)(2,1)}, u32[]{:S(2)}, u32[]{:S(2)}) collective-permute-start(bf16[3,32,4096]{2,1,0:T(8,128)(2,1)S(1)} %slice_bitcast_fusion.2), channel_id=1, source_target_pairs={{0,16},{4,12},{8,24},{12,4},{16,0},{20,28},{24,8},{28,20},{1,17},{... | collective-permute-start | bytes 2359304 | tf_op jit(solution)/shard_map/ppermute | solution.py:64
  97.4 11.3 %collective-permute-start.17 = (bf16[2,3,32,4096]{3,2,1,0:T(8,128)(2,1)}, bf16[2,3,32,4096]{3,2,1,0:T(8,128)(2,1)}, u32[]{:S(2)}, u32[]{:S(2)}) collective-permute-start(bf16[2,3,32,4096]{3,2,1,0:T(8,128)(2,1)} %collective-permute-done.15.refs_4_), channel_id=1, source_target_pairs={{0,4},{4,0},{8,12},{12,8},{16,20},{20,16},{24,28},{28,24},{1,5},{5... | collective-permute-start | bytes 4718600 | tf_op jit(solution)/shard_map/ppermute | solution.py:56
  103.9 15.6 %collective-permute-start.23 = (bf16[512,1024]{1,0:T(8,128)(2,1)}, bf16[512,1024]{1,0:T(8,128)(2,1)S(1)}, u32[]{:S(2)}, u32[]{:S(2)}) collective-permute-start(bf16[512,1024]{1,0:T(8,128)(2,1)} %add_convert_fusion.8), channel_id=1, source_target_pairs={{0,4},{4,0},{8,12},{12,8},{16,20},{20,16},{24,28},{28,24},{1,5},{5... | collective-permute-start | bytes 3145736 | tf_op jit(solution)/shard_map/ppermute | solution.py:56
  104.0 15.4 %collective-permute-start.24 = (bf16[128,1024]{1,0:T(8,128)(2,1)}, bf16[128,1024]{1,0:T(8,128)(2,1)S(1)}, u32[]{:S(2)}, u32[]{:S(2)}) collective-permute-start(bf16[128,1024]{1,0:T(8,128)(2,1)} %constant_dynamic-slice_fusion.10), channel_id=1, source_target_pairs={{0,2},{1,3},{2,0},{3,1},{4,6},{5,7},{6,4},{7,5},{8,10},{9,11},{10,... | collective-permute-start | bytes 786440 | tf_op jit(solution)/shard_map/ppermute | solution.py:74
  106.9 25.2 %collective-permute-start.26 = (bf16[2,3,32,4096]{3,2,1,0:T(8,128)(2,1)S(1)}, bf16[2,3,32,4096]{3,2,1,0:T(8,128)(2,1)}, u32[]{:S(2)}, u32[]{:S(2)}) collective-permute-start(bf16[2,3,32,4096]{3,2,1,0:T(8,128)(2,1)S(1)} %pad_maximum_fusion.2), channel_id=1, source_target_pairs={{0,8},{4,20},{8,0},{12,28},{16,24},{20,4},{24,16},{28,12},{1,9},{5... | collective-permute-start | bytes 4718600 | tf_op jit(solution)/shard_map/ppermute | solution.py:60
  119.4 14.9 %collective-permute-start.25 = (bf16[2,128,1024]{2,1,0:T(8,128)(2,1)S(1)}, bf16[2,128,1024]{2,1,0:T(8,128)(2,1)S(1)}, u32[]{:S(2)}, u32[]{:S(2)}) collective-permute-start(bf16[2,128,1024]{2,1,0:T(8,128)(2,1)S(1)} %pad_maximum_fusion.13), channel_id=1, source_target_pairs={{0,1},{1,0},{2,3},{3,2},{4,5},{5,4},{6,7},{7,6},{8,9},{9,8},{10,11... | collective-permute-start | bytes 1572872 | tf_op jit(solution)/shard_map/ppermute | solution.py:74
  132.1 18.7 %collective-permute-start.27 = (bf16[512,1024]{1,0:T(8,128)(2,1)}, bf16[512,1024]{1,0:T(8,128)(2,1)}, u32[]{:S(2)}, u32[]{:S(2)}) collective-permute-start(bf16[512,1024]{1,0:T(8,128)(2,1)} %get-tuple-element.301), channel_id=1, source_target_pairs={{0,4},{4,0},{8,12},{12,8},{16,20},{20,16},{24,28},{28,24},{1,5},{5... | collective-permute-start | bytes 3145736 | tf_op jit(solution)/shard_map/ppermute | solution.py:56
  135.6 9.5 %collective-permute-start.31 = (bf16[3,128,1024]{2,1,0:T(8,128)(2,1)}, bf16[3,128,1024]{2,1,0:T(8,128)(2,1)}, u32[]{:S(2)}, u32[]{:S(2)}) collective-permute-start(bf16[3,128,1024]{2,1,0:T(8,128)(2,1)} %get-tuple-element.323.refs_1_), channel_id=1, source_target_pairs={{0,4},{4,0},{8,12},{12,8},{16,20},{20,16},{24,28},{28,24},{1,5},{5... | collective-permute-start | bytes 2359304 | tf_op jit(solution)/shard_map/ppermute | solution.py:56
  136.0 12.3 %collective-permute-start.30 = (bf16[3,32,4096]{2,1,0:T(8,128)(2,1)}, bf16[3,32,4096]{2,1,0:T(8,128)(2,1)}, u32[]{:S(2)}, u32[]{:S(2)}) collective-permute-start(bf16[3,32,4096]{2,1,0:T(8,128)(2,1)} %slice_bitcast_fusion.1), channel_id=1, source_target_pairs={{0,16},{4,12},{8,24},{12,4},{16,0},{20,28},{24,8},{28,20},{1,17},{... | collective-permute-start | bytes 2359304 | tf_op jit(solution)/shard_map/ppermute | solution.py:64
  137.6 12.2 %collective-permute-start.29 = (bf16[2,3,32,4096]{3,2,1,0:T(8,128)(2,1)}, bf16[2,3,32,4096]{3,2,1,0:T(8,128)(2,1)}, u32[]{:S(2)}, u32[]{:S(2)}) collective-permute-start(bf16[2,3,32,4096]{3,2,1,0:T(8,128)(2,1)} %collective-permute-done.26.refs_3_), channel_id=1, source_target_pairs={{0,4},{4,0},{8,12},{12,8},{16,20},{20,16},{24,28},{28,24},{1,5},{5... | collective-permute-start | bytes 4718600 | tf_op jit(solution)/shard_map/ppermute | solution.py:56
  142.0 8.8 %collective-permute-start.28 = (bf16[512,1024]{1,0:T(8,128)(2,1)S(1)}, bf16[512,1024]{1,0:T(8,128)(2,1)}, u32[]{:S(2)}, u32[]{:S(2)}) collective-permute-start(bf16[512,1024]{1,0:T(8,128)(2,1)S(1)} %add_convert_fusion.7.rows_ref), channel_id=1, source_target_pairs={{0,4},{4,0},{8,12},{12,8},{16,20},{20,16},{24,28},{28,24},{1,5},{5... | collective-permute-start | bytes 3145736 | tf_op jit(solution)/shard_map/ppermute | solution.py:56
  148.3 20.4 %collective-permute-start.34 = (bf16[2,3,128,1024]{3,2,1,0:T(8,128)(2,1)S(1)}, bf16[2,3,128,1024]{3,2,1,0:T(8,128)(2,1)S(1)}, u32[]{:S(2)}, u32[]{:S(2)}) collective-permute-start(bf16[2,3,128,1024]{3,2,1,0:T(8,128)(2,1)S(1)} %pad_maximum_fusion.3), channel_id=1, source_target_pairs={{0,8},{4,20},{8,0},{12,28},{16,24},{20,4},{24,16},{28,12},{1,9},{5... | collective-permute-start | bytes 4718600 | tf_op jit(solution)/shard_map/ppermute | solution.py:60
  168.8 12.1 %collective-permute-start.36 = (bf16[3,128,1024]{2,1,0:T(8,128)(2,1)S(1)}, bf16[3,128,1024]{2,1,0:T(8,128)(2,1)S(1)}, u32[]{:S(2)}, u32[]{:S(2)}) collective-permute-start(bf16[3,128,1024]{2,1,0:T(8,128)(2,1)S(1)} %slice_bitcast_fusion), channel_id=1, source_target_pairs={{0,16},{4,12},{8,24},{12,4},{16,0},{20,28},{24,8},{28,20},{1,17},{... | collective-permute-start | bytes 2359304 | tf_op jit(solution)/shard_map/ppermute | solution.py:64
  170.4 11.5 %collective-permute-start.35 = (bf16[2,3,128,1024]{3,2,1,0:T(8,128)(2,1)S(1)}, bf16[2,3,128,1024]{3,2,1,0:T(8,128)(2,1)S(1)}, u32[]{:S(2)}, u32[]{:S(2)}) collective-permute-start(bf16[2,3,128,1024]{3,2,1,0:T(8,128)(2,1)S(1)} %collective-permute-done.34.refs_3_), channel_id=1, source_target_pairs={{0,4},{4,0},{8,12},{12,8},{16,20},{20,16},{24,28},{28,24},{1,5},{5... | collective-permute-start | bytes 4718600 | tf_op jit(solution)/shard_map/ppermute | solution.py:56
  170.4 29.2 %collective-permute-start.33 = (bf16[512,4096]{1,0:T(8,128)(2,1)S(1)}, bf16[512,4096]{1,0:T(8,128)(2,1)}, u32[]{:S(2)}, u32[]{:S(2)}) collective-permute-start(bf16[512,4096]{1,0:T(8,128)(2,1)S(1)} %get-tuple-element.405), channel_id=1, source_target_pairs={{0,4},{4,0},{8,12},{12,8},{16,20},{20,16},{24,28},{28,24},{1,5},{5... | collective-permute-start | bytes 12582920 | tf_op jit(solution)/shard_map/ppermute | solution.py:56
  181.4 18.2 %collective-permute-start.38 = (bf16[512,512]{1,0:T(8,128)(2,1)S(1)}, bf16[512,512]{1,0:T(8,128)(2,1)S(1)}, u32[]{:S(2)}, u32[]{:S(2)}) collective-permute-start(bf16[512,512]{1,0:T(8,128)(2,1)S(1)} %copy-done.83), channel_id=1, source_target_pairs={{0,4},{4,0},{8,12},{12,8},{16,20},{20,16},{24,28},{28,24},{1,5},{5... | collective-permute-start | bytes 1572872 | tf_op jit(solution)/shard_map/ppermute | solution.py:56
  199.1 23.3 %collective-permute-start.41 = (bf16[512,2048]{1,0:T(8,128)(2,1)}, bf16[512,2048]{1,0:T(8,128)(2,1)}, u32[]{:S(2)}, u32[]{:S(2)}) collective-permute-start(bf16[512,2048]{1,0:T(8,128)(2,1)} %get-tuple-element.332), channel_id=1, source_target_pairs={{0,4},{4,0},{8,12},{12,8},{16,20},{20,16},{24,28},{28,24},{1,5},{5... | collective-permute-start | bytes 6291464 | tf_op jit(solution)/shard_map/ppermute | solution.py:56
  210.5 26.4 %collective-permute-start.39 = (bf16[4,2,256,512]{3,2,1,0:T(8,128)(2,1)}, bf16[4,2,256,512]{3,2,1,0:T(8,128)(2,1)}, u32[]{:S(2)}, u32[]{:S(2)}) collective-permute-start(bf16[4,2,256,512]{3,2,1,0:T(8,128)(2,1)} %pick_first.4), channel_id=1, source_target_pairs={{0,8},{4,20},{8,0},{12,28},{16,24},{20,4},{24,16},{28,12},{1,9},{5... | collective-permute-start | bytes 6291464 | tf_op jit(solution)/shard_map/ppermute | solution.py:60
  219.2 10.3 %collective-permute-start.40 = (bf16[512,512]{1,0:T(8,128)(2,1)S(1)}, bf16[512,512]{1,0:T(8,128)(2,1)S(1)}, u32[]{:S(2)}, u32[]{:S(2)}) collective-permute-start(bf16[512,512]{1,0:T(8,128)(2,1)S(1)} %get-tuple-element.486), channel_id=1, source_target_pairs={{0,4},{4,0},{8,12},{12,8},{16,20},{20,16},{24,28},{28,24},{1,5},{5... | collective-permute-start | bytes 1572872 | tf_op jit(solution)/shard_map/ppermute | solution.py:56
  220.5 21.3 %collective-permute-start.43 = (bf16[2,256,256]{2,1,0:T(8,128)(2,1)}, bf16[2,256,256]{2,1,0:T(8,128)(2,1)}, u32[]{:S(2)}, u32[]{:S(2)}) collective-permute-start(bf16[2,256,256]{2,1,0:T(8,128)(2,1)} %dynamic-slice_bitcast_fusion), channel_id=1, source_target_pairs={{0,1},{1,0},{2,3},{3,2},{4,5},{5,4},{6,7},{7,6},{8,9},{9,8},{10,11... | collective-permute-start | bytes 786440 | tf_op jit(solution)/shard_map/ppermute | solution.py:74
  234.3 43.0 %collective-permute-start.47 = (bf16[4,2,64,2560]{3,2,1,0:T(8,128)(2,1)S(1)}, bf16[4,2,64,2560]{3,2,1,0:T(8,128)(2,1)S(1)}, u32[]{:S(2)}, u32[]{:S(2)}) collective-permute-start(bf16[4,2,64,2560]{3,2,1,0:T(8,128)(2,1)S(1)} %pick_first.5), channel_id=1, source_target_pairs={{0,8},{4,20},{8,0},{12,28},{16,24},{20,4},{24,16},{28,12},{1,9},{5... | collective-permute-start | bytes 7864328 | tf_op jit(solution)/shard_map/ppermute | solution.py:60
  240.3 26.2 %collective-permute-start.42 = (bf16[4,256,512]{2,1,0:T(8,128)(2,1)S(1)}, bf16[4,256,512]{2,1,0:T(8,128)(2,1)S(1)}, u32[]{:S(2)}, u32[]{:S(2)}) collective-permute-start(bf16[4,256,512]{2,1,0:T(8,128)(2,1)S(1)} %get-tuple-element.349), channel_id=1, source_target_pairs={{0,16},{4,12},{8,24},{12,4},{16,0},{20,28},{24,8},{28,20},{1,17},{... | collective-permute-start | bytes 3145736 | tf_op jit(solution)/shard_map/ppermute | solution.py:64
  261.2 19.7 %collective-permute-start.45 = (bf16[512,1536]{1,0:T(8,128)(2,1)S(1)}, bf16[512,1536]{1,0:T(8,128)(2,1)S(1)}, u32[]{:S(2)}, u32[]{:S(2)}) collective-permute-start(bf16[512,1536]{1,0:T(8,128)(2,1)S(1)} %get-tuple-element.482), channel_id=1, source_target_pairs={{0,4},{4,0},{8,12},{12,8},{16,20},{20,16},{24,28},{28,24},{1,5},{5... | collective-permute-start | bytes 4718600 | tf_op jit(solution)/shard_map/ppermute | solution.py:56
  261.3 19.5 %collective-permute-start.46 = (bf16[256,256]{1,0:T(8,128)(2,1)S(1)}, bf16[256,256]{1,0:T(8,128)(2,1)S(1)}, u32[]{:S(2)}, u32[]{:S(2)}) collective-permute-start(bf16[256,256]{1,0:T(8,128)(2,1)S(1)} %dynamic-slice_bitcast_fusion.1), channel_id=1, source_target_pairs={{0,2},{1,3},{2,0},{3,1},{4,6},{5,7},{6,4},{7,5},{8,10},{9,11},{10,... | collective-permute-start | bytes 393224 | tf_op jit(solution)/shard_map/ppermute | solution.py:74
  267.3 24.5 %collective-permute-start.44 = (bf16[2,256,512]{2,1,0:T(8,128)(2,1)S(1)}, bf16[2,256,512]{2,1,0:T(8,128)(2,1)S(1)}, u32[]{:S(2)}, u32[]{:S(2)}) collective-permute-start(bf16[2,256,512]{2,1,0:T(8,128)(2,1)S(1)} %get-tuple-element.358), channel_id=1, source_target_pairs={{0,1},{1,0},{2,3},{3,2},{4,5},{5,4},{6,7},{7,6},{8,9},{9,8},{10,11... | collective-permute-start | bytes 1572872 | tf_op jit(solution)/shard_map/ppermute | solution.py:74
  279.6 20.6 %collective-permute-start.49 = (bf16[4,64,2560]{2,1,0:T(8,128)(2,1)}, bf16[4,64,2560]{2,1,0:T(8,128)(2,1)}, u32[]{:S(2)}, u32[]{:S(2)}) collective-permute-start(bf16[4,64,2560]{2,1,0:T(8,128)(2,1)} %get-tuple-element.363), channel_id=1, source_target_pairs={{0,16},{4,12},{8,24},{12,4},{16,0},{20,28},{24,8},{28,20},{1,17},{... | collective-permute-start | bytes 3932168 | tf_op jit(solution)/shard_map/ppermute | solution.py:64
  293.1 24.3 %collective-permute-start.48 = (bf16[1,256,512]{2,1,0:T(8,128)(2,1)}, bf16[1,256,512]{2,1,0:T(8,128)(2,1)}, u32[]{:S(2)}, u32[]{:S(2)}) collective-permute-start(bf16[1,256,512]{2,1,0:T(8,128)(2,1)} %get-tuple-element.371), channel_id=1, source_target_pairs={{0,2},{1,3},{2,0},{3,1},{4,6},{5,7},{6,4},{7,5},{8,10},{9,11},{10,... | collective-permute-start | bytes 786440 | tf_op jit(solution)/shard_map/ppermute | solution.py:74
  294.0 28.8 %collective-permute-start.52 = (bf16[4,2,64,1536]{3,2,1,0:T(8,128)(2,1)S(1)}, bf16[4,2,64,1536]{3,2,1,0:T(8,128)(2,1)}, u32[]{:S(2)}, u32[]{:S(2)}) collective-permute-start(bf16[4,2,64,1536]{3,2,1,0:T(8,128)(2,1)S(1)} %pick_first.6), channel_id=1, source_target_pairs={{0,8},{4,20},{8,0},{12,28},{16,24},{20,4},{24,16},{28,12},{1,9},{5... | collective-permute-start | bytes 4718600 | tf_op jit(solution)/shard_map/ppermute | solution.py:60
  296.8 30.0 %collective-permute-start.51 = (bf16[512,512]{1,0:T(8,128)(2,1)}, bf16[512,512]{1,0:T(8,128)(2,1)}, u32[]{:S(2)}, u32[]{:S(2)}) collective-permute-start(bf16[512,512]{1,0:T(8,128)(2,1)} %get-tuple-element.483), channel_id=1, source_target_pairs={{0,4},{4,0},{8,12},{12,8},{16,20},{20,16},{24,28},{28,24},{1,5},{5... | collective-permute-start | bytes 1572872 | tf_op jit(solution)/shard_map/ppermute | solution.py:56
  302.3 18.5 %collective-permute-start.53 = (bf16[2,64,2560]{2,1,0:T(8,128)(2,1)S(1)}, bf16[2,64,2560]{2,1,0:T(8,128)(2,1)S(1)}, u32[]{:S(2)}, u32[]{:S(2)}) collective-permute-start(bf16[2,64,2560]{2,1,0:T(8,128)(2,1)S(1)} %get-tuple-element.375), channel_id=1, source_target_pairs={{0,1},{1,0},{2,3},{3,2},{4,5},{5,4},{6,7},{7,6},{8,9},{9,8},{10,11... | collective-permute-start | bytes 1966088 | tf_op jit(solution)/shard_map/ppermute | solution.py:74
  317.6 11.9 %collective-permute-start.54 = (bf16[2,2,80,512]{3,2,1,0:T(8,128)(2,1)S(1)}, bf16[2,2,80,512]{3,2,1,0:T(8,128)(2,1)S(1)}, u32[]{:S(2)}, u32[]{:S(2)}) collective-permute-start(bf16[2,2,80,512]{3,2,1,0:T(8,128)(2,1)S(1)} %fusion.6), channel_id=1, source_target_pairs={{0,4},{4,0},{8,12},{12,8},{16,20},{20,16},{24,28},{28,24},{1,5},{5... | collective-permute-start | bytes 983048 | tf_op jit(solution)/shard_map/ppermute | solution.py:56
  318.9 29.1 %collective-permute-start.50 = (bf16[256,512]{1,0:T(8,128)(2,1)S(1)}, bf16[256,512]{1,0:T(8,128)(2,1)S(1)}, u32[]{:S(2)}, u32[]{:S(2)}) collective-permute-start(bf16[256,512]{1,0:T(8,128)(2,1)S(1)} %bitcast.196), channel_id=1, source_target_pairs={{0,4},{4,0},{8,12},{12,8},{16,20},{20,16},{24,28},{28,24},{1,5},{5... | collective-permute-start | bytes 786440 | tf_op jit(solution)/shard_map/ppermute | solution.py:56
  321.6 23.9 %collective-permute-start.56 = (bf16[1,64,2560]{2,1,0:T(8,128)(2,1)S(1)}, bf16[1,64,2560]{2,1,0:T(8,128)(2,1)S(1)}, u32[]{:S(2)}, u32[]{:S(2)}) collective-permute-start(bf16[1,64,2560]{2,1,0:T(8,128)(2,1)S(1)} %get-tuple-element.382), channel_id=1, source_target_pairs={{0,2},{1,3},{2,0},{3,1},{4,6},{5,7},{6,4},{7,5},{8,10},{9,11},{10,... | collective-permute-start | bytes 983048 | tf_op jit(solution)/shard_map/ppermute | solution.py:74
  325.8 17.8 %collective-permute-start.57 = (bf16[4,64,1536]{2,1,0:T(8,128)(2,1)S(1)}, bf16[4,64,1536]{2,1,0:T(8,128)(2,1)S(1)}, u32[]{:S(2)}, u32[]{:S(2)}) collective-permute-start(bf16[4,64,1536]{2,1,0:T(8,128)(2,1)S(1)} %get-tuple-element.384), channel_id=1, source_target_pairs={{0,16},{4,12},{8,24},{12,4},{16,0},{20,28},{24,8},{28,20},{1,17},{... | collective-permute-start | bytes 2359304 | tf_op jit(solution)/shard_map/ppermute | solution.py:64
  329.8 15.9 %collective-permute-start.55 = (bf16[1,2,336,512]{3,2,1,0:T(8,128)(2,1)S(1)}, bf16[1,2,336,512]{3,2,1,0:T(8,128)(2,1)S(1)}, u32[]{:S(2)}, u32[]{:S(2)}) collective-permute-start(bf16[1,2,336,512]{3,2,1,0:T(8,128)(2,1)S(1)} %pick_first.7), channel_id=1, source_target_pairs={{0,8},{4,20},{8,0},{12,28},{16,24},{20,4},{24,16},{28,12},{1,9},{5... | collective-permute-start | bytes 2064392 | tf_op jit(solution)/shard_map/ppermute | solution.py:60
  345.6 21.1 %collective-permute-start.65 = (bf16[64,2560]{1,0:T(8,128)(2,1)S(1)}, bf16[64,2560]{1,0:T(8,128)(2,1)S(1)}, u32[]{:S(2)}, u32[]{:S(2)}) collective-permute-start(bf16[64,2560]{1,0:T(8,128)(2,1)S(1)} %bitcast.193), channel_id=1, source_target_pairs={{0,4},{4,0},{8,12},{12,8},{16,20},{20,16},{24,28},{28,24},{1,5},{5... | collective-permute-start | bytes 983048 | tf_op jit(solution)/shard_map/ppermute | solution.py:56
  346.4 10.6 %collective-permute-start.59 = (bf16[1,336,512]{2,1,0:T(8,128)(2,1)S(1)}, bf16[1,336,512]{2,1,0:T(8,128)(2,1)S(1)}, u32[]{:S(2)}, u32[]{:S(2)}) collective-permute-start(bf16[1,336,512]{2,1,0:T(8,128)(2,1)S(1)} %get-tuple-element.397), channel_id=1, source_target_pairs={{0,16},{4,12},{8,24},{12,4},{16,0},{20,28},{24,8},{28,20},{1,17},{... | collective-permute-start | bytes 1032200 | tf_op jit(solution)/shard_map/ppermute | solution.py:64
  348.1 10.8 %collective-permute-start.58 = (bf16[2,256,512]{2,1,0:T(8,128)(2,1)S(1)}, bf16[2,256,512]{2,1,0:T(8,128)(2,1)S(1)}, u32[]{:S(2)}, u32[]{:S(2)}) collective-permute-start(bf16[2,256,512]{2,1,0:T(8,128)(2,1)S(1)} %pad_maximum_fusion.14), channel_id=1, source_target_pairs={{0,8},{4,20},{8,0},{12,28},{16,24},{20,4},{24,16},{28,12},{1,9},{5... | collective-permute-start | bytes 1572872 | tf_op jit(solution)/shard_map/ppermute | solution.py:60
  353.4 12.6 %collective-permute-start.61 = (bf16[1,64,1536]{2,1,0:T(8,128)(2,1)S(1)}, bf16[1,64,1536]{2,1,0:T(8,128)(2,1)S(1)}, u32[]{:S(2)}, u32[]{:S(2)}) collective-permute-start(bf16[1,64,1536]{2,1,0:T(8,128)(2,1)S(1)} %get-tuple-element.401), channel_id=1, source_target_pairs={{0,2},{1,3},{2,0},{3,1},{4,6},{5,7},{6,4},{7,5},{8,10},{9,11},{10,... | collective-permute-start | bytes 589832 | tf_op jit(solution)/shard_map/ppermute | solution.py:74
  357.2 9.9 %collective-permute-start.64 = (bf16[208,512]{1,0:T(8,128)(2,1)S(1)}, bf16[208,512]{1,0:T(8,128)(2,1)S(1)}, u32[]{:S(2)}, u32[]{:S(2)}) collective-permute-start(bf16[208,512]{1,0:T(8,128)(2,1)S(1)} %pad_maximum_fusion.20), channel_id=1, source_target_pairs={{0,1},{1,0},{2,3},{3,2},{4,5},{5,4},{6,7},{7,6},{8,9},{9,8},{10,11... | collective-permute-start | bytes 638984 | tf_op jit(solution)/shard_map/ppermute | solution.py:74
  358.9 10.3 %collective-permute-start.63 = (bf16[256,512]{1,0:T(8,128)(2,1)S(1)}, bf16[256,512]{1,0:T(8,128)(2,1)S(1)}, u32[]{:S(2)}, u32[]{:S(2)}) collective-permute-start(bf16[256,512]{1,0:T(8,128)(2,1)S(1)} %slice_bitcast_fusion.4), channel_id=1, source_target_pairs={{0,16},{4,12},{8,24},{12,4},{16,0},{20,28},{24,8},{28,20},{1,17},{... | collective-permute-start | bytes 786440 | tf_op jit(solution)/shard_map/ppermute | solution.py:64
  360.5 21.5 %collective-permute-start.71 = (bf16[2,256,512]{2,1,0:T(8,128)(2,1)S(1)}, bf16[2,256,512]{2,1,0:T(8,128)(2,1)S(1)}, u32[]{:S(2)}, u32[]{:S(2)}) collective-permute-start(bf16[2,256,512]{2,1,0:T(8,128)(2,1)S(1)} %collective-permute-done.58.refs_2_), channel_id=1, source_target_pairs={{0,4},{4,0},{8,12},{12,8},{16,20},{20,16},{24,28},{28,24},{1,5},{5... | collective-permute-start | bytes 1572872 | tf_op jit(solution)/shard_map/ppermute | solution.py:56
  366.7 10.7 %collective-permute-start.68 = (bf16[2,64,2560]{2,1,0:T(8,128)(2,1)S(1)}, bf16[2,64,2560]{2,1,0:T(8,128)(2,1)S(1)}, u32[]{:S(2)}, u32[]{:S(2)}) collective-permute-start(bf16[2,64,2560]{2,1,0:T(8,128)(2,1)S(1)} %pad_maximum_fusion.9), channel_id=1, source_target_pairs={{0,8},{4,20},{8,0},{12,28},{16,24},{20,4},{24,16},{28,12},{1,9},{5... | collective-permute-start | bytes 1966088 | tf_op jit(solution)/shard_map/ppermute | solution.py:60
  367.3 9.9 %collective-permute-start.66 = (bf16[144,512]{1,0:T(8,128)(2,1)S(1)}, bf16[144,512]{1,0:T(8,128)(2,1)S(1)}, u32[]{:S(2)}, u32[]{:S(2)}) collective-permute-start(bf16[144,512]{1,0:T(8,128)(2,1)S(1)} %pad_maximum_fusion.22), channel_id=1, source_target_pairs={{0,2},{1,3},{2,0},{3,1},{4,6},{5,7},{6,4},{7,5},{8,10},{9,11},{10,... | collective-permute-start | bytes 442376 | tf_op jit(solution)/shard_map/ppermute | solution.py:74
  369.2 12.7 %collective-permute-start.72 = (bf16[256,512]{1,0:T(8,128)(2,1)S(1)}, bf16[256,512]{1,0:T(8,128)(2,1)S(1)}, u32[]{:S(2)}, u32[]{:S(2)}) collective-permute-start(bf16[256,512]{1,0:T(8,128)(2,1)S(1)} %collective-permute-done.63.refs_4_), channel_id=1, source_target_pairs={{0,4},{4,0},{8,12},{12,8},{16,20},{20,16},{24,28},{28,24},{1,5},{5... | collective-permute-start | bytes 786440 | tf_op jit(solution)/shard_map/ppermute | solution.py:56
  369.3 12.4 %collective-permute-start.73 = (bf16[2,64,1536]{2,1,0:T(8,128)(2,1)S(1)}, bf16[2,64,1536]{2,1,0:T(8,128)(2,1)S(1)}, u32[]{:S(2)}, u32[]{:S(2)}) collective-permute-start(bf16[2,64,1536]{2,1,0:T(8,128)(2,1)S(1)} %pad_maximum_fusion.15), channel_id=1, source_target_pairs={{0,8},{4,20},{8,0},{12,28},{16,24},{20,4},{24,16},{28,12},{1,9},{5... | collective-permute-start | bytes 1179656 | tf_op jit(solution)/shard_map/ppermute | solution.py:60
  377.4 18.8 %collective-permute-start.76 = (bf16[2,64,2560]{2,1,0:T(8,128)(2,1)S(1)}, bf16[2,64,2560]{2,1,0:T(8,128)(2,1)S(1)}, u32[]{:S(2)}, u32[]{:S(2)}) collective-permute-start(bf16[2,64,2560]{2,1,0:T(8,128)(2,1)S(1)} %collective-permute-done.68.refs_2_), channel_id=1, source_target_pairs={{0,4},{4,0},{8,12},{12,8},{16,20},{20,16},{24,28},{28,24},{1,5},{5... | collective-permute-start | bytes 1966088 | tf_op jit(solution)/shard_map/ppermute | solution.py:56
  378.7 9.4 %collective-permute-start.70 = (bf16[64,2560]{1,0:T(8,128)(2,1)S(1)}, bf16[64,2560]{1,0:T(8,128)(2,1)S(1)}, u32[]{:S(2)}, u32[]{:S(2)}) collective-permute-start(bf16[64,2560]{1,0:T(8,128)(2,1)S(1)} %slice_bitcast_fusion.3), channel_id=1, source_target_pairs={{0,16},{4,12},{8,24},{12,4},{16,0},{20,28},{24,8},{28,20},{1,17},{... | collective-permute-start | bytes 983048 | tf_op jit(solution)/shard_map/ppermute | solution.py:64
  381.7 8.9 %collective-permute-start.69 = (bf16[2,144,512]{2,1,0:T(8,128)(2,1)S(1)}, bf16[2,144,512]{2,1,0:T(8,128)(2,1)S(1)}, u32[]{:S(2)}, u32[]{:S(2)}) collective-permute-start(bf16[2,144,512]{2,1,0:T(8,128)(2,1)S(1)} %pad_maximum_fusion.16), channel_id=1, source_target_pairs={{0,8},{4,20},{8,0},{12,28},{16,24},{20,4},{24,16},{28,12},{1,9},{5... | collective-permute-start | bytes 884744 | tf_op jit(solution)/shard_map/ppermute | solution.py:60
  388.1 8.1 %collective-permute-start.77 = (bf16[64,2560]{1,0:T(8,128)(2,1)S(1)}, bf16[64,2560]{1,0:T(8,128)(2,1)S(1)}, u32[]{:S(2)}, u32[]{:S(2)}) collective-permute-start(bf16[64,2560]{1,0:T(8,128)(2,1)S(1)} %collective-permute-done.70.refs_4_), channel_id=1, source_target_pairs={{0,4},{4,0},{8,12},{12,8},{16,20},{20,16},{24,28},{28,24},{1,5},{5... | collective-permute-start | bytes 983048 | tf_op jit(solution)/shard_map/ppermute | solution.py:56
  390.5 9.4 %collective-permute-start.80 = (bf16[2,64,1536]{2,1,0:T(8,128)(2,1)S(1)}, bf16[2,64,1536]{2,1,0:T(8,128)(2,1)S(1)}, u32[]{:S(2)}, u32[]{:S(2)}) collective-permute-start(bf16[2,64,1536]{2,1,0:T(8,128)(2,1)S(1)} %collective-permute-done.73.refs_2_), channel_id=1, source_target_pairs={{0,4},{4,0},{8,12},{12,8},{16,20},{20,16},{24,28},{28,24},{1,5},{5... | collective-permute-start | bytes 1179656 | tf_op jit(solution)/shard_map/ppermute | solution.py:56
  390.6 11.8 %collective-permute-start.74 = (bf16[2,144,512]{2,1,0:T(8,128)(2,1)S(1)}, bf16[2,144,512]{2,1,0:T(8,128)(2,1)S(1)}, u32[]{:S(2)}, u32[]{:S(2)}) collective-permute-start(bf16[2,144,512]{2,1,0:T(8,128)(2,1)S(1)} %collective-permute-done.69.refs_2_), channel_id=1, source_target_pairs={{0,4},{4,0},{8,12},{12,8},{16,20},{20,16},{24,28},{28,24},{1,5},{5... | collective-permute-start | bytes 884744 | tf_op jit(solution)/shard_map/ppermute | solution.py:56
  (129 other events, 1191.1 us)
